TPU v7x, 256 devices: a whole 4x4x8 slice. The times are simulated.
256 devices in a mesh: row: 16 (over y_hi, x, core), col: 16 (over y_lo, z).
Axes of the slice: x: 4, y: 4 (y_hi: 2, y_lo: 2; y = y_hi * 2 + y_lo), z: 8, core: 2. Of those that a mesh axis runs over, the one named last changes fastest.
Arguments:
- features: bfloat16 [256, 256, 4, 128], P('row', 'col'), may hold values from -6 to 6
- conv_first: bfloat16 [3, 3, 128, 128], replicated, may hold values from -0.1875 to 0.1875
- conv_second: bfloat16 [3, 3, 128, 128], replicated, may hold values from -0.1875 to 0.1875
- coarse_conv: bfloat16 [3, 3, 128, 256], P(None, None, None, 'row'), may hold values from -0.1875 to 0.1875
- coarse_proj: bfloat16 [256, 128], P('row'), may hold values from -0.375 to 0.375
- cotangent: bfloat16 [256, 256, 4, 128], P('row', 'col'), may hold values from -6 to 6
Outputs:
- blended: bfloat16 [256, 256, 4, 128], P('row', 'col')
- feature_grad: bfloat16 [256, 256, 4, 128], P('row', 'col')
- first_grad: float32 [3, 3, 128, 128], replicated
- second_grad: float32 [3, 3, 128, 128], replicated
- coarse_conv_grad: float32 [3, 3, 128, 256], P(None, None, None, 'row')
- coarse_proj_grad: float32 [256, 128], P('row')
All inputs are finite; a program needn't handle non-finite values.
Results may differ from a plain program's by a relative error of at most 0.015.
Values may be sent and summed in bfloat16 or wider, within the bound.
No kernel may reach another device: no remote copies, remote signals or barrier semaphores. Data moves between devices by JAX's collectives and lax.ppermute only.
A program may use at most 64 MiB of HBM per device.

v0:
```python
import jax
import jax.numpy as jnp
from jax import lax
from jax.sharding import PartitionSpec as P


def padded_2(value, sides, width):
    for axis, dim in sides:
        count, length = (lax.axis_size(axis), value.shape[dim])
        up = [(i, (i + 1) % count) for i in range(count - 1)]
        down = [(j, i) for i, j in up]
        last = lax.slice_in_dim(value, length - width, length, axis=dim)
        first = lax.slice_in_dim(value, 0, width, axis=dim)
        before = lax.ppermute(last, axis, up)
        after = lax.ppermute(first, axis, down)
        value = jnp.concatenate([before, value, after], axis=dim)
    return value


def silu_slope(value):
    sigma = jax.nn.sigmoid(value)
    return sigma * (1.0 + value * (1.0 - sigma))


def convolve(padded, weight):
    height, breadth = (padded.shape[0] - 2, padded.shape[1] - 2)
    summed = jnp.zeros((height, breadth, padded.shape[2], weight.shape[3]), jnp.float32)
    for row_off in range(3):
        for col_off in range(3):
            summed = summed + jnp.einsum(
                "hwbc,cd->hwbd",
                padded[row_off : row_off + height, col_off : col_off + breadth],
                weight[row_off, col_off],
                preferred_element_type=jnp.float32,
            )
    return summed


def transposed(padded, weight):
    height, breadth = (padded.shape[0] - 2, padded.shape[1] - 2)
    summed = jnp.zeros((height, breadth, padded.shape[2], weight.shape[2]), jnp.float32)
    for row_off in range(3):
        for col_off in range(3):
            summed = summed + jnp.einsum(
                "hwbd,cd->hwbc",
                padded[2 - row_off : 2 - row_off + height, 2 - col_off : 2 - col_off + breadth],
                weight[row_off, col_off],
                preferred_element_type=jnp.float32,
            )
    return summed


def weight_grad(padded, grad):
    height, breadth = (grad.shape[0], grad.shape[1])
    pieces = []
    for row_off in range(3):
        for col_off in range(3):
            pieces.append(
                jnp.einsum(
                    "hwbc,hwbd->cd",
                    padded[row_off : row_off + height, col_off : col_off + breadth],
                    grad,
                    preferred_element_type=jnp.float32,
                )
            )
    return jnp.stack(pieces).reshape((3, 3) + pieces[0].shape)


def block_sum(value):
    height, breadth, images, chans = value.shape
    return (
        value.astype(jnp.float32)
        .reshape(height // 2, 2, breadth // 2, 2, images, chans)
        .sum(axis=(1, 3))
    )


def enlarge(value):
    return jnp.repeat(jnp.repeat(value, 2, axis=0), 2, axis=1)


def tile_edges(field):
    return padded_2(field, (("row", 0), ("col", 1)), 1)


def local(features, conv_first, conv_second, coarse_conv, coarse_proj, cotangent):
    pixels = (
        features.shape[0]
        * lax.axis_size("row")
        * features.shape[1]
        * lax.axis_size("col")
        * features.shape[2]
    )
    fine_scale = 1.0 / pixels**0.5
    coarse_scale = 2.0 * fine_scale
    feat_pad = tile_edges(features)
    first_pre = convolve(feat_pad, conv_first)
    first_act = jax.nn.silu(first_pre).astype(jnp.bfloat16)
    first_pad = tile_edges(first_act)
    second_pre = convolve(first_pad, conv_second)
    second_act = jax.nn.silu(second_pre).astype(jnp.bfloat16)
    pooled_act = (0.25 * block_sum(second_act)).astype(jnp.bfloat16)
    proj_in = block_sum(cotangent).astype(jnp.bfloat16)
    conv_whole, proj_whole = (
        lax.all_gather(coarse_conv, "row", axis=3, tiled=True),
        lax.all_gather(coarse_proj, "row", axis=0, tiled=True),
    )
    pooled_pad = tile_edges(pooled_act)
    coarse_pre = convolve(pooled_pad, conv_whole)
    coarse_act = jax.nn.silu(coarse_pre).astype(jnp.bfloat16)
    projected = jnp.einsum(
        "hwbk,kc->hwbc", coarse_act, proj_whole, preferred_element_type=jnp.float32
    )
    proj_whole_grad = jnp.einsum(
        "hwbk,hwbc->kc", coarse_act, proj_in, preferred_element_type=jnp.float32
    )
    act_grad = jnp.einsum("hwbc,kc->hwbk", proj_in, proj_whole, preferred_element_type=jnp.float32)
    coarse_pre_grad = (act_grad * silu_slope(coarse_pre)).astype(jnp.bfloat16)
    conv_whole_grad = weight_grad(pooled_pad, coarse_pre_grad)
    pooled_grad = transposed(tile_edges(coarse_pre_grad), conv_whole)
    conv_part, proj_part = (
        lax.psum_scatter(conv_whole_grad, "row", scatter_dimension=3, tiled=True),
        lax.psum_scatter(proj_whole_grad, "row", scatter_dimension=0, tiled=True),
    )
    coarse_conv_sum, coarse_proj_sum = lax.psum((conv_part, proj_part), "col")
    coarse_conv_grad = coarse_scale * coarse_conv_sum
    coarse_proj_grad = coarse_scale * coarse_proj_sum
    blended = (second_act.astype(jnp.float32) + enlarge(projected)).astype(jnp.bfloat16)
    second_in = cotangent.astype(jnp.float32) + 0.25 * enlarge(pooled_grad)
    second_pre_grad = (second_in * silu_slope(second_pre)).astype(jnp.bfloat16)
    second_part = weight_grad(first_pad, second_pre_grad)
    first_in = transposed(tile_edges(second_pre_grad), conv_second)
    first_pre_grad = (first_in * silu_slope(first_pre)).astype(jnp.bfloat16)
    first_part = weight_grad(feat_pad, first_pre_grad)
    feature_grad = transposed(tile_edges(first_pre_grad), conv_first).astype(jnp.bfloat16)
    first_sum, second_sum = lax.psum((first_part, second_part), ("row", "col"))
    first_grad = fine_scale * first_sum
    second_grad = fine_scale * second_sum
    return (blended, feature_grad, first_grad, second_grad, coarse_conv_grad, coarse_proj_grad)


def solution(mesh):
    in_specs = (
        P("row", "col", None, None),
        P(),
        P(),
        P(None, None, None, "row"),
        P("row", None),
        P("row", "col", None, None),
    )
    out_specs = (
        P("row", "col", None, None),
        P("row", "col", None, None),
        P(),
        P(),
        P(None, None, None, "row"),
        P("row", None),
    )
    return jax.shard_map(local, mesh=mesh, in_specs=in_specs, out_specs=out_specs, check_vma=False)
```

profile of v0, /device:TPU:1, one launch (start us, length us, event | category | flops | bytes accessed | tf_op | source)
XLA Modules:
  0.0 573.2 jit_solution(6283902141966480975)
XLA Ops:
  8.9 4.5 collective-permute-start
  13.4 1.9 collective-permute-start.1
  16.5 26.8 %all_gather.6 = bf16[3,3,128,256]{2,3,1,0:T(8,128)(2,1)S(1)} all-gather(bf16[3,3,128,16]{2,3,1,0:T(8,128)(2,1)} %param.9), channel_id=1, replica_groups=mesh['row'=16,'col'=16] {'row'}, dimensions={3}, use_global_device_ids=true | all-gather | bytes 626688 | tf_op jit(solution)/shard_map/all_gather | solution.py:105
  43.8 19.4 %all_gather.7 = bf16[256,128]{1,0:T(8,128)(2,1)S(1)} all-gather(bf16[16,128]{1,0:T(8,128)(2,1)S(1)} %copy-done.43), channel_id=1, replica_groups=mesh['row'=16,'col'=16] {'row'}, dimensions={0}, use_global_device_ids=true | all-gather | bytes 69632 | tf_op jit(solution)/shard_map/all_gather | solution.py:106
  63.6 3.5 collective-permute-start.2
  68.9 3.1 collective-permute-done.3
  75.2 4.6 collective-permute-start.4
  79.7 1.9 collective-permute-start.5
  81.9 2.9 collective-permute-done.5
  84.9 3.5 collective-permute-start.6
  91.0 3.4 collective-permute-done.7
  97.8 3.1 collective-permute-start.8
  100.9 1.9 collective-permute-start.9
  103.0 2.8 collective-permute-done.9
  105.9 4.9 collective-permute-start.10
  113.1 2.4 collective-permute-done.11
  119.5 1.8 convolution_bitcast_fusion
  122.4 1.9 collective-permute-start.13
  124.4 3.6 collective-permute-start.12
  130.2 4.0 collective-permute-start.15
  141.6 2.1 collective-permute-start.17
  143.6 5.3 collective-permute-start.16
  152.2 4.8 collective-permute-start.19
  171.2 1.9 collective-permute-start.21
  173.1 4.1 collective-permute-start.20
  179.4 4.7 collective-permute-start.23
  187.7 19.6 %reduce-scatter.5.cloned.1.call-done = f32[16,128]{1,0:T(8,128)} async-done(((f32[256,128]{1,0:T(8,128)}), f32[16,128]{1,0:T(8,128)}) %reduce-scatter.5.cloned.1.call-update) | async-done | bytes 8208 | tf_op jit(solution)/shard_map/reduce_scatter | solution.py:123
  207.4 27.4 %psum.31 = f32[16,128]{1,0:T(8,128)S(1)} all-reduce(f32[16,128]{1,0:T(8,128)} %reduce-scatter.5.cloned.1.call-done), channel_id=1, replica_groups=mesh['row'=16,'col'=16] {'col'}, use_global_device_ids=true, to_apply=%region_7.8 | all-reduce | flops 2048 | bytes 16384 | tf_op jit(solution)/shard_map/psum | solution.py:125
  235.4 209.8 %all-reduce.6.cloned.1.call-done = (f32[3,3,128,128]{3,2,1,0:T(8,128)}, f32[3,3,128,128]{3,2,1,0:T(8,128)}) async-done(((f32[3,3,128,128]{3,2,1,0:T(8,128)}, f32[3,3,128,128]{3,2,1,0:T(8,128)}), (f32[3,3,128,128]{3,2,1,0:T(8,128)}, f32[3,3,128,128]{3,2,1,0:T(8,128)})) %all-reduce.6.cloned.1.call-update) | async-done | bytes 1179664 | tf_op jit(solution)/shard_map/psum | solution.py:136
  445.2 2.0 broadcast_multiply_fusion
  448.0 116.5 %all-reduce.4.cloned.1.call-done = f32[3,3,128,16]{2,3,1,0:T(8,128)} async-done(((f32[3,3,128,16]{2,3,1,0:T(8,128)}), f32[3,3,128,16]{2,3,1,0:T(8,128)}) %all-reduce.4.cloned.1.call-update) | async-done | bytes 73744 | tf_op jit(solution)/shard_map/psum | solution.py:125
  564.5 1.5 broadcast_multiply_fusion.2
  (246 shorter events, 54.8 us)
Async XLA Ops:
  8.0 35.3 %copy-start.7 = (bf16[16,16,4,128]{3,2,1,0:T(4,128)(2,1)S(1)}, bf16[16,16,4,128]{3,2,1,0:T(4,128)(2,1)}, u32[]{:S(2)}) copy-start(bf16[16,16,4,128]{3,2,1,0:T(4,128)(2,1)} %param.11) | copy-start | bytes 786436
  8.0 199.4 %reduce-scatter.5.cloned.1.call-start = ((), (), s32[]{:S(2)}) async-start(), calls=%async_computation.4 | async-start | bytes 139264 | tf_op jit(solution)/shard_map/reduce_scatter | solution.py:123
  8.9 54.4 %collective-permute-start = (bf16[1,16,4,128]{3,1,2,0:T(8,128)(2,1)S(1)}, bf16[1,16,4,128]{3,1,2,0:T(8,128)(2,1)S(1)}, u32[]{:S(2)}, u32[]{:S(2)}) collective-permute-start(bf16[1,16,4,128]{3,1,2,0:T(8,128)(2,1)S(1)} %copy.342), channel_id=1, source_target_pairs={{0,16},{16,32},{32,48},{48,64},{64,80},{80,96},{96,112},{112,128},... | collective-permute-start | bytes 49160 | tf_op jit(solution)/shard_map/ppermute | solution.py:14
  13.4 50.1 %collective-permute-start.1 = (bf16[1,16,4,128]{3,1,2,0:T(8,128)(2,1)S(1)}, bf16[1,16,4,128]{3,1,2,0:T(8,128)(2,1)S(1)}, u32[]{:S(2)}, u32[]{:S(2)}) collective-permute-start(bf16[1,16,4,128]{3,1,2,0:T(8,128)(2,1)S(1)} %copy.343), channel_id=1, source_target_pairs={{16,0},{32,16},{48,32},{64,48},{80,64},{96,80},{112,96},{128,112},... | collective-permute-start | bytes 49160 | tf_op jit(solution)/shard_map/ppermute | solution.py:15
  16.5 27.3 %copy-start.43 = (bf16[16,128]{1,0:T(8,128)(2,1)S(1)}, bf16[16,128]{1,0:T(8,128)(2,1)}, u32[]{:S(2)}) copy-start(bf16[16,128]{1,0:T(8,128)(2,1)} %param.10) | copy-start | bytes 12292
  16.5 46.7 %copy-start = (bf16[16,16,4,128]{3,2,1,0:T(4,128)(2,1)S(1)}, bf16[16,16,4,128]{3,2,1,0:T(4,128)(2,1)}, u32[]{:S(2)}) copy-start(bf16[16,16,4,128]{3,2,1,0:T(4,128)(2,1)} %param.6) | copy-start | bytes 786436
  43.8 73.9 %copy-start.42 = (bf16[8,8,4,128]{3,1,2,0:T(8,128)(2,1)}, bf16[8,8,4,128]{3,1,2,0:T(8,128)(2,1)S(1)}, u32[]{:S(2)}) copy-start(bf16[8,8,4,128]{3,1,2,0:T(8,128)(2,1)S(1)} %reduce_sum.19) | copy-start | bytes 196612
  63.6 5.3 collective-permute-start.2
  67.1 4.9 collective-permute-start.3
  75.2 6.7 %collective-permute-start.4 = (bf16[1,16,4,128]{3,1,2,0:T(8,128)(2,1)S(1)}, bf16[1,16,4,128]{3,1,2,0:T(8,128)(2,1)S(1)}, u32[]{:S(2)}, u32[]{:S(2)}) collective-permute-start(bf16[1,16,4,128]{3,1,2,0:T(8,128)(2,1)S(1)} %get-tuple-element.57), channel_id=1, source_target_pairs={{0,16},{16,32},{32,48},{48,64},{64,80},{80,96},{96,112},{112,128},... | collective-permute-start | bytes 49160 | tf_op jit(solution)/shard_map/ppermute | solution.py:14
  79.7 5.1 collective-permute-start.5
  84.9 6.2 %collective-permute-start.6 = (bf16[18,1,4,128]{3,1,2,0:T(2,128)(2,1)S(1)}, bf16[18,1,4,128]{3,1,2,0:T(2,128)(2,1)S(1)}, u32[]{:S(2)}, u32[]{:S(2)}) collective-permute-start(bf16[18,1,4,128]{3,1,2,0:T(2,128)(2,1)S(1)} %get-tuple-element.44), channel_id=1, source_target_pairs={{0,1},{1,2},{2,3},{3,4},{4,5},{5,6},{6,7},{7,8},{8,9},{9,10},{10,1... | collective-permute-start | bytes 55304 | tf_op jit(solution)/shard_map/ppermute | solution.py:14
  88.4 6.0 %collective-permute-start.7 = (bf16[18,1,4,128]{3,1,2,0:T(2,128)(2,1)S(1)}, bf16[18,1,4,128]{3,1,2,0:T(2,128)(2,1)S(1)}, u32[]{:S(2)}, u32[]{:S(2)}) collective-permute-start(bf16[18,1,4,128]{3,1,2,0:T(2,128)(2,1)S(1)} %get-tuple-element.45), channel_id=1, source_target_pairs={{1,0},{2,1},{3,2},{4,3},{5,4},{6,5},{7,6},{8,7},{9,8},{10,9},{11,1... | collective-permute-start | bytes 55304 | tf_op jit(solution)/shard_map/ppermute | solution.py:15
  97.8 5.2 collective-permute-start.8
  100.9 5.0 collective-permute-start.9
  105.9 7.2 %collective-permute-start.10 = (bf16[10,1,4,128]{3,1,2,0:T(2,128)(2,1)S(1)}, bf16[10,1,4,128]{3,1,2,0:T(2,128)(2,1)S(1)}, u32[]{:S(2)}, u32[]{:S(2)}) collective-permute-start(bf16[10,1,4,128]{3,1,2,0:T(2,128)(2,1)S(1)} %get-tuple-element.78), channel_id=1, source_target_pairs={{0,1},{1,2},{2,3},{3,4},{4,5},{5,6},{6,7},{7,8},{8,9},{9,10},{10,1... | collective-permute-start | bytes 30728 | tf_op jit(solution)/shard_map/ppermute | solution.py:14
  110.8 4.8 collective-permute-start.11
  122.4 5.9 %collective-permute-start.13 = (bf16[1,8,4,256]{3,1,2,0:T(8,128)(2,1)}, bf16[1,8,4,256]{3,1,2,0:T(8,128)(2,1)S(1)}, u32[]{:S(2)}, u32[]{:S(2)}) collective-permute-start(bf16[1,8,4,256]{3,1,2,0:T(8,128)(2,1)} %get-tuple-element.75), channel_id=1, source_target_pairs={{16,0},{32,16},{48,32},{64,48},{80,64},{96,80},{112,96},{128,112},... | collective-permute-start | bytes 49160 | tf_op jit(solution)/shard_map/ppermute | solution.py:15
  124.4 4.5 collective-permute-start.12
  128.0 317.1 %all-reduce.6.cloned.1.call-start = ((), (), s32[]{:S(2)}) async-start(), calls=%async_computation.5 | async-start | bytes 2359296 | tf_op jit(solution)/shard_map/psum | solution.py:136
  128.9 5.7 collective-permute-start.14
  130.2 5.1 collective-permute-start.15
  141.6 9.2 %collective-permute-start.17 = (bf16[1,16,4,128]{3,1,2,0:T(8,128)(2,1)S(1)}, bf16[1,16,4,128]{3,1,2,0:T(8,128)(2,1)S(1)}, u32[]{:S(2)}, u32[]{:S(2)}) collective-permute-start(bf16[1,16,4,128]{3,1,2,0:T(8,128)(2,1)S(1)} %get-tuple-element.56), channel_id=1, source_target_pairs={{16,0},{32,16},{48,32},{64,48},{80,64},{96,80},{112,96},{128,112},... | collective-permute-start | bytes 49160 | tf_op jit(solution)/shard_map/ppermute | solution.py:15
  143.6 7.2 %collective-permute-start.16 = (bf16[1,16,4,128]{3,1,2,0:T(8,128)(2,1)S(1)}, bf16[1,16,4,128]{3,1,2,0:T(8,128)(2,1)S(1)}, u32[]{:S(2)}, u32[]{:S(2)}) collective-permute-start(bf16[1,16,4,128]{3,1,2,0:T(8,128)(2,1)S(1)} %get-tuple-element.55), channel_id=1, source_target_pairs={{0,16},{16,32},{32,48},{48,64},{64,80},{80,96},{96,112},{112,128},... | collective-permute-start | bytes 49160 | tf_op jit(solution)/shard_map/ppermute | solution.py:14
  150.9 6.5 %collective-permute-start.18 = (bf16[18,1,4,128]{3,1,2,0:T(2,128)(2,1)S(1)}, bf16[18,1,4,128]{3,1,2,0:T(2,128)(2,1)S(1)}, u32[]{:S(2)}, u32[]{:S(2)}) collective-permute-start(bf16[18,1,4,128]{3,1,2,0:T(2,128)(2,1)S(1)} %get-tuple-element.40), channel_id=1, source_target_pairs={{1,0},{2,1},{3,2},{4,3},{5,4},{6,5},{7,6},{8,7},{9,8},{10,9},{11,1... | collective-permute-start | bytes 55304 | tf_op jit(solution)/shard_map/ppermute | solution.py:15
  152.2 5.6 collective-permute-start.19
  168.2 279.0 %reduce-scatter.3.cloned.1.call-start = ((), (), s32[]{:S(2)}) async-start(), calls=%async_computation.2 | async-start | bytes 1253376 | tf_op jit(solution)/shard_map/reduce_scatter | solution.py:122
  170.3 394.2 %all-reduce.4.cloned.1.call-start = ((), (), s32[]{:S(2)}) async-start(), calls=%async_computation.3 | async-start | bytes 147456 | tf_op jit(solution)/shard_map/psum | solution.py:125
  171.2 6.2 %collective-permute-start.21 = (bf16[1,16,4,128]{3,1,2,0:T(8,128)(2,1)S(1)}, bf16[1,16,4,128]{3,1,2,0:T(8,128)(2,1)S(1)}, u32[]{:S(2)}, u32[]{:S(2)}) collective-permute-start(bf16[1,16,4,128]{3,1,2,0:T(8,128)(2,1)S(1)} %get-tuple-element.54), channel_id=1, source_target_pairs={{16,0},{32,16},{48,32},{64,48},{80,64},{96,80},{112,96},{128,112},... | collective-permute-start | bytes 49160 | tf_op jit(solution)/shard_map/ppermute | solution.py:15
  173.1 4.9 collective-permute-start.20
  178.1 6.5 %collective-permute-start.22 = (bf16[18,1,4,128]{3,1,2,0:T(2,128)(2,1)S(1)}, bf16[18,1,4,128]{3,1,2,0:T(2,128)(2,1)S(1)}, u32[]{:S(2)}, u32[]{:S(2)}) collective-permute-start(bf16[18,1,4,128]{3,1,2,0:T(2,128)(2,1)S(1)} %get-tuple-element.36), channel_id=1, source_target_pairs={{1,0},{2,1},{3,2},{4,3},{5,4},{6,5},{7,6},{8,7},{9,8},{10,9},{11,1... | collective-permute-start | bytes 55304 | tf_op jit(solution)/shard_map/ppermute | solution.py:15
  179.4 5.8 %collective-permute-start.23 = (bf16[18,1,4,128]{3,1,2,0:T(2,128)(2,1)S(1)}, bf16[18,1,4,128]{3,1,2,0:T(2,128)(2,1)S(1)}, u32[]{:S(2)}, u32[]{:S(2)}) collective-permute-start(bf16[18,1,4,128]{3,1,2,0:T(2,128)(2,1)S(1)} %get-tuple-element.37), channel_id=1, source_target_pairs={{0,1},{1,2},{2,3},{3,4},{4,5},{5,6},{6,7},{7,8},{8,9},{9,10},{10,1... | collective-permute-start | bytes 55304 | tf_op jit(solution)/shard_map/ppermute | solution.py:14
  (40 other events, 114.8 us)
Sparse Core Ops, SparseCore 0:
  128.1 79.1 reduce-scatter.4
  211.5 74.2 reduce-scatter.2
  447.3 117.2 all-reduce.3
Sparse Core Ops, SparseCore 1:
  168.3 276.8 all-reduce.5
where the time goes:
time: 583 us; the launch traced here: 573 us
  waiting for transfers between devices  364 us (62%)
  blocking collectives  73.6 us (13%)
  starting transfers between devices  70.2 us (12%)
  matrix products  23 us (4%)
  between operations  16.7 us (3%)
  local copies, waits for them, and re-layouts  16.6 us (3%)
  other arithmetic  9.67 us (2%)
    psum x1, waiting for transfers between devices, local(): first_sum, second_sum = lax.psum((first_part, second_part), ('row', 'col'))  210 us
    psum x1, waiting for transfers between devices, local(): coarse_conv_sum, coarse_proj_sum = lax.psum((conv_part, proj_part), 'col')  117 us
    ppermute x12, starting transfers between devices, padded_2(): before = lax.ppermute(last, axis, up)  50.6 us
    psum x1, blocking collectives, local(): coarse_conv_sum, coarse_proj_sum = lax.psum((conv_part, proj_part), 'col')  27.4 us
    all_gather x1, blocking collectives, local(): lax.all_gather(coarse_conv, 'row', axis=3, tiled=True)  26.8 us
    reduce_scatter x1, waiting for transfers between devices, local(): lax.psum_scatter(proj_whole_grad, 'row', scatter_dimension=0, tiled=True)  19.6 us
    all_gather x1, blocking collectives, local(): lax.all_gather(coarse_proj, 'row', axis=0, tiled=True)  19.4 us
    ppermute x12, starting transfers between devices, padded_2(): after = lax.ppermute(first, axis, down)  19.4 us
  transfers between devices with their start and end apart: 28, of which 13 were waited for; matrix products, arithmetic and copies ran while one was open for 4% of the time, Pallas kernels for 0%

commit v1 on v0

v1 whole, which is shorter than its diff:
```python
import functools

import jax
import jax.numpy as jnp
from jax import lax
from jax.experimental import pallas as pl
from jax.experimental.pallas import tpu as pltpu
from jax.sharding import PartitionSpec as P

BF = jnp.bfloat16
F32 = jnp.float32
CH = 128
WIDE = 256
PARAMS = pltpu.CompilerParams(vmem_limit_bytes=48 * 1024 * 1024)


def dot_nn(a, b):
    return jnp.dot(a, b, preferred_element_type=F32)


def dot_nt(a, b):
    return lax.dot_general(a, b, (((1,), (1,)), ((), ())), preferred_element_type=F32)


def dot_tn(a, b):
    return lax.dot_general(a, b, (((0,), (0,)), ((), ())), preferred_element_type=F32)


def sigmoid(value):
    return 0.5 * jnp.tanh(0.5 * value) + 0.5


def slope_of(value):
    sigma = sigmoid(value)
    return sigma * (1.0 + value * (1.0 - sigma))


def rounded(value):
    return value.astype(BF).astype(F32)


def three(value):
    count = value.shape[0]
    left = pltpu.roll(value, 4, 0)
    right = pltpu.roll(value, count - 4, 0)
    return jnp.concatenate([left.astype(BF), value.astype(BF), right.astype(BF)], axis=1)


def taps(ref, start, rows, cols=None):
    parts = []
    for r in range(3):
        part = ref[pl.ds(start + r, rows)] if cols is None else ref[pl.ds(start + r, rows), cols[0] : cols[1], :]
        parts.append(part.reshape(part.shape[0] * part.shape[1], part.shape[2]))
    return jnp.concatenate(parts, axis=1)


def column_mask(first, width, limit):
    place = first + lax.broadcasted_iota(jnp.int32, (width, CH), 0) // 4
    return jnp.where((place >= 0) & (place < limit), 1.0, 0.0).astype(F32)


def row_ok(place, limit):
    return jnp.where((place >= 0) & (place < limit), 1.0, 0.0).astype(F32)


def masked(value, mask, first, limit):
    rows = []
    for k in range(value.shape[0]):
        rows.append((value[k] * (mask * row_ok(first + k, limit)))[None])
    return jnp.concatenate(rows, axis=0)


def pooled_pair(row):
    count = row.shape[0]
    low = (row + pltpu.roll(row, count - 4, 0)).reshape(count // 16, 2, 8, CH)
    high = (row + pltpu.roll(row, 4, 0)).reshape(count // 16, 2, 8, CH)
    first = lax.broadcasted_iota(jnp.int32, (count // 16, 8, CH), 1) < 4
    return jnp.where(first, low[:, 0], high[:, 1]).reshape(count // 2, CH)


def repeated(row):
    count = row.shape[0]
    first = lax.broadcasted_iota(jnp.int32, (count, CH), 0) % 8 < 4
    even = jnp.where(first, row, pltpu.roll(row, 4, 0)).reshape(count // 8, 1, 8, CH)
    odd = jnp.where(first, pltpu.roll(row, count - 4, 0), row).reshape(count // 8, 1, 8, CH)
    return jnp.concatenate([even, odd], axis=1).reshape(count * 2, CH)


def forward_kernel(meta, window, w1, w2, pool3, slope1, slope2, act, feat3o, act3o, feat3, act3, pre1, pre2, act2):
    top, left, height, breadth = (meta[0], meta[1], meta[2], meta[3])
    mask = column_mask(left - 8, 128, breadth)
    coarse_mask = column_mask(left // 2 - 4, 64, breadth // 2)

    @pl.loop(0, 8)
    def _(b):
        block = window[pl.ds(4 * b, 4)].reshape(512, CH).astype(F32)
        feat3[pl.ds(4 * b, 4)] = three(block).reshape(4, 128, 3 * CH)

    first_w = w1[...]

    @pl.loop(0, 6)
    def _(b):
        pre = dot_nn(taps(feat3, 5 * b, 5), first_w)
        pre1[pl.ds(5 * b, 5)] = pre.reshape(5, 128, CH)
        value = rounded(pre * sigmoid(pre)).reshape(5, 128, CH)
        value = masked(value, mask, top - 7 + 5 * b, height)
        act3[pl.ds(5 * b, 5)] = three(value.reshape(640, CH)).reshape(5, 128, 3 * CH)

    second_w = w2[...]

    @pl.loop(0, 7)
    def _(b):
        pre = dot_nn(taps(act3, 4 * b, 4), second_w)
        pre2[pl.ds(4 * b, 4)] = pre.reshape(4, 128, CH)
        value = (pre * sigmoid(pre)).astype(BF)
        act2[pl.ds(4 * b, 4)] = value.reshape(4, 128, CH)
        value = value.astype(F32).reshape(4, 128, CH)
        coarse = []
        for k in range(2):
            small = rounded(0.25 * pooled_pair(value[2 * k] + value[2 * k + 1]))
            coarse.append(small * (coarse_mask * row_ok(top // 2 - 3 + 2 * b + k, height // 2)))
        coarse = jnp.concatenate(coarse, axis=0)
        pool3[pl.ds(2 * b, 2)] = three(coarse).reshape(2, 64, 3 * CH)

    @pl.loop(0, 18)
    def _(k):
        slope1[k] = slope_of(pre1[k + 6, 16:112, :])
        feat3o[k] = feat3[k + 7, 32:96, :]
        act3o[k] = act3[k + 6, 32:96, :]

    @pl.loop(0, 20)
    def _(k):
        slope2[k] = slope_of(pre2[k + 4, 16:112, :])

    @pl.loop(0, 16)
    def _(k):
        act[k] = act2[k + 6, 32:96, :]


def fine_forward(meta, window, w1, w2):
    sds = jax.ShapeDtypeStruct
    vm = pl.BlockSpec(memory_space=pltpu.VMEM)
    return pl.pallas_call(
        forward_kernel,
        name="fine_forward",
        out_shape=(
            sds((14, 64, 384), BF),
            sds((18, 96, CH), F32),
            sds((20, 96, CH), F32),
            sds((16, 64, CH), BF),
            sds((18, 64, 384), BF),
            sds((18, 64, 384), BF),
        ),
        in_specs=[pl.BlockSpec(memory_space=pltpu.SMEM), vm, vm, vm],
        out_specs=[vm] * 6,
        scratch_shapes=[
            pltpu.VMEM((32, 128, 384), BF),
            pltpu.VMEM((30, 128, 384), BF),
            pltpu.VMEM((30, 128, CH), F32),
            pltpu.VMEM((28, 128, CH), F32),
            pltpu.VMEM((28, 128, CH), BF),
        ],
        compiler_params=PARAMS,
    )(meta, window, w1, w2)


def coarse_kernel(meta, pool3, cot, wg, proj, act, blended, grads, pooled_grad, wcat, wide3, projin):
    top, left, height, breadth = (meta[0], meta[1], meta[2], meta[3])
    for t in range(9):
        wcat[:, t * CH : (t + 1) * CH] = wg[:, t].reshape(WIDE, CH)
    proj_w = proj[...]

    @pl.loop(0, 12)
    def _(k):
        pair = cot[pl.ds(2 * k, 2)].astype(F32)
        projin[k] = pooled_pair(pair[0] + pair[1])

    proj_in = projin[...].reshape(576, CH)
    proj_in_bf = proj_in.astype(BF)
    pre = dot_nt(taps(pool3, 0, 12), wcat[...]).reshape(12, 64, WIDE)[:, 8:56].reshape(576, WIDE)
    sigma = sigmoid(pre)
    coarse_act = pre * sigma
    act_grad = dot_nt(proj_in_bf, proj_w)
    grad = rounded(act_grad * (sigma * (1.0 + pre * (1.0 - sigma)))).reshape(12, 48, WIDE)
    mask = column_mask(left // 2 - 2, 48, breadth // 2)
    mask = jnp.concatenate([mask, mask], axis=1)
    grad = masked(grad, mask, top // 2 - 2, height // 2)
    wide3[...] = three(grad.reshape(576, WIDE)).reshape(12, 48, 3 * WIDE)
    own_grad = grad[2:10, 8:40].reshape(256, WIDE).astype(BF)
    own_act = coarse_act.reshape(12, 48, WIDE)[2:10, 8:40].reshape(256, WIDE).astype(BF)
    own_in = proj_in.reshape(12, 48, CH)[2:10, 8:40].reshape(256, CH).astype(BF)
    for r in range(3):
        source = pool3[2 + r : 10 + r, 16:48, :].reshape(256, 3 * CH)
        part = dot_tn(own_grad, source).astype(BF)
        for s in range(3):
            t = 3 * r + s
            grads[:, 16 * t : 16 * t + 16, :] = part[:, s * CH : (s + 1) * CH].reshape(16, 16, CH)
    grads[:, 144:160, :] = dot_tn(own_act, own_in).astype(BF).reshape(16, 16, CH)
    total = None
    for r in range(3):
        lhs = wide3[r : r + 10].reshape(480, 3 * WIDE)
        rhs = jnp.concatenate([wg[:, 3 * (2 - r) + (2 - s)].reshape(WIDE, CH) for s in range(3)], axis=0)
        part = dot_nn(lhs, rhs)
        total = part if total is None else total + part
    pooled_grad[...] = total.reshape(10, 48, CH)
    projected = dot_nn(own_act, proj_w).reshape(8, 32, CH)
    for k in range(8):
        row = repeated(projected[k])
        for e in range(2):
            blended[2 * k + e] = (act[2 * k + e].astype(F32) + row).astype(BF)


def coarse_step(meta, pool3, cot, wg, proj, act):
    sds = jax.ShapeDtypeStruct
    vm = pl.BlockSpec(memory_space=pltpu.VMEM)
    return pl.pallas_call(
        coarse_kernel,
        name="coarse_step",
        out_shape=(sds((16, 64, CH), BF), sds((16, 160, CH), BF), sds((10, 48, CH), F32)),
        in_specs=[pl.BlockSpec(memory_space=pltpu.SMEM)] + [vm] * 5,
        out_specs=[vm] * 3,
        scratch_shapes=[
            pltpu.VMEM((WIDE, 9 * CH), BF),
            pltpu.VMEM((12, 48, 3 * WIDE), BF),
            pltpu.VMEM((12, 48, CH), F32),
        ],
        compiler_params=PARAMS,
    )(meta, pool3, cot, wg, proj, act)


def flipped(weight):
    return jnp.concatenate([weight[8 - t] for t in range(9)], axis=1)


def backward_kernel(meta, pooled_grad, cot, slope1, slope2, feat3, act3, w2, grads, first3, second3):
    top, left, height, breadth = (meta[0], meta[1], meta[2], meta[3])
    mask = column_mask(left - 4, 96, breadth)

    @pl.loop(0, 10)
    def _(k):
        wide = 0.25 * repeated(pooled_grad[k])
        rows = []
        for e in range(2):
            value = cot[2 * k + e + 2].astype(F32) + wide
            value = rounded(value * slope2[2 * k + e])
            rows.append(value * (mask * row_ok(top - 2 + 2 * k + e, height)))
        second3[pl.ds(2 * k, 2)] = three(jnp.concatenate(rows, axis=0)).reshape(2, 96, 3 * CH)

    def weight_grad(source, grad):
        return [dot_tn(source[r : r + 16].reshape(1024, 3 * CH), grad) for r in range(3)]

    def emit(base, parts):
        for r in range(3):
            grads[base + 384 * r : base + 384 * (r + 1), :] = parts[r].astype(BF)

    second_own = second3[2:18, 16:80, CH : 2 * CH].reshape(1024, CH)
    emit(1152, weight_grad(act3, second_own))
    back_w = flipped(w2)

    @pl.loop(0, 3)
    def _(b):
        value = dot_nt(taps(second3, 6 * b, 6), back_w).reshape(6, 96, CH)
        value = rounded(value * slope1[pl.ds(6 * b, 6)])
        value = masked(value, mask, top - 1 + 6 * b, height)
        out = three(value.reshape(576, CH)).reshape(6, 96, 3 * CH)
        first3[pl.ds(6 * b, 6)] = out[:, 16:80, :]

    first_own = first3[1:17, :, CH : 2 * CH].reshape(1024, CH)
    emit(0, weight_grad(feat3, first_own))


def fine_backward(meta, pooled_grad, cot, slope1, slope2, feat3, act3, w2):
    sds = jax.ShapeDtypeStruct
    vm = pl.BlockSpec(memory_space=pltpu.VMEM)
    return pl.pallas_call(
        backward_kernel,
        name="fine_backward",
        out_shape=(sds((2304, CH), BF), sds((18, 64, 384), BF)),
        in_specs=[pl.BlockSpec(memory_space=pltpu.SMEM)] + [vm] * 7,
        out_specs=[vm] * 2,
        scratch_shapes=[pltpu.VMEM((20, 96, 384), BF)],
        compiler_params=PARAMS,
    )(meta, pooled_grad, cot, slope1, slope2, feat3, act3, w2)


def feature_kernel(first3, w1, out):
    back_w = flipped(w1)

    @pl.loop(0, 2)
    def _(b):
        out[pl.ds(8 * b, 8)] = dot_nt(taps(first3, 8 * b, 8), back_w).astype(BF).reshape(8, 64, CH)


def feature_step(first3, w1):
    vm = pl.BlockSpec(memory_space=pltpu.VMEM)
    return pl.pallas_call(
        feature_kernel,
        name="feature_step",
        out_shape=jax.ShapeDtypeStruct((16, 64, CH), BF),
        in_specs=[vm] * 2,
        out_specs=vm,
        compiler_params=PARAMS,
    )(first3, w1)


def tile_compute(meta, window, cot, w1, w2, wg, proj):
    pool3, slope1, slope2, act, feat3, act3 = fine_forward(meta, window, w1.reshape(1152, CH), w2.reshape(1152, CH))
    blended, coarse_grads, pooled_grad = coarse_step(meta, pool3, cot, wg, proj, act)
    fine_grads, first3 = fine_backward(meta, pooled_grad, cot, slope1, slope2, feat3, act3, w2.reshape(9, CH, CH))
    feature_grad = feature_step(first3, w1.reshape(9, CH, CH))
    return blended, feature_grad, coarse_grads, fine_grads


def swap(value, axis, mask):
    count = lax.axis_size(axis)
    return lax.ppermute(value, axis, [(i, i ^ mask) for i in range(count)])


def shifted(value, axis, step):
    count = lax.axis_size(axis)
    pairs = [(i, i + step) for i in range(count) if 0 <= i + step < count]
    return lax.ppermute(value, axis, pairs)


def halo(features, cotangent):
    feat = features.reshape(16, 64, CH)
    cot = cotangent.reshape(16, 64, CH)

    def side(feat_part, cot_part):
        return jnp.concatenate([feat_part, cot_part], axis=1)

    right = shifted(side(feat[:, 32:], cot[:, 48:]), "col", 1)
    left = shifted(side(feat[:, :32], cot[:, :16]), "col", -1)
    feat = jnp.concatenate([right[:, :32], feat, left[:, :32]], axis=1)
    cot = jnp.concatenate([right[:, 32:], cot, left[:, 32:]], axis=1)

    def edge(feat_part, cot_part):
        return jnp.concatenate([feat_part, cot_part.reshape(3, 128, CH)], axis=0)

    down = shifted(edge(feat[8:], cot[12:]), "row", 1)
    up = shifted(edge(feat[:8], cot[:4]), "row", -1)
    feat = jnp.concatenate([down[:8], feat, up[:8]], axis=0)
    cot = jnp.concatenate([down[8:].reshape(4, 96, CH), cot, up[8:].reshape(4, 96, CH)], axis=0)
    return feat, cot


def gather_weights(coarse_conv, coarse_proj, me):
    own = jnp.concatenate(
        [coarse_conv.reshape(9, CH, 16).swapaxes(1, 2).reshape(144, CH), coarse_proj], axis=0
    )
    one = jnp.stack([own, swap(own, "row", 8)])
    two = jnp.stack([one] + [swap(one, "row", 2 * k) for k in range(1, 4)])
    whole = jnp.stack([two, swap(two, "row", 1)])
    return absolute(whole, me)


def absolute(value, me):
    rest = value.shape[3:]
    core, x, y = (me % 2, (me // 2) % 4, me // 8)
    value = jnp.where(core == 0, value, value[::-1])
    value = jnp.where(x % 2 == 0, value, value[:, jnp.array([1, 0, 3, 2])])
    value = jnp.where(x // 2 == 0, value, value[:, jnp.array([2, 3, 0, 1])])
    value = jnp.where(y == 0, value, value[:, :, ::-1])
    return value.transpose((2, 1, 0) + tuple(range(3, value.ndim))).reshape((16,) + rest)


def reduce_all(coarse_grads, fine_grads, me):
    core, x, y = (me % 2, (me // 2) % 4, me // 8)
    pick = functools.partial(lax.dynamic_index_in_dim, axis=0, keepdims=False)
    whole = jnp.concatenate([coarse_grads, fine_grads.reshape(16, 144, CH)], axis=1)
    whole = whole.reshape(2, 4, 2, 304, CH).transpose(2, 1, 0, 3, 4)
    got = swap(pick(whole, 1 - core), "row", 1)
    part = pick(whole, core).astype(F32) + got.astype(F32)
    got = [swap(pick(part, x ^ k).astype(BF), "row", 2 * k) for k in range(1, 4)]
    part = pick(part, x) + sum(g.astype(F32) for g in got)
    got = swap(pick(part, 1 - y).astype(BF), "row", 8)
    part = (pick(part, y) + got.astype(F32)).astype(BF)
    for base in (1, 4):
        got = [swap(part, "col", base * k) for k in range(1, 4)]
        a, b, c, d = (v.astype(F32) for v in [part] + got)
        total = (a + b) + (c + d)
        part = total.astype(BF)
    coarse = total[:160]
    own = part[160:]
    one = jnp.stack([own, swap(own, "row", 8)])
    two = jnp.stack([one] + [swap(one, "row", 2 * k) for k in range(1, 4)])
    fine = jnp.stack([two, swap(two, "row", 1)])
    return coarse, absolute(fine, me).reshape(2304, CH)


def local(features, conv_first, conv_second, coarse_conv, coarse_proj, cotangent):
    rows, cols = (lax.axis_size("row"), lax.axis_size("col"))
    height, breadth = (features.shape[0] * rows, features.shape[1] * cols)
    fine_scale = 1.0 / (height * breadth * features.shape[2]) ** 0.5
    coarse_scale = 2.0 * fine_scale
    me, mine = (lax.axis_index("row"), lax.axis_index("col"))
    meta = jnp.stack([me * 16, mine * 16, jnp.int32(height), jnp.int32(breadth)]).astype(jnp.int32)
    window, cot = halo(features, cotangent)
    slabs = gather_weights(coarse_conv, coarse_proj, me)
    wg = slabs[:, :144].reshape(16, 9, 16, CH)
    proj = slabs[:, 144:].reshape(WIDE, CH)
    blended, feature_grad, coarse_grads, fine_grads = tile_compute(meta, window, cot, conv_first, conv_second, wg, proj)
    coarse, fine = reduce_all(coarse_grads, fine_grads, me)
    fine = fine_scale * fine.astype(F32)
    coarse = coarse_scale * coarse
    shape = features.shape
    return (
        blended.reshape(shape),
        feature_grad.reshape(shape),
        fine[:1152].reshape(3, 3, CH, CH),
        fine[1152:].reshape(3, 3, CH, CH),
        coarse[:144].reshape(3, 3, 16, CH).swapaxes(2, 3),
        coarse[144:],
    )


def solution(mesh):
    in_specs = (
        P("row", "col", None, None),
        P(),
        P(),
        P(None, None, None, "row"),
        P("row", None),
        P("row", "col", None, None),
    )
    out_specs = (
        P("row", "col", None, None),
        P("row", "col", None, None),
        P(),
        P(),
        P(None, None, None, "row"),
        P("row", None),
    )
    return jax.shard_map(local, mesh=mesh, in_specs=in_specs, out_specs=out_specs, check_vma=False)
```

time: 583 us -> 134 us (0.23); the launches traced: 573 us -> 134 us
  waiting for transfers between devices: 364 us -> 33.2 us
  blocking collectives: 73.6 us -> 0 us
  matrix products: 23 us -> 0 us
  Pallas kernels: 0 us -> 21 us
  between operations: 16.7 us -> 1.27 us
  starting transfers between devices: 70.2 us -> 58 us
    psum x2 -> x0, waiting for transfers between devices: 326 us -> none  [the longest x1 210 us: local(): first_sum, second_sum = lax.psum((first_part, second_part), ('row', 'col'))]
    all_gather x2 -> x0, blocking collectives: 46.2 us -> none  [the longest x1 26.8 us: local(): lax.all_gather(coarse_conv, 'row', axis=3, tiled=True)]
    psum x1 -> x0, blocking collectives: 27.4 us -> none  [local(): coarse_conv_sum, coarse_proj_sum = lax.psum((conv_part, proj_part), 'col')]
    dot_general x84 -> x0, matrix products: 23 us -> none  [the longest x27 7.58 us: convolve(): jnp.einsum('hwbc,cd->hwbd', padded[row_off:row_off + height, col_off:col_...]
    pallas_call x0 -> x4, Pallas kernels: none -> 21 us  [the longest x1 10.3 us: fine_forward(): pl.pallas_call(forward_kernel, name='fine_forward', out_shape=(sds((14, 6...]
    reduce_scatter x2 -> x0, waiting for transfers between devices: 19.6 us -> none  [the longest x1 19.6 us: local(): lax.psum_scatter(proj_whole_grad, 'row', scatter_dimension=0, tiled=True)]
    ppermute x24 -> x25, waiting for transfers between devices: 17.5 us -> 33.2 us  [the longest x21 31.7 us: swap(): return lax.ppermute(value, axis, [(i, i ^ mask) for i in range(count)])]
    ppermute x24 -> x25, starting transfers between devices: 70 us -> 58 us  [the longest x21 46.9 us: swap(): return lax.ppermute(value, axis, [(i, i ^ mask) for i in range(count)])]
  transfers between devices with their start and end apart: 28 -> 25, of which waited for: 13 -> 18; matrix products, arithmetic and copies ran while one was open for 4% -> 6% of each run, Pallas kernels for 0% -> 1%
where the time goes in v1:
time: 134 us
  starting transfers between devices  58 us (43%)
  waiting for transfers between devices  33.2 us (25%)
  Pallas kernels  21 us (16%)
  local copies, waits for them, and re-layouts  13.8 us (10%)
  other arithmetic  6.46 us (5%)
    ppermute x21, starting transfers between devices, swap(): return lax.ppermute(value, axis, [(i, i ^ mask) for i in range(count)])  46.9 us
    ppermute x21, waiting for transfers between devices, swap(): return lax.ppermute(value, axis, [(i, i ^ mask) for i in range(count)])  31.7 us
    ppermute x4, starting transfers between devices, shifted(): return lax.ppermute(value, axis, pairs)  11.1 us
    pallas_call x1, Pallas kernels, fine_forward(): pl.pallas_call(forward_kernel, name='fine_forward', out_shape=(sds((14, 6...  10.3 us
    pallas_call x1, Pallas kernels, fine_backward(): pl.pallas_call(backward_kernel, name='fine_backward', out_shape=(sds((230...  4.88 us
    pallas_call x1, Pallas kernels, coarse_step(): pl.pallas_call(coarse_kernel, name='coarse_step', out_shape=(sds((16, 64,...  4.14 us
  transfers between devices with their start and end apart: 25, of which 18 were waited for; matrix products, arithmetic and copies ran while one was open for 6% of the time, Pallas kernels for 1%

profile of v1, /device:TPU:1, one launch (start us, length us, event | category | flops | bytes accessed | tf_op | source)
XLA Modules:
  0.0 133.7 jit_solution(5643206536684341164)
XLA Ops:
  1.5 3.8 %collective-permute-start.4 = (bf16[160,128]{1,0:T(8,128)(2,1)S(1)}, bf16[160,128]{1,0:T(8,128)(2,1)S(1)}, u32[]{:S(2)}, u32[]{:S(2)}) collective-permute-start(bf16[160,128]{1,0:T(8,128)(2,1)S(1)} %get-tuple-element.52), channel_id=1, source_target_pairs={{0,128},{16,144},{32,160},{48,176},{64,192},{80,208},{96,224},{112... | collective-permute-start | bytes 122888 | tf_op jit(solution)/shard_map/ppermute | solution.py:316
  7.2 1.4 %collective-permute-start.1 = (bf16[16,48,128]{2,1,0:T(8,128)(2,1)S(1)}, bf16[16,48,128]{2,1,0:T(8,128)(2,1)S(1)}, u32[]{:S(2)}, u32[]{:S(2)}) collective-permute-start(bf16[16,48,128]{2,1,0:T(8,128)(2,1)S(1)} %pad_maximum_fusion.10), channel_id=1, source_target_pairs={{1,0},{2,1},{3,2},{4,3},{5,4},{6,5},{7,6},{8,7},{9,8},{10,9},{11,1... | collective-permute-start | bytes 589832 | tf_op jit(solution)/shard_map/ppermute | solution.py:322
  8.7 4.2 %collective-permute-start = (bf16[16,48,128]{2,1,0:T(8,128)(2,1)S(1)}, bf16[16,48,128]{2,1,0:T(8,128)(2,1)S(1)}, u32[]{:S(2)}, u32[]{:S(2)}) collective-permute-start(bf16[16,48,128]{2,1,0:T(8,128)(2,1)S(1)} %pad_maximum_fusion.9), channel_id=1, source_target_pairs={{0,1},{1,2},{2,3},{3,4},{4,5},{5,6},{6,7},{7,8},{8,9},{9,10},{10,1... | collective-permute-start | bytes 589832 | tf_op jit(solution)/shard_map/ppermute | solution.py:322
  13.0 2.8 %collective-permute-start.6 = (bf16[2,160,128]{2,1,0:T(8,128)(2,1)S(1)}, bf16[2,160,128]{2,1,0:T(8,128)(2,1)S(1)}, u32[]{:S(2)}, u32[]{:S(2)}) collective-permute-start(bf16[2,160,128]{2,1,0:T(8,128)(2,1)S(1)} %get-tuple-element.48), channel_id=1, source_target_pairs={{0,64},{16,80},{32,96},{48,112},{64,0},{80,16},{96,32},{112,48},{1... | collective-permute-start | bytes 245768 | tf_op jit(solution)/shard_map/ppermute | solution.py:316
  17.9 1.8 %collective-permute-done.5 = bf16[2,160,128]{2,1,0:T(8,128)(2,1)S(1)} collective-permute-done((bf16[2,160,128]{2,1,0:T(8,128)(2,1)S(1)}, bf16[2,160,128]{2,1,0:T(8,128)(2,1)S(1)}, u32[]{:S(2)}, u32[]{:S(2)}) %collective-permute-start.5) | collective-permute-done | bytes 81952 | tf_op jit(solution)/shard_map/ppermute | solution.py:316
  19.7 1.3 collective-permute-done.7
  21.1 2.7 %collective-permute-start.8 = (bf16[4,2,160,128]{3,2,1,0:T(8,128)(2,1)S(1)}, bf16[4,2,160,128]{3,2,1,0:T(8,128)(2,1)S(1)}, u32[]{:S(2)}, u32[]{:S(2)}) collective-permute-start(bf16[4,2,160,128]{3,2,1,0:T(8,128)(2,1)S(1)} %get-tuple-element.40), channel_id=1, source_target_pairs={{0,16},{16,0},{32,48},{48,32},{64,80},{80,64},{96,112},{112,96},{1... | collective-permute-start | bytes 983048 | tf_op jit(solution)/shard_map/ppermute | solution.py:316
  25.6 1.9 %collective-permute-start.3 = (bf16[11,128,128]{2,1,0:T(8,128)(2,1)}, bf16[11,128,128]{2,1,0:T(8,128)(2,1)}, u32[]{:S(2)}, u32[]{:S(2)}) collective-permute-start(bf16[11,128,128]{2,1,0:T(8,128)(2,1)} %pad_maximum_fusion.6), channel_id=1, source_target_pairs={{16,0},{32,16},{48,32},{64,48},{80,64},{96,80},{112,96},{128,112},... | collective-permute-start | bytes 1081352 | tf_op jit(solution)/shard_map/ppermute | solution.py:322
  28.3 3.6 %collective-permute-start.2 = (bf16[11,128,128]{2,1,0:T(8,128)(2,1)}, bf16[11,128,128]{2,1,0:T(8,128)(2,1)}, u32[]{:S(2)}, u32[]{:S(2)}) collective-permute-start(bf16[11,128,128]{2,1,0:T(8,128)(2,1)} %pad_maximum_fusion.5), channel_id=1, source_target_pairs={{0,16},{16,32},{32,48},{48,64},{64,80},{80,96},{96,112},{112,128},... | collective-permute-start | bytes 1081352 | tf_op jit(solution)/shard_map/ppermute | solution.py:322
  40.7 10.3 %fine_forward.1 = (bf16[14,64,384]{2,1,0:T(8,128)(2,1)S(1)}, f32[18,96,128]{2,1,0:T(8,128)S(1)}, f32[20,96,128]{2,1,0:T(8,128)S(1)}, bf16[16,64,128]{2,1,0:T(8,1...) custom-call(s32[4]{0:T(128)S(1)} %pad_add_fusion.meta, ...), custom_call_target="tpu_custom_call" | custom-call | tf_op jit(solution)/shard_map/fine_forward/pallas_call | solution.py:143
  52.0 4.1 %coarse_step.1 = (bf16[16,64,128]{2,1,0:T(8,128)(2,1)}, bf16[16,160,128]{2,1,0:T(8,128)(2,1)S(1)}, f32[10,48,128]{2,1,0:T(8,128)S(1)}) custom-call(s32[4]{0:T(128)S(1)} %pad_add_fusion.meta, bf16[14,64,384]{2,1,0:T(8,128)(2,1)S(1)} %get-tuple-element.17.pool3, bf16[24,96,128]{2,1,0:T(8,128)(2,1)S(1)} %pad_maximum_fusion.2.cot, ...), custom_call_target="tpu_custom_call" | custom-call | tf_op jit(solution)/shard_map/coarse_step/pallas_call | solution.py:216
  56.1 4.9 %fine_backward.1 = (bf16[2304,128]{1,0:T(8,128)(2,1)S(1)}, bf16[18,64,384]{2,1,0:T(8,128)(2,1)S(1)}) custom-call(s32[4]{0:T(128)S(1)} %pad_add_fusion.meta, f32[10,48,128]{2,1,0:T(8,128)S(1)} %get-tuple-element.20.pooled_grad, bf16[24,96,128]{2,1,0:T(8,128)(2,1)S(1)} %pad_maximum_fusion.2.cot, f32[18,96,128]{2,1,0:T(8,128)S(1)} %get-tuple-element.21.slope1, ...), custom_call_target="tpu_custom_call" | custom-call | tf_op jit(solution)/shard_map/fine_backward/pallas_call | solution.py:275
  61.3 2.0 %collective-permute-done.9 = bf16[4,2,304,128]{3,2,1,0:T(8,128)(2,1)S(1)} collective-permute-done((bf16[4,2,304,128]{3,2,1,0:T(8,128)(2,1)S(1)}, bf16[4,2,304,128]{3,2,1,0:T(8,128)(2,1)S(1)}, u32[]{:S(2)}, u32[]{:S(2)}) %collective-permute-start.9) | collective-permute-done | bytes 622624 | tf_op jit(solution)/shard_map/ppermute | solution.py:316
  65.4 2.3 %collective-permute-start.10 = (bf16[2,304,128]{2,1,0:T(8,128)(2,1)S(1)}, bf16[2,304,128]{2,1,0:T(8,128)(2,1)S(1)}, u32[]{:S(2)}, u32[]{:S(2)}) collective-permute-start(bf16[2,304,128]{2,1,0:T(8,128)(2,1)S(1)} %get-tuple-element.28), channel_id=1, source_target_pairs={{0,32},{16,48},{32,0},{48,16},{64,96},{80,112},{96,64},{112,80},{1... | collective-permute-start | bytes 466952 | tf_op jit(solution)/shard_map/ppermute | solution.py:316
  67.7 2.0 %collective-permute-start.12 = (bf16[2,304,128]{2,1,0:T(8,128)(2,1)S(1)}, bf16[2,304,128]{2,1,0:T(8,128)(2,1)S(1)}, u32[]{:S(2)}, u32[]{:S(2)}) collective-permute-start(bf16[2,304,128]{2,1,0:T(8,128)(2,1)S(1)} %get-tuple-element.29), channel_id=1, source_target_pairs={{0,96},{16,112},{32,64},{48,80},{64,32},{80,48},{96,0},{112,16},{1... | collective-permute-start | bytes 466952 | tf_op jit(solution)/shard_map/ppermute | solution.py:316
  71.8 4.5 %collective-permute-done.12 = bf16[2,304,128]{2,1,0:T(8,128)(2,1)S(1)} collective-permute-done((bf16[2,304,128]{2,1,0:T(8,128)(2,1)S(1)}, bf16[2,304,128]{2,1,0:T(8,128)(2,1)S(1)}, u32[]{:S(2)}, u32[]{:S(2)}) %collective-permute-start.12) | collective-permute-done | bytes 155680 | tf_op jit(solution)/shard_map/ppermute | solution.py:316
  76.3 1.6 %collective-permute-done.11 = bf16[2,304,128]{2,1,0:T(8,128)(2,1)S(1)} collective-permute-done((bf16[2,304,128]{2,1,0:T(8,128)(2,1)S(1)}, bf16[2,304,128]{2,1,0:T(8,128)(2,1)S(1)}, u32[]{:S(2)}, u32[]{:S(2)}) %collective-permute-start.11) | collective-permute-done | bytes 155680 | tf_op jit(solution)/shard_map/ppermute | solution.py:316
  78.0 5.4 %collective-permute-start.13 = (bf16[304,128]{1,0:T(8,128)(2,1)S(1)}, bf16[304,128]{1,0:T(8,128)(2,1)S(1)}, u32[]{:S(2)}, u32[]{:S(2)}) collective-permute-start(bf16[304,128]{1,0:T(8,128)(2,1)S(1)} %fusion.7), channel_id=1, source_target_pairs={{0,128},{16,144},{32,160},{48,176},{64,192},{80,208},{96,224},{112... | collective-permute-start | bytes 233480 | tf_op jit(solution)/shard_map/ppermute | solution.py:316
  83.4 1.8 %collective-permute-done.13 = bf16[304,128]{1,0:T(8,128)(2,1)S(1)} collective-permute-done((bf16[304,128]{1,0:T(8,128)(2,1)S(1)}, bf16[304,128]{1,0:T(8,128)(2,1)S(1)}, u32[]{:S(2)}, u32[]{:S(2)}) %collective-permute-start.13) | collective-permute-done | bytes 77856 | tf_op jit(solution)/shard_map/ppermute | solution.py:316
  85.2 5.6 %collective-permute-start.16 = (bf16[304,128]{1,0:T(8,128)(2,1)S(1)}, bf16[304,128]{1,0:T(8,128)(2,1)S(1)}, u32[]{:S(2)}, u32[]{:S(2)}) collective-permute-start(bf16[304,128]{1,0:T(8,128)(2,1)S(1)} %fusion.6), channel_id=1, source_target_pairs={{0,3},{1,2},{2,1},{3,0},{4,7},{5,6},{6,5},{7,4},{8,11},{9,10},{10,... | collective-permute-start | bytes 233480 | tf_op jit(solution)/shard_map/ppermute | solution.py:316
  91.2 1.5 %collective-permute-done.16 = bf16[304,128]{1,0:T(8,128)(2,1)S(1)} collective-permute-done((bf16[304,128]{1,0:T(8,128)(2,1)S(1)}, bf16[304,128]{1,0:T(8,128)(2,1)S(1)}, u32[]{:S(2)}, u32[]{:S(2)}) %collective-permute-start.16) | collective-permute-done | bytes 77856 | tf_op jit(solution)/shard_map/ppermute | solution.py:316
  92.8 3.6 %collective-permute-done.15 = bf16[304,128]{1,0:T(8,128)(2,1)S(1)} collective-permute-done((bf16[304,128]{1,0:T(8,128)(2,1)S(1)}, bf16[304,128]{1,0:T(8,128)(2,1)S(1)}, u32[]{:S(2)}, u32[]{:S(2)}) %collective-permute-start.15) | collective-permute-done | bytes 77856 | tf_op jit(solution)/shard_map/ppermute | solution.py:316
  96.4 2.4 %collective-permute-start.19 = (bf16[304,128]{1,0:T(8,128)(2,1)S(1)}, bf16[304,128]{1,0:T(8,128)(2,1)S(1)}, u32[]{:S(2)}, u32[]{:S(2)}) collective-permute-start(bf16[304,128]{1,0:T(8,128)(2,1)S(1)} %add_convert_fusion), channel_id=1, source_target_pairs={{0,12},{1,13},{2,14},{3,15},{4,8},{5,9},{6,10},{7,11},{8,4},{9,5},... | collective-permute-start | bytes 233480 | tf_op jit(solution)/shard_map/ppermute | solution.py:316
  98.8 4.8 %collective-permute-start.18 = (bf16[304,128]{1,0:T(8,128)(2,1)S(1)}, bf16[304,128]{1,0:T(8,128)(2,1)S(1)}, u32[]{:S(2)}, u32[]{:S(2)}) collective-permute-start(bf16[304,128]{1,0:T(8,128)(2,1)S(1)} %add_convert_fusion), channel_id=1, source_target_pairs={{0,8},{1,9},{2,10},{3,11},{4,12},{5,13},{6,14},{7,15},{8,0},{9,1},... | collective-permute-start | bytes 233480 | tf_op jit(solution)/shard_map/ppermute | solution.py:316
  105.5 5.4 %collective-permute-done.17 = bf16[304,128]{1,0:T(8,128)(2,1)S(1)} collective-permute-done((bf16[304,128]{1,0:T(8,128)(2,1)S(1)}, bf16[304,128]{1,0:T(8,128)(2,1)S(1)}, u32[]{:S(2)}, u32[]{:S(2)}) %collective-permute-start.17) | collective-permute-done | bytes 77856 | tf_op jit(solution)/shard_map/ppermute | solution.py:316
  110.9 3.0 %collective-permute-start.20 = (bf16[144,128]{1,0:T(8,128)(2,1)S(1)}, bf16[144,128]{1,0:T(8,128)(2,1)S(1)}, u32[]{:S(2)}, u32[]{:S(2)}) collective-permute-start(bf16[144,128]{1,0:T(8,128)(2,1)S(1)} %slice.130), channel_id=1, source_target_pairs={{0,128},{16,144},{32,160},{48,176},{64,192},{80,208},{96,224},{112... | collective-permute-start | bytes 110600 | tf_op jit(solution)/shard_map/ppermute | solution.py:316
  113.9 1.4 %collective-permute-done.20 = bf16[144,128]{1,0:T(8,128)(2,1)S(1)} collective-permute-done((bf16[144,128]{1,0:T(8,128)(2,1)S(1)}, bf16[144,128]{1,0:T(8,128)(2,1)S(1)}, u32[]{:S(2)}, u32[]{:S(2)}) %collective-permute-start.20) | collective-permute-done | bytes 36896 | tf_op jit(solution)/shard_map/ppermute | solution.py:316
  115.4 1.5 %collective-permute-start.21 = (bf16[2,144,128]{2,1,0:T(8,128)(2,1)S(1)}, bf16[2,144,128]{2,1,0:T(8,128)(2,1)S(1)}, u32[]{:S(2)}, u32[]{:S(2)}) collective-permute-start(bf16[2,144,128]{2,1,0:T(8,128)(2,1)S(1)} %get-tuple-element.50), channel_id=1, source_target_pairs={{0,32},{16,48},{32,0},{48,16},{64,96},{80,112},{96,64},{112,80},{1... | collective-permute-start | bytes 221192 | tf_op jit(solution)/shard_map/ppermute | solution.py:316
  116.9 1.8 %collective-permute-start.23 = (bf16[2,144,128]{2,1,0:T(8,128)(2,1)S(1)}, bf16[2,144,128]{2,1,0:T(8,128)(2,1)S(1)}, u32[]{:S(2)}, u32[]{:S(2)}) collective-permute-start(bf16[2,144,128]{2,1,0:T(8,128)(2,1)S(1)} %get-tuple-element.50), channel_id=1, source_target_pairs={{0,96},{16,112},{32,64},{48,80},{64,32},{80,48},{96,0},{112,16},{1... | collective-permute-start | bytes 221192 | tf_op jit(solution)/shard_map/ppermute | solution.py:316
  118.6 1.5 %collective-permute-done.22 = bf16[2,144,128]{2,1,0:T(8,128)(2,1)S(1)} collective-permute-done((bf16[2,144,128]{2,1,0:T(8,128)(2,1)S(1)}, bf16[2,144,128]{2,1,0:T(8,128)(2,1)S(1)}, u32[]{:S(2)}, u32[]{:S(2)}) %collective-permute-start.22) | collective-permute-done | bytes 73760 | tf_op jit(solution)/shard_map/ppermute | solution.py:316
  121.3 6.3 %collective-permute-start.24 = (bf16[4,2,144,128]{3,2,1,0:T(8,128)(2,1)S(1)}, bf16[4,2,144,128]{3,2,1,0:T(8,128)(2,1)S(1)}, u32[]{:S(2)}, u32[]{:S(2)}) collective-permute-start(bf16[4,2,144,128]{3,2,1,0:T(8,128)(2,1)S(1)} %get-tuple-element.42), channel_id=1, source_target_pairs={{0,16},{16,0},{32,48},{48,32},{64,80},{80,64},{96,112},{112,96},{1... | collective-permute-start | bytes 884744 | tf_op jit(solution)/shard_map/ppermute | solution.py:316
  127.6 1.7 %feature_step.1 = bf16[16,64,128]{2,1,0:T(8,128)(2,1)} custom-call(bf16[18,64,384]{2,1,0:T(8,128)(2,1)S(1)} %get-tuple-element.25.first3, bf16[9,128,128]{2,1,0:T(8,128)(2,1)S(1)} %bitcast.94), custom_call_target="tpu_custom_call" | custom-call | tf_op jit(solution)/shard_map/feature_step/pallas_call | solution.py:296
  (102 shorter events, 29.4 us)
Async XLA Ops:
  0.6 12.2 %copy-start.6 = (s32[4]{0:T(128)S(1)}, s32[4]{0:T(128)}, u32[]{:S(2)}) copy-start(s32[4]{0:T(128)} %constant.133) | copy-start | bytes 52
  0.6 12.2 %copy-start.7 = (s32[4]{0:T(128)S(1)}, s32[4]{0:T(128)}, u32[]{:S(2)}) copy-start(s32[4]{0:T(128)} %constant.134) | copy-start | bytes 52
  1.5 11.5 %collective-permute-start.4 = (bf16[160,128]{1,0:T(8,128)(2,1)S(1)}, bf16[160,128]{1,0:T(8,128)(2,1)S(1)}, u32[]{:S(2)}, u32[]{:S(2)}) collective-permute-start(bf16[160,128]{1,0:T(8,128)(2,1)S(1)} %get-tuple-element.52), channel_id=1, source_target_pairs={{0,128},{16,144},{32,160},{48,176},{64,192},{80,208},{96,224},{112... | collective-permute-start | bytes 122888 | tf_op jit(solution)/shard_map/ppermute | solution.py:316
  7.2 16.7 %copy-start.3 = (bf16[16,16,4,128]{3,2,1,0:T(4,128)(2,1)S(1)}, bf16[16,16,4,128]{3,2,1,0:T(4,128)(2,1)}, u32[]{:S(2)}) copy-start(bf16[16,16,4,128]{3,2,1,0:T(4,128)(2,1)} %param.10) | copy-start | bytes 786436
  7.2 16.7 %collective-permute-start.1 = (bf16[16,48,128]{2,1,0:T(8,128)(2,1)S(1)}, bf16[16,48,128]{2,1,0:T(8,128)(2,1)S(1)}, u32[]{:S(2)}, u32[]{:S(2)}) collective-permute-start(bf16[16,48,128]{2,1,0:T(8,128)(2,1)S(1)} %pad_maximum_fusion.10), channel_id=1, source_target_pairs={{1,0},{2,1},{3,2},{4,3},{5,4},{6,5},{7,6},{8,7},{9,8},{10,9},{11,1... | collective-permute-start | bytes 589832 | tf_op jit(solution)/shard_map/ppermute | solution.py:322
  8.7 15.2 %collective-permute-start = (bf16[16,48,128]{2,1,0:T(8,128)(2,1)S(1)}, bf16[16,48,128]{2,1,0:T(8,128)(2,1)S(1)}, u32[]{:S(2)}, u32[]{:S(2)}) collective-permute-start(bf16[16,48,128]{2,1,0:T(8,128)(2,1)S(1)} %pad_maximum_fusion.9), channel_id=1, source_target_pairs={{0,1},{1,2},{2,3},{3,4},{4,5},{5,6},{6,7},{7,8},{8,9},{9,10},{10,1... | collective-permute-start | bytes 589832 | tf_op jit(solution)/shard_map/ppermute | solution.py:322
  13.0 4.9 %collective-permute-start.6 = (bf16[2,160,128]{2,1,0:T(8,128)(2,1)S(1)}, bf16[2,160,128]{2,1,0:T(8,128)(2,1)S(1)}, u32[]{:S(2)}, u32[]{:S(2)}) collective-permute-start(bf16[2,160,128]{2,1,0:T(8,128)(2,1)S(1)} %get-tuple-element.48), channel_id=1, source_target_pairs={{0,64},{16,80},{32,96},{48,112},{64,0},{80,16},{96,32},{112,48},{1... | collective-permute-start | bytes 245768 | tf_op jit(solution)/shard_map/ppermute | solution.py:316
  15.9 3.9 %collective-permute-start.5 = (bf16[2,160,128]{2,1,0:T(8,128)(2,1)S(1)}, bf16[2,160,128]{2,1,0:T(8,128)(2,1)S(1)}, u32[]{:S(2)}, u32[]{:S(2)}) collective-permute-start(bf16[2,160,128]{2,1,0:T(8,128)(2,1)S(1)} %get-tuple-element.48), channel_id=1, source_target_pairs={{0,32},{16,48},{32,0},{48,16},{64,96},{80,112},{96,64},{112,80},{1... | collective-permute-start | bytes 245768 | tf_op jit(solution)/shard_map/ppermute | solution.py:316
  16.2 4.9 %collective-permute-start.7 = (bf16[2,160,128]{2,1,0:T(8,128)(2,1)S(1)}, bf16[2,160,128]{2,1,0:T(8,128)(2,1)S(1)}, u32[]{:S(2)}, u32[]{:S(2)}) collective-permute-start(bf16[2,160,128]{2,1,0:T(8,128)(2,1)S(1)} %get-tuple-element.48), channel_id=1, source_target_pairs={{0,96},{16,112},{32,64},{48,80},{64,32},{80,48},{96,0},{112,16},{1... | collective-permute-start | bytes 245768 | tf_op jit(solution)/shard_map/ppermute | solution.py:316
  21.1 10.8 %collective-permute-start.8 = (bf16[4,2,160,128]{3,2,1,0:T(8,128)(2,1)S(1)}, bf16[4,2,160,128]{3,2,1,0:T(8,128)(2,1)S(1)}, u32[]{:S(2)}, u32[]{:S(2)}) collective-permute-start(bf16[4,2,160,128]{3,2,1,0:T(8,128)(2,1)S(1)} %get-tuple-element.40), channel_id=1, source_target_pairs={{0,16},{16,0},{32,48},{48,32},{64,80},{80,64},{96,112},{112,96},{1... | collective-permute-start | bytes 983048 | tf_op jit(solution)/shard_map/ppermute | solution.py:316
  23.9 1.0 copy-start.4
  25.6 9.1 %collective-permute-start.3 = (bf16[11,128,128]{2,1,0:T(8,128)(2,1)}, bf16[11,128,128]{2,1,0:T(8,128)(2,1)}, u32[]{:S(2)}, u32[]{:S(2)}) collective-permute-start(bf16[11,128,128]{2,1,0:T(8,128)(2,1)} %pad_maximum_fusion.6), channel_id=1, source_target_pairs={{16,0},{32,16},{48,32},{64,48},{80,64},{96,80},{112,96},{128,112},... | collective-permute-start | bytes 1081352 | tf_op jit(solution)/shard_map/ppermute | solution.py:322
  28.3 8.3 %collective-permute-start.2 = (bf16[11,128,128]{2,1,0:T(8,128)(2,1)}, bf16[11,128,128]{2,1,0:T(8,128)(2,1)}, u32[]{:S(2)}, u32[]{:S(2)}) collective-permute-start(bf16[11,128,128]{2,1,0:T(8,128)(2,1)} %pad_maximum_fusion.5), channel_id=1, source_target_pairs={{0,16},{16,32},{32,48},{48,64},{64,80},{80,96},{96,112},{112,128},... | collective-permute-start | bytes 1081352 | tf_op jit(solution)/shard_map/ppermute | solution.py:322
  38.5 2.2 %copy-start = (bf16[3,3,128,128]{3,2,1,0:T(8,128)(2,1)S(1)}, bf16[3,3,128,128]{3,2,1,0:T(8,128)(2,1)}, u32[]{:S(2)}) copy-start(bf16[3,3,128,128]{3,2,1,0:T(8,128)(2,1)} %param.12) | copy-start | bytes 884740
  38.5 2.2 %copy-start.1 = (bf16[3,3,128,128]{3,2,1,0:T(8,128)(2,1)S(1)}, bf16[3,3,128,128]{3,2,1,0:T(8,128)(2,1)}, u32[]{:S(2)}) copy-start(bf16[3,3,128,128]{3,2,1,0:T(8,128)(2,1)} %param.11) | copy-start | bytes 884740
  51.0 1.0 copy-start.2
  61.2 2.1 %collective-permute-start.9 = (bf16[4,2,304,128]{3,2,1,0:T(8,128)(2,1)S(1)}, bf16[4,2,304,128]{3,2,1,0:T(8,128)(2,1)S(1)}, u32[]{:S(2)}, u32[]{:S(2)}) collective-permute-start(bf16[4,2,304,128]{3,2,1,0:T(8,128)(2,1)S(1)} %bitcast.106), channel_id=1, source_target_pairs={{0,16},{16,0},{32,48},{48,32},{64,80},{80,64},{96,112},{112,96},{1... | collective-permute-start | bytes 1867784 | tf_op jit(solution)/shard_map/ppermute | solution.py:316
  65.4 6.4 %collective-permute-start.10 = (bf16[2,304,128]{2,1,0:T(8,128)(2,1)S(1)}, bf16[2,304,128]{2,1,0:T(8,128)(2,1)S(1)}, u32[]{:S(2)}, u32[]{:S(2)}) collective-permute-start(bf16[2,304,128]{2,1,0:T(8,128)(2,1)S(1)} %get-tuple-element.28), channel_id=1, source_target_pairs={{0,32},{16,48},{32,0},{48,16},{64,96},{80,112},{96,64},{112,80},{1... | collective-permute-start | bytes 466952 | tf_op jit(solution)/shard_map/ppermute | solution.py:316
  67.7 8.6 %collective-permute-start.12 = (bf16[2,304,128]{2,1,0:T(8,128)(2,1)S(1)}, bf16[2,304,128]{2,1,0:T(8,128)(2,1)S(1)}, u32[]{:S(2)}, u32[]{:S(2)}) collective-permute-start(bf16[2,304,128]{2,1,0:T(8,128)(2,1)S(1)} %get-tuple-element.29), channel_id=1, source_target_pairs={{0,96},{16,112},{32,64},{48,80},{64,32},{80,48},{96,0},{112,16},{1... | collective-permute-start | bytes 466952 | tf_op jit(solution)/shard_map/ppermute | solution.py:316
  69.7 8.3 %collective-permute-start.11 = (bf16[2,304,128]{2,1,0:T(8,128)(2,1)S(1)}, bf16[2,304,128]{2,1,0:T(8,128)(2,1)S(1)}, u32[]{:S(2)}, u32[]{:S(2)}) collective-permute-start(bf16[2,304,128]{2,1,0:T(8,128)(2,1)S(1)} %get-tuple-element.30), channel_id=1, source_target_pairs={{0,64},{16,80},{32,96},{48,112},{64,0},{80,16},{96,32},{112,48},{1... | collective-permute-start | bytes 466952 | tf_op jit(solution)/shard_map/ppermute | solution.py:316
  78.0 7.2 %collective-permute-start.13 = (bf16[304,128]{1,0:T(8,128)(2,1)S(1)}, bf16[304,128]{1,0:T(8,128)(2,1)S(1)}, u32[]{:S(2)}, u32[]{:S(2)}) collective-permute-start(bf16[304,128]{1,0:T(8,128)(2,1)S(1)} %fusion.7), channel_id=1, source_target_pairs={{0,128},{16,144},{32,160},{48,176},{64,192},{80,208},{96,224},{112... | collective-permute-start | bytes 233480 | tf_op jit(solution)/shard_map/ppermute | solution.py:316
  85.2 7.5 %collective-permute-start.16 = (bf16[304,128]{1,0:T(8,128)(2,1)S(1)}, bf16[304,128]{1,0:T(8,128)(2,1)S(1)}, u32[]{:S(2)}, u32[]{:S(2)}) collective-permute-start(bf16[304,128]{1,0:T(8,128)(2,1)S(1)} %fusion.6), channel_id=1, source_target_pairs={{0,3},{1,2},{2,1},{3,0},{4,7},{5,6},{6,5},{7,4},{8,11},{9,10},{10,... | collective-permute-start | bytes 233480 | tf_op jit(solution)/shard_map/ppermute | solution.py:316
  90.9 5.5 %collective-permute-start.15 = (bf16[304,128]{1,0:T(8,128)(2,1)S(1)}, bf16[304,128]{1,0:T(8,128)(2,1)S(1)}, u32[]{:S(2)}, u32[]{:S(2)}) collective-permute-start(bf16[304,128]{1,0:T(8,128)(2,1)S(1)} %fusion.6), channel_id=1, source_target_pairs={{0,2},{1,3},{2,0},{3,1},{4,6},{5,7},{6,4},{7,5},{8,10},{9,11},{10,... | collective-permute-start | bytes 233480 | tf_op jit(solution)/shard_map/ppermute | solution.py:316
  90.9 5.5 %collective-permute-start.14 = (bf16[304,128]{1,0:T(8,128)(2,1)S(1)}, bf16[304,128]{1,0:T(8,128)(2,1)S(1)}, u32[]{:S(2)}, u32[]{:S(2)}) collective-permute-start(bf16[304,128]{1,0:T(8,128)(2,1)S(1)} %fusion.6), channel_id=1, source_target_pairs={{0,1},{1,0},{2,3},{3,2},{4,5},{5,4},{6,7},{7,6},{8,9},{9,8},{10,11... | collective-permute-start | bytes 233480 | tf_op jit(solution)/shard_map/ppermute | solution.py:316
  96.4 8.1 %collective-permute-start.19 = (bf16[304,128]{1,0:T(8,128)(2,1)S(1)}, bf16[304,128]{1,0:T(8,128)(2,1)S(1)}, u32[]{:S(2)}, u32[]{:S(2)}) collective-permute-start(bf16[304,128]{1,0:T(8,128)(2,1)S(1)} %add_convert_fusion), channel_id=1, source_target_pairs={{0,12},{1,13},{2,14},{3,15},{4,8},{5,9},{6,10},{7,11},{8,4},{9,5},... | collective-permute-start | bytes 233480 | tf_op jit(solution)/shard_map/ppermute | solution.py:316
  98.8 6.6 %collective-permute-start.18 = (bf16[304,128]{1,0:T(8,128)(2,1)S(1)}, bf16[304,128]{1,0:T(8,128)(2,1)S(1)}, u32[]{:S(2)}, u32[]{:S(2)}) collective-permute-start(bf16[304,128]{1,0:T(8,128)(2,1)S(1)} %add_convert_fusion), channel_id=1, source_target_pairs={{0,8},{1,9},{2,10},{3,11},{4,12},{5,13},{6,14},{7,15},{8,0},{9,1},... | collective-permute-start | bytes 233480 | tf_op jit(solution)/shard_map/ppermute | solution.py:316
  103.6 7.2 %collective-permute-start.17 = (bf16[304,128]{1,0:T(8,128)(2,1)S(1)}, bf16[304,128]{1,0:T(8,128)(2,1)S(1)}, u32[]{:S(2)}, u32[]{:S(2)}) collective-permute-start(bf16[304,128]{1,0:T(8,128)(2,1)S(1)} %add_convert_fusion), channel_id=1, source_target_pairs={{0,4},{1,5},{2,6},{3,7},{4,0},{5,1},{6,2},{7,3},{8,12},{9,13},{10,... | collective-permute-start | bytes 233480 | tf_op jit(solution)/shard_map/ppermute | solution.py:316
  110.9 4.4 %collective-permute-start.20 = (bf16[144,128]{1,0:T(8,128)(2,1)S(1)}, bf16[144,128]{1,0:T(8,128)(2,1)S(1)}, u32[]{:S(2)}, u32[]{:S(2)}) collective-permute-start(bf16[144,128]{1,0:T(8,128)(2,1)S(1)} %slice.130), channel_id=1, source_target_pairs={{0,128},{16,144},{32,160},{48,176},{64,192},{80,208},{96,224},{112... | collective-permute-start | bytes 110600 | tf_op jit(solution)/shard_map/ppermute | solution.py:316
  115.3 4.8 %collective-permute-start.22 = (bf16[2,144,128]{2,1,0:T(8,128)(2,1)S(1)}, bf16[2,144,128]{2,1,0:T(8,128)(2,1)S(1)}, u32[]{:S(2)}, u32[]{:S(2)}) collective-permute-start(bf16[2,144,128]{2,1,0:T(8,128)(2,1)S(1)} %get-tuple-element.50), channel_id=1, source_target_pairs={{0,64},{16,80},{32,96},{48,112},{64,0},{80,16},{96,32},{112,48},{1... | collective-permute-start | bytes 221192 | tf_op jit(solution)/shard_map/ppermute | solution.py:316
  115.4 4.7 %collective-permute-start.21 = (bf16[2,144,128]{2,1,0:T(8,128)(2,1)S(1)}, bf16[2,144,128]{2,1,0:T(8,128)(2,1)S(1)}, u32[]{:S(2)}, u32[]{:S(2)}) collective-permute-start(bf16[2,144,128]{2,1,0:T(8,128)(2,1)S(1)} %get-tuple-element.50), channel_id=1, source_target_pairs={{0,32},{16,48},{32,0},{48,16},{64,96},{80,112},{96,64},{112,80},{1... | collective-permute-start | bytes 221192 | tf_op jit(solution)/shard_map/ppermute | solution.py:316
  116.9 4.4 %collective-permute-start.23 = (bf16[2,144,128]{2,1,0:T(8,128)(2,1)S(1)}, bf16[2,144,128]{2,1,0:T(8,128)(2,1)S(1)}, u32[]{:S(2)}, u32[]{:S(2)}) collective-permute-start(bf16[2,144,128]{2,1,0:T(8,128)(2,1)S(1)} %get-tuple-element.50), channel_id=1, source_target_pairs={{0,96},{16,112},{32,64},{48,80},{64,32},{80,48},{96,0},{112,16},{1... | collective-permute-start | bytes 221192 | tf_op jit(solution)/shard_map/ppermute | solution.py:316
  121.3 9.2 %collective-permute-start.24 = (bf16[4,2,144,128]{3,2,1,0:T(8,128)(2,1)S(1)}, bf16[4,2,144,128]{3,2,1,0:T(8,128)(2,1)S(1)}, u32[]{:S(2)}, u32[]{:S(2)}) collective-permute-start(bf16[4,2,144,128]{3,2,1,0:T(8,128)(2,1)S(1)} %get-tuple-element.42), channel_id=1, source_target_pairs={{0,16},{16,0},{32,48},{48,32},{64,80},{80,64},{96,112},{112,96},{1... | collective-permute-start | bytes 884744 | tf_op jit(solution)/shard_map/ppermute | solution.py:316
  (1 other events, 0.8 us)

commit v2 on v1

v2 whole, which is shorter than its diff:
```python
import functools

import jax
import jax.numpy as jnp
from jax import lax
from jax.experimental import pallas as pl
from jax.experimental.pallas import tpu as pltpu
from jax.sharding import PartitionSpec as P

BF = jnp.bfloat16
F32 = jnp.float32
CH = 128
WIDE = 256
MIB = 1024 * 1024
VM = pl.BlockSpec(memory_space=pltpu.VMEM)
SM = pl.BlockSpec(memory_space=pltpu.SMEM)


def call(kernel, name, outs, ins, scratch=(), limit=16, flops=0, moved=0):
    shapes = tuple(jax.ShapeDtypeStruct(shape, dtype) for shape, dtype in outs)
    return pl.pallas_call(
        kernel,
        name=name,
        out_shape=shapes,
        in_specs=[SM if v.ndim == 1 else VM for v in ins],
        out_specs=tuple(VM for _ in outs),
        scratch_shapes=[pltpu.VMEM(shape, dtype) for shape, dtype in scratch],
        compiler_params=pltpu.CompilerParams(vmem_limit_bytes=limit * MIB),
        cost_estimate=pl.CostEstimate(flops=flops, bytes_accessed=moved, transcendentals=0),
    )(*ins)


def dot_nn(a, b):
    return jnp.dot(a, b, preferred_element_type=F32)


def dot_nt(a, b):
    return lax.dot_general(a, b, (((1,), (1,)), ((), ())), preferred_element_type=F32)


def dot_tn(a, b):
    return lax.dot_general(a, b, (((0,), (0,)), ((), ())), preferred_element_type=F32)


def sigmoid(value):
    return 0.5 * jnp.tanh(0.5 * value) + 0.5


def slope_of(value):
    sigma = sigmoid(value)
    return sigma * (1.0 + value * (1.0 - sigma))


def rounded(value):
    return value.astype(BF).astype(F32)


def three(value):
    count = value.shape[0]
    left = pltpu.roll(value, 4, 0)
    right = pltpu.roll(value, count - 4, 0)
    return jnp.concatenate([left.astype(BF), value.astype(BF), right.astype(BF)], axis=1)


def taps(ref, start, rows, cols=None):
    parts = []
    for r in range(3):
        part = ref[pl.ds(start + r, rows)] if cols is None else ref[pl.ds(start + r, rows), cols[0] : cols[1], :]
        parts.append(part.reshape(part.shape[0] * part.shape[1], part.shape[2]))
    return jnp.concatenate(parts, axis=1)


def column_mask(first, width, limit):
    place = first + lax.broadcasted_iota(jnp.int32, (width, CH), 0) // 4
    return jnp.where((place >= 0) & (place < limit), 1.0, 0.0).astype(F32)


def row_ok(place, limit):
    return jnp.where((place >= 0) & (place < limit), 1.0, 0.0).astype(F32)


def masked(value, mask, first, limit):
    rows = []
    for k in range(value.shape[0]):
        rows.append((value[k] * (mask * row_ok(first + k, limit)))[None])
    return jnp.concatenate(rows, axis=0)


def pooled_pair(row):
    count = row.shape[0]
    low = (row + pltpu.roll(row, count - 4, 0)).reshape(count // 16, 2, 8, CH)
    high = (row + pltpu.roll(row, 4, 0)).reshape(count // 16, 2, 8, CH)
    first = lax.broadcasted_iota(jnp.int32, (count // 16, 8, CH), 1) < 4
    return jnp.where(first, low[:, 0], high[:, 1]).reshape(count // 2, CH)


def repeated(row):
    count = row.shape[0]
    first = lax.broadcasted_iota(jnp.int32, (count, CH), 0) % 8 < 4
    even = jnp.where(first, row, pltpu.roll(row, 4, 0)).reshape(count // 8, 1, 8, CH)
    odd = jnp.where(first, pltpu.roll(row, count - 4, 0), row).reshape(count // 8, 1, 8, CH)
    return jnp.concatenate([even, odd], axis=1).reshape(count * 2, CH)


def pack_columns_kernel(feat, cot, conv, proj, right, left, weights):
    right[:, 0:32, :] = feat[:, 32:64, :]
    right[:, 32:48, :] = cot[:, 48:64, :]
    left[:, 0:32, :] = feat[:, 0:32, :]
    left[:, 32:48, :] = cot[:, 0:16, :]
    weights[0:144, :] = conv[...].reshape(144, CH)
    weights[144:160, :] = proj[...]


def pack_rows_kernel(feat, cot, before, after, own, other, down, up, weights):
    for out, first, second in ((down, 8, 12), (up, 0, 0)):
        out[0:8, 0:32, :] = before[first : first + 8, 0:32, :]
        out[0:8, 32:96, :] = feat[first : first + 8]
        out[0:8, 96:128, :] = after[first : first + 8, 0:32, :]
        out[8:12, 0:16, :] = before[second : second + 4, 32:48, :]
        out[8:12, 16:80, :] = cot[second : second + 4]
        out[8:12, 80:96, :] = after[second : second + 4, 32:48, :]
        out[8:12, 96:128, :] = jnp.zeros((4, 32, CH), BF)
    weights[0] = own[...]
    weights[1] = other[...]


def stack_kernel(*refs):
    out = refs[-1]
    for k, ref in enumerate(refs[:-1]):
        out[k] = ref[...]


def forward_kernel(
    meta, feat, before, after, above, below, w1, w2, pool3, slope1, slope2, act, feat3o, act3o, feat3, act3, pre1, pre2, act2
):
    top, left, height, breadth = (meta[0], meta[1], meta[2], meta[3])
    mask = column_mask(left - 8, 128, breadth)
    coarse_mask = column_mask(left // 2 - 4, 64, breadth // 2)

    @pl.loop(0, 4)
    def _(b):
        rows = pl.ds(4 * b, 4)
        middle = jnp.concatenate([before[rows, 0:32, :], feat[rows], after[rows, 0:32, :]], axis=1)
        feat3[pl.ds(4 * b + 8, 4)] = three(middle.reshape(512, CH).astype(F32)).reshape(4, 128, 3 * CH)

    @pl.loop(0, 2)
    def _(b):
        block = above[pl.ds(4 * b, 4)].reshape(512, CH).astype(F32)
        feat3[pl.ds(4 * b, 4)] = three(block).reshape(4, 128, 3 * CH)
        block = below[pl.ds(4 * b, 4)].reshape(512, CH).astype(F32)
        feat3[pl.ds(4 * b + 24, 4)] = three(block).reshape(4, 128, 3 * CH)

    first_w = w1[...]

    @pl.loop(0, 6)
    def _(b):
        pre = dot_nn(taps(feat3, 5 * b, 5), first_w)
        pre1[pl.ds(5 * b, 5)] = pre.reshape(5, 128, CH)
        value = rounded(pre * sigmoid(pre)).reshape(5, 128, CH)
        value = masked(value, mask, top - 7 + 5 * b, height)
        act3[pl.ds(5 * b, 5)] = three(value.reshape(640, CH)).reshape(5, 128, 3 * CH)

    second_w = w2[...]

    @pl.loop(0, 7)
    def _(b):
        pre = dot_nn(taps(act3, 4 * b, 4), second_w)
        pre2[pl.ds(4 * b, 4)] = pre.reshape(4, 128, CH)
        value = (pre * sigmoid(pre)).astype(BF)
        act2[pl.ds(4 * b, 4)] = value.reshape(4, 128, CH)
        value = value.astype(F32).reshape(4, 128, CH)
        coarse = []
        for k in range(2):
            small = rounded(0.25 * pooled_pair(value[2 * k] + value[2 * k + 1]))
            coarse.append(small * (coarse_mask * row_ok(top // 2 - 3 + 2 * b + k, height // 2)))
        coarse = jnp.concatenate(coarse, axis=0)
        pool3[pl.ds(2 * b, 2)] = three(coarse).reshape(2, 64, 3 * CH)

    @pl.loop(0, 18)
    def _(k):
        slope1[k] = slope_of(pre1[k + 6, 16:112, :])
        feat3o[k] = feat3[k + 7, 32:96, :]
        act3o[k] = act3[k + 6, 32:96, :]

    @pl.loop(0, 20)
    def _(k):
        slope2[k] = slope_of(pre2[k + 4, 16:112, :])

    @pl.loop(0, 16)
    def _(k):
        act[k] = act2[k + 6, 32:96, :]


def fine_forward(meta, feat, before, after, above, below, w1, w2):
    return call(
        forward_kernel,
        "fine_forward",
        (
            ((14, 64, 384), BF),
            ((18, 96, CH), F32),
            ((20, 96, CH), F32),
            ((16, 64, CH), BF),
            ((18, 64, 384), BF),
            ((18, 64, 384), BF),
        ),
        (meta, feat, before, after, above, below, w1, w2),
        (
            ((32, 128, 384), BF),
            ((30, 128, 384), BF),
            ((30, 128, CH), F32),
            ((28, 128, CH), F32),
            ((28, 128, CH), BF),
        ),
        limit=24,
        flops=4 * 10**9,
    )


def coarse_kernel(
    meta, pool3, cot, before, after, above, below, near0, near1, near2, near3, far, act,
    blended, keep, send, pooled_grad, wcat, projs, wide3, projin,
):
    top, left, height, breadth, me = (meta[0], meta[1], meta[2], meta[3], meta[4])
    core = me % 2
    near = (near0, near1, near2, near3)
    for rel in range(16):
        c, x, y = (rel % 2, (rel // 2) % 4, rel // 8)
        place = pl.ds(pl.multiple_of((me ^ rel) * 16, 16), 16)
        source = far.at[x, y] if c else near[x].at[y]
        for t in range(9):
            wcat[place, t * CH : (t + 1) * CH] = source[16 * t : 16 * t + 16, :]
        projs[place, :] = source[144:160, :]
    proj_w = projs[...]

    def pair_sum(a, b):
        return pooled_pair(a.astype(F32) + b.astype(F32))

    for k in range(2):
        projin[k] = pair_sum(above[8 + 2 * k, 0:96, :], above[9 + 2 * k, 0:96, :])
        projin[k + 10] = pair_sum(below[8 + 2 * k, 0:96, :], below[9 + 2 * k, 0:96, :])

    @pl.loop(0, 8)
    def _(k):
        rows = pl.ds(2 * k, 2)
        pair = jnp.concatenate([before[rows, 32:48, :], cot[rows], after[rows, 32:48, :]], axis=1)
        projin[k + 2] = pair_sum(pair[0], pair[1])

    proj_in = projin[...].reshape(576, CH)
    proj_in_bf = proj_in.astype(BF)
    pre = dot_nt(taps(pool3, 0, 12), wcat[...]).reshape(12, 64, WIDE)[:, 8:56].reshape(576, WIDE)
    sigma = sigmoid(pre)
    coarse_act = pre * sigma
    act_grad = dot_nt(proj_in_bf, proj_w)
    grad = rounded(act_grad * (sigma * (1.0 + pre * (1.0 - sigma)))).reshape(12, 48, WIDE)
    mask = column_mask(left // 2 - 2, 48, breadth // 2)
    mask = jnp.concatenate([mask, mask], axis=1)
    grad = masked(grad, mask, top // 2 - 2, height // 2)
    wide3[...] = three(grad.reshape(576, WIDE)).reshape(12, 48, 3 * WIDE)
    own_grad = grad[2:10, 8:40].reshape(256, WIDE).astype(BF)
    own_act = coarse_act.reshape(12, 48, WIDE)[2:10, 8:40].reshape(256, WIDE).astype(BF)
    own_in = proj_in.reshape(12, 48, CH)[2:10, 8:40].reshape(256, CH).astype(BF)

    def emit(first, last, value):
        value = value.reshape(8, 2, 16, CH)
        even, odd = (value[:, 0], value[:, 1])
        keep[:, first:last, :] = jnp.where(core == 0, even, odd).astype(BF)
        send[:, first:last, :] = jnp.where(core == 0, odd, even).astype(BF)

    for r in range(3):
        source = pool3[2 + r : 10 + r, 16:48, :].reshape(256, 3 * CH)
        part = dot_tn(own_grad, source)
        for s in range(3):
            t = 3 * r + s
            emit(16 * t, 16 * t + 16, part[:, s * CH : (s + 1) * CH])
    emit(144, 160, dot_tn(own_act, own_in))
    total = None
    for r in range(3):
        lhs = wide3[r : r + 10].reshape(480, 3 * WIDE)
        first = 3 * (2 - r)
        rhs = jnp.concatenate([wcat[:, (first + 2 - s) * CH : (first + 3 - s) * CH] for s in range(3)], axis=0)
        part = dot_nn(lhs, rhs)
        total = part if total is None else total + part
    pooled_grad[...] = total.reshape(10, 48, CH)
    projected = dot_nn(own_act, proj_w).reshape(8, 32, CH)
    for k in range(8):
        row = repeated(projected[k])
        for e in range(2):
            blended[2 * k + e] = (act[2 * k + e].astype(F32) + row).astype(BF)


def coarse_step(meta, pool3, cot, before, after, above, below, near, far, act):
    return call(
        coarse_kernel,
        "coarse_step",
        (((16, 64, CH), BF), ((8, 160, CH), BF), ((8, 160, CH), BF), ((10, 48, CH), F32)),
        (meta, pool3, cot, before, after, above, below) + tuple(near) + (far, act),
        (
            ((WIDE, 9 * CH), BF),
            ((WIDE, CH), BF),
            ((12, 48, 3 * WIDE), BF),
            ((12, 48, CH), F32),
        ),
        limit=20,
        flops=2 * 10**9,
    )


def flipped(weight):
    return jnp.concatenate([weight[8 - t] for t in range(9)], axis=1)


def backward_kernel(
    meta, pooled_grad, cot, before, after, above, below, slope1, slope2, feat3, act3, w2,
    keep, send, first3, second3, grads,
):
    top, left, height, breadth = (meta[0], meta[1], meta[2], meta[3])
    mask = column_mask(left - 4, 96, breadth)

    def second_rows(k, pair):
        wide = 0.25 * repeated(pooled_grad[k])
        rows = []
        for e in range(2):
            value = rounded((pair[e].astype(F32) + wide) * slope2[2 * k + e])
            rows.append(value * (mask * row_ok(top - 2 + 2 * k + e, height)))
        second3[pl.ds(2 * k, 2)] = three(jnp.concatenate(rows, axis=0)).reshape(2, 96, 3 * CH)

    second_rows(0, above[10:12, 0:96, :])
    second_rows(9, below[8:10, 0:96, :])

    @pl.loop(0, 8)
    def _(k):
        rows = pl.ds(2 * k, 2)
        second_rows(k + 1, jnp.concatenate([before[rows, 32:48, :], cot[rows], after[rows, 32:48, :]], axis=1))

    def weight_grad(source, grad):
        return [dot_tn(source[r : r + 16].reshape(1024, 3 * CH), grad) for r in range(3)]

    def emit(base, parts):
        for r in range(3):
            grads[base + 384 * r : base + 384 * (r + 1), :] = parts[r].astype(BF)

    second_own = second3[2:18, 16:80, CH : 2 * CH].reshape(1024, CH)
    emit(1152, weight_grad(act3, second_own))
    back_w = flipped(w2)

    @pl.loop(0, 3)
    def _(b):
        value = dot_nt(taps(second3, 6 * b, 6), back_w).reshape(6, 96, CH)
        value = rounded(value * slope1[pl.ds(6 * b, 6)])
        value = masked(value, mask, top - 1 + 6 * b, height)
        out = three(value.reshape(576, CH)).reshape(6, 96, 3 * CH)
        first3[pl.ds(6 * b, 6)] = out[:, 16:80, :]

    first_own = first3[1:17, :, CH : 2 * CH].reshape(1024, CH)
    emit(0, weight_grad(feat3, first_own))
    core = meta[4] % 2
    for k in range(8):
        keep[k] = grads[pl.ds(pl.multiple_of((2 * k + core) * 144, 16), 144), :]
        send[k] = grads[pl.ds(pl.multiple_of((2 * k + 1 - core) * 144, 16), 144), :]


def fine_backward(meta, pooled_grad, cot, before, after, above, below, slope1, slope2, feat3, act3, w2):
    return call(
        backward_kernel,
        "fine_backward",
        (((8, 144, CH), BF), ((8, 144, CH), BF), ((18, 64, 384), BF)),
        (meta, pooled_grad, cot, before, after, above, below, slope1, slope2, feat3, act3, w2),
        (((20, 96, 384), BF), ((2304, CH), BF)),
        limit=20,
        flops=2 * 10**9,
    )


def feature_kernel(first3, w1, out):
    back_w = flipped(w1)

    @pl.loop(0, 2)
    def _(b):
        out[pl.ds(8 * b, 8)] = dot_nt(taps(first3, 8 * b, 8), back_w).astype(BF).reshape(8, 64, CH)


def feature_step(first3, w1):
    return call(feature_kernel, "feature_step", (((16, 64, CH), BF),), (first3, w1), limit=12, flops=10**9)[0]


def scatter_core_kernel(meta, keep_c, keep_f, got_c, got_f, own, *sends):
    block = (meta[4] // 2) % 8
    for k in range(8):
        at = block ^ k
        coarse = keep_c[at].astype(F32) + got_c[at].astype(F32)
        fine = keep_f[at].astype(F32) + got_f[at].astype(F32)
        out = own if k == 0 else sends[k - 1]
        out[0:160, :] = coarse.astype(out.dtype)
        out[160:304, :] = fine.astype(out.dtype)


def scatter_row_kernel(meta, own, *refs):
    got, (mine, *sends), (total,) = (refs[:7], refs[7:11], refs[11:])
    value = own[...]
    for ref in got:
        value = value + ref[...].astype(F32)
    for k in range(3):
        total[k] = value[80 * k : 80 * k + 80]
    total[3, 0:64, :] = value[240:304]
    total[3, 64:80, :] = jnp.zeros((16, CH), F32)
    part = meta[5] % 4
    mine[...] = total[part]
    for k in range(1, 4):
        sends[k - 1][...] = total[part ^ k].astype(BF)


def sum_kernel(a, b, c, d, out):
    out[...] = ((a[...].astype(F32) + b[...].astype(F32)) + (c[...].astype(F32) + d[...].astype(F32))).astype(BF)


def column_kernel(scale, meta, a, b, c, d, conv, proj, fine, parts):
    for k, ref in enumerate((a, b, c, d)):
        parts[(meta[5] % 4) ^ k] = ref[...]
    for k in range(9):
        conv[k] = parts[k // 5, 16 * (k % 5) : 16 * (k % 5) + 16, :].astype(F32) * scale
    proj[...] = parts[1, 64:80, :].astype(F32) * scale
    fine[0:80, :] = parts[2]
    fine[80:144, :] = parts[3, 0:64, :]


def finish_kernel(scale, meta, mine, other, first, second):
    block, core = ((meta[4] // 2) % 8, meta[4] % 2)
    for at in range(8):
        out = first if at < 4 else second
        a = mine[block ^ at].astype(F32) * scale
        b = other[block ^ at].astype(F32) * scale
        out[2 * (at % 4)] = jnp.where(core == 0, a, b)
        out[2 * (at % 4) + 1] = jnp.where(core == 0, b, a)


def swap(value, axis, mask):
    count = lax.axis_size(axis)
    return lax.ppermute(value, axis, [(i, i ^ mask) for i in range(count)])


def shifted(value, axis, step):
    count = lax.axis_size(axis)
    pairs = [(i, i + step) for i in range(count) if 0 <= i + step < count]
    return lax.ppermute(value, axis, pairs)


def local(features, conv_first, conv_second, coarse_conv, coarse_proj, cotangent):
    rows, cols = (lax.axis_size("row"), lax.axis_size("col"))
    height, breadth = (features.shape[0] * rows, features.shape[1] * cols)
    fine_scale = 1.0 / (height * breadth * features.shape[2]) ** 0.5
    coarse_scale = 2.0 * fine_scale
    me, mine = (lax.axis_index("row"), lax.axis_index("col"))
    fixed = [jnp.int32(height), jnp.int32(breadth)]
    meta = jnp.stack([me * 16, mine * 16] + fixed + [me, mine]).astype(jnp.int32)
    feat = features.reshape(16, 64, CH)
    cot = cotangent.reshape(16, 64, CH)
    conv = coarse_conv.reshape(9, CH, 16).swapaxes(1, 2)
    slab = ((160, CH), BF)

    right, left, own = call(
        pack_columns_kernel, "pack_columns", (((16, 48, CH), BF), ((16, 48, CH), BF), slab), (feat, cot, conv, coarse_proj)
    )
    before = shifted(right, "col", 1)
    after = shifted(left, "col", -1)
    other = swap(own, "row", 8)
    down, up, near0 = call(
        pack_rows_kernel,
        "pack_rows",
        (((12, 128, CH), BF), ((12, 128, CH), BF), ((2, 160, CH), BF)),
        (feat, cot, before, after, own, other),
    )
    above = shifted(down, "row", 1)
    below = shifted(up, "row", -1)
    near = [near0] + [swap(near0, "row", 2 * k) for k in range(1, 4)]
    far = swap(call(stack_kernel, "stack_weights", (((4, 2, 160, CH), BF),), near)[0], "row", 1)

    halo = (before, after, above, below)
    w1, w2 = (conv_first.reshape(1152, CH), conv_second.reshape(1152, CH))
    pool3, slope1, slope2, act, feat3, act3 = fine_forward(meta, feat, *halo, w1, w2)
    blended, keep_c, send_c, pooled_grad = coarse_step(meta, pool3, cot, *halo, near, far, act)
    got_c = swap(send_c, "row", 1)
    keep_f, send_f, first3 = fine_backward(
        meta, pooled_grad, cot, *halo, slope1, slope2, feat3, act3, conv_second.reshape(9, CH, CH)
    )
    got_f = swap(send_f, "row", 1)
    feature_grad = feature_step(first3, conv_first.reshape(9, CH, CH))

    whole = (304, CH)
    total, *sends = call(
        scatter_core_kernel, "scatter_core", ((whole, F32),) + ((whole, BF),) * 7, (meta, keep_c, keep_f, got_c, got_f)
    )
    got = [swap(v, "row", 2 * (k + 1)) for k, v in enumerate(sends)]
    quarter = (80, CH)
    part, *sends = call(
        scatter_row_kernel,
        "scatter_row",
        ((quarter, F32),) + ((quarter, BF),) * 3,
        (meta, total, *got),
        (((4, 80, CH), F32),),
    )
    got = [swap(v, "col", k + 1) for k, v in enumerate(sends)]
    part = call(sum_kernel, "sum_four", ((quarter, BF),), (part, *got))[0]
    got = [swap(part, "col", 4 * k) for k in range(1, 4)]
    part = call(sum_kernel, "sum_four", ((quarter, BF),), (part, *got))[0]
    got = [swap(part, "col", k) for k in range(1, 4)]
    conv_grad, proj_grad, fine = call(
        functools.partial(column_kernel, coarse_scale),
        "gather_column",
        (((9, 16, CH), F32), ((16, CH), F32), ((144, CH), BF)),
        (meta, part, *got),
        (((4, 80, CH), BF),),
    )
    got = [swap(fine, "row", 2 * k) for k in range(1, 8)]
    fine = call(stack_kernel, "stack_grads", (((8, 144, CH), BF),), (fine, *got))[0]
    first, second = call(
        functools.partial(finish_kernel, fine_scale),
        "finish",
        (((8, 144, CH), F32), ((8, 144, CH), F32)),
        (meta, fine, swap(fine, "row", 1)),
    )
    shape = features.shape
    return (
        blended.reshape(shape),
        feature_grad.reshape(shape),
        first.reshape(3, 3, CH, CH),
        second.reshape(3, 3, CH, CH),
        conv_grad.reshape(3, 3, 16, CH).swapaxes(2, 3),
        proj_grad,
    )


def solution(mesh):
    in_specs = (
        P("row", "col", None, None),
        P(),
        P(),
        P(None, None, None, "row"),
        P("row", None),
        P("row", "col", None, None),
    )
    out_specs = (
        P("row", "col", None, None),
        P("row", "col", None, None),
        P(),
        P(),
        P(None, None, None, "row"),
        P("row", None),
    )
    return jax.shard_map(local, mesh=mesh, in_specs=in_specs, out_specs=out_specs, check_vma=False)
```

time: 134 us -> 132 us (0.985)
  starting transfers between devices: 58 us -> 73.2 us
  local copies, waits for them, and re-layouts: 13.8 us -> 3.45 us
  other arithmetic: 6.46 us -> 0 us
  waiting for transfers between devices: 33.2 us -> 30.5 us
  Pallas kernels: 21 us -> 23.6 us
    ppermute x21 -> x31, starting transfers between devices: 46.9 us -> 61.9 us  [swap(): return lax.ppermute(value, axis, [(i, i ^ mask) for i in range(count)])]
    slice x17 -> x0, local copies, waits for them, and re-layouts: 8.13 us -> none  [the longest x2 2 us: halo(): feat = jnp.concatenate([down[:8], feat, up[:8]], axis=0)]
    concatenate x8 -> x0, other arithmetic: 2.86 us -> none  [the longest x2 1.54 us: edge(): return jnp.concatenate([feat_part, cot_part.reshape(3, 128, CH)], axis=0)]
    gather x4 -> x0, local copies, waits for them, and re-layouts: 2.67 us -> none  [the longest x2 1.34 us: absolute(): value = jnp.where(x // 2 == 0, value, value[:, jnp.array([2, 3, 0, 1])])]
    pallas_call x4 -> x14, Pallas kernels: 21 us -> 23.6 us  [call(): pl.pallas_call(kernel, name=name, out_shape=shapes, in_specs=[SM if v.ndi...]
    ppermute x4, waiting for transfers between devices: 1.52 us -> 0.01 us  [shifted(): return lax.ppermute(value, axis, pairs)]
    ppermute x21 -> x31, waiting for transfers between devices: 31.7 us -> 30.5 us  [swap(): return lax.ppermute(value, axis, [(i, i ^ mask) for i in range(count)])]
    unnamed x17 -> x16, local copies, waits for them, and re-layouts: 2.65 us -> 3.36 us
  transfers between devices with their start and end apart: 25 -> 35, of which waited for: 18 -> 13; matrix products, arithmetic and copies ran while one was open for 6% -> 0% of each run, Pallas kernels for 1% -> 12%
where the time goes in v2:
time: 132 us
  starting transfers between devices  73.2 us (55%)
  waiting for transfers between devices  30.5 us (23%)
  Pallas kernels  23.6 us (18%)
  local copies, waits for them, and re-layouts  3.45 us (3%)
    ppermute x31, starting transfers between devices, swap(): return lax.ppermute(value, axis, [(i, i ^ mask) for i in range(count)])  61.9 us
    ppermute x31, waiting for transfers between devices, swap(): return lax.ppermute(value, axis, [(i, i ^ mask) for i in range(count)])  30.5 us
    pallas_call x14, Pallas kernels, call(): pl.pallas_call(kernel, name=name, out_shape=shapes, in_specs=[SM if v.ndi...  23.6 us
    ppermute x4, starting transfers between devices, shifted(): return lax.ppermute(value, axis, pairs)  11.4 us
    unnamed x16, local copies, waits for them, and re-layouts  3.36 us
  transfers between devices with their start and end apart: 35, of which 13 were waited for; matrix products, arithmetic and copies ran while one was open for 0% of the time, Pallas kernels for 12%

profile of v2, /device:TPU:1, one launch (start us, length us, event | category | flops | bytes accessed | tf_op | source)
XLA Modules:
  0.0 131.7 jit_solution(13989324220897745633)
XLA Ops:
  4.0 4.4 %collective-permute-start = (bf16[16,48,128]{2,1,0:T(8,128)(2,1)S(1)}, bf16[16,48,128]{2,1,0:T(8,128)(2,1)S(1)}, u32[]{:S(2)}, u32[]{:S(2)}) collective-permute-start(bf16[16,48,128]{2,1,0:T(8,128)(2,1)S(1)} %get-tuple-element.42), channel_id=1, source_target_pairs={{0,1},{1,2},{2,3},{3,4},{4,5},{5,6},{6,7},{7,8},{8,9},{9,10},{10,1... | collective-permute-start | bytes 589832 | tf_op jit(solution)/shard_map/ppermute | solution.py:444
  8.4 1.3 collective-permute-start.1
  9.7 3.0 %collective-permute-start.2 = (bf16[160,128]{1,0:T(8,128)(2,1)S(1)}, bf16[160,128]{1,0:T(8,128)(2,1)S(1)}, u32[]{:S(2)}, u32[]{:S(2)}) collective-permute-start(bf16[160,128]{1,0:T(8,128)(2,1)S(1)} %get-tuple-element.44.own), channel_id=1, source_target_pairs={{0,128},{16,144},{32,160},{48,176},{64,192},{80,208},{96,224},{112... | collective-permute-start | bytes 122888 | tf_op jit(solution)/shard_map/ppermute | solution.py:438
  12.7 4.7 %collective-permute-done.2.other = bf16[160,128]{1,0:T(8,128)(2,1)S(1)} collective-permute-done((bf16[160,128]{1,0:T(8,128)(2,1)S(1)}, bf16[160,128]{1,0:T(8,128)(2,1)S(1)}, u32[]{:S(2)}, u32[]{:S(2)}) %collective-permute-start.2) | collective-permute-done | bytes 40992 | tf_op jit(solution)/shard_map/ppermute | solution.py:438
  17.5 3.8 %collective-permute-start.3 = (bf16[12,128,128]{2,1,0:T(8,128)(2,1)S(1)}, bf16[12,128,128]{2,1,0:T(8,128)(2,1)S(1)}, u32[]{:S(2)}, u32[]{:S(2)}) collective-permute-start(bf16[12,128,128]{2,1,0:T(8,128)(2,1)S(1)} %get-tuple-element.45), channel_id=1, source_target_pairs={{0,16},{16,32},{32,48},{48,64},{64,80},{80,96},{96,112},{112,128},... | collective-permute-start | bytes 1179656 | tf_op jit(solution)/shard_map/ppermute | solution.py:444
  21.3 1.9 %collective-permute-start.4 = (bf16[12,128,128]{2,1,0:T(8,128)(2,1)S(1)}, bf16[12,128,128]{2,1,0:T(8,128)(2,1)S(1)}, u32[]{:S(2)}, u32[]{:S(2)}) collective-permute-start(bf16[12,128,128]{2,1,0:T(8,128)(2,1)S(1)} %get-tuple-element.46), channel_id=1, source_target_pairs={{16,0},{32,16},{48,32},{64,48},{80,64},{96,80},{112,96},{128,112},... | collective-permute-start | bytes 1179656 | tf_op jit(solution)/shard_map/ppermute | solution.py:444
  23.2 5.0 %collective-permute-start.7 = (bf16[2,160,128]{2,1,0:T(8,128)(2,1)S(1)}, bf16[2,160,128]{2,1,0:T(8,128)(2,1)S(1)}, u32[]{:S(2)}, u32[]{:S(2)}) collective-permute-start(bf16[2,160,128]{2,1,0:T(8,128)(2,1)S(1)} %get-tuple-element.48.refs_0_.near0), channel_id=1, source_target_pairs={{0,96},{16,112},{32,64},{48,80},{64,32},{80,48},{96,0},{112,16},{1... | collective-permute-start | bytes 245768 | tf_op jit(solution)/shard_map/ppermute | solution.py:438
  28.9 5.9 %collective-permute-done.7.refs_3_.near3 = bf16[2,160,128]{2,1,0:T(8,128)(2,1)S(1)} collective-permute-done((bf16[2,160,128]{2,1,0:T(8,128)(2,1)S(1)}, bf16[2,160,128]{2,1,0:T(8,128)(2,1)S(1)}, u32[]{:S(2)}, u32[]{:S(2)}) %collective-permute-start.7) | collective-permute-done | bytes 81952 | tf_op jit(solution)/shard_map/ppermute | solution.py:438
  35.0 9.6 %fine_forward.1 = (bf16[14,64,384]{2,1,0:T(8,128)(2,1)S(1)}, f32[18,96,128]{2,1,0:T(8,128)S(1)}, f32[20,96,128]{2,1,0:T(8,128)S(1)}, bf16[16,64,128]{2,1,0:T(8,1...) custom-call(s32[6]{0:T(128)S(1)} %stack.19.meta, bf16[16,64,128]{2,1,0:T(8,128)(2,1)S(1)} %bitcast.22, ...), custom_call_target="tpu_custom_call" | custom-call | flops 4000000000 | tf_op jit(solution)/shard_map/fine_forward/pallas_call | solution.py:21
  44.6 3.8 %coarse_step.1 = (bf16[16,64,128]{2,1,0:T(8,128)(2,1)}, bf16[8,160,128]{2,1,0:T(8,128)(2,1)S(1)}, bf16[8,160,128]{2,1,0:T(8,128)(2,1)S(1)}, f32[10,48,128]{2,1,0:T(8,128)S(1)}) custom-call(s32[6]{0:T(128)S(1)} %stack.19.meta, bf16[14,64,384]{2,1,0:T(8,128)(2,1)S(1)} %get-tuple-element.47.pool3, bf16[16,64,128]{2,1,0:T(8,128)(2,1)S(1)} %bitcast.25, ...), custom_call_target="tpu_custom_call" | custom-call | flops 2000000000 | tf_op jit(solution)/shard_map/coarse_step/pallas_call | solution.py:21
  49.0 4.2 %fine_backward.1 = (bf16[8,144,128]{2,1,0:T(8,128)(2,1)S(1)}, bf16[8,144,128]{2,1,0:T(8,128)(2,1)S(1)}, bf16[18,64,384]{2,1,0:T(8,128)(2,1)S(1)}) custom-call(s32[6]{0:T(128)S(1)} %stack.19.meta, f32[10,48,128]{2,1,0:T(8,128)S(1)} %get-tuple-element.51.pooled_grad, bf16[16,64,128]{2,1,0:T(8,128)(2,1)S(1)} %bitcast.26, ...), custom_call_target="tpu_custom_call" | custom-call | flops 2000000000 | tf_op jit(solution)/shard_map/fine_backward/pallas_call | solution.py:21
  53.3 1.6 %collective-permute-done.10.got_f = bf16[8,144,128]{2,1,0:T(8,128)(2,1)S(1)} collective-permute-done((bf16[8,144,128]{2,1,0:T(8,128)(2,1)S(1)}, bf16[8,144,128]{2,1,0:T(8,128)(2,1)S(1)}, u32[]{:S(2)}, u32[]{:S(2)}) %collective-permute-start.10) | collective-permute-done | bytes 294944 | tf_op jit(solution)/shard_map/ppermute | solution.py:438
  56.0 5.5 %collective-permute-start.12 = (bf16[304,128]{1,0:T(8,128)(2,1)S(1)}, bf16[304,128]{1,0:T(8,128)(2,1)S(1)}, u32[]{:S(2)}, u32[]{:S(2)}) collective-permute-start(bf16[304,128]{1,0:T(8,128)(2,1)S(1)} %get-tuple-element.63), channel_id=1, source_target_pairs={{0,64},{16,80},{32,96},{48,112},{64,0},{80,16},{96,32},{112,48},{1... | collective-permute-start | bytes 233480 | tf_op jit(solution)/shard_map/ppermute | solution.py:438
  61.5 2.0 %collective-permute-start.14 = (bf16[304,128]{1,0:T(8,128)(2,1)S(1)}, bf16[304,128]{1,0:T(8,128)(2,1)S(1)}, u32[]{:S(2)}, u32[]{:S(2)}) collective-permute-start(bf16[304,128]{1,0:T(8,128)(2,1)S(1)} %get-tuple-element.65), channel_id=1, source_target_pairs={{0,128},{16,144},{32,160},{48,176},{64,192},{80,208},{96,224},{112... | collective-permute-start | bytes 233480 | tf_op jit(solution)/shard_map/ppermute | solution.py:438
  63.9 5.9 %collective-permute-start.16 = (bf16[304,128]{1,0:T(8,128)(2,1)S(1)}, bf16[304,128]{1,0:T(8,128)(2,1)S(1)}, u32[]{:S(2)}, u32[]{:S(2)}) collective-permute-start(bf16[304,128]{1,0:T(8,128)(2,1)S(1)} %get-tuple-element.67), channel_id=1, source_target_pairs={{0,192},{16,208},{32,224},{48,240},{64,128},{80,144},{96,160},{112... | collective-permute-start | bytes 233480 | tf_op jit(solution)/shard_map/ppermute | solution.py:438
  70.5 1.9 %collective-permute-done.16.refs_5_ = bf16[304,128]{1,0:T(8,128)(2,1)S(1)} collective-permute-done((bf16[304,128]{1,0:T(8,128)(2,1)S(1)}, bf16[304,128]{1,0:T(8,128)(2,1)S(1)}, u32[]{:S(2)}, u32[]{:S(2)}) %collective-permute-start.16) | collective-permute-done | bytes 77856 | tf_op jit(solution)/shard_map/ppermute | solution.py:438
  72.4 4.3 %collective-permute-done.17.refs_6_ = bf16[304,128]{1,0:T(8,128)(2,1)S(1)} collective-permute-done((bf16[304,128]{1,0:T(8,128)(2,1)S(1)}, bf16[304,128]{1,0:T(8,128)(2,1)S(1)}, u32[]{:S(2)}, u32[]{:S(2)}) %collective-permute-start.17) | collective-permute-done | bytes 77856 | tf_op jit(solution)/shard_map/ppermute | solution.py:438
  78.0 5.2 %collective-permute-start.19 = (bf16[80,128]{1,0:T(8,128)(2,1)S(1)}, bf16[80,128]{1,0:T(8,128)(2,1)S(1)}, u32[]{:S(2)}, u32[]{:S(2)}) collective-permute-start(bf16[80,128]{1,0:T(8,128)(2,1)S(1)} %get-tuple-element.71), channel_id=1, source_target_pairs={{0,2},{1,3},{2,0},{3,1},{4,6},{5,7},{6,4},{7,5},{8,10},{9,11},{10,... | collective-permute-start | bytes 61448 | tf_op jit(solution)/shard_map/ppermute | solution.py:438
  83.2 1.3 %collective-permute-done.19.c = bf16[80,128]{1,0:T(8,128)(2,1)S(1)} collective-permute-done((bf16[80,128]{1,0:T(8,128)(2,1)S(1)}, bf16[80,128]{1,0:T(8,128)(2,1)S(1)}, u32[]{:S(2)}, u32[]{:S(2)}) %collective-permute-start.19) | collective-permute-done | bytes 20512 | tf_op jit(solution)/shard_map/ppermute | solution.py:438
  84.5 3.3 %collective-permute-done.20.d = bf16[80,128]{1,0:T(8,128)(2,1)S(1)} collective-permute-done((bf16[80,128]{1,0:T(8,128)(2,1)S(1)}, bf16[80,128]{1,0:T(8,128)(2,1)S(1)}, u32[]{:S(2)}, u32[]{:S(2)}) %collective-permute-start.20) | collective-permute-done | bytes 20512 | tf_op jit(solution)/shard_map/ppermute | solution.py:438
  87.9 2.9 %collective-permute-start.23 = (bf16[80,128]{1,0:T(8,128)(2,1)S(1)}, bf16[80,128]{1,0:T(8,128)(2,1)S(1)}, u32[]{:S(2)}, u32[]{:S(2)}) collective-permute-start(bf16[80,128]{1,0:T(8,128)(2,1)S(1)} %sum_four.2.a), channel_id=1, source_target_pairs={{0,12},{1,13},{2,14},{3,15},{4,8},{5,9},{6,10},{7,11},{8,4},{9,5},... | collective-permute-start | bytes 61448 | tf_op jit(solution)/shard_map/ppermute | solution.py:438
  91.4 3.1 %collective-permute-start.21 = (bf16[80,128]{1,0:T(8,128)(2,1)S(1)}, bf16[80,128]{1,0:T(8,128)(2,1)S(1)}, u32[]{:S(2)}, u32[]{:S(2)}) collective-permute-start(bf16[80,128]{1,0:T(8,128)(2,1)S(1)} %sum_four.2.a), channel_id=1, source_target_pairs={{0,4},{1,5},{2,6},{3,7},{4,0},{5,1},{6,2},{7,3},{8,12},{9,13},{10,... | collective-permute-start | bytes 61448 | tf_op jit(solution)/shard_map/ppermute | solution.py:438
  95.4 2.6 %collective-permute-done.21.b = bf16[80,128]{1,0:T(8,128)(2,1)S(1)} collective-permute-done((bf16[80,128]{1,0:T(8,128)(2,1)S(1)}, bf16[80,128]{1,0:T(8,128)(2,1)S(1)}, u32[]{:S(2)}, u32[]{:S(2)}) %collective-permute-start.21) | collective-permute-done | bytes 20512 | tf_op jit(solution)/shard_map/ppermute | solution.py:438
  98.0 1.9 %collective-permute-start.26 = (bf16[80,128]{1,0:T(8,128)(2,1)S(1)}, bf16[80,128]{1,0:T(8,128)(2,1)S(1)}, u32[]{:S(2)}, u32[]{:S(2)}) collective-permute-start(bf16[80,128]{1,0:T(8,128)(2,1)S(1)} %sum_four.3.a), channel_id=1, source_target_pairs={{0,3},{1,2},{2,1},{3,0},{4,7},{5,6},{6,5},{7,4},{8,11},{9,10},{10,... | collective-permute-start | bytes 61448 | tf_op jit(solution)/shard_map/ppermute | solution.py:438
  99.9 1.8 %collective-permute-start.24 = (bf16[80,128]{1,0:T(8,128)(2,1)S(1)}, bf16[80,128]{1,0:T(8,128)(2,1)S(1)}, u32[]{:S(2)}, u32[]{:S(2)}) collective-permute-start(bf16[80,128]{1,0:T(8,128)(2,1)S(1)} %sum_four.3.a), channel_id=1, source_target_pairs={{0,1},{1,0},{2,3},{3,2},{4,5},{5,4},{6,7},{7,6},{8,9},{9,8},{10,11... | collective-permute-start | bytes 61448 | tf_op jit(solution)/shard_map/ppermute | solution.py:438
  106.0 5.1 %collective-permute-start.31 = (bf16[144,128]{1,0:T(8,128)(2,1)S(1)}, bf16[144,128]{1,0:T(8,128)(2,1)S(1)}, u32[]{:S(2)}, u32[]{:S(2)}) collective-permute-start(bf16[144,128]{1,0:T(8,128)(2,1)S(1)} %get-tuple-element.73.refs_0_), channel_id=1, source_target_pairs={{0,160},{16,176},{32,128},{48,144},{64,224},{80,240},{96,192},{112... | collective-permute-start | bytes 110600 | tf_op jit(solution)/shard_map/ppermute | solution.py:438
  111.1 2.1 %collective-permute-start.30 = (bf16[144,128]{1,0:T(8,128)(2,1)S(1)}, bf16[144,128]{1,0:T(8,128)(2,1)S(1)}, u32[]{:S(2)}, u32[]{:S(2)}) collective-permute-start(bf16[144,128]{1,0:T(8,128)(2,1)S(1)} %get-tuple-element.73.refs_0_), channel_id=1, source_target_pairs={{0,128},{16,144},{32,160},{48,176},{64,192},{80,208},{96,224},{112... | collective-permute-start | bytes 110600 | tf_op jit(solution)/shard_map/ppermute | solution.py:438
  113.3 3.2 %collective-permute-start.27 = (bf16[144,128]{1,0:T(8,128)(2,1)S(1)}, bf16[144,128]{1,0:T(8,128)(2,1)S(1)}, u32[]{:S(2)}, u32[]{:S(2)}) collective-permute-start(bf16[144,128]{1,0:T(8,128)(2,1)S(1)} %get-tuple-element.73.refs_0_), channel_id=1, source_target_pairs={{0,32},{16,48},{32,0},{48,16},{64,96},{80,112},{96,64},{112,80},{1... | collective-permute-start | bytes 110600 | tf_op jit(solution)/shard_map/ppermute | solution.py:438
  116.5 1.6 %collective-permute-done.29.refs_3_ = bf16[144,128]{1,0:T(8,128)(2,1)S(1)} collective-permute-done((bf16[144,128]{1,0:T(8,128)(2,1)S(1)}, bf16[144,128]{1,0:T(8,128)(2,1)S(1)}, u32[]{:S(2)}, u32[]{:S(2)}) %collective-permute-start.29) | collective-permute-done | bytes 36896 | tf_op jit(solution)/shard_map/ppermute | solution.py:438
  118.6 9.8 %collective-permute-start.34 = (bf16[8,144,128]{2,1,0:T(8,128)(2,1)S(1)}, bf16[8,144,128]{2,1,0:T(8,128)(2,1)S(1)}, u32[]{:S(2)}, u32[]{:S(2)}) collective-permute-start(bf16[8,144,128]{2,1,0:T(8,128)(2,1)S(1)} %stack_grads.1.mine), channel_id=1, source_target_pairs={{0,16},{16,0},{32,48},{48,32},{64,80},{80,64},{96,112},{112,96},{1... | collective-permute-start | bytes 884744 | tf_op jit(solution)/shard_map/ppermute | solution.py:438
  128.4 1.7 %feature_step.1 = bf16[16,64,128]{2,1,0:T(8,128)(2,1)} custom-call(bf16[18,64,384]{2,1,0:T(8,128)(2,1)S(1)} %get-tuple-element.56.first3, bf16[9,128,128]{2,1,0:T(8,128)(2,1)S(1)} %bitcast.31), custom_call_target="tpu_custom_call" | custom-call | flops 1000000000 | tf_op jit(solution)/shard_map/feature_step/pallas_call | solution.py:21
  130.0 1.6 %finish.1 = (f32[8,144,128]{2,1,0:T(8,128)}, f32[8,144,128]{2,1,0:T(8,128)}) custom-call(s32[6]{0:T(128)S(1)} %stack.19.meta, bf16[8,144,128]{2,1,0:T(8,128)(2,1)S(1)} %stack_grads.1.mine, bf16[8,144,128]{2,1,0:T(8,128)(2,1)S(1)} %collective-permute-done.34.other), custom_call_target="tpu_custom_call" | custom-call | tf_op jit(solution)/shard_map/finish/pallas_call | solution.py:21
  (70 shorter events, 15.1 us)
Async XLA Ops:
  4.0 13.4 %collective-permute-start = (bf16[16,48,128]{2,1,0:T(8,128)(2,1)S(1)}, bf16[16,48,128]{2,1,0:T(8,128)(2,1)S(1)}, u32[]{:S(2)}, u32[]{:S(2)}) collective-permute-start(bf16[16,48,128]{2,1,0:T(8,128)(2,1)S(1)} %get-tuple-element.42), channel_id=1, source_target_pairs={{0,1},{1,2},{2,3},{3,4},{4,5},{5,6},{6,7},{7,8},{8,9},{9,10},{10,1... | collective-permute-start | bytes 589832 | tf_op jit(solution)/shard_map/ppermute | solution.py:444
  8.4 9.0 %collective-permute-start.1 = (bf16[16,48,128]{2,1,0:T(8,128)(2,1)S(1)}, bf16[16,48,128]{2,1,0:T(8,128)(2,1)S(1)}, u32[]{:S(2)}, u32[]{:S(2)}) collective-permute-start(bf16[16,48,128]{2,1,0:T(8,128)(2,1)S(1)} %get-tuple-element.43), channel_id=1, source_target_pairs={{1,0},{2,1},{3,2},{4,3},{5,4},{6,5},{7,6},{8,7},{9,8},{10,9},{11,1... | collective-permute-start | bytes 589832 | tf_op jit(solution)/shard_map/ppermute | solution.py:444
  9.7 7.7 %collective-permute-start.2 = (bf16[160,128]{1,0:T(8,128)(2,1)S(1)}, bf16[160,128]{1,0:T(8,128)(2,1)S(1)}, u32[]{:S(2)}, u32[]{:S(2)}) collective-permute-start(bf16[160,128]{1,0:T(8,128)(2,1)S(1)} %get-tuple-element.44.own), channel_id=1, source_target_pairs={{0,128},{16,144},{32,160},{48,176},{64,192},{80,208},{96,224},{112... | collective-permute-start | bytes 122888 | tf_op jit(solution)/shard_map/ppermute | solution.py:438
  17.5 17.5 %collective-permute-start.3 = (bf16[12,128,128]{2,1,0:T(8,128)(2,1)S(1)}, bf16[12,128,128]{2,1,0:T(8,128)(2,1)S(1)}, u32[]{:S(2)}, u32[]{:S(2)}) collective-permute-start(bf16[12,128,128]{2,1,0:T(8,128)(2,1)S(1)} %get-tuple-element.45), channel_id=1, source_target_pairs={{0,16},{16,32},{32,48},{48,64},{64,80},{80,96},{96,112},{112,128},... | collective-permute-start | bytes 1179656 | tf_op jit(solution)/shard_map/ppermute | solution.py:444
  21.3 13.7 %collective-permute-start.4 = (bf16[12,128,128]{2,1,0:T(8,128)(2,1)S(1)}, bf16[12,128,128]{2,1,0:T(8,128)(2,1)S(1)}, u32[]{:S(2)}, u32[]{:S(2)}) collective-permute-start(bf16[12,128,128]{2,1,0:T(8,128)(2,1)S(1)} %get-tuple-element.46), channel_id=1, source_target_pairs={{16,0},{32,16},{48,32},{64,48},{80,64},{96,80},{112,96},{128,112},... | collective-permute-start | bytes 1179656 | tf_op jit(solution)/shard_map/ppermute | solution.py:444
  23.2 11.6 %collective-permute-start.7 = (bf16[2,160,128]{2,1,0:T(8,128)(2,1)S(1)}, bf16[2,160,128]{2,1,0:T(8,128)(2,1)S(1)}, u32[]{:S(2)}, u32[]{:S(2)}) collective-permute-start(bf16[2,160,128]{2,1,0:T(8,128)(2,1)S(1)} %get-tuple-element.48.refs_0_.near0), channel_id=1, source_target_pairs={{0,96},{16,112},{32,64},{48,80},{64,32},{80,48},{96,0},{112,16},{1... | collective-permute-start | bytes 245768 | tf_op jit(solution)/shard_map/ppermute | solution.py:438
  28.2 6.6 %collective-permute-start.6 = (bf16[2,160,128]{2,1,0:T(8,128)(2,1)S(1)}, bf16[2,160,128]{2,1,0:T(8,128)(2,1)S(1)}, u32[]{:S(2)}, u32[]{:S(2)}) collective-permute-start(bf16[2,160,128]{2,1,0:T(8,128)(2,1)S(1)} %get-tuple-element.48.refs_0_.near0), channel_id=1, source_target_pairs={{0,64},{16,80},{32,96},{48,112},{64,0},{80,16},{96,32},{112,48},{1... | collective-permute-start | bytes 245768 | tf_op jit(solution)/shard_map/ppermute | solution.py:438
  28.2 6.6 %collective-permute-start.5 = (bf16[2,160,128]{2,1,0:T(8,128)(2,1)S(1)}, bf16[2,160,128]{2,1,0:T(8,128)(2,1)S(1)}, u32[]{:S(2)}, u32[]{:S(2)}) collective-permute-start(bf16[2,160,128]{2,1,0:T(8,128)(2,1)S(1)} %get-tuple-element.48.refs_0_.near0), channel_id=1, source_target_pairs={{0,32},{16,48},{32,0},{48,16},{64,96},{80,112},{96,64},{112,80},{1... | collective-permute-start | bytes 245768 | tf_op jit(solution)/shard_map/ppermute | solution.py:438
  34.8 9.8 %collective-permute-start.8 = (bf16[4,2,160,128]{3,2,1,0:T(8,128)(2,1)S(1)}, bf16[4,2,160,128]{3,2,1,0:T(8,128)(2,1)S(1)}, u32[]{:S(2)}, u32[]{:S(2)}) collective-permute-start(bf16[4,2,160,128]{3,2,1,0:T(8,128)(2,1)S(1)} %stack_weights.1), channel_id=1, source_target_pairs={{0,16},{16,0},{32,48},{48,32},{64,80},{80,64},{96,112},{112,96},{1... | collective-permute-start | bytes 983048 | tf_op jit(solution)/shard_map/ppermute | solution.py:438
  48.4 6.5 %collective-permute-start.9 = (bf16[8,160,128]{2,1,0:T(8,128)(2,1)S(1)}, bf16[8,160,128]{2,1,0:T(8,128)(2,1)S(1)}, u32[]{:S(2)}, u32[]{:S(2)}) collective-permute-start(bf16[8,160,128]{2,1,0:T(8,128)(2,1)S(1)} %get-tuple-element.59), channel_id=1, source_target_pairs={{0,16},{16,0},{32,48},{48,32},{64,80},{80,64},{96,112},{112,96},{1... | collective-permute-start | bytes 983048 | tf_op jit(solution)/shard_map/ppermute | solution.py:438
  55.6 8.3 %collective-permute-start.11 = (bf16[304,128]{1,0:T(8,128)(2,1)S(1)}, bf16[304,128]{1,0:T(8,128)(2,1)S(1)}, u32[]{:S(2)}, u32[]{:S(2)}) collective-permute-start(bf16[304,128]{1,0:T(8,128)(2,1)S(1)} %get-tuple-element.62), channel_id=1, source_target_pairs={{0,32},{16,48},{32,0},{48,16},{64,96},{80,112},{96,64},{112,80},{1... | collective-permute-start | bytes 233480 | tf_op jit(solution)/shard_map/ppermute | solution.py:438
  56.0 13.8 %collective-permute-start.12 = (bf16[304,128]{1,0:T(8,128)(2,1)S(1)}, bf16[304,128]{1,0:T(8,128)(2,1)S(1)}, u32[]{:S(2)}, u32[]{:S(2)}) collective-permute-start(bf16[304,128]{1,0:T(8,128)(2,1)S(1)} %get-tuple-element.63), channel_id=1, source_target_pairs={{0,64},{16,80},{32,96},{48,112},{64,0},{80,16},{96,32},{112,48},{1... | collective-permute-start | bytes 233480 | tf_op jit(solution)/shard_map/ppermute | solution.py:438
  61.5 9.0 %collective-permute-start.13 = (bf16[304,128]{1,0:T(8,128)(2,1)S(1)}, bf16[304,128]{1,0:T(8,128)(2,1)S(1)}, u32[]{:S(2)}, u32[]{:S(2)}) collective-permute-start(bf16[304,128]{1,0:T(8,128)(2,1)S(1)} %get-tuple-element.64), channel_id=1, source_target_pairs={{0,96},{16,112},{32,64},{48,80},{64,32},{80,48},{96,0},{112,16},{1... | collective-permute-start | bytes 233480 | tf_op jit(solution)/shard_map/ppermute | solution.py:438
  61.5 9.0 %collective-permute-start.14 = (bf16[304,128]{1,0:T(8,128)(2,1)S(1)}, bf16[304,128]{1,0:T(8,128)(2,1)S(1)}, u32[]{:S(2)}, u32[]{:S(2)}) collective-permute-start(bf16[304,128]{1,0:T(8,128)(2,1)S(1)} %get-tuple-element.65), channel_id=1, source_target_pairs={{0,128},{16,144},{32,160},{48,176},{64,192},{80,208},{96,224},{112... | collective-permute-start | bytes 233480 | tf_op jit(solution)/shard_map/ppermute | solution.py:438
  63.5 7.0 %collective-permute-start.15 = (bf16[304,128]{1,0:T(8,128)(2,1)S(1)}, bf16[304,128]{1,0:T(8,128)(2,1)S(1)}, u32[]{:S(2)}, u32[]{:S(2)}) collective-permute-start(bf16[304,128]{1,0:T(8,128)(2,1)S(1)} %get-tuple-element.66), channel_id=1, source_target_pairs={{0,160},{16,176},{32,128},{48,144},{64,224},{80,240},{96,192},{112... | collective-permute-start | bytes 233480 | tf_op jit(solution)/shard_map/ppermute | solution.py:438
  63.9 8.5 %collective-permute-start.16 = (bf16[304,128]{1,0:T(8,128)(2,1)S(1)}, bf16[304,128]{1,0:T(8,128)(2,1)S(1)}, u32[]{:S(2)}, u32[]{:S(2)}) collective-permute-start(bf16[304,128]{1,0:T(8,128)(2,1)S(1)} %get-tuple-element.67), channel_id=1, source_target_pairs={{0,192},{16,208},{32,224},{48,240},{64,128},{80,144},{96,160},{112... | collective-permute-start | bytes 233480 | tf_op jit(solution)/shard_map/ppermute | solution.py:438
  69.8 6.9 %collective-permute-start.17 = (bf16[304,128]{1,0:T(8,128)(2,1)S(1)}, bf16[304,128]{1,0:T(8,128)(2,1)S(1)}, u32[]{:S(2)}, u32[]{:S(2)}) collective-permute-start(bf16[304,128]{1,0:T(8,128)(2,1)S(1)} %get-tuple-element.68), channel_id=1, source_target_pairs={{0,224},{16,240},{32,192},{48,208},{64,160},{80,176},{96,128},{112... | collective-permute-start | bytes 233480 | tf_op jit(solution)/shard_map/ppermute | solution.py:438
  77.3 5.9 %collective-permute-start.18 = (bf16[80,128]{1,0:T(8,128)(2,1)S(1)}, bf16[80,128]{1,0:T(8,128)(2,1)S(1)}, u32[]{:S(2)}, u32[]{:S(2)}) collective-permute-start(bf16[80,128]{1,0:T(8,128)(2,1)S(1)} %get-tuple-element.70), channel_id=1, source_target_pairs={{0,1},{1,0},{2,3},{3,2},{4,5},{5,4},{6,7},{7,6},{8,9},{9,8},{10,11... | collective-permute-start | bytes 61448 | tf_op jit(solution)/shard_map/ppermute | solution.py:438
  78.0 6.6 %collective-permute-start.19 = (bf16[80,128]{1,0:T(8,128)(2,1)S(1)}, bf16[80,128]{1,0:T(8,128)(2,1)S(1)}, u32[]{:S(2)}, u32[]{:S(2)}) collective-permute-start(bf16[80,128]{1,0:T(8,128)(2,1)S(1)} %get-tuple-element.71), channel_id=1, source_target_pairs={{0,2},{1,3},{2,0},{3,1},{4,6},{5,7},{6,4},{7,5},{8,10},{9,11},{10,... | collective-permute-start | bytes 61448 | tf_op jit(solution)/shard_map/ppermute | solution.py:438
  83.2 4.7 %collective-permute-start.20 = (bf16[80,128]{1,0:T(8,128)(2,1)S(1)}, bf16[80,128]{1,0:T(8,128)(2,1)S(1)}, u32[]{:S(2)}, u32[]{:S(2)}) collective-permute-start(bf16[80,128]{1,0:T(8,128)(2,1)S(1)} %get-tuple-element.72), channel_id=1, source_target_pairs={{0,3},{1,2},{2,1},{3,0},{4,7},{5,6},{6,5},{7,4},{8,11},{9,10},{10,... | collective-permute-start | bytes 61448 | tf_op jit(solution)/shard_map/ppermute | solution.py:438
  87.9 7.5 %collective-permute-start.23 = (bf16[80,128]{1,0:T(8,128)(2,1)S(1)}, bf16[80,128]{1,0:T(8,128)(2,1)S(1)}, u32[]{:S(2)}, u32[]{:S(2)}) collective-permute-start(bf16[80,128]{1,0:T(8,128)(2,1)S(1)} %sum_four.2.a), channel_id=1, source_target_pairs={{0,12},{1,13},{2,14},{3,15},{4,8},{5,9},{6,10},{7,11},{8,4},{9,5},... | collective-permute-start | bytes 61448 | tf_op jit(solution)/shard_map/ppermute | solution.py:438
  90.7 4.7 %collective-permute-start.22 = (bf16[80,128]{1,0:T(8,128)(2,1)S(1)}, bf16[80,128]{1,0:T(8,128)(2,1)S(1)}, u32[]{:S(2)}, u32[]{:S(2)}) collective-permute-start(bf16[80,128]{1,0:T(8,128)(2,1)S(1)} %sum_four.2.a), channel_id=1, source_target_pairs={{0,8},{1,9},{2,10},{3,11},{4,12},{5,13},{6,14},{7,15},{8,0},{9,1},... | collective-permute-start | bytes 61448 | tf_op jit(solution)/shard_map/ppermute | solution.py:438
  91.4 6.5 %collective-permute-start.21 = (bf16[80,128]{1,0:T(8,128)(2,1)S(1)}, bf16[80,128]{1,0:T(8,128)(2,1)S(1)}, u32[]{:S(2)}, u32[]{:S(2)}) collective-permute-start(bf16[80,128]{1,0:T(8,128)(2,1)S(1)} %sum_four.2.a), channel_id=1, source_target_pairs={{0,4},{1,5},{2,6},{3,7},{4,0},{5,1},{6,2},{7,3},{8,12},{9,13},{10,... | collective-permute-start | bytes 61448 | tf_op jit(solution)/shard_map/ppermute | solution.py:438
  98.0 4.5 %collective-permute-start.26 = (bf16[80,128]{1,0:T(8,128)(2,1)S(1)}, bf16[80,128]{1,0:T(8,128)(2,1)S(1)}, u32[]{:S(2)}, u32[]{:S(2)}) collective-permute-start(bf16[80,128]{1,0:T(8,128)(2,1)S(1)} %sum_four.3.a), channel_id=1, source_target_pairs={{0,3},{1,2},{2,1},{3,0},{4,7},{5,6},{6,5},{7,4},{8,11},{9,10},{10,... | collective-permute-start | bytes 61448 | tf_op jit(solution)/shard_map/ppermute | solution.py:438
  104.9 8.4 %collective-permute-start.33 = (bf16[144,128]{1,0:T(8,128)(2,1)S(1)}, bf16[144,128]{1,0:T(8,128)(2,1)S(1)}, u32[]{:S(2)}, u32[]{:S(2)}) collective-permute-start(bf16[144,128]{1,0:T(8,128)(2,1)S(1)} %get-tuple-element.73.refs_0_), channel_id=1, source_target_pairs={{0,224},{16,240},{32,192},{48,208},{64,160},{80,176},{96,128},{112... | collective-permute-start | bytes 110600 | tf_op jit(solution)/shard_map/ppermute | solution.py:438
  105.5 7.8 %collective-permute-start.32 = (bf16[144,128]{1,0:T(8,128)(2,1)S(1)}, bf16[144,128]{1,0:T(8,128)(2,1)S(1)}, u32[]{:S(2)}, u32[]{:S(2)}) collective-permute-start(bf16[144,128]{1,0:T(8,128)(2,1)S(1)} %get-tuple-element.73.refs_0_), channel_id=1, source_target_pairs={{0,192},{16,208},{32,224},{48,240},{64,128},{80,144},{96,160},{112... | collective-permute-start | bytes 110600 | tf_op jit(solution)/shard_map/ppermute | solution.py:438
  106.0 10.5 %collective-permute-start.31 = (bf16[144,128]{1,0:T(8,128)(2,1)S(1)}, bf16[144,128]{1,0:T(8,128)(2,1)S(1)}, u32[]{:S(2)}, u32[]{:S(2)}) collective-permute-start(bf16[144,128]{1,0:T(8,128)(2,1)S(1)} %get-tuple-element.73.refs_0_), channel_id=1, source_target_pairs={{0,160},{16,176},{32,128},{48,144},{64,224},{80,240},{96,192},{112... | collective-permute-start | bytes 110600 | tf_op jit(solution)/shard_map/ppermute | solution.py:438
  111.1 5.4 %collective-permute-start.30 = (bf16[144,128]{1,0:T(8,128)(2,1)S(1)}, bf16[144,128]{1,0:T(8,128)(2,1)S(1)}, u32[]{:S(2)}, u32[]{:S(2)}) collective-permute-start(bf16[144,128]{1,0:T(8,128)(2,1)S(1)} %get-tuple-element.73.refs_0_), channel_id=1, source_target_pairs={{0,128},{16,144},{32,160},{48,176},{64,192},{80,208},{96,224},{112... | collective-permute-start | bytes 110600 | tf_op jit(solution)/shard_map/ppermute | solution.py:438
  113.2 4.8 %collective-permute-start.29 = (bf16[144,128]{1,0:T(8,128)(2,1)S(1)}, bf16[144,128]{1,0:T(8,128)(2,1)S(1)}, u32[]{:S(2)}, u32[]{:S(2)}) collective-permute-start(bf16[144,128]{1,0:T(8,128)(2,1)S(1)} %get-tuple-element.73.refs_0_), channel_id=1, source_target_pairs={{0,96},{16,112},{32,64},{48,80},{64,32},{80,48},{96,0},{112,16},{1... | collective-permute-start | bytes 110600 | tf_op jit(solution)/shard_map/ppermute | solution.py:438
  113.2 4.8 %collective-permute-start.28 = (bf16[144,128]{1,0:T(8,128)(2,1)S(1)}, bf16[144,128]{1,0:T(8,128)(2,1)S(1)}, u32[]{:S(2)}, u32[]{:S(2)}) collective-permute-start(bf16[144,128]{1,0:T(8,128)(2,1)S(1)} %get-tuple-element.73.refs_0_), channel_id=1, source_target_pairs={{0,64},{16,80},{32,96},{48,112},{64,0},{80,16},{96,32},{112,48},{1... | collective-permute-start | bytes 110600 | tf_op jit(solution)/shard_map/ppermute | solution.py:438
  113.3 5.3 %collective-permute-start.27 = (bf16[144,128]{1,0:T(8,128)(2,1)S(1)}, bf16[144,128]{1,0:T(8,128)(2,1)S(1)}, u32[]{:S(2)}, u32[]{:S(2)}) collective-permute-start(bf16[144,128]{1,0:T(8,128)(2,1)S(1)} %get-tuple-element.73.refs_0_), channel_id=1, source_target_pairs={{0,32},{16,48},{32,0},{48,16},{64,96},{80,112},{96,64},{112,80},{1... | collective-permute-start | bytes 110600 | tf_op jit(solution)/shard_map/ppermute | solution.py:438
  118.6 11.5 %collective-permute-start.34 = (bf16[8,144,128]{2,1,0:T(8,128)(2,1)S(1)}, bf16[8,144,128]{2,1,0:T(8,128)(2,1)S(1)}, u32[]{:S(2)}, u32[]{:S(2)}) collective-permute-start(bf16[8,144,128]{2,1,0:T(8,128)(2,1)S(1)} %stack_grads.1.mine), channel_id=1, source_target_pairs={{0,16},{16,0},{32,48},{48,32},{64,80},{80,64},{96,112},{112,96},{1... | collective-permute-start | bytes 884744 | tf_op jit(solution)/shard_map/ppermute | solution.py:438
  (11 other events, 51.9 us)

commit v3 on v2

--- a/solution.py
+++ b/solution.py
@@ -16,15 +16,15 @@
 SM = pl.BlockSpec(memory_space=pltpu.SMEM)
 
 
-def call(kernel, name, outs, ins, scratch=(), limit=16, flops=0, moved=0):
+def call(kernel, name, outs, ins, scratch=(), limit=16, flops=0, moved=0, far=False):
     shapes = tuple(jax.ShapeDtypeStruct(shape, dtype) for shape, dtype in outs)
     return pl.pallas_call(
         kernel,
         name=name,
         out_shape=shapes,
-        in_specs=[SM if v.ndim == 1 else VM for v in ins],
+        in_specs=[pl.BlockSpec(memory_space=pl.ANY) if far else SM if v.ndim == 1 else VM for v in ins],
         out_specs=tuple(VM for _ in outs),
-        scratch_shapes=[pltpu.VMEM(shape, dtype) for shape, dtype in scratch],
+        scratch_shapes=[v if len(v) != 2 else pltpu.VMEM(*v) for v in scratch] if not far else list(scratch),
         compiler_params=pltpu.CompilerParams(vmem_limit_bytes=limit * MIB),
         cost_estimate=pl.CostEstimate(flops=flops, bytes_accessed=moved, transcendentals=0),
     )(*ins)
@@ -102,16 +102,22 @@
     return jnp.concatenate([even, odd], axis=1).reshape(count * 2, CH)
 
 
-def pack_columns_kernel(feat, cot, conv, proj, right, left, weights):
-    right[:, 0:32, :] = feat[:, 32:64, :]
-    right[:, 32:48, :] = cot[:, 48:64, :]
-    left[:, 0:32, :] = feat[:, 0:32, :]
-    left[:, 32:48, :] = cot[:, 0:16, :]
-    weights[0:144, :] = conv[...].reshape(144, CH)
-    weights[144:160, :] = proj[...]
-
-
-def pack_rows_kernel(feat, cot, before, after, own, other, down, up, weights):
+def pack_columns_kernel(feat, cot, conv, proj, right, left, weights, done):
+    pairs = [
+        (feat.at[:, 32:64, :], right.at[:, 0:32, :]),
+        (cot.at[:, 48:64, :], right.at[:, 32:48, :]),
+        (feat.at[:, 0:32, :], left.at[:, 0:32, :]),
+        (cot.at[:, 0:16, :], left.at[:, 32:48, :]),
+        (proj, weights.at[144:160, :]),
+    ] + [(conv.at[t], weights.at[16 * t : 16 * t + 16, :]) for t in range(9)]
+    copies = [pltpu.make_async_copy(a, b, done.at[k]) for k, (a, b) in enumerate(pairs)]
+    for copy in copies:
+        copy.start()
+    for copy in copies:
+        copy.wait()
+
+
+def pack_rows_kernel(feat, cot, before, after, down, up):
     for out, first, second in ((down, 8, 12), (up, 0, 0)):
         out[0:8, 0:32, :] = before[first : first + 8, 0:32, :]
         out[0:8, 32:96, :] = feat[first : first + 8]
@@ -120,8 +126,6 @@
         out[8:12, 16:80, :] = cot[second : second + 4]
         out[8:12, 80:96, :] = after[second : second + 4, 32:48, :]
         out[8:12, 96:128, :] = jnp.zeros((4, 32, CH), BF)
-    weights[0] = own[...]
-    weights[1] = other[...]
 
 
 def stack_kernel(*refs):
@@ -130,12 +134,9 @@
         out[k] = ref[...]
 
 
-def forward_kernel(
-    meta, feat, before, after, above, below, w1, w2, pool3, slope1, slope2, act, feat3o, act3o, feat3, act3, pre1, pre2, act2
-):
+def first_kernel(meta, feat, before, after, above, below, w1, act3, slope1, feat3o, feat3, pre1):
     top, left, height, breadth = (meta[0], meta[1], meta[2], meta[3])
     mask = column_mask(left - 8, 128, breadth)
-    coarse_mask = column_mask(left // 2 - 4, 64, breadth // 2)
 
     @pl.loop(0, 4)
     def _(b):
@@ -160,6 +161,15 @@
         value = masked(value, mask, top - 7 + 5 * b, height)
         act3[pl.ds(5 * b, 5)] = three(value.reshape(640, CH)).reshape(5, 128, 3 * CH)
 
+    @pl.loop(0, 18)
+    def _(k):
+        slope1[k] = slope_of(pre1[k + 6, 16:112, :])
+        feat3o[k] = feat3[k + 7, 32:96, :]
+
+
+def second_kernel(meta, act3, w2, pool3, slope2, act, act3o, pre2, act2):
+    top, left, height, breadth = (meta[0], meta[1], meta[2], meta[3])
+    coarse_mask = column_mask(left // 2 - 4, 64, breadth // 2)
     second_w = w2[...]
 
     @pl.loop(0, 7)
@@ -178,8 +188,6 @@
 
     @pl.loop(0, 18)
     def _(k):
-        slope1[k] = slope_of(pre1[k + 6, 16:112, :])
-        feat3o[k] = feat3[k + 7, 32:96, :]
         act3o[k] = act3[k + 6, 32:96, :]
 
     @pl.loop(0, 20)
@@ -191,27 +199,26 @@
         act[k] = act2[k + 6, 32:96, :]
 
 
-def fine_forward(meta, feat, before, after, above, below, w1, w2):
+def first_step(meta, feat, before, after, above, below, w1):
     return call(
-        forward_kernel,
-        "fine_forward",
-        (
-            ((14, 64, 384), BF),
-            ((18, 96, CH), F32),
-            ((20, 96, CH), F32),
-            ((16, 64, CH), BF),
-            ((18, 64, 384), BF),
-            ((18, 64, 384), BF),
-        ),
-        (meta, feat, before, after, above, below, w1, w2),
-        (
-            ((32, 128, 384), BF),
-            ((30, 128, 384), BF),
-            ((30, 128, CH), F32),
-            ((28, 128, CH), F32),
-            ((28, 128, CH), BF),
-        ),
-        limit=24,
+        first_kernel,
+        "first_conv",
+        (((30, 128, 384), BF), ((18, 96, CH), F32), ((18, 64, 384), BF)),
+        (meta, feat, before, after, above, below, w1),
+        (((32, 128, 384), BF), ((30, 128, CH), F32)),
+        limit=20,
+        flops=4 * 10**9,
+    )
+
+
+def second_step(meta, act3, w2):
+    return call(
+        second_kernel,
+        "second_conv",
+        (((14, 64, 384), BF), ((20, 96, CH), F32), ((16, 64, CH), BF), ((18, 64, 384), BF)),
+        (meta, act3, w2),
+        (((28, 128, CH), F32), ((28, 128, CH), BF)),
+        limit=20,
         flops=4 * 10**9,
     )
 
@@ -383,52 +390,48 @@
     return call(feature_kernel, "feature_step", (((16, 64, CH), BF),), (first3, w1), limit=12, flops=10**9)[0]
 
 
-def scatter_core_kernel(meta, keep_c, keep_f, got_c, got_f, own, *sends):
-    block = (meta[4] // 2) % 8
+def scatter_core_kernel(keep_c, keep_f, got_c, got_f, out):
     for k in range(8):
-        at = block ^ k
-        coarse = keep_c[at].astype(F32) + got_c[at].astype(F32)
-        fine = keep_f[at].astype(F32) + got_f[at].astype(F32)
-        out = own if k == 0 else sends[k - 1]
-        out[0:160, :] = coarse.astype(out.dtype)
-        out[160:304, :] = fine.astype(out.dtype)
-
-
-def scatter_row_kernel(meta, own, *refs):
-    got, (mine, *sends), (total,) = (refs[:7], refs[7:11], refs[11:])
-    value = own[...]
-    for ref in got:
-        value = value + ref[...].astype(F32)
-    for k in range(3):
-        total[k] = value[80 * k : 80 * k + 80]
-    total[3, 0:64, :] = value[240:304]
-    total[3, 64:80, :] = jnp.zeros((16, CH), F32)
-    part = meta[5] % 4
-    mine[...] = total[part]
-    for k in range(1, 4):
-        sends[k - 1][...] = total[part ^ k].astype(BF)
-
-
-def sum_kernel(a, b, c, d, out):
-    out[...] = ((a[...].astype(F32) + b[...].astype(F32)) + (c[...].astype(F32) + d[...].astype(F32))).astype(BF)
-
-
-def column_kernel(scale, meta, a, b, c, d, conv, proj, fine, parts):
-    for k, ref in enumerate((a, b, c, d)):
-        parts[(meta[5] % 4) ^ k] = ref[...]
+        out[k, 0:160, :] = (keep_c[k].astype(F32) + got_c[k].astype(F32)).astype(BF)
+        out[k, 160:304, :] = (keep_f[k].astype(F32) + got_f[k].astype(F32)).astype(BF)
+
+
+def scatter_row_kernel(got, out, total):
+    value = got[0].astype(F32)
+    for k in range(1, 8):
+        value = value + got[k].astype(F32)
+    total[0:304, :] = value
+    total[304:336, :] = jnp.zeros((32, CH), F32)
+    for k in range(16):
+        out[k] = total[20 * k : 20 * k + 32, :].astype(BF)
+
+
+def scatter_column_kernel(got, out):
+    value = got[0].astype(F32)
+    for k in range(1, 16):
+        value = value + got[k].astype(F32)
+    value = value.astype(BF)
+    for k in range(16):
+        out[k] = value
+
+
+def gather_column_kernel(scale, got, conv, proj, fine, total):
+    for k in range(16):
+        total[20 * k : 20 * k + 32, :] = got[k].astype(F32)
     for k in range(9):
-        conv[k] = parts[k // 5, 16 * (k % 5) : 16 * (k % 5) + 16, :].astype(F32) * scale
-    proj[...] = parts[1, 64:80, :].astype(F32) * scale
-    fine[0:80, :] = parts[2]
-    fine[80:144, :] = parts[3, 0:64, :]
+        conv[k] = total[16 * k : 16 * k + 16, :] * scale
+    proj[...] = total[144:160, :] * scale
+    value = total[160:304, :].astype(BF)
+    for k in range(8):
+        fine[k] = value
 
 
 def finish_kernel(scale, meta, mine, other, first, second):
-    block, core = ((meta[4] // 2) % 8, meta[4] % 2)
+    core = meta[4] % 2
     for at in range(8):
         out = first if at < 4 else second
-        a = mine[block ^ at].astype(F32) * scale
-        b = other[block ^ at].astype(F32) * scale
+        a = mine[at].astype(F32) * scale
+        b = other[at].astype(F32) * scale
         out[2 * (at % 4)] = jnp.where(core == 0, a, b)
         out[2 * (at % 4) + 1] = jnp.where(core == 0, b, a)
 
@@ -442,6 +445,20 @@
     count = lax.axis_size(axis)
     pairs = [(i, i + step) for i in range(count) if 0 <= i + step < count]
     return lax.ppermute(value, axis, pairs)
+
+
+def exchange_row(value):
+    count = lax.axis_size("row")
+    groups = [list(range(c, count, 2)) for c in range(2)]
+    return lax.all_to_all(value, "row", 0, 0, axis_index_groups=groups, tiled=True)
+
+
+def exchange_column(value):
+    return lax.all_to_all(value, "col", 0, 0, tiled=True)
+
+
+def after_all(value, *others):
+    return lax.optimization_barrier((value,) + others)[0]
 
 
 def local(features, conv_first, conv_second, coarse_conv, coarse_proj, cotangent):
@@ -458,25 +475,30 @@
     slab = ((160, CH), BF)
 
     right, left, own = call(
-        pack_columns_kernel, "pack_columns", (((16, 48, CH), BF), ((16, 48, CH), BF), slab), (feat, cot, conv, coarse_proj)
+        pack_columns_kernel,
+        "pack_columns",
+        (((16, 48, CH), BF), ((16, 48, CH), BF), slab),
+        (feat, cot, conv, coarse_proj),
+        (pltpu.SemaphoreType.DMA((14,)),),
+        far=True,
     )
     before = shifted(right, "col", 1)
     after = shifted(left, "col", -1)
-    other = swap(own, "row", 8)
-    down, up, near0 = call(
-        pack_rows_kernel,
-        "pack_rows",
-        (((12, 128, CH), BF), ((12, 128, CH), BF), ((2, 160, CH), BF)),
-        (feat, cot, before, after, own, other),
+    down, up = call(
+        pack_rows_kernel, "pack_rows", (((12, 128, CH), BF), ((12, 128, CH), BF)), (feat, cot, before, after)
     )
     above = shifted(down, "row", 1)
     below = shifted(up, "row", -1)
+    own = after_all(own, down)
+    near0 = call(stack_kernel, "stack_two", (((2, 160, CH), BF),), (own, swap(own, "row", 8)))[0]
+    near0 = after_all(near0, above, below)
     near = [near0] + [swap(near0, "row", 2 * k) for k in range(1, 4)]
-    far = swap(call(stack_kernel, "stack_weights", (((4, 2, 160, CH), BF),), near)[0], "row", 1)
+    far = swap(call(stack_kernel, "stack_eight", (((4, 2, 160, CH), BF),), near)[0], "row", 1)
 
     halo = (before, after, above, below)
     w1, w2 = (conv_first.reshape(1152, CH), conv_second.reshape(1152, CH))
-    pool3, slope1, slope2, act, feat3, act3 = fine_forward(meta, feat, *halo, w1, w2)
+    act3w, slope1, feat3 = first_step(meta, feat, *halo, w1)
+    pool3, slope2, act, act3 = second_step(meta, act3w, w2)
     blended, keep_c, send_c, pooled_grad = coarse_step(meta, pool3, cot, *halo, near, far, act)
     got_c = swap(send_c, "row", 1)
     keep_f, send_f, first3 = fine_backward(
@@ -485,33 +507,19 @@
     got_f = swap(send_f, "row", 1)
     feature_grad = feature_step(first3, conv_first.reshape(9, CH, CH))
 
-    whole = (304, CH)
-    total, *sends = call(
-        scatter_core_kernel, "scatter_core", ((whole, F32),) + ((whole, BF),) * 7, (meta, keep_c, keep_f, got_c, got_f)
-    )
-    got = [swap(v, "row", 2 * (k + 1)) for k, v in enumerate(sends)]
-    quarter = (80, CH)
-    part, *sends = call(
-        scatter_row_kernel,
-        "scatter_row",
-        ((quarter, F32),) + ((quarter, BF),) * 3,
-        (meta, total, *got),
-        (((4, 80, CH), F32),),
-    )
-    got = [swap(v, "col", k + 1) for k, v in enumerate(sends)]
-    part = call(sum_kernel, "sum_four", ((quarter, BF),), (part, *got))[0]
-    got = [swap(part, "col", 4 * k) for k in range(1, 4)]
-    part = call(sum_kernel, "sum_four", ((quarter, BF),), (part, *got))[0]
-    got = [swap(part, "col", k) for k in range(1, 4)]
+    part = call(scatter_core_kernel, "scatter_core", (((8, 304, CH), BF),), (keep_c, keep_f, got_c, got_f))[0]
+    part = call(
+        scatter_row_kernel, "scatter_row", (((16, 32, CH), BF),), (exchange_row(part),), (((336, CH), F32),)
+    )[0]
+    part = call(scatter_column_kernel, "scatter_column", (((16, 32, CH), BF),), (exchange_column(part),))[0]
     conv_grad, proj_grad, fine = call(
-        functools.partial(column_kernel, coarse_scale),
+        functools.partial(gather_column_kernel, coarse_scale),
         "gather_column",
-        (((9, 16, CH), F32), ((16, CH), F32), ((144, CH), BF)),
-        (meta, part, *got),
-        (((4, 80, CH), BF),),
-    )
-    got = [swap(fine, "row", 2 * k) for k in range(1, 8)]
-    fine = call(stack_kernel, "stack_grads", (((8, 144, CH), BF),), (fine, *got))[0]
+        (((9, 16, CH), F32), ((16, CH), F32), ((8, 144, CH), BF)),
+        (exchange_column(part),),
+        (((336, CH), F32),),
+    )
+    fine = exchange_row(fine)
     first, second = call(
         functools.partial(finish_kernel, fine_scale),
         "finish",

time: 132 us -> 125 us (0.947)
  blocking collectives: 0 us -> 52.7 us
  starting transfers between devices: 73.2 us -> 30.2 us
  waiting for transfers between devices: 30.5 us -> 12.1 us
  local copies, waits for them, and re-layouts: 3.45 us -> 5.36 us
    all_to_all x0 -> x4, blocking collectives: none -> 52.7 us  [the longest x2 26.9 us: exchange_row(): lax.all_to_all(value, 'row', 0, 0, axis_index_groups=groups, tiled=True)]
    ppermute x31 -> x8, starting transfers between devices: 61.9 us -> 17.9 us  [swap(): return lax.ppermute(value, axis, [(i, i ^ mask) for i in range(count)])]
    ppermute x31 -> x8, waiting for transfers between devices: 30.5 us -> 5.51 us  [swap(): return lax.ppermute(value, axis, [(i, i ^ mask) for i in range(count)])]
    ppermute x4, waiting for transfers between devices: 0.01 us -> 6.55 us  [shifted(): return lax.ppermute(value, axis, pairs)]
    unnamed x16 -> x18, local copies, waits for them, and re-layouts: 3.36 us -> 5.27 us
  transfers between devices with their start and end apart: 35 -> 12, of which waited for: 13 -> 5; matrix products, arithmetic and copies ran while one was open for 0% -> 0% of each run, Pallas kernels for 12% -> 13%
where the time goes in v3:
time: 125 us; the launch traced here: 124 us
  blocking collectives  52.7 us (42%)
  starting transfers between devices  30.2 us (24%)
  Pallas kernels  22.9 us (18%)
  waiting for transfers between devices  12.1 us (10%)
  local copies, waits for them, and re-layouts  5.36 us (4%)
    all_to_all x2, blocking collectives, exchange_row(): lax.all_to_all(value, 'row', 0, 0, axis_index_groups=groups, tiled=True)  26.9 us
    all_to_all x2, blocking collectives, exchange_column(): return lax.all_to_all(value, 'col', 0, 0, tiled=True)  25.8 us
    pallas_call x14, Pallas kernels, call(): pl.pallas_call(kernel, name=name, out_shape=shapes, in_specs=[pl.BlockSpe...  22.9 us
    ppermute x8, starting transfers between devices, swap(): return lax.ppermute(value, axis, [(i, i ^ mask) for i in range(count)])  17.9 us
    ppermute x4, starting transfers between devices, shifted(): return lax.ppermute(value, axis, pairs)  12.3 us
    ppermute x4, waiting for transfers between devices, shifted(): return lax.ppermute(value, axis, pairs)  6.55 us
    ppermute x8, waiting for transfers between devices, swap(): return lax.ppermute(value, axis, [(i, i ^ mask) for i in range(count)])  5.51 us
    unnamed x18, local copies, waits for them, and re-layouts  5.27 us
  transfers between devices with their start and end apart: 12, of which 5 were waited for; matrix products, arithmetic and copies ran while one was open for 0% of the time, Pallas kernels for 13%

profile of v3, /device:TPU:1, one launch (start us, length us, event | category | flops | bytes accessed | tf_op | source)
XLA Modules:
  0.0 124.0 jit_solution(16184893447666517651)
XLA Ops:
  0.6 0.9 copy-done
  1.6 0.9 copy-done.2
  2.5 0.8 copy-done.4
  3.3 0.7 copy-done.5
  4.0 0.3 pack_columns.1
  4.3 4.4 %collective-permute-start = (bf16[16,48,128]{2,1,0:T(8,128)(2,1)S(1)}, bf16[16,48,128]{2,1,0:T(8,128)(2,1)S(1)}, u32[]{:S(2)}, u32[]{:S(2)}) collective-permute-start(bf16[16,48,128]{2,1,0:T(8,128)(2,1)S(1)} %get-tuple-element.32), channel_id=1, source_target_pairs={{0,1},{1,2},{2,3},{3,4},{4,5},{5,6},{6,7},{7,8},{8,9},{9,10},{10,1... | collective-permute-start | bytes 589832 | tf_op jit(solution)/shard_map/ppermute | solution.py:447
  8.6 1.3 %collective-permute-start.1 = (bf16[16,48,128]{2,1,0:T(8,128)(2,1)S(1)}, bf16[16,48,128]{2,1,0:T(8,128)(2,1)S(1)}, u32[]{:S(2)}, u32[]{:S(2)}) collective-permute-start(bf16[16,48,128]{2,1,0:T(8,128)(2,1)S(1)} %get-tuple-element.33), channel_id=1, source_target_pairs={{1,0},{2,1},{3,2},{4,3},{5,4},{6,5},{7,6},{8,7},{9,8},{10,9},{11,1... | collective-permute-start | bytes 589832 | tf_op jit(solution)/shard_map/ppermute | solution.py:447
  9.9 2.2 %collective-permute-done.before = bf16[16,48,128]{2,1,0:T(8,128)(2,1)S(1)} collective-permute-done((bf16[16,48,128]{2,1,0:T(8,128)(2,1)S(1)}, bf16[16,48,128]{2,1,0:T(8,128)(2,1)S(1)}, u32[]{:S(2)}, u32[]{:S(2)}) %collective-permute-start) | collective-permute-done | bytes 196640 | tf_op jit(solution)/shard_map/ppermute | solution.py:447
  12.2 4.2 %collective-permute-done.1.after = bf16[16,48,128]{2,1,0:T(8,128)(2,1)S(1)} collective-permute-done((bf16[16,48,128]{2,1,0:T(8,128)(2,1)S(1)}, bf16[16,48,128]{2,1,0:T(8,128)(2,1)S(1)}, u32[]{:S(2)}, u32[]{:S(2)}) %collective-permute-start.1) | collective-permute-done | bytes 196640 | tf_op jit(solution)/shard_map/ppermute | solution.py:447
  16.4 4.7 %collective-permute-start.2 = (bf16[12,128,128]{2,1,0:T(8,128)(2,1)S(1)}, bf16[12,128,128]{2,1,0:T(8,128)(2,1)S(1)}, u32[]{:S(2)}, u32[]{:S(2)}) collective-permute-start(bf16[12,128,128]{2,1,0:T(8,128)(2,1)S(1)} %get-tuple-element.34), channel_id=1, source_target_pairs={{0,16},{16,32},{32,48},{48,64},{64,80},{80,96},{96,112},{112,128},... | collective-permute-start | bytes 1179656 | tf_op jit(solution)/shard_map/ppermute | solution.py:447
  21.1 1.9 %collective-permute-start.3 = (bf16[12,128,128]{2,1,0:T(8,128)(2,1)S(1)}, bf16[12,128,128]{2,1,0:T(8,128)(2,1)S(1)}, u32[]{:S(2)}, u32[]{:S(2)}) collective-permute-start(bf16[12,128,128]{2,1,0:T(8,128)(2,1)S(1)} %get-tuple-element.35), channel_id=1, source_target_pairs={{16,0},{32,16},{48,32},{64,48},{80,64},{96,80},{112,96},{128,112},... | collective-permute-start | bytes 1179656 | tf_op jit(solution)/shard_map/ppermute | solution.py:447
  23.0 3.0 %collective-permute-start.4 = (bf16[160,128]{1,0:T(8,128)(2,1)S(1)}, bf16[160,128]{1,0:T(8,128)(2,1)S(1)}, u32[]{:S(2)}, u32[]{:S(2)}) collective-permute-start(bf16[160,128]{1,0:T(8,128)(2,1)S(1)} %get-tuple-element.39.refs_0_), channel_id=1, source_target_pairs={{0,128},{16,144},{32,160},{48,176},{64,192},{80,208},{96,224},{112... | collective-permute-start | bytes 122888 | tf_op jit(solution)/shard_map/ppermute | solution.py:441
  26.1 3.9 %collective-permute-done.4.refs_1_ = bf16[160,128]{1,0:T(8,128)(2,1)S(1)} collective-permute-done((bf16[160,128]{1,0:T(8,128)(2,1)S(1)}, bf16[160,128]{1,0:T(8,128)(2,1)S(1)}, u32[]{:S(2)}, u32[]{:S(2)}) %collective-permute-start.4) | collective-permute-done | bytes 40992 | tf_op jit(solution)/shard_map/ppermute | solution.py:441
  30.2 1.2 collective-permute-start.5
  31.4 7.7 %collective-permute-start.6 = (bf16[2,160,128]{2,1,0:T(8,128)(2,1)S(1)}, bf16[2,160,128]{2,1,0:T(8,128)(2,1)S(1)}, u32[]{:S(2)}, u32[]{:S(2)}) collective-permute-start(bf16[2,160,128]{2,1,0:T(8,128)(2,1)S(1)} %stack_two.1.refs_0_.near0), channel_id=1, source_target_pairs={{0,64},{16,80},{32,96},{48,112},{64,0},{80,16},{96,32},{112,48},{1... | collective-permute-start | bytes 245768 | tf_op jit(solution)/shard_map/ppermute | solution.py:441
  39.1 0.9 copy-done.1
  40.1 1.0 copy-done.7
  41.0 5.2 %first_conv.1 = (bf16[30,128,384]{2,1,0:T(8,128)(2,1)S(1)}, f32[18,96,128]{2,1,0:T(8,128)S(1)}, bf16[18,64,384]{2,1,0:T(8,128)(2,1)S(1)}) custom-call(s32[6]{0:T(128)S(1)} %stack.19.meta, bf16[16,64,128]{2,1,0:T(8,128)(2,1)S(1)} %bitcast.22, bf16[16,48,128]{2,1,0:T(8,128)(2,1)S(1)} %collective-permute-done.before, ...), custom_call_target="tpu_custom_call" | custom-call | flops 4000000000 | tf_op jit(solution)/shard_map/first_conv/pallas_call | solution.py:21
  46.4 5.1 %second_conv.1 = (bf16[14,64,384]{2,1,0:T(8,128)(2,1)S(1)}, f32[20,96,128]{2,1,0:T(8,128)S(1)}, bf16[16,64,128]{2,1,0:T(8,128)(2,1)S(1)}, bf16[18,64,384]{2,1,0:T(8,128)(2,1)S(1)}) custom-call(s32[6]{0:T(128)S(1)} %stack.19.meta, bf16[30,128,384]{2,1,0:T(8,128)(2,1)S(1)} %get-tuple-element.36.act3, bf16[1152,128]{1,0:T(8,128)(2,1)S(1)} %bitcast.28), custom_call_target="tpu_custom_call" | custom-call | flops 4000000000 | tf_op jit(solution)/shard_map/second_conv/pallas_call | solution.py:21
  51.5 3.8 %coarse_step.1 = (bf16[16,64,128]{2,1,0:T(8,128)(2,1)}, bf16[8,160,128]{2,1,0:T(8,128)(2,1)S(1)}, bf16[8,160,128]{2,1,0:T(8,128)(2,1)S(1)}, f32[10,48,128]{2,1,0:T(8,128)S(1)}) custom-call(s32[6]{0:T(128)S(1)} %stack.19.meta, bf16[14,64,384]{2,1,0:T(8,128)(2,1)S(1)} %get-tuple-element.37.pool3, bf16[16,64,128]{2,1,0:T(8,128)(2,1)S(1)} %bitcast.25, ...), custom_call_target="tpu_custom_call" | custom-call | flops 2000000000 | tf_op jit(solution)/shard_map/coarse_step/pallas_call | solution.py:21
  55.3 0.6 collective-permute-start.9
  55.9 4.3 %fine_backward.1 = (bf16[8,144,128]{2,1,0:T(8,128)(2,1)S(1)}, bf16[8,144,128]{2,1,0:T(8,128)(2,1)S(1)}, bf16[18,64,384]{2,1,0:T(8,128)(2,1)S(1)}) custom-call(s32[6]{0:T(128)S(1)} %stack.19.meta, f32[10,48,128]{2,1,0:T(8,128)S(1)} %get-tuple-element.43.pooled_grad, bf16[16,64,128]{2,1,0:T(8,128)(2,1)S(1)} %bitcast.26, ...), custom_call_target="tpu_custom_call" | custom-call | flops 2000000000 | tf_op jit(solution)/shard_map/fine_backward/pallas_call | solution.py:21
  60.2 1.6 %collective-permute-done.10.got_f = bf16[8,144,128]{2,1,0:T(8,128)(2,1)S(1)} collective-permute-done((bf16[8,144,128]{2,1,0:T(8,128)(2,1)S(1)}, bf16[8,144,128]{2,1,0:T(8,128)(2,1)S(1)}, u32[]{:S(2)}, u32[]{:S(2)}) %collective-permute-start.10) | collective-permute-done | bytes 294944 | tf_op jit(solution)/shard_map/ppermute | solution.py:441
  61.8 0.1 scatter_core.1
  61.9 16.3 %all_to_all.20.got = bf16[8,304,128]{2,1,0:T(8,128)(2,1)S(1)} all-to-all(bf16[8,304,128]{2,1,0:T(8,128)(2,1)S(1)} %scatter_core.1), channel_id=1, replica_groups={{0,32,64,96,128,160,192,224},{16,48,80,112,144,176,208,240},{1,33,65,97..., dimensions={0} | all-to-all | bytes 1245184 | tf_op jit(solution)/shard_map/all_to_all | solution.py:453
  78.4 15.3 %all_to_all.21.got = bf16[16,32,128]{2,1,0:T(8,128)(2,1)S(1)} all-to-all(bf16[16,32,128]{2,1,0:T(8,128)(2,1)S(1)} %scatter_row.1), channel_id=1, replica_groups=mesh['row'=16,'col'=16] {'col'}, dimensions={0} | all-to-all | bytes 262144 | tf_op jit(solution)/shard_map/all_to_all | solution.py:457
  93.7 10.5 %all_to_all.22.got = bf16[16,32,128]{2,1,0:T(8,128)(2,1)S(1)} all-to-all(bf16[16,32,128]{2,1,0:T(8,128)(2,1)S(1)} %scatter_column.1), channel_id=1, replica_groups=mesh['row'=16,'col'=16] {'col'}, dimensions={0} | all-to-all | bytes 262144 | tf_op jit(solution)/shard_map/all_to_all | solution.py:457
  104.2 0.7 gather_column.1
  104.9 10.6 %all_to_all.23.mine = bf16[8,144,128]{2,1,0:T(8,128)(2,1)S(1)} all-to-all(bf16[8,144,128]{2,1,0:T(8,128)(2,1)S(1)} %get-tuple-element.53), channel_id=1, replica_groups={{0,32,64,96,128,160,192,224},{16,48,80,112,144,176,208,240},{1,33,65,97..., dimensions={0} | all-to-all | bytes 589824 | tf_op jit(solution)/shard_map/all_to_all | solution.py:453
  115.5 5.3 %collective-permute-start.11 = (bf16[8,144,128]{2,1,0:T(8,128)(2,1)S(1)}, bf16[8,144,128]{2,1,0:T(8,128)(2,1)S(1)}, u32[]{:S(2)}, u32[]{:S(2)}) collective-permute-start(bf16[8,144,128]{2,1,0:T(8,128)(2,1)S(1)} %all_to_all.23.mine), channel_id=1, source_target_pairs={{0,16},{16,0},{32,48},{48,32},{64,80},{80,64},{96,112},{112,96},{1... | collective-permute-start | bytes 884744 | tf_op jit(solution)/shard_map/ppermute | solution.py:441
  120.7 1.7 %feature_step.1 = bf16[16,64,128]{2,1,0:T(8,128)(2,1)} custom-call(bf16[18,64,384]{2,1,0:T(8,128)(2,1)S(1)} %get-tuple-element.48.first3, bf16[9,128,128]{2,1,0:T(8,128)(2,1)S(1)} %bitcast.31), custom_call_target="tpu_custom_call" | custom-call | flops 1000000000 | tf_op jit(solution)/shard_map/feature_step/pallas_call | solution.py:21
  122.4 1.6 %finish.1 = (f32[8,144,128]{2,1,0:T(8,128)}, f32[8,144,128]{2,1,0:T(8,128)}) custom-call(s32[6]{0:T(128)S(1)} %stack.19.meta, bf16[8,144,128]{2,1,0:T(8,128)(2,1)S(1)} %all_to_all.23.mine, bf16[8,144,128]{2,1,0:T(8,128)(2,1)S(1)} %collective-permute-done.11.other), custom_call_target="tpu_custom_call" | custom-call | tf_op jit(solution)/shard_map/finish/pallas_call | solution.py:21
  (30 shorter events, 0.7 us)
Async XLA Ops:
  0.6 1.0 copy-start
  1.6 0.9 copy-start.2
  2.5 0.8 copy-start.4
  3.3 0.7 copy-start.5
  4.3 7.9 %collective-permute-start = (bf16[16,48,128]{2,1,0:T(8,128)(2,1)S(1)}, bf16[16,48,128]{2,1,0:T(8,128)(2,1)S(1)}, u32[]{:S(2)}, u32[]{:S(2)}) collective-permute-start(bf16[16,48,128]{2,1,0:T(8,128)(2,1)S(1)} %get-tuple-element.32), channel_id=1, source_target_pairs={{0,1},{1,2},{2,3},{3,4},{4,5},{5,6},{6,7},{7,8},{8,9},{9,10},{10,1... | collective-permute-start | bytes 589832 | tf_op jit(solution)/shard_map/ppermute | solution.py:447
  8.6 7.7 %collective-permute-start.1 = (bf16[16,48,128]{2,1,0:T(8,128)(2,1)S(1)}, bf16[16,48,128]{2,1,0:T(8,128)(2,1)S(1)}, u32[]{:S(2)}, u32[]{:S(2)}) collective-permute-start(bf16[16,48,128]{2,1,0:T(8,128)(2,1)S(1)} %get-tuple-element.33), channel_id=1, source_target_pairs={{1,0},{2,1},{3,2},{4,3},{5,4},{6,5},{7,6},{8,7},{9,8},{10,9},{11,1... | collective-permute-start | bytes 589832 | tf_op jit(solution)/shard_map/ppermute | solution.py:447
  16.4 13.6 %collective-permute-start.2 = (bf16[12,128,128]{2,1,0:T(8,128)(2,1)S(1)}, bf16[12,128,128]{2,1,0:T(8,128)(2,1)S(1)}, u32[]{:S(2)}, u32[]{:S(2)}) collective-permute-start(bf16[12,128,128]{2,1,0:T(8,128)(2,1)S(1)} %get-tuple-element.34), channel_id=1, source_target_pairs={{0,16},{16,32},{32,48},{48,64},{64,80},{80,96},{96,112},{112,128},... | collective-permute-start | bytes 1179656 | tf_op jit(solution)/shard_map/ppermute | solution.py:447
  21.1 9.1 %collective-permute-start.3 = (bf16[12,128,128]{2,1,0:T(8,128)(2,1)S(1)}, bf16[12,128,128]{2,1,0:T(8,128)(2,1)S(1)}, u32[]{:S(2)}, u32[]{:S(2)}) collective-permute-start(bf16[12,128,128]{2,1,0:T(8,128)(2,1)S(1)} %get-tuple-element.35), channel_id=1, source_target_pairs={{16,0},{32,16},{48,32},{64,48},{80,64},{96,80},{112,96},{128,112},... | collective-permute-start | bytes 1179656 | tf_op jit(solution)/shard_map/ppermute | solution.py:447
  23.0 7.0 %collective-permute-start.4 = (bf16[160,128]{1,0:T(8,128)(2,1)S(1)}, bf16[160,128]{1,0:T(8,128)(2,1)S(1)}, u32[]{:S(2)}, u32[]{:S(2)}) collective-permute-start(bf16[160,128]{1,0:T(8,128)(2,1)S(1)} %get-tuple-element.39.refs_0_), channel_id=1, source_target_pairs={{0,128},{16,144},{32,160},{48,176},{64,192},{80,208},{96,224},{112... | collective-permute-start | bytes 122888 | tf_op jit(solution)/shard_map/ppermute | solution.py:441
  30.2 16.0 %collective-permute-start.5 = (bf16[2,160,128]{2,1,0:T(8,128)(2,1)S(1)}, bf16[2,160,128]{2,1,0:T(8,128)(2,1)S(1)}, u32[]{:S(2)}, u32[]{:S(2)}) collective-permute-start(bf16[2,160,128]{2,1,0:T(8,128)(2,1)S(1)} %stack_two.1.refs_0_.near0), channel_id=1, source_target_pairs={{0,32},{16,48},{32,0},{48,16},{64,96},{80,112},{96,64},{112,80},{1... | collective-permute-start | bytes 245768 | tf_op jit(solution)/shard_map/ppermute | solution.py:441
  31.4 14.8 %collective-permute-start.6 = (bf16[2,160,128]{2,1,0:T(8,128)(2,1)S(1)}, bf16[2,160,128]{2,1,0:T(8,128)(2,1)S(1)}, u32[]{:S(2)}, u32[]{:S(2)}) collective-permute-start(bf16[2,160,128]{2,1,0:T(8,128)(2,1)S(1)} %stack_two.1.refs_0_.near0), channel_id=1, source_target_pairs={{0,64},{16,80},{32,96},{48,112},{64,0},{80,16},{96,32},{112,48},{1... | collective-permute-start | bytes 245768 | tf_op jit(solution)/shard_map/ppermute | solution.py:441
  39.1 7.2 %collective-permute-start.7 = (bf16[2,160,128]{2,1,0:T(8,128)(2,1)S(1)}, bf16[2,160,128]{2,1,0:T(8,128)(2,1)S(1)}, u32[]{:S(2)}, u32[]{:S(2)}) collective-permute-start(bf16[2,160,128]{2,1,0:T(8,128)(2,1)S(1)} %stack_two.1.refs_0_.near0), channel_id=1, source_target_pairs={{0,96},{16,112},{32,64},{48,80},{64,32},{80,48},{96,0},{112,16},{1... | collective-permute-start | bytes 245768 | tf_op jit(solution)/shard_map/ppermute | solution.py:441
  39.1 1.0 copy-start.1
  40.1 1.0 copy-start.7
  41.0 5.4 %copy-start.6 = (bf16[3,3,128,128]{3,2,1,0:T(8,128)(2,1)S(1)}, bf16[3,3,128,128]{3,2,1,0:T(8,128)(2,1)}, u32[]{:S(2)}) copy-start(bf16[3,3,128,128]{3,2,1,0:T(8,128)(2,1)} %param.8) | copy-start | bytes 884740
  46.3 5.2 %collective-permute-start.8 = (bf16[4,2,160,128]{3,2,1,0:T(8,128)(2,1)S(1)}, bf16[4,2,160,128]{3,2,1,0:T(8,128)(2,1)S(1)}, u32[]{:S(2)}, u32[]{:S(2)}) collective-permute-start(bf16[4,2,160,128]{3,2,1,0:T(8,128)(2,1)S(1)} %stack_eight.1), channel_id=1, source_target_pairs={{0,16},{16,0},{32,48},{48,32},{64,80},{80,64},{96,112},{112,96},{1... | collective-permute-start | bytes 983048 | tf_op jit(solution)/shard_map/ppermute | solution.py:441
  46.4 5.1 %copy-start.3 = (bf16[16,16,4,128]{3,2,1,0:T(4,128)(2,1)S(1)}, bf16[16,16,4,128]{3,2,1,0:T(4,128)(2,1)}, u32[]{:S(2)}) copy-start(bf16[16,16,4,128]{3,2,1,0:T(4,128)(2,1)} %param.11) | copy-start | bytes 786436
  55.3 6.5 %collective-permute-start.9 = (bf16[8,160,128]{2,1,0:T(8,128)(2,1)S(1)}, bf16[8,160,128]{2,1,0:T(8,128)(2,1)S(1)}, u32[]{:S(2)}, u32[]{:S(2)}) collective-permute-start(bf16[8,160,128]{2,1,0:T(8,128)(2,1)S(1)} %get-tuple-element.51), channel_id=1, source_target_pairs={{0,16},{16,0},{32,48},{48,32},{64,80},{80,64},{96,112},{112,96},{1... | collective-permute-start | bytes 983048 | tf_op jit(solution)/shard_map/ppermute | solution.py:441
  60.1 60.6 %copy-start.8 = (bf16[3,3,128,128]{3,2,1,0:T(8,128)(2,1)S(1)}, bf16[3,3,128,128]{3,2,1,0:T(8,128)(2,1)}, u32[]{:S(2)}) copy-start(bf16[3,3,128,128]{3,2,1,0:T(8,128)(2,1)} %param.7) | copy-start | bytes 884740
  60.1 1.7 %collective-permute-start.10 = (bf16[8,144,128]{2,1,0:T(8,128)(2,1)S(1)}, bf16[8,144,128]{2,1,0:T(8,128)(2,1)S(1)}, u32[]{:S(2)}, u32[]{:S(2)}) collective-permute-start(bf16[8,144,128]{2,1,0:T(8,128)(2,1)S(1)} %get-tuple-element.52), channel_id=1, source_target_pairs={{0,16},{16,0},{32,48},{48,32},{64,80},{80,64},{96,112},{112,96},{1... | collective-permute-start | bytes 884744 | tf_op jit(solution)/shard_map/ppermute | solution.py:441
  115.5 6.9 %collective-permute-start.11 = (bf16[8,144,128]{2,1,0:T(8,128)(2,1)S(1)}, bf16[8,144,128]{2,1,0:T(8,128)(2,1)S(1)}, u32[]{:S(2)}, u32[]{:S(2)}) collective-permute-start(bf16[8,144,128]{2,1,0:T(8,128)(2,1)S(1)} %all_to_all.23.mine), channel_id=1, source_target_pairs={{0,16},{16,0},{32,48},{48,32},{64,80},{80,64},{96,112},{112,96},{1... | collective-permute-start | bytes 884744 | tf_op jit(solution)/shard_map/ppermute | solution.py:441

commit v4 on v3

--- a/solution.py
+++ b/solution.py
@@ -14,17 +14,19 @@
 MIB = 1024 * 1024
 VM = pl.BlockSpec(memory_space=pltpu.VMEM)
 SM = pl.BlockSpec(memory_space=pltpu.SMEM)
-
-
-def call(kernel, name, outs, ins, scratch=(), limit=16, flops=0, moved=0, far=False):
+HBM = pl.BlockSpec(memory_space=pltpu.HBM)
+
+
+def call(kernel, name, outs, ins, scratch=(), limit=16, flops=0, moved=0, far=()):
+    ins = [pltpu.with_memory_space_constraint(v, pltpu.HBM) if k in far else v for k, v in enumerate(ins)]
     shapes = tuple(jax.ShapeDtypeStruct(shape, dtype) for shape, dtype in outs)
     return pl.pallas_call(
         kernel,
         name=name,
         out_shape=shapes,
-        in_specs=[pl.BlockSpec(memory_space=pl.ANY) if far else SM if v.ndim == 1 else VM for v in ins],
+        in_specs=[HBM if k in far else SM if v.ndim == 1 else VM for k, v in enumerate(ins)],
         out_specs=tuple(VM for _ in outs),
-        scratch_shapes=[v if len(v) != 2 else pltpu.VMEM(*v) for v in scratch] if not far else list(scratch),
+        scratch_shapes=[pltpu.VMEM(*v) if isinstance(v, tuple) else v for v in scratch],
         compiler_params=pltpu.CompilerParams(vmem_limit_bytes=limit * MIB),
         cost_estimate=pl.CostEstimate(flops=flops, bytes_accessed=moved, transcendentals=0),
     )(*ins)
@@ -102,12 +104,22 @@
     return jnp.concatenate([even, odd], axis=1).reshape(count * 2, CH)
 
 
-def pack_columns_kernel(feat, cot, conv, proj, right, left, weights, done):
+def aligned(start, size):
+    return pl.ds(pl.multiple_of(start, 16), size)
+
+
+def sides(meta, pair, other):
+    even = meta[5] % 2 == 0
+    return lax.select(even, other, pair), lax.select(even, pair, other)
+
+
+def pack_columns_kernel(meta, feat, cot, conv, proj, pair, other, weights, done):
+    odd = meta[5] % 2
     pairs = [
-        (feat.at[:, 32:64, :], right.at[:, 0:32, :]),
-        (cot.at[:, 48:64, :], right.at[:, 32:48, :]),
-        (feat.at[:, 0:32, :], left.at[:, 0:32, :]),
-        (cot.at[:, 0:16, :], left.at[:, 32:48, :]),
+        (feat.at[:, aligned(32 - 32 * odd, 32), :], pair.at[:, 0:32, :]),
+        (cot.at[:, aligned(48 - 48 * odd, 16), :], pair.at[:, 32:48, :]),
+        (feat.at[:, aligned(32 * odd, 32), :], other.at[:, 0:32, :]),
+        (cot.at[:, aligned(48 * odd, 16), :], other.at[:, 32:48, :]),
         (proj, weights.at[144:160, :]),
     ] + [(conv.at[t], weights.at[16 * t : 16 * t + 16, :]) for t in range(9)]
     copies = [pltpu.make_async_copy(a, b, done.at[k]) for k, (a, b) in enumerate(pairs)]
@@ -117,15 +129,29 @@
         copy.wait()
 
 
-def pack_rows_kernel(feat, cot, before, after, down, up):
-    for out, first, second in ((down, 8, 12), (up, 0, 0)):
-        out[0:8, 0:32, :] = before[first : first + 8, 0:32, :]
-        out[0:8, 32:96, :] = feat[first : first + 8]
-        out[0:8, 96:128, :] = after[first : first + 8, 0:32, :]
-        out[8:12, 0:16, :] = before[second : second + 4, 32:48, :]
-        out[8:12, 16:80, :] = cot[second : second + 4]
-        out[8:12, 80:96, :] = after[second : second + 4, 32:48, :]
+def pack_rows_kernel(meta, feat, cot, pair, other, inner, outer, done):
+    core = meta[4] % 2
+    copies = []
+    for k, (out, low) in enumerate(((inner, 1 - core), (outer, core))):
+        pairs = (
+            (feat.at[pl.ds(8 * low, 8)], out.at[0:8, 32:96, :]),
+            (cot.at[pl.ds(12 * low, 4)], out.at[8:12, 16:80, :]),
+        )
+        copies += [pltpu.make_async_copy(a, b, done.at[2 * k + n]) for n, (a, b) in enumerate(pairs)]
+    for copy in copies:
+        copy.start()
+    for out, low in ((inner, 1 - core), (outer, core)):
+        for out_rows, first, inside, edge in (
+            (slice(0, 8), 8 * low, slice(0, 32), slice(96, 128)),
+            (slice(8, 12), 12 * low, slice(32, 48), slice(80, 96)),
+        ):
+            source = pl.ds(first, out_rows.stop - out_rows.start)
+            before, after = sides(meta, pair[source, inside, :], other[source, inside, :])
+            out[out_rows, 0 : inside.stop - inside.start, :] = before
+            out[out_rows, edge, :] = after
         out[8:12, 96:128, :] = jnp.zeros((4, 32, CH), BF)
+    for copy in copies:
+        copy.wait()
 
 
 def stack_kernel(*refs):
@@ -134,22 +160,31 @@
         out[k] = ref[...]
 
 
-def first_kernel(meta, feat, before, after, above, below, w1, act3, slope1, feat3o, feat3, pre1):
+def first_kernel(meta, feat_far, pair, other, inner, outer, w1_far, act3, slope1, feat3o, feat3, pre1, feat, w1, done):
+    copies = [pltpu.make_async_copy(feat_far, feat, done.at[0]), pltpu.make_async_copy(w1_far, w1, done.at[1])]
+    for copy in copies:
+        copy.start()
     top, left, height, breadth = (meta[0], meta[1], meta[2], meta[3])
     mask = column_mask(left - 8, 128, breadth)
+
+    below_at = 24 * (meta[4] % 2)
+
+    @pl.loop(0, 2)
+    def _(b):
+        block = outer[pl.ds(4 * b, 4)].reshape(512, CH).astype(F32)
+        feat3[pl.ds(4 * b + below_at, 4)] = three(block).reshape(4, 128, 3 * CH)
+        block = inner[pl.ds(4 * b, 4)].reshape(512, CH).astype(F32)
+        feat3[pl.ds(4 * b + 24 - below_at, 4)] = three(block).reshape(4, 128, 3 * CH)
+
+    for copy in copies:
+        copy.wait()
 
     @pl.loop(0, 4)
     def _(b):
         rows = pl.ds(4 * b, 4)
-        middle = jnp.concatenate([before[rows, 0:32, :], feat[rows], after[rows, 0:32, :]], axis=1)
+        before, after = sides(meta, pair[rows, 0:32, :], other[rows, 0:32, :])
+        middle = jnp.concatenate([before, feat[rows], after], axis=1)
         feat3[pl.ds(4 * b + 8, 4)] = three(middle.reshape(512, CH).astype(F32)).reshape(4, 128, 3 * CH)
-
-    @pl.loop(0, 2)
-    def _(b):
-        block = above[pl.ds(4 * b, 4)].reshape(512, CH).astype(F32)
-        feat3[pl.ds(4 * b, 4)] = three(block).reshape(4, 128, 3 * CH)
-        block = below[pl.ds(4 * b, 4)].reshape(512, CH).astype(F32)
-        feat3[pl.ds(4 * b + 24, 4)] = three(block).reshape(4, 128, 3 * CH)
 
     first_w = w1[...]
 
@@ -199,13 +234,20 @@
         act[k] = act2[k + 6, 32:96, :]
 
 
-def first_step(meta, feat, before, after, above, below, w1):
+def first_step(meta, feat, halo, w1):
     return call(
         first_kernel,
         "first_conv",
         (((30, 128, 384), BF), ((18, 96, CH), F32), ((18, 64, 384), BF)),
-        (meta, feat, before, after, above, below, w1),
-        (((32, 128, 384), BF), ((30, 128, CH), F32)),
+        (meta, feat) + halo + (w1,),
+        (
+            ((32, 128, 384), BF),
+            ((30, 128, CH), F32),
+            ((16, 64, CH), BF),
+            ((1152, CH), BF),
+            pltpu.SemaphoreType.DMA((2,)),
+        ),
+        far=(1, 6),
         limit=20,
         flops=4 * 10**9,
     )
@@ -224,7 +266,7 @@
 
 
 def coarse_kernel(
-    meta, pool3, cot, before, after, above, below, near0, near1, near2, near3, far, act,
+    meta, pool3, cot, pair, other, inner, outer, near0, near1, near2, near3, far, act,
     blended, keep, send, pooled_grad, wcat, projs, wide3, projin,
 ):
     top, left, height, breadth, me = (meta[0], meta[1], meta[2], meta[3], meta[4])
@@ -242,15 +284,17 @@
     def pair_sum(a, b):
         return pooled_pair(a.astype(F32) + b.astype(F32))
 
+    below_at = 10 * core
     for k in range(2):
-        projin[k] = pair_sum(above[8 + 2 * k, 0:96, :], above[9 + 2 * k, 0:96, :])
-        projin[k + 10] = pair_sum(below[8 + 2 * k, 0:96, :], below[9 + 2 * k, 0:96, :])
+        projin[k + below_at] = pair_sum(outer[8 + 2 * k, 0:96, :], outer[9 + 2 * k, 0:96, :])
+        projin[k + 10 - below_at] = pair_sum(inner[8 + 2 * k, 0:96, :], inner[9 + 2 * k, 0:96, :])
 
     @pl.loop(0, 8)
     def _(k):
         rows = pl.ds(2 * k, 2)
-        pair = jnp.concatenate([before[rows, 32:48, :], cot[rows], after[rows, 32:48, :]], axis=1)
-        projin[k + 2] = pair_sum(pair[0], pair[1])
+        before, after = sides(meta, pair[rows, 32:48, :], other[rows, 32:48, :])
+        both = jnp.concatenate([before, cot[rows], after], axis=1)
+        projin[k + 2] = pair_sum(both[0], both[1])
 
     proj_in = projin[...].reshape(576, CH)
     proj_in_bf = proj_in.astype(BF)
@@ -295,12 +339,12 @@
             blended[2 * k + e] = (act[2 * k + e].astype(F32) + row).astype(BF)
 
 
-def coarse_step(meta, pool3, cot, before, after, above, below, near, far, act):
+def coarse_step(meta, pool3, cot, halo, near, far, act):
     return call(
         coarse_kernel,
         "coarse_step",
         (((16, 64, CH), BF), ((8, 160, CH), BF), ((8, 160, CH), BF), ((10, 48, CH), F32)),
-        (meta, pool3, cot, before, after, above, below) + tuple(near) + (far, act),
+        (meta, pool3, cot) + halo + tuple(near) + (far, act),
         (
             ((WIDE, 9 * CH), BF),
             ((WIDE, CH), BF),
@@ -317,27 +361,29 @@
 
 
 def backward_kernel(
-    meta, pooled_grad, cot, before, after, above, below, slope1, slope2, feat3, act3, w2,
+    meta, pooled_grad, cot, pair, other, inner, outer, slope1, slope2, feat3, act3, w2,
     keep, send, first3, second3, grads,
 ):
     top, left, height, breadth = (meta[0], meta[1], meta[2], meta[3])
     mask = column_mask(left - 4, 96, breadth)
 
-    def second_rows(k, pair):
+    def second_rows(k, both):
         wide = 0.25 * repeated(pooled_grad[k])
         rows = []
         for e in range(2):
-            value = rounded((pair[e].astype(F32) + wide) * slope2[2 * k + e])
+            value = rounded((both[e].astype(F32) + wide) * slope2[2 * k + e])
             rows.append(value * (mask * row_ok(top - 2 + 2 * k + e, height)))
         second3[pl.ds(2 * k, 2)] = three(jnp.concatenate(rows, axis=0)).reshape(2, 96, 3 * CH)
 
-    second_rows(0, above[10:12, 0:96, :])
-    second_rows(9, below[8:10, 0:96, :])
+    first_core = meta[4] % 2 == 0
+    second_rows(0, lax.select(first_core, outer[10:12, 0:96, :], inner[10:12, 0:96, :]))
+    second_rows(9, lax.select(first_core, inner[8:10, 0:96, :], outer[8:10, 0:96, :]))
 
     @pl.loop(0, 8)
     def _(k):
         rows = pl.ds(2 * k, 2)
-        second_rows(k + 1, jnp.concatenate([before[rows, 32:48, :], cot[rows], after[rows, 32:48, :]], axis=1))
+        before, after = sides(meta, pair[rows, 32:48, :], other[rows, 32:48, :])
+        second_rows(k + 1, jnp.concatenate([before, cot[rows], after], axis=1))
 
     def weight_grad(source, grad):
         return [dot_tn(source[r : r + 16].reshape(1024, 3 * CH), grad) for r in range(3)]
@@ -366,12 +412,12 @@
         send[k] = grads[pl.ds(pl.multiple_of((2 * k + 1 - core) * 144, 16), 144), :]
 
 
-def fine_backward(meta, pooled_grad, cot, before, after, above, below, slope1, slope2, feat3, act3, w2):
+def fine_backward(meta, pooled_grad, cot, halo, slope1, slope2, feat3, act3, w2):
     return call(
         backward_kernel,
         "fine_backward",
         (((8, 144, CH), BF), ((8, 144, CH), BF), ((18, 64, 384), BF)),
-        (meta, pooled_grad, cot, before, after, above, below, slope1, slope2, feat3, act3, w2),
+        (meta, pooled_grad, cot) + halo + (slope1, slope2, feat3, act3, w2),
         (((20, 96, 384), BF), ((2304, CH), BF)),
         limit=20,
         flops=2 * 10**9,
@@ -441,9 +487,9 @@
     return lax.ppermute(value, axis, [(i, i ^ mask) for i in range(count)])
 
 
-def shifted(value, axis, step):
+def swap_outer(value, axis):
     count = lax.axis_size(axis)
-    pairs = [(i, i + step) for i in range(count) if 0 <= i + step < count]
+    pairs = [(i, i + 1 if i % 2 else i - 1) for i in range(1, count - 1)]
     return lax.ppermute(value, axis, pairs)
 
 
@@ -474,39 +520,46 @@
     conv = coarse_conv.reshape(9, CH, 16).swapaxes(1, 2)
     slab = ((160, CH), BF)
 
-    right, left, own = call(
+    side = ((16, 48, CH), BF)
+    pair, other, own = call(
         pack_columns_kernel,
         "pack_columns",
-        (((16, 48, CH), BF), ((16, 48, CH), BF), slab),
-        (feat, cot, conv, coarse_proj),
+        (side, side, slab),
+        (meta, feat, cot, conv, coarse_proj),
         (pltpu.SemaphoreType.DMA((14,)),),
-        far=True,
-    )
-    before = shifted(right, "col", 1)
-    after = shifted(left, "col", -1)
-    down, up = call(
-        pack_rows_kernel, "pack_rows", (((12, 128, CH), BF), ((12, 128, CH), BF)), (feat, cot, before, after)
-    )
-    above = shifted(down, "row", 1)
-    below = shifted(up, "row", -1)
-    own = after_all(own, down)
-    near0 = call(stack_kernel, "stack_two", (((2, 160, CH), BF),), (own, swap(own, "row", 8)))[0]
-    near0 = after_all(near0, above, below)
+        far=(1, 2, 3, 4),
+    )
+    pair = swap(pair, "col", 1)
+    other = swap_outer(other, "col")
+    own_far = swap(own, "row", 8)
+    edge = ((12, 128, CH), BF)
+    inner, outer = call(
+        pack_rows_kernel,
+        "pack_rows",
+        (edge, edge),
+        (meta, feat, cot, pair, other),
+        (pltpu.SemaphoreType.DMA((4,)),),
+        far=(1, 2),
+    )
+    inner = swap(inner, "row", 1)
+    outer = swap_outer(outer, "row")
+    halo = (pair, other, inner, outer)
+    w1, w2 = (conv_first.reshape(1152, CH), conv_second.reshape(1152, CH))
+    act3w, slope1, feat3 = first_step(meta, feat, halo, w1)
+    near0 = call(stack_kernel, "stack_two", (((2, 160, CH), BF),), (own, after_all(own_far, slope1)))[0]
     near = [near0] + [swap(near0, "row", 2 * k) for k in range(1, 4)]
+    pool3, slope2, act, act3 = second_step(meta, act3w, w2)
+    near = list(lax.optimization_barrier((slope2, *near)))[1:]
     far = swap(call(stack_kernel, "stack_eight", (((4, 2, 160, CH), BF),), near)[0], "row", 1)
-
-    halo = (before, after, above, below)
-    w1, w2 = (conv_first.reshape(1152, CH), conv_second.reshape(1152, CH))
-    act3w, slope1, feat3 = first_step(meta, feat, *halo, w1)
-    pool3, slope2, act, act3 = second_step(meta, act3w, w2)
-    blended, keep_c, send_c, pooled_grad = coarse_step(meta, pool3, cot, *halo, near, far, act)
+    blended, keep_c, send_c, pooled_grad = coarse_step(meta, pool3, cot, halo, near, far, act)
     got_c = swap(send_c, "row", 1)
     keep_f, send_f, first3 = fine_backward(
-        meta, pooled_grad, cot, *halo, slope1, slope2, feat3, act3, conv_second.reshape(9, CH, CH)
+        meta, pooled_grad, cot, halo, slope1, slope2, feat3, act3, conv_second.reshape(9, CH, CH)
     )
     got_f = swap(send_f, "row", 1)
     feature_grad = feature_step(first3, conv_first.reshape(9, CH, CH))
 
+    got_f = after_all(got_f, feature_grad)
     part = call(scatter_core_kernel, "scatter_core", (((8, 304, CH), BF),), (keep_c, keep_f, got_c, got_f))[0]
     part = call(
         scatter_row_kernel, "scatter_row", (((16, 32, CH), BF),), (exchange_row(part),), (((336, CH), F32),)

time: 125 us -> 120 us (0.960)
  starting transfers between devices: 30.2 us -> 24.9 us
  local copies, waits for them, and re-layouts: 5.36 us -> 0.1 us
  blocking collectives: 52.7 us -> 57.4 us
  Pallas kernels: 22.9 us -> 26.8 us
  waiting for transfers between devices: 12.1 us -> 9.39 us
    ppermute x4 -> x2, starting transfers between devices: 12.3 us -> 3.09 us  [swap_outer(): return lax.ppermute(value, axis, pairs)]
    unnamed x18 -> x6, local copies, waits for them, and re-layouts: 5.27 us -> 0.01 us
    all_to_all x2, blocking collectives: 25.8 us -> 29.9 us  [exchange_column(): return lax.all_to_all(value, 'col', 0, 0, tiled=True)]
    ppermute x8 -> x10, starting transfers between devices: 17.9 us -> 21.8 us  [swap(): return lax.ppermute(value, axis, [(i, i ^ mask) for i in range(count)])]
    pallas_call x14, Pallas kernels: 22.9 us -> 26.8 us  [call(): pl.pallas_call(kernel, name=name, out_shape=shapes, in_specs=[HBM if k in...]
    ppermute x4 -> x2, waiting for transfers between devices: 6.55 us -> 3.64 us  [swap_outer(): return lax.ppermute(value, axis, pairs)]
    ppermute x8 -> x10, waiting for transfers between devices: 5.51 us -> 5.74 us  [swap(): return lax.ppermute(value, axis, [(i, i ^ mask) for i in range(count)])]
  transfers between devices with their start and end apart: 12 -> 12, of which waited for: 5 -> 4; matrix products, arithmetic and copies ran while one was open for 0% -> 0% of each run, Pallas kernels for 13% -> 14%
where the time goes in v4:
time: 120 us; the launch traced here: 119 us
  blocking collectives  57.4 us (48%)
  Pallas kernels  26.8 us (22%)
  starting transfers between devices  24.9 us (21%)
  waiting for transfers between devices  9.39 us (8%)
    all_to_all x2, blocking collectives, exchange_column(): return lax.all_to_all(value, 'col', 0, 0, tiled=True)  29.9 us
    all_to_all x2, blocking collectives, exchange_row(): lax.all_to_all(value, 'row', 0, 0, axis_index_groups=groups, tiled=True)  27.6 us
    pallas_call x14, Pallas kernels, call(): pl.pallas_call(kernel, name=name, out_shape=shapes, in_specs=[HBM if k in...  26.8 us
    ppermute x10, starting transfers between devices, swap(): return lax.ppermute(value, axis, [(i, i ^ mask) for i in range(count)])  21.8 us
    ppermute x10, waiting for transfers between devices, swap(): return lax.ppermute(value, axis, [(i, i ^ mask) for i in range(count)])  5.74 us
    ppermute x2, waiting for transfers between devices, swap_outer(): return lax.ppermute(value, axis, pairs)  3.64 us
    ppermute x2, starting transfers between devices, swap_outer(): return lax.ppermute(value, axis, pairs)  3.09 us
  transfers between devices with their start and end apart: 12, of which 4 were waited for; matrix products, arithmetic and copies ran while one was open for 0% of the time, Pallas kernels for 14%

profile of v4, /device:TPU:1, one launch (start us, length us, event | category | flops | bytes accessed | tf_op | source)
XLA Modules:
  0.0 119.3 jit_solution(61696246957801900)
XLA Ops:
  0.6 0.1 stack.19.meta
  0.7 1.7 %pack_columns.1 = (bf16[16,48,128]{2,1,0:T(8,128)(2,1)S(1)}, bf16[16,48,128]{2,1,0:T(8,128)(2,1)S(1)}, bf16[160,128]{1,0:T(8,128)(2,1)S(1)}) custom-call(s32[6]{0:T(128)S(1)} %stack.19.meta, bf16[16,64,128]{2,1,0:T(8,128)(2,1)} %bitcast.28, bf16[16,64,128]{2,1,0:T(8,128)(2,1)} %bitcast.20, bf16[9,16,128]{2,1,0:T(8,128)(2,1)} %bitcast.31, bf16[16,128]{1,0:T(8,128)(2,1)} %proj.1), custom_call_target="tpu_custom_call" | custom-call | tf_op jit(solution)/shard_map/pack_columns/pallas_call | solution.py:23
  2.4 2.6 %collective-permute-start = (bf16[16,48,128]{2,1,0:T(8,128)(2,1)S(1)}, bf16[16,48,128]{2,1,0:T(8,128)(2,1)S(1)}, u32[]{:S(2)}, u32[]{:S(2)}) collective-permute-start(bf16[16,48,128]{2,1,0:T(8,128)(2,1)S(1)} %get-tuple-element.36), channel_id=1, source_target_pairs={{0,1},{1,0},{2,3},{3,2},{4,5},{5,4},{6,7},{7,6},{8,9},{9,8},{10,11... | collective-permute-start | bytes 589832 | tf_op jit(solution)/shard_map/ppermute | solution.py:487
  5.0 0.7 collective-permute-start.1
  5.7 2.9 %collective-permute-done.pair = bf16[16,48,128]{2,1,0:T(8,128)(2,1)S(1)} collective-permute-done((bf16[16,48,128]{2,1,0:T(8,128)(2,1)S(1)}, bf16[16,48,128]{2,1,0:T(8,128)(2,1)S(1)}, u32[]{:S(2)}, u32[]{:S(2)}) %collective-permute-start) | collective-permute-done | bytes 196640 | tf_op jit(solution)/shard_map/ppermute | solution.py:487
  8.6 0.0 collective-permute-done.1.other
  8.6 1.6 %pack_rows.1 = (bf16[12,128,128]{2,1,0:T(8,128)(2,1)S(1)}, bf16[12,128,128]{2,1,0:T(8,128)(2,1)S(1)}) custom-call(s32[6]{0:T(128)S(1)} %stack.19.meta, bf16[16,64,128]{2,1,0:T(8,128)(2,1)} %bitcast.29, bf16[16,64,128]{2,1,0:T(8,128)(2,1)} %bitcast.21, bf16[16,48,128]{2,1,0:T(8,128)(2,1)S(1)} %collective-permute-done.pair, ...), custom_call_target="tpu_custom_call" | custom-call | tf_op jit(solution)/shard_map/pack_rows/pallas_call | solution.py:23
  10.2 3.0 %collective-permute-start.2 = (bf16[12,128,128]{2,1,0:T(8,128)(2,1)S(1)}, bf16[12,128,128]{2,1,0:T(8,128)(2,1)S(1)}, u32[]{:S(2)}, u32[]{:S(2)}) collective-permute-start(bf16[12,128,128]{2,1,0:T(8,128)(2,1)S(1)} %get-tuple-element.38), channel_id=1, source_target_pairs={{0,16},{16,0},{32,48},{48,32},{64,80},{80,64},{96,112},{112,96},{1... | collective-permute-start | bytes 1179656 | tf_op jit(solution)/shard_map/ppermute | solution.py:487
  13.1 2.4 %collective-permute-start.3 = (bf16[12,128,128]{2,1,0:T(8,128)(2,1)S(1)}, bf16[12,128,128]{2,1,0:T(8,128)(2,1)S(1)}, u32[]{:S(2)}, u32[]{:S(2)}) collective-permute-start(bf16[12,128,128]{2,1,0:T(8,128)(2,1)S(1)} %get-tuple-element.39), channel_id=1, source_target_pairs={{16,32},{32,16},{48,64},{64,48},{80,96},{96,80},{112,128},{128,112... | collective-permute-start | bytes 1179656 | tf_op jit(solution)/shard_map/ppermute | solution.py:493
  15.6 3.0 %collective-permute-start.4 = (bf16[160,128]{1,0:T(8,128)(2,1)S(1)}, bf16[160,128]{1,0:T(8,128)(2,1)S(1)}, u32[]{:S(2)}, u32[]{:S(2)}) collective-permute-start(bf16[160,128]{1,0:T(8,128)(2,1)S(1)} %get-tuple-element.43.refs_0_), channel_id=1, source_target_pairs={{0,128},{16,144},{32,160},{48,176},{64,192},{80,208},{96,224},{112... | collective-permute-start | bytes 122888 | tf_op jit(solution)/shard_map/ppermute | solution.py:487
  18.6 3.6 %collective-permute-done.3.outer = bf16[12,128,128]{2,1,0:T(8,128)(2,1)S(1)} collective-permute-done((bf16[12,128,128]{2,1,0:T(8,128)(2,1)S(1)}, bf16[12,128,128]{2,1,0:T(8,128)(2,1)S(1)}, u32[]{:S(2)}, u32[]{:S(2)}) %collective-permute-start.3) | collective-permute-done | bytes 393248 | tf_op jit(solution)/shard_map/ppermute | solution.py:493
  22.2 6.1 %first_conv.1 = (bf16[30,128,384]{2,1,0:T(8,128)(2,1)S(1)}, f32[18,96,128]{2,1,0:T(8,128)S(1)}, bf16[18,64,384]{2,1,0:T(8,128)(2,1)S(1)}) custom-call(s32[6]{0:T(128)S(1)} %stack.19.meta, bf16[16,64,128]{2,1,0:T(8,128)(2,1)} %bitcast.30, bf16[16,48,128]{2,1,0:T(8,128)(2,1)S(1)} %collective-permute-done.pair, ...), custom_call_target="tpu_custom_call" | custom-call | flops 4000000000 | tf_op jit(solution)/shard_map/first_conv/pallas_call | solution.py:23
  28.3 0.7 collective-permute-start.5
  29.0 6.2 %collective-permute-start.6 = (bf16[2,160,128]{2,1,0:T(8,128)(2,1)S(1)}, bf16[2,160,128]{2,1,0:T(8,128)(2,1)S(1)}, u32[]{:S(2)}, u32[]{:S(2)}) collective-permute-start(bf16[2,160,128]{2,1,0:T(8,128)(2,1)S(1)} %stack_two.1.refs_0_.near0), channel_id=1, source_target_pairs={{0,64},{16,80},{32,96},{48,112},{64,0},{80,16},{96,32},{112,48},{1... | collective-permute-start | bytes 245768 | tf_op jit(solution)/shard_map/ppermute | solution.py:487
  35.2 5.1 %second_conv.1 = (bf16[14,64,384]{2,1,0:T(8,128)(2,1)S(1)}, f32[20,96,128]{2,1,0:T(8,128)S(1)}, bf16[16,64,128]{2,1,0:T(8,128)(2,1)S(1)}, bf16[18,64,384]{2,1,0:T(8,128)(2,1)S(1)}) custom-call(s32[6]{0:T(128)S(1)} %stack.19.meta, bf16[30,128,384]{2,1,0:T(8,128)(2,1)S(1)} %get-tuple-element.40.act3, bf16[1152,128]{1,0:T(8,128)(2,1)S(1)} %bitcast.24), custom_call_target="tpu_custom_call" | custom-call | flops 4000000000 | tf_op jit(solution)/shard_map/second_conv/pallas_call | solution.py:23
  40.3 0.1 collective-permute-start.8
  40.4 1.6 %collective-permute-done.8.far = bf16[4,2,160,128]{3,2,1,0:T(8,128)(2,1)S(1)} collective-permute-done((bf16[4,2,160,128]{3,2,1,0:T(8,128)(2,1)S(1)}, bf16[4,2,160,128]{3,2,1,0:T(8,128)(2,1)S(1)}, u32[]{:S(2)}, u32[]{:S(2)}) %collective-permute-start.8) | collective-permute-done | bytes 327712 | tf_op jit(solution)/shard_map/ppermute | solution.py:487
  42.0 3.8 %coarse_step.1 = (bf16[16,64,128]{2,1,0:T(8,128)(2,1)}, bf16[8,160,128]{2,1,0:T(8,128)(2,1)S(1)}, bf16[8,160,128]{2,1,0:T(8,128)(2,1)S(1)}, f32[10,48,128]{2,1,0:T(8,128)S(1)}) custom-call(s32[6]{0:T(128)S(1)} %stack.19.meta, bf16[14,64,384]{2,1,0:T(8,128)(2,1)S(1)} %get-tuple-element.41.pool3, bf16[16,64,128]{2,1,0:T(8,128)(2,1)S(1)} %bitcast.22, ...), custom_call_target="tpu_custom_call" | custom-call | flops 2000000000 | tf_op jit(solution)/shard_map/coarse_step/pallas_call | solution.py:23
  45.8 0.2 collective-permute-start.9
  46.1 4.3 %fine_backward.1 = (bf16[8,144,128]{2,1,0:T(8,128)(2,1)S(1)}, bf16[8,144,128]{2,1,0:T(8,128)(2,1)S(1)}, bf16[18,64,384]{2,1,0:T(8,128)(2,1)S(1)}) custom-call(s32[6]{0:T(128)S(1)} %stack.19.meta, f32[10,48,128]{2,1,0:T(8,128)S(1)} %get-tuple-element.52.pooled_grad, bf16[16,64,128]{2,1,0:T(8,128)(2,1)S(1)} %bitcast.23, ...), custom_call_target="tpu_custom_call" | custom-call | flops 2000000000 | tf_op jit(solution)/shard_map/fine_backward/pallas_call | solution.py:23
  50.4 0.4 collective-permute-start.10
  50.8 1.7 %feature_step.1 = bf16[16,64,128]{2,1,0:T(8,128)(2,1)} custom-call(bf16[18,64,384]{2,1,0:T(8,128)(2,1)S(1)} %get-tuple-element.55.first3, bf16[9,128,128]{2,1,0:T(8,128)(2,1)S(1)} %bitcast.27), custom_call_target="tpu_custom_call" | custom-call | flops 1000000000 | tf_op jit(solution)/shard_map/feature_step/pallas_call | solution.py:23
  52.5 0.1 scatter_core.1
  52.6 17.2 %all_to_all.20.got = bf16[8,304,128]{2,1,0:T(8,128)(2,1)S(1)} all-to-all(bf16[8,304,128]{2,1,0:T(8,128)(2,1)S(1)} %scatter_core.1), channel_id=1, replica_groups={{0,32,64,96,128,160,192,224},{16,48,80,112,144,176,208,240},{1,33,65,97..., dimensions={0} | all-to-all | bytes 1245184 | tf_op jit(solution)/shard_map/all_to_all | solution.py:499
  69.8 0.1 scatter_row.1
  69.9 19.3 %all_to_all.21.got = bf16[16,32,128]{2,1,0:T(8,128)(2,1)S(1)} all-to-all(bf16[16,32,128]{2,1,0:T(8,128)(2,1)S(1)} %scatter_row.1), channel_id=1, replica_groups=mesh['row'=16,'col'=16] {'col'}, dimensions={0} | all-to-all | bytes 262144 | tf_op jit(solution)/shard_map/all_to_all | solution.py:503
  89.2 10.6 %all_to_all.22.got = bf16[16,32,128]{2,1,0:T(8,128)(2,1)S(1)} all-to-all(bf16[16,32,128]{2,1,0:T(8,128)(2,1)S(1)} %scatter_column.1), channel_id=1, replica_groups=mesh['row'=16,'col'=16] {'col'}, dimensions={0} | all-to-all | bytes 262144 | tf_op jit(solution)/shard_map/all_to_all | solution.py:503
  99.8 0.7 gather_column.1
  100.5 10.4 %all_to_all.23.mine = bf16[8,144,128]{2,1,0:T(8,128)(2,1)S(1)} all-to-all(bf16[8,144,128]{2,1,0:T(8,128)(2,1)S(1)} %get-tuple-element.61), channel_id=1, replica_groups={{0,32,64,96,128,160,192,224},{16,48,80,112,144,176,208,240},{1,33,65,97..., dimensions={0} | all-to-all | bytes 589824 | tf_op jit(solution)/shard_map/all_to_all | solution.py:499
  110.9 5.7 %collective-permute-start.11 = (bf16[8,144,128]{2,1,0:T(8,128)(2,1)S(1)}, bf16[8,144,128]{2,1,0:T(8,128)(2,1)S(1)}, u32[]{:S(2)}, u32[]{:S(2)}) collective-permute-start(bf16[8,144,128]{2,1,0:T(8,128)(2,1)S(1)} %all_to_all.23.mine), channel_id=1, source_target_pairs={{0,16},{16,0},{32,48},{48,32},{64,80},{80,64},{96,112},{112,96},{1... | collective-permute-start | bytes 884744 | tf_op jit(solution)/shard_map/ppermute | solution.py:487
  116.5 1.2 %collective-permute-done.11.other = bf16[8,144,128]{2,1,0:T(8,128)(2,1)S(1)} collective-permute-done((bf16[8,144,128]{2,1,0:T(8,128)(2,1)S(1)}, bf16[8,144,128]{2,1,0:T(8,128)(2,1)S(1)}, u32[]{:S(2)}, u32[]{:S(2)}) %collective-permute-start.11) | collective-permute-done | bytes 294944 | tf_op jit(solution)/shard_map/ppermute | solution.py:487
  117.7 1.6 %finish.1 = (f32[8,144,128]{2,1,0:T(8,128)}, f32[8,144,128]{2,1,0:T(8,128)}) custom-call(s32[6]{0:T(128)S(1)} %stack.19.meta, bf16[8,144,128]{2,1,0:T(8,128)(2,1)S(1)} %all_to_all.23.mine, bf16[8,144,128]{2,1,0:T(8,128)(2,1)S(1)} %collective-permute-done.11.other), custom_call_target="tpu_custom_call" | custom-call | tf_op jit(solution)/shard_map/finish/pallas_call | solution.py:23
  (18 shorter events, 0.1 us)
Async XLA Ops:
  2.4 6.1 %collective-permute-start = (bf16[16,48,128]{2,1,0:T(8,128)(2,1)S(1)}, bf16[16,48,128]{2,1,0:T(8,128)(2,1)S(1)}, u32[]{:S(2)}, u32[]{:S(2)}) collective-permute-start(bf16[16,48,128]{2,1,0:T(8,128)(2,1)S(1)} %get-tuple-element.36), channel_id=1, source_target_pairs={{0,1},{1,0},{2,3},{3,2},{4,5},{5,4},{6,7},{7,6},{8,9},{9,8},{10,11... | collective-permute-start | bytes 589832 | tf_op jit(solution)/shard_map/ppermute | solution.py:487
  5.0 3.6 %collective-permute-start.1 = (bf16[16,48,128]{2,1,0:T(8,128)(2,1)S(1)}, bf16[16,48,128]{2,1,0:T(8,128)(2,1)S(1)}, u32[]{:S(2)}, u32[]{:S(2)}) collective-permute-start(bf16[16,48,128]{2,1,0:T(8,128)(2,1)S(1)} %get-tuple-element.37), channel_id=1, source_target_pairs={{1,2},{2,1},{3,4},{4,3},{5,6},{6,5},{7,8},{8,7},{9,10},{10,9},{11,... | collective-permute-start | bytes 589832 | tf_op jit(solution)/shard_map/ppermute | solution.py:493
  10.2 8.4 %collective-permute-start.2 = (bf16[12,128,128]{2,1,0:T(8,128)(2,1)S(1)}, bf16[12,128,128]{2,1,0:T(8,128)(2,1)S(1)}, u32[]{:S(2)}, u32[]{:S(2)}) collective-permute-start(bf16[12,128,128]{2,1,0:T(8,128)(2,1)S(1)} %get-tuple-element.38), channel_id=1, source_target_pairs={{0,16},{16,0},{32,48},{48,32},{64,80},{80,64},{96,112},{112,96},{1... | collective-permute-start | bytes 1179656 | tf_op jit(solution)/shard_map/ppermute | solution.py:487
  13.1 9.1 %collective-permute-start.3 = (bf16[12,128,128]{2,1,0:T(8,128)(2,1)S(1)}, bf16[12,128,128]{2,1,0:T(8,128)(2,1)S(1)}, u32[]{:S(2)}, u32[]{:S(2)}) collective-permute-start(bf16[12,128,128]{2,1,0:T(8,128)(2,1)S(1)} %get-tuple-element.39), channel_id=1, source_target_pairs={{16,32},{32,16},{48,64},{64,48},{80,96},{96,80},{112,128},{128,112... | collective-permute-start | bytes 1179656 | tf_op jit(solution)/shard_map/ppermute | solution.py:493
  15.6 12.7 %collective-permute-start.4 = (bf16[160,128]{1,0:T(8,128)(2,1)S(1)}, bf16[160,128]{1,0:T(8,128)(2,1)S(1)}, u32[]{:S(2)}, u32[]{:S(2)}) collective-permute-start(bf16[160,128]{1,0:T(8,128)(2,1)S(1)} %get-tuple-element.43.refs_0_), channel_id=1, source_target_pairs={{0,128},{16,144},{32,160},{48,176},{64,192},{80,208},{96,224},{112... | collective-permute-start | bytes 122888 | tf_op jit(solution)/shard_map/ppermute | solution.py:487
  22.2 13.0 %copy-start.1 = (bf16[3,3,128,128]{3,2,1,0:T(8,128)(2,1)S(1)}, bf16[3,3,128,128]{3,2,1,0:T(8,128)(2,1)}, u32[]{:S(2)}) copy-start(bf16[3,3,128,128]{3,2,1,0:T(8,128)(2,1)} %param.8) | copy-start | bytes 884740
  28.3 11.9 %collective-permute-start.5 = (bf16[2,160,128]{2,1,0:T(8,128)(2,1)S(1)}, bf16[2,160,128]{2,1,0:T(8,128)(2,1)S(1)}, u32[]{:S(2)}, u32[]{:S(2)}) collective-permute-start(bf16[2,160,128]{2,1,0:T(8,128)(2,1)S(1)} %stack_two.1.refs_0_.near0), channel_id=1, source_target_pairs={{0,32},{16,48},{32,0},{48,16},{64,96},{80,112},{96,64},{112,80},{1... | collective-permute-start | bytes 245768 | tf_op jit(solution)/shard_map/ppermute | solution.py:487
  29.0 11.3 %collective-permute-start.6 = (bf16[2,160,128]{2,1,0:T(8,128)(2,1)S(1)}, bf16[2,160,128]{2,1,0:T(8,128)(2,1)S(1)}, u32[]{:S(2)}, u32[]{:S(2)}) collective-permute-start(bf16[2,160,128]{2,1,0:T(8,128)(2,1)S(1)} %stack_two.1.refs_0_.near0), channel_id=1, source_target_pairs={{0,64},{16,80},{32,96},{48,112},{64,0},{80,16},{96,32},{112,48},{1... | collective-permute-start | bytes 245768 | tf_op jit(solution)/shard_map/ppermute | solution.py:487
  35.2 5.1 %collective-permute-start.7 = (bf16[2,160,128]{2,1,0:T(8,128)(2,1)S(1)}, bf16[2,160,128]{2,1,0:T(8,128)(2,1)S(1)}, u32[]{:S(2)}, u32[]{:S(2)}) collective-permute-start(bf16[2,160,128]{2,1,0:T(8,128)(2,1)S(1)} %stack_two.1.refs_0_.near0), channel_id=1, source_target_pairs={{0,96},{16,112},{32,64},{48,80},{64,32},{80,48},{96,0},{112,16},{1... | collective-permute-start | bytes 245768 | tf_op jit(solution)/shard_map/ppermute | solution.py:487
  35.2 6.8 %copy-start = (bf16[16,16,4,128]{3,2,1,0:T(4,128)(2,1)S(1)}, bf16[16,16,4,128]{3,2,1,0:T(4,128)(2,1)}, u32[]{:S(2)}) copy-start(bf16[16,16,4,128]{3,2,1,0:T(4,128)(2,1)} %param.11) | copy-start | bytes 786436
  40.3 1.7 %collective-permute-start.8 = (bf16[4,2,160,128]{3,2,1,0:T(8,128)(2,1)S(1)}, bf16[4,2,160,128]{3,2,1,0:T(8,128)(2,1)S(1)}, u32[]{:S(2)}, u32[]{:S(2)}) collective-permute-start(bf16[4,2,160,128]{3,2,1,0:T(8,128)(2,1)S(1)} %stack_eight.1), channel_id=1, source_target_pairs={{0,16},{16,0},{32,48},{48,32},{64,80},{80,64},{96,112},{112,96},{1... | collective-permute-start | bytes 983048 | tf_op jit(solution)/shard_map/ppermute | solution.py:487
  45.8 6.7 %collective-permute-start.9 = (bf16[8,160,128]{2,1,0:T(8,128)(2,1)S(1)}, bf16[8,160,128]{2,1,0:T(8,128)(2,1)S(1)}, u32[]{:S(2)}, u32[]{:S(2)}) collective-permute-start(bf16[8,160,128]{2,1,0:T(8,128)(2,1)S(1)} %get-tuple-element.58), channel_id=1, source_target_pairs={{0,16},{16,0},{32,48},{48,32},{64,80},{80,64},{96,112},{112,96},{1... | collective-permute-start | bytes 983048 | tf_op jit(solution)/shard_map/ppermute | solution.py:487
  46.1 4.7 %copy-start.2 = (bf16[3,3,128,128]{3,2,1,0:T(8,128)(2,1)S(1)}, bf16[3,3,128,128]{3,2,1,0:T(8,128)(2,1)}, u32[]{:S(2)}) copy-start(bf16[3,3,128,128]{3,2,1,0:T(8,128)(2,1)} %param.7) | copy-start | bytes 884740
  50.4 2.1 %collective-permute-start.10 = (bf16[8,144,128]{2,1,0:T(8,128)(2,1)S(1)}, bf16[8,144,128]{2,1,0:T(8,128)(2,1)S(1)}, u32[]{:S(2)}, u32[]{:S(2)}) collective-permute-start(bf16[8,144,128]{2,1,0:T(8,128)(2,1)S(1)} %get-tuple-element.59), channel_id=1, source_target_pairs={{0,16},{16,0},{32,48},{48,32},{64,80},{80,64},{96,112},{112,96},{1... | collective-permute-start | bytes 884744 | tf_op jit(solution)/shard_map/ppermute | solution.py:487
  110.9 6.9 %collective-permute-start.11 = (bf16[8,144,128]{2,1,0:T(8,128)(2,1)S(1)}, bf16[8,144,128]{2,1,0:T(8,128)(2,1)S(1)}, u32[]{:S(2)}, u32[]{:S(2)}) collective-permute-start(bf16[8,144,128]{2,1,0:T(8,128)(2,1)S(1)} %all_to_all.23.mine), channel_id=1, source_target_pairs={{0,16},{16,0},{32,48},{48,32},{64,80},{80,64},{96,112},{112,96},{1... | collective-permute-start | bytes 884744 | tf_op jit(solution)/shard_map/ppermute | solution.py:487

commit v5 on v4

--- a/solution.py
+++ b/solution.py
@@ -541,16 +541,17 @@
         (pltpu.SemaphoreType.DMA((4,)),),
         far=(1, 2),
     )
+    near0 = call(stack_kernel, "stack_two", (((2, 160, CH), BF),), (own, own_far))[0]
+    inner, outer, near0 = lax.optimization_barrier((inner, outer, near0))
     inner = swap(inner, "row", 1)
     outer = swap_outer(outer, "row")
+    near = [near0] + [swap(near0, "row", 2 * k) for k in range(1, 4)]
     halo = (pair, other, inner, outer)
     w1, w2 = (conv_first.reshape(1152, CH), conv_second.reshape(1152, CH))
     act3w, slope1, feat3 = first_step(meta, feat, halo, w1)
-    near0 = call(stack_kernel, "stack_two", (((2, 160, CH), BF),), (own, after_all(own_far, slope1)))[0]
-    near = [near0] + [swap(near0, "row", 2 * k) for k in range(1, 4)]
+    near = list(lax.optimization_barrier((slope1, *near)))[1:]
+    far = swap(call(stack_kernel, "stack_eight", (((4, 2, 160, CH), BF),), near)[0], "row", 1)
     pool3, slope2, act, act3 = second_step(meta, act3w, w2)
-    near = list(lax.optimization_barrier((slope2, *near)))[1:]
-    far = swap(call(stack_kernel, "stack_eight", (((4, 2, 160, CH), BF),), near)[0], "row", 1)
     blended, keep_c, send_c, pooled_grad = coarse_step(meta, pool3, cot, halo, near, far, act)
     got_c = swap(send_c, "row", 1)
     keep_f, send_f, first3 = fine_backward(

time: 120 us -> 117 us (0.975)
  waiting for transfers between devices: 9.39 us -> 5.41 us
  blocking collectives: 57.4 us -> 59.9 us
  starting transfers between devices: 24.9 us -> 23.2 us
    all_to_all x2, blocking collectives: 27.6 us -> 31.2 us  [exchange_row(): lax.all_to_all(value, 'row', 0, 0, axis_index_groups=groups, tiled=True)]
    ppermute x10, waiting for transfers between devices: 5.74 us -> 2.67 us  [swap(): return lax.ppermute(value, axis, [(i, i ^ mask) for i in range(count)])]
    ppermute x10, starting transfers between devices: 21.8 us -> 19.5 us  [swap(): return lax.ppermute(value, axis, [(i, i ^ mask) for i in range(count)])]
  transfers between devices with their start and end apart: 12 -> 12, of which waited for: 4 -> 3; matrix products, arithmetic and copies ran while one was open for 0% -> 0% of each run, Pallas kernels for 14% -> 15%
where the time goes in v5:
time: 117 us; the launch traced here: 116 us
  blocking collectives  59.9 us (51%)
  Pallas kernels  26.8 us (23%)
  starting transfers between devices  23.2 us (20%)
  waiting for transfers between devices  5.41 us (5%)
    all_to_all x2, blocking collectives, exchange_row(): lax.all_to_all(value, 'row', 0, 0, axis_index_groups=groups, tiled=True)  31.2 us
    all_to_all x2, blocking collectives, exchange_column(): return lax.all_to_all(value, 'col', 0, 0, tiled=True)  28.7 us
    pallas_call x14, Pallas kernels, call(): pl.pallas_call(kernel, name=name, out_shape=shapes, in_specs=[HBM if k in...  26.8 us
    ppermute x10, starting transfers between devices, swap(): return lax.ppermute(value, axis, [(i, i ^ mask) for i in range(count)])  19.5 us
    ppermute x2, starting transfers between devices, swap_outer(): return lax.ppermute(value, axis, pairs)  3.68 us
    ppermute x2, waiting for transfers between devices, swap_outer(): return lax.ppermute(value, axis, pairs)  2.74 us
    ppermute x10, waiting for transfers between devices, swap(): return lax.ppermute(value, axis, [(i, i ^ mask) for i in range(count)])  2.67 us
  transfers between devices with their start and end apart: 12, of which 3 were waited for; matrix products, arithmetic and copies ran while one was open for 0% of the time, Pallas kernels for 15%

profile of v5, /device:TPU:1, one launch (start us, length us, event | category | flops | bytes accessed | tf_op | source)
XLA Modules:
  0.0 116.2 jit_solution(6681391587582197427)
XLA Ops:
  0.6 0.1 stack.19.meta
  0.7 1.7 %pack_columns.1 = (bf16[16,48,128]{2,1,0:T(8,128)(2,1)S(1)}, bf16[16,48,128]{2,1,0:T(8,128)(2,1)S(1)}, bf16[160,128]{1,0:T(8,128)(2,1)S(1)}) custom-call(s32[6]{0:T(128)S(1)} %stack.19.meta, bf16[16,64,128]{2,1,0:T(8,128)(2,1)} %bitcast.28, bf16[16,64,128]{2,1,0:T(8,128)(2,1)} %bitcast.20, bf16[9,16,128]{2,1,0:T(8,128)(2,1)} %bitcast.31, bf16[16,128]{1,0:T(8,128)(2,1)} %proj.1), custom_call_target="tpu_custom_call" | custom-call | tf_op jit(solution)/shard_map/pack_columns/pallas_call | solution.py:23
  2.4 2.6 %collective-permute-start = (bf16[16,48,128]{2,1,0:T(8,128)(2,1)S(1)}, bf16[16,48,128]{2,1,0:T(8,128)(2,1)S(1)}, u32[]{:S(2)}, u32[]{:S(2)}) collective-permute-start(bf16[16,48,128]{2,1,0:T(8,128)(2,1)S(1)} %get-tuple-element.38), channel_id=1, source_target_pairs={{0,1},{1,0},{2,3},{3,2},{4,5},{5,4},{6,7},{7,6},{8,9},{9,8},{10,11... | collective-permute-start | bytes 589832 | tf_op jit(solution)/shard_map/ppermute | solution.py:487
  5.0 0.7 collective-permute-start.1
  5.7 3.0 %collective-permute-start.2 = (bf16[160,128]{1,0:T(8,128)(2,1)S(1)}, bf16[160,128]{1,0:T(8,128)(2,1)S(1)}, u32[]{:S(2)}, u32[]{:S(2)}) collective-permute-start(bf16[160,128]{1,0:T(8,128)(2,1)S(1)} %get-tuple-element.42.refs_0_), channel_id=1, source_target_pairs={{0,128},{16,144},{32,160},{48,176},{64,192},{80,208},{96,224},{112... | collective-permute-start | bytes 122888 | tf_op jit(solution)/shard_map/ppermute | solution.py:487
  8.7 1.4 %collective-permute-done.2.refs_1_ = bf16[160,128]{1,0:T(8,128)(2,1)S(1)} collective-permute-done((bf16[160,128]{1,0:T(8,128)(2,1)S(1)}, bf16[160,128]{1,0:T(8,128)(2,1)S(1)}, u32[]{:S(2)}, u32[]{:S(2)}) %collective-permute-start.2) | collective-permute-done | bytes 40992 | tf_op jit(solution)/shard_map/ppermute | solution.py:487
  10.1 0.0 collective-permute-done.1.other
  10.1 1.6 %pack_rows.1 = (bf16[12,128,128]{2,1,0:T(8,128)(2,1)S(1)}, bf16[12,128,128]{2,1,0:T(8,128)(2,1)S(1)}) custom-call(s32[6]{0:T(128)S(1)} %stack.19.meta, bf16[16,64,128]{2,1,0:T(8,128)(2,1)} %bitcast.29, bf16[16,64,128]{2,1,0:T(8,128)(2,1)} %bitcast.21, bf16[16,48,128]{2,1,0:T(8,128)(2,1)S(1)} %collective-permute-done.pair, ...), custom_call_target="tpu_custom_call" | custom-call | tf_op jit(solution)/shard_map/pack_rows/pallas_call | solution.py:23
  11.7 2.2 %collective-permute-start.3 = (bf16[12,128,128]{2,1,0:T(8,128)(2,1)S(1)}, bf16[12,128,128]{2,1,0:T(8,128)(2,1)S(1)}, u32[]{:S(2)}, u32[]{:S(2)}) collective-permute-start(bf16[12,128,128]{2,1,0:T(8,128)(2,1)S(1)} %get-tuple-element.43), channel_id=1, source_target_pairs={{0,16},{16,0},{32,48},{48,32},{64,80},{80,64},{96,112},{112,96},{1... | collective-permute-start | bytes 1179656 | tf_op jit(solution)/shard_map/ppermute | solution.py:487
  13.9 3.0 %collective-permute-start.4 = (bf16[12,128,128]{2,1,0:T(8,128)(2,1)S(1)}, bf16[12,128,128]{2,1,0:T(8,128)(2,1)S(1)}, u32[]{:S(2)}, u32[]{:S(2)}) collective-permute-start(bf16[12,128,128]{2,1,0:T(8,128)(2,1)S(1)} %get-tuple-element.44), channel_id=1, source_target_pairs={{16,32},{32,16},{48,64},{64,48},{80,96},{96,80},{112,128},{128,112... | collective-permute-start | bytes 1179656 | tf_op jit(solution)/shard_map/ppermute | solution.py:493
  16.9 1.3 %collective-permute-start.5 = (bf16[2,160,128]{2,1,0:T(8,128)(2,1)S(1)}, bf16[2,160,128]{2,1,0:T(8,128)(2,1)S(1)}, u32[]{:S(2)}, u32[]{:S(2)}) collective-permute-start(bf16[2,160,128]{2,1,0:T(8,128)(2,1)S(1)} %stack_two.1.refs_0_.near0), channel_id=1, source_target_pairs={{0,32},{16,48},{32,0},{48,16},{64,96},{80,112},{96,64},{112,80},{1... | collective-permute-start | bytes 245768 | tf_op jit(solution)/shard_map/ppermute | solution.py:487
  18.2 4.1 %collective-permute-start.6 = (bf16[2,160,128]{2,1,0:T(8,128)(2,1)S(1)}, bf16[2,160,128]{2,1,0:T(8,128)(2,1)S(1)}, u32[]{:S(2)}, u32[]{:S(2)}) collective-permute-start(bf16[2,160,128]{2,1,0:T(8,128)(2,1)S(1)} %stack_two.1.refs_0_.near0), channel_id=1, source_target_pairs={{0,64},{16,80},{32,96},{48,112},{64,0},{80,16},{96,32},{112,48},{1... | collective-permute-start | bytes 245768 | tf_op jit(solution)/shard_map/ppermute | solution.py:487
  22.3 2.7 %collective-permute-done.4.outer = bf16[12,128,128]{2,1,0:T(8,128)(2,1)S(1)} collective-permute-done((bf16[12,128,128]{2,1,0:T(8,128)(2,1)S(1)}, bf16[12,128,128]{2,1,0:T(8,128)(2,1)S(1)}, u32[]{:S(2)}, u32[]{:S(2)}) %collective-permute-start.4) | collective-permute-done | bytes 393248 | tf_op jit(solution)/shard_map/ppermute | solution.py:493
  25.0 6.1 %first_conv.1 = (bf16[30,128,384]{2,1,0:T(8,128)(2,1)S(1)}, f32[18,96,128]{2,1,0:T(8,128)S(1)}, bf16[18,64,384]{2,1,0:T(8,128)(2,1)S(1)}) custom-call(s32[6]{0:T(128)S(1)} %stack.19.meta, bf16[16,64,128]{2,1,0:T(8,128)(2,1)} %bitcast.30, bf16[16,48,128]{2,1,0:T(8,128)(2,1)S(1)} %collective-permute-done.pair, ...), custom_call_target="tpu_custom_call" | custom-call | flops 4000000000 | tf_op jit(solution)/shard_map/first_conv/pallas_call | solution.py:23
  31.2 0.1 collective-permute-start.8
  31.3 0.0 copy-start
  31.3 5.1 %second_conv.1 = (bf16[14,64,384]{2,1,0:T(8,128)(2,1)S(1)}, f32[20,96,128]{2,1,0:T(8,128)S(1)}, bf16[16,64,128]{2,1,0:T(8,128)(2,1)S(1)}, bf16[18,64,384]{2,1,0:T(8,128)(2,1)S(1)}) custom-call(s32[6]{0:T(128)S(1)} %stack.19.meta, bf16[30,128,384]{2,1,0:T(8,128)(2,1)S(1)} %get-tuple-element.45.act3, bf16[1152,128]{1,0:T(8,128)(2,1)S(1)} %bitcast.24), custom_call_target="tpu_custom_call" | custom-call | flops 4000000000 | tf_op jit(solution)/shard_map/second_conv/pallas_call | solution.py:23
  36.4 3.8 %coarse_step.1 = (bf16[16,64,128]{2,1,0:T(8,128)(2,1)}, bf16[8,160,128]{2,1,0:T(8,128)(2,1)S(1)}, bf16[8,160,128]{2,1,0:T(8,128)(2,1)S(1)}, f32[10,48,128]{2,1,0:T(8,128)S(1)}) custom-call(s32[6]{0:T(128)S(1)} %stack.19.meta, bf16[14,64,384]{2,1,0:T(8,128)(2,1)S(1)} %get-tuple-element.46.pool3, bf16[16,64,128]{2,1,0:T(8,128)(2,1)S(1)} %bitcast.22, ...), custom_call_target="tpu_custom_call" | custom-call | flops 2000000000 | tf_op jit(solution)/shard_map/coarse_step/pallas_call | solution.py:23
  40.2 0.6 collective-permute-start.9
  40.8 4.3 %fine_backward.1 = (bf16[8,144,128]{2,1,0:T(8,128)(2,1)S(1)}, bf16[8,144,128]{2,1,0:T(8,128)(2,1)S(1)}, bf16[18,64,384]{2,1,0:T(8,128)(2,1)S(1)}) custom-call(s32[6]{0:T(128)S(1)} %stack.19.meta, f32[10,48,128]{2,1,0:T(8,128)S(1)} %get-tuple-element.55.pooled_grad, bf16[16,64,128]{2,1,0:T(8,128)(2,1)S(1)} %bitcast.23, ...), custom_call_target="tpu_custom_call" | custom-call | flops 2000000000 | tf_op jit(solution)/shard_map/fine_backward/pallas_call | solution.py:23
  45.1 0.1 collective-permute-start.10
  45.2 1.7 %feature_step.1 = bf16[16,64,128]{2,1,0:T(8,128)(2,1)} custom-call(bf16[18,64,384]{2,1,0:T(8,128)(2,1)S(1)} %get-tuple-element.59.first3, bf16[9,128,128]{2,1,0:T(8,128)(2,1)S(1)} %bitcast.27), custom_call_target="tpu_custom_call" | custom-call | flops 1000000000 | tf_op jit(solution)/shard_map/feature_step/pallas_call | solution.py:23
  46.9 0.1 scatter_core.1
  47.0 20.7 %all_to_all.20.got = bf16[8,304,128]{2,1,0:T(8,128)(2,1)S(1)} all-to-all(bf16[8,304,128]{2,1,0:T(8,128)(2,1)S(1)} %scatter_core.1), channel_id=1, replica_groups={{0,32,64,96,128,160,192,224},{16,48,80,112,144,176,208,240},{1,33,65,97..., dimensions={0} | all-to-all | bytes 1245184 | tf_op jit(solution)/shard_map/all_to_all | solution.py:499
  67.8 0.1 scatter_row.1
  67.9 18.2 %all_to_all.21.got = bf16[16,32,128]{2,1,0:T(8,128)(2,1)S(1)} all-to-all(bf16[16,32,128]{2,1,0:T(8,128)(2,1)S(1)} %scatter_row.1), channel_id=1, replica_groups=mesh['row'=16,'col'=16] {'col'}, dimensions={0} | all-to-all | bytes 262144 | tf_op jit(solution)/shard_map/all_to_all | solution.py:503
  86.1 10.5 %all_to_all.22.got = bf16[16,32,128]{2,1,0:T(8,128)(2,1)S(1)} all-to-all(bf16[16,32,128]{2,1,0:T(8,128)(2,1)S(1)} %scatter_column.1), channel_id=1, replica_groups=mesh['row'=16,'col'=16] {'col'}, dimensions={0} | all-to-all | bytes 262144 | tf_op jit(solution)/shard_map/all_to_all | solution.py:503
  96.6 0.7 gather_column.1
  97.3 10.5 %all_to_all.23.mine = bf16[8,144,128]{2,1,0:T(8,128)(2,1)S(1)} all-to-all(bf16[8,144,128]{2,1,0:T(8,128)(2,1)S(1)} %get-tuple-element.65), channel_id=1, replica_groups={{0,32,64,96,128,160,192,224},{16,48,80,112,144,176,208,240},{1,33,65,97..., dimensions={0} | all-to-all | bytes 589824 | tf_op jit(solution)/shard_map/all_to_all | solution.py:499
  107.8 5.6 %collective-permute-start.11 = (bf16[8,144,128]{2,1,0:T(8,128)(2,1)S(1)}, bf16[8,144,128]{2,1,0:T(8,128)(2,1)S(1)}, u32[]{:S(2)}, u32[]{:S(2)}) collective-permute-start(bf16[8,144,128]{2,1,0:T(8,128)(2,1)S(1)} %all_to_all.23.mine), channel_id=1, source_target_pairs={{0,16},{16,0},{32,48},{48,32},{64,80},{80,64},{96,112},{112,96},{1... | collective-permute-start | bytes 884744 | tf_op jit(solution)/shard_map/ppermute | solution.py:487
  113.4 1.2 %collective-permute-done.11.other = bf16[8,144,128]{2,1,0:T(8,128)(2,1)S(1)} collective-permute-done((bf16[8,144,128]{2,1,0:T(8,128)(2,1)S(1)}, bf16[8,144,128]{2,1,0:T(8,128)(2,1)S(1)}, u32[]{:S(2)}, u32[]{:S(2)}) %collective-permute-start.11) | collective-permute-done | bytes 294944 | tf_op jit(solution)/shard_map/ppermute | solution.py:487
  114.6 1.6 %finish.1 = (f32[8,144,128]{2,1,0:T(8,128)}, f32[8,144,128]{2,1,0:T(8,128)}) custom-call(s32[6]{0:T(128)S(1)} %stack.19.meta, bf16[8,144,128]{2,1,0:T(8,128)(2,1)S(1)} %all_to_all.23.mine, bf16[8,144,128]{2,1,0:T(8,128)(2,1)S(1)} %collective-permute-done.11.other), custom_call_target="tpu_custom_call" | custom-call | tf_op jit(solution)/shard_map/finish/pallas_call | solution.py:23
  (18 shorter events, 0.1 us)
Async XLA Ops:
  2.4 7.7 %collective-permute-start = (bf16[16,48,128]{2,1,0:T(8,128)(2,1)S(1)}, bf16[16,48,128]{2,1,0:T(8,128)(2,1)S(1)}, u32[]{:S(2)}, u32[]{:S(2)}) collective-permute-start(bf16[16,48,128]{2,1,0:T(8,128)(2,1)S(1)} %get-tuple-element.38), channel_id=1, source_target_pairs={{0,1},{1,0},{2,3},{3,2},{4,5},{5,4},{6,7},{7,6},{8,9},{9,8},{10,11... | collective-permute-start | bytes 589832 | tf_op jit(solution)/shard_map/ppermute | solution.py:487
  5.0 5.1 %collective-permute-start.1 = (bf16[16,48,128]{2,1,0:T(8,128)(2,1)S(1)}, bf16[16,48,128]{2,1,0:T(8,128)(2,1)S(1)}, u32[]{:S(2)}, u32[]{:S(2)}) collective-permute-start(bf16[16,48,128]{2,1,0:T(8,128)(2,1)S(1)} %get-tuple-element.39), channel_id=1, source_target_pairs={{1,2},{2,1},{3,4},{4,3},{5,6},{6,5},{7,8},{8,7},{9,10},{10,9},{11,... | collective-permute-start | bytes 589832 | tf_op jit(solution)/shard_map/ppermute | solution.py:493
  5.7 4.4 %collective-permute-start.2 = (bf16[160,128]{1,0:T(8,128)(2,1)S(1)}, bf16[160,128]{1,0:T(8,128)(2,1)S(1)}, u32[]{:S(2)}, u32[]{:S(2)}) collective-permute-start(bf16[160,128]{1,0:T(8,128)(2,1)S(1)} %get-tuple-element.42.refs_0_), channel_id=1, source_target_pairs={{0,128},{16,144},{32,160},{48,176},{64,192},{80,208},{96,224},{112... | collective-permute-start | bytes 122888 | tf_op jit(solution)/shard_map/ppermute | solution.py:487
  11.7 10.6 %collective-permute-start.3 = (bf16[12,128,128]{2,1,0:T(8,128)(2,1)S(1)}, bf16[12,128,128]{2,1,0:T(8,128)(2,1)S(1)}, u32[]{:S(2)}, u32[]{:S(2)}) collective-permute-start(bf16[12,128,128]{2,1,0:T(8,128)(2,1)S(1)} %get-tuple-element.43), channel_id=1, source_target_pairs={{0,16},{16,0},{32,48},{48,32},{64,80},{80,64},{96,112},{112,96},{1... | collective-permute-start | bytes 1179656 | tf_op jit(solution)/shard_map/ppermute | solution.py:487
  13.9 11.1 %collective-permute-start.4 = (bf16[12,128,128]{2,1,0:T(8,128)(2,1)S(1)}, bf16[12,128,128]{2,1,0:T(8,128)(2,1)S(1)}, u32[]{:S(2)}, u32[]{:S(2)}) collective-permute-start(bf16[12,128,128]{2,1,0:T(8,128)(2,1)S(1)} %get-tuple-element.44), channel_id=1, source_target_pairs={{16,32},{32,16},{48,64},{64,48},{80,96},{96,80},{112,128},{128,112... | collective-permute-start | bytes 1179656 | tf_op jit(solution)/shard_map/ppermute | solution.py:493
  16.9 14.2 %collective-permute-start.5 = (bf16[2,160,128]{2,1,0:T(8,128)(2,1)S(1)}, bf16[2,160,128]{2,1,0:T(8,128)(2,1)S(1)}, u32[]{:S(2)}, u32[]{:S(2)}) collective-permute-start(bf16[2,160,128]{2,1,0:T(8,128)(2,1)S(1)} %stack_two.1.refs_0_.near0), channel_id=1, source_target_pairs={{0,32},{16,48},{32,0},{48,16},{64,96},{80,112},{96,64},{112,80},{1... | collective-permute-start | bytes 245768 | tf_op jit(solution)/shard_map/ppermute | solution.py:487
  18.2 12.9 %collective-permute-start.6 = (bf16[2,160,128]{2,1,0:T(8,128)(2,1)S(1)}, bf16[2,160,128]{2,1,0:T(8,128)(2,1)S(1)}, u32[]{:S(2)}, u32[]{:S(2)}) collective-permute-start(bf16[2,160,128]{2,1,0:T(8,128)(2,1)S(1)} %stack_two.1.refs_0_.near0), channel_id=1, source_target_pairs={{0,64},{16,80},{32,96},{48,112},{64,0},{80,16},{96,32},{112,48},{1... | collective-permute-start | bytes 245768 | tf_op jit(solution)/shard_map/ppermute | solution.py:487
  22.3 8.8 %collective-permute-start.7 = (bf16[2,160,128]{2,1,0:T(8,128)(2,1)S(1)}, bf16[2,160,128]{2,1,0:T(8,128)(2,1)S(1)}, u32[]{:S(2)}, u32[]{:S(2)}) collective-permute-start(bf16[2,160,128]{2,1,0:T(8,128)(2,1)S(1)} %stack_two.1.refs_0_.near0), channel_id=1, source_target_pairs={{0,96},{16,112},{32,64},{48,80},{64,32},{80,48},{96,0},{112,16},{1... | collective-permute-start | bytes 245768 | tf_op jit(solution)/shard_map/ppermute | solution.py:487
  25.0 6.2 %copy-start.1 = (bf16[3,3,128,128]{3,2,1,0:T(8,128)(2,1)S(1)}, bf16[3,3,128,128]{3,2,1,0:T(8,128)(2,1)}, u32[]{:S(2)}) copy-start(bf16[3,3,128,128]{3,2,1,0:T(8,128)(2,1)} %param.8) | copy-start | bytes 884740
  31.2 5.2 %collective-permute-start.8 = (bf16[4,2,160,128]{3,2,1,0:T(8,128)(2,1)S(1)}, bf16[4,2,160,128]{3,2,1,0:T(8,128)(2,1)S(1)}, u32[]{:S(2)}, u32[]{:S(2)}) collective-permute-start(bf16[4,2,160,128]{3,2,1,0:T(8,128)(2,1)S(1)} %stack_eight.1), channel_id=1, source_target_pairs={{0,16},{16,0},{32,48},{48,32},{64,80},{80,64},{96,112},{112,96},{1... | collective-permute-start | bytes 983048 | tf_op jit(solution)/shard_map/ppermute | solution.py:487
  31.3 5.1 %copy-start = (bf16[16,16,4,128]{3,2,1,0:T(4,128)(2,1)S(1)}, bf16[16,16,4,128]{3,2,1,0:T(4,128)(2,1)}, u32[]{:S(2)}) copy-start(bf16[16,16,4,128]{3,2,1,0:T(4,128)(2,1)} %param.11) | copy-start | bytes 786436
  40.2 6.7 %collective-permute-start.9 = (bf16[8,160,128]{2,1,0:T(8,128)(2,1)S(1)}, bf16[8,160,128]{2,1,0:T(8,128)(2,1)S(1)}, u32[]{:S(2)}, u32[]{:S(2)}) collective-permute-start(bf16[8,160,128]{2,1,0:T(8,128)(2,1)S(1)} %get-tuple-element.62), channel_id=1, source_target_pairs={{0,16},{16,0},{32,48},{48,32},{64,80},{80,64},{96,112},{112,96},{1... | collective-permute-start | bytes 983048 | tf_op jit(solution)/shard_map/ppermute | solution.py:487
  40.8 4.4 %copy-start.2 = (bf16[3,3,128,128]{3,2,1,0:T(8,128)(2,1)S(1)}, bf16[3,3,128,128]{3,2,1,0:T(8,128)(2,1)}, u32[]{:S(2)}) copy-start(bf16[3,3,128,128]{3,2,1,0:T(8,128)(2,1)} %param.7) | copy-start | bytes 884740
  45.1 1.8 %collective-permute-start.10 = (bf16[8,144,128]{2,1,0:T(8,128)(2,1)S(1)}, bf16[8,144,128]{2,1,0:T(8,128)(2,1)S(1)}, u32[]{:S(2)}, u32[]{:S(2)}) collective-permute-start(bf16[8,144,128]{2,1,0:T(8,128)(2,1)S(1)} %get-tuple-element.63), channel_id=1, source_target_pairs={{0,16},{16,0},{32,48},{48,32},{64,80},{80,64},{96,112},{112,96},{1... | collective-permute-start | bytes 884744 | tf_op jit(solution)/shard_map/ppermute | solution.py:487
  107.8 6.8 %collective-permute-start.11 = (bf16[8,144,128]{2,1,0:T(8,128)(2,1)S(1)}, bf16[8,144,128]{2,1,0:T(8,128)(2,1)S(1)}, u32[]{:S(2)}, u32[]{:S(2)}) collective-permute-start(bf16[8,144,128]{2,1,0:T(8,128)(2,1)S(1)} %all_to_all.23.mine), channel_id=1, source_target_pairs={{0,16},{16,0},{32,48},{48,32},{64,80},{80,64},{96,112},{112,96},{1... | collective-permute-start | bytes 884744 | tf_op jit(solution)/shard_map/ppermute | solution.py:487

commit v6 on v4

--- a/solution.py
+++ b/solution.py
@@ -64,12 +64,33 @@
     return jnp.concatenate([left.astype(BF), value.astype(BF), right.astype(BF)], axis=1)
 
 
-def taps(ref, start, rows, cols=None):
+def paired(weight, axis):
+    pad = jnp.zeros((3 * CH, CH) if axis == 0 else (CH, 3 * CH), BF)
+    return jnp.concatenate(
+        [jnp.concatenate([weight, pad], axis=axis), jnp.concatenate([pad, weight], axis=axis)], axis=1 - axis
+    )
+
+
+def four_rows(row, starts):
+    parts = [jnp.concatenate([row(h + k) for h in starts], axis=0) for k in range(4)]
+    return jnp.concatenate(parts, axis=1)
+
+
+def split_rows(value, starts):
+    size = value.shape[0] // len(starts)
+    out = []
+    for k in range(len(starts)):
+        out += [value[k * size : (k + 1) * size, e * CH : (e + 1) * CH] for e in range(2)]
+    return out
+
+
+def weight_grad(source, grad):
+    gap = jnp.zeros((64, CH), BF)
     parts = []
     for r in range(3):
-        part = ref[pl.ds(start + r, rows)] if cols is None else ref[pl.ds(start + r, rows), cols[0] : cols[1], :]
-        parts.append(part.reshape(part.shape[0] * part.shape[1], part.shape[2]))
-    return jnp.concatenate(parts, axis=1)
+        parts.append(jnp.concatenate([gap] * r + [grad.reshape(1024, CH)] + [gap] * (2 - r), axis=0))
+    whole = dot_tn(source.reshape(1152, 3 * CH), jnp.concatenate(parts, axis=1))
+    return [whole[:, r * CH : (r + 1) * CH] for r in range(3)]
 
 
 def column_mask(first, width, limit):
@@ -129,27 +150,20 @@
         copy.wait()
 
 
-def pack_rows_kernel(meta, feat, cot, pair, other, inner, outer, done):
+def pack_rows_kernel(meta, feat, cot, pair, other, inner, outer, inner_cot, outer_cot, done):
     core = meta[4] % 2
+    jobs = []
+    for low, first, second in ((1 - core, inner, inner_cot), (core, outer, outer_cot)):
+        jobs.append((first, feat, pl.ds(8 * low, 8), 0, 32))
+        jobs.append((second, cot, pl.ds(12 * low, 4), 32, 16))
     copies = []
-    for k, (out, low) in enumerate(((inner, 1 - core), (outer, core))):
-        pairs = (
-            (feat.at[pl.ds(8 * low, 8)], out.at[0:8, 32:96, :]),
-            (cot.at[pl.ds(12 * low, 4)], out.at[8:12, 16:80, :]),
-        )
-        copies += [pltpu.make_async_copy(a, b, done.at[2 * k + n]) for n, (a, b) in enumerate(pairs)]
-    for copy in copies:
-        copy.start()
-    for out, low in ((inner, 1 - core), (outer, core)):
-        for out_rows, first, inside, edge in (
-            (slice(0, 8), 8 * low, slice(0, 32), slice(96, 128)),
-            (slice(8, 12), 12 * low, slice(32, 48), slice(80, 96)),
-        ):
-            source = pl.ds(first, out_rows.stop - out_rows.start)
-            before, after = sides(meta, pair[source, inside, :], other[source, inside, :])
-            out[out_rows, 0 : inside.stop - inside.start, :] = before
-            out[out_rows, edge, :] = after
-        out[8:12, 96:128, :] = jnp.zeros((4, 32, CH), BF)
+    for k, (out, middle, rows, _, width) in enumerate(jobs):
+        copies.append(pltpu.make_async_copy(middle.at[rows], out.at[:, width : width + 64, :], done.at[k]))
+        copies[k].start()
+    for out, _, rows, first, width in jobs:
+        before, after = sides(meta, pair[rows, first : first + width, :], other[rows, first : first + width, :])
+        out[:, 0:width, :] = before
+        out[:, width + 64 :, :] = after
     for copy in copies:
         copy.wait()
 
@@ -160,107 +174,135 @@
         out[k] = ref[...]
 
 
-def first_kernel(meta, feat_far, pair, other, inner, outer, w1_far, act3, slope1, feat3o, feat3, pre1, feat, w1, done):
-    copies = [pltpu.make_async_copy(feat_far, feat, done.at[0]), pltpu.make_async_copy(w1_far, w1, done.at[1])]
+def first_rows(meta, row, starts, weight):
+    top, left, height, breadth = (meta[0], meta[1], meta[2], meta[3])
+    mask = column_mask(left - 8, 128, breadth)
+    pre = dot_nn(four_rows(row, [h - 1 for h in starts]), weight)
+    out = {}
+    for k, value in enumerate(split_rows(pre, starts)):
+        h = starts[k // 2] + k % 2
+        act = rounded(value * sigmoid(value)) * (mask * row_ok(top - 8 + h, height))
+        out[h] = (value, three(act))
+    return out
+
+
+def second_rows(meta, row, starts, weight):
+    top, left, height, breadth = (meta[0], meta[1], meta[2], meta[3])
+    mask = column_mask(left // 2 - 4, 64, breadth // 2)
+    rows = split_rows(dot_nn(four_rows(row, [h - 1 for h in starts]), weight), starts)
+    out = {}
+    for k, h in enumerate(starts):
+        pre = rows[2 * k : 2 * k + 2]
+        act = [(v * sigmoid(v)).astype(BF) for v in pre]
+        small = rounded(0.25 * pooled_pair(act[0].astype(F32) + act[1].astype(F32)))
+        small = small * (mask * row_ok(top // 2 - 4 + h // 2, height // 2))
+        out[h] = (pre, act, three(small))
+    return out
+
+
+INNER_FIRST = [9, 11, 13, 15, 17, 19, 21]
+INNER_SECOND = [10, 12, 14, 16, 18, 20]
+
+
+def inner_kernel(
+    meta, feat_far, pair, other, w1_far, w2_far,
+    feat3, act3, slope1, pool3, slope2, act, weight1, weight2, feat, w1, w2, done,
+):
+    copies = [
+        pltpu.make_async_copy(a, b, done.at[k]) for k, (a, b) in enumerate(((feat_far, feat), (w1_far, w1), (w2_far, w2)))
+    ]
     for copy in copies:
         copy.start()
-    top, left, height, breadth = (meta[0], meta[1], meta[2], meta[3])
-    mask = column_mask(left - 8, 128, breadth)
-
-    below_at = 24 * (meta[4] % 2)
-
-    @pl.loop(0, 2)
-    def _(b):
-        block = outer[pl.ds(4 * b, 4)].reshape(512, CH).astype(F32)
-        feat3[pl.ds(4 * b + below_at, 4)] = three(block).reshape(4, 128, 3 * CH)
-        block = inner[pl.ds(4 * b, 4)].reshape(512, CH).astype(F32)
-        feat3[pl.ds(4 * b + 24 - below_at, 4)] = three(block).reshape(4, 128, 3 * CH)
-
     for copy in copies:
         copy.wait()
-
-    @pl.loop(0, 4)
-    def _(b):
-        rows = pl.ds(4 * b, 4)
-        before, after = sides(meta, pair[rows, 0:32, :], other[rows, 0:32, :])
-        middle = jnp.concatenate([before, feat[rows], after], axis=1)
-        feat3[pl.ds(4 * b + 8, 4)] = three(middle.reshape(512, CH).astype(F32)).reshape(4, 128, 3 * CH)
-
-    first_w = w1[...]
-
-    @pl.loop(0, 6)
-    def _(b):
-        pre = dot_nn(taps(feat3, 5 * b, 5), first_w)
-        pre1[pl.ds(5 * b, 5)] = pre.reshape(5, 128, CH)
-        value = rounded(pre * sigmoid(pre)).reshape(5, 128, CH)
-        value = masked(value, mask, top - 7 + 5 * b, height)
-        act3[pl.ds(5 * b, 5)] = three(value.reshape(640, CH)).reshape(5, 128, 3 * CH)
-
-    @pl.loop(0, 18)
-    def _(k):
-        slope1[k] = slope_of(pre1[k + 6, 16:112, :])
-        feat3o[k] = feat3[k + 7, 32:96, :]
-
-
-def second_kernel(meta, act3, w2, pool3, slope2, act, act3o, pre2, act2):
-    top, left, height, breadth = (meta[0], meta[1], meta[2], meta[3])
-    coarse_mask = column_mask(left // 2 - 4, 64, breadth // 2)
-    second_w = w2[...]
-
-    @pl.loop(0, 7)
-    def _(b):
-        pre = dot_nn(taps(act3, 4 * b, 4), second_w)
-        pre2[pl.ds(4 * b, 4)] = pre.reshape(4, 128, CH)
-        value = (pre * sigmoid(pre)).astype(BF)
-        act2[pl.ds(4 * b, 4)] = value.reshape(4, 128, CH)
-        value = value.astype(F32).reshape(4, 128, CH)
-        coarse = []
-        for k in range(2):
-            small = rounded(0.25 * pooled_pair(value[2 * k] + value[2 * k + 1]))
-            coarse.append(small * (coarse_mask * row_ok(top // 2 - 3 + 2 * b + k, height // 2)))
-        coarse = jnp.concatenate(coarse, axis=0)
-        pool3[pl.ds(2 * b, 2)] = three(coarse).reshape(2, 64, 3 * CH)
-
-    @pl.loop(0, 18)
-    def _(k):
-        act3o[k] = act3[k + 6, 32:96, :]
-
-    @pl.loop(0, 20)
-    def _(k):
-        slope2[k] = slope_of(pre2[k + 4, 16:112, :])
-
-    @pl.loop(0, 16)
-    def _(k):
-        act[k] = act2[k + 6, 32:96, :]
-
-
-def first_step(meta, feat, halo, w1):
+    weight1[...] = paired(w1[...], 0)
+    weight2[...] = paired(w2[...], 0)
+    for k in range(16):
+        before, after = sides(meta, pair[k, 0:32, :], other[k, 0:32, :])
+        feat3[k] = three(jnp.concatenate([before, feat[k], after], axis=0).astype(F32))
+    for h, (pre, wide) in first_rows(meta, lambda h: feat3[h - 8], INNER_FIRST, weight1[...]).items():
+        act3[h - 9] = wide
+        slope1[h - 9] = slope_of(pre[16:112])
+    for h, (pre, value, small) in second_rows(meta, lambda h: act3[h - 9], INNER_SECOND, weight2[...]).items():
+        pool3[h // 2 - 5] = small
+        for e in range(2):
+            slope2[h - 10 + e] = slope_of(pre[e][16:112])
+            act[h - 10 + e] = value[e][32:96]
+
+
+def outer_kernel(
+    meta, inner, outer, feat3i, act3i, slope1i, pool3i, slope2i, acti, weight1, weight2,
+    pool3, slope1, slope2, act, feat3o, act3o, feat3, act3,
+):
+    below_at = 24 * (meta[4] % 2)
+    for k in range(8):
+        feat3[k + below_at] = three(outer[k].astype(F32))
+        feat3[k + 24 - below_at] = three(inner[k].astype(F32))
+    feat3[8:24] = feat3i[...]
+    for starts in ([1, 3, 5, 7], [23, 25, 27, 29]):
+        for h, (pre, wide) in first_rows(meta, lambda h: feat3[h], starts, weight1[...]).items():
+            act3[h - 1] = wide
+            if 7 <= h <= 24:
+                slope1[h - 7] = slope_of(pre[16:112])
+    slope1[2:16] = slope1i[...]
+    act3[8:22] = act3i[...]
+    for starts in ([2, 4, 6, 8], [22, 24, 26, 28]):
+        for h, (pre, value, small) in second_rows(meta, lambda h: act3[h - 1], starts, weight2[...]).items():
+            pool3[h // 2 - 1] = small
+            for e in range(2):
+                if 6 <= h + e < 26:
+                    slope2[h + e - 6] = slope_of(pre[e][16:112])
+                if 8 <= h + e < 24:
+                    act[h + e - 8] = value[e][32:96]
+    pool3[4:10] = pool3i[...]
+    slope2[4:16] = slope2i[...]
+    act[2:14] = acti[...]
+    feat3o[...] = feat3[7:25, 32:96, :]
+    act3o[...] = act3[6:24, 32:96, :]
+
+
+def inner_step(meta, feat, pair, other, w1, w2):
     return call(
-        first_kernel,
-        "first_conv",
-        (((30, 128, 384), BF), ((18, 96, CH), F32), ((18, 64, 384), BF)),
-        (meta, feat) + halo + (w1,),
+        inner_kernel,
+        "forward_inner",
         (
-            ((32, 128, 384), BF),
-            ((30, 128, CH), F32),
+            ((16, 128, 384), BF),
+            ((14, 128, 384), BF),
+            ((14, 96, CH), F32),
+            ((6, 64, 384), BF),
+            ((12, 96, CH), F32),
+            ((12, 64, CH), BF),
+            ((1536, 256), BF),
+            ((1536, 256), BF),
+        ),
+        (meta, feat, pair, other, w1, w2),
+        (
             ((16, 64, CH), BF),
             ((1152, CH), BF),
-            pltpu.SemaphoreType.DMA((2,)),
+            ((1152, CH), BF),
+            pltpu.SemaphoreType.DMA((3,)),
         ),
-        far=(1, 6),
-        limit=20,
-        flops=4 * 10**9,
-    )
-
-
-def second_step(meta, act3, w2):
+        far=(1, 4, 5),
+        limit=24,
+        flops=0,
+    )
+
+
+def outer_step(meta, inner, outer, parts):
     return call(
-        second_kernel,
-        "second_conv",
-        (((14, 64, 384), BF), ((20, 96, CH), F32), ((16, 64, CH), BF), ((18, 64, 384), BF)),
-        (meta, act3, w2),
-        (((28, 128, CH), F32), ((28, 128, CH), BF)),
-        limit=20,
+        outer_kernel,
+        "forward_outer",
+        (
+            ((14, 64, 384), BF),
+            ((18, 96, CH), F32),
+            ((20, 96, CH), F32),
+            ((16, 64, CH), BF),
+            ((18, 64, 384), BF),
+            ((18, 64, 384), BF),
+        ),
+        (meta, inner, outer) + tuple(parts),
+        (((32, 128, 384), BF), ((30, 128, 384), BF)),
+        limit=24,
         flops=4 * 10**9,
     )
 
@@ -286,19 +328,19 @@
 
     below_at = 10 * core
     for k in range(2):
-        projin[k + below_at] = pair_sum(outer[8 + 2 * k, 0:96, :], outer[9 + 2 * k, 0:96, :])
-        projin[k + 10 - below_at] = pair_sum(inner[8 + 2 * k, 0:96, :], inner[9 + 2 * k, 0:96, :])
-
-    @pl.loop(0, 8)
-    def _(k):
-        rows = pl.ds(2 * k, 2)
+        projin[k + below_at] = pair_sum(outer[2 * k], outer[2 * k + 1])
+        projin[k + 10 - below_at] = pair_sum(inner[2 * k], inner[2 * k + 1])
+
+    for k in range(8):
+        rows = slice(2 * k, 2 * k + 2)
         before, after = sides(meta, pair[rows, 32:48, :], other[rows, 32:48, :])
         both = jnp.concatenate([before, cot[rows], after], axis=1)
         projin[k + 2] = pair_sum(both[0], both[1])
 
     proj_in = projin[...].reshape(576, CH)
     proj_in_bf = proj_in.astype(BF)
-    pre = dot_nt(taps(pool3, 0, 12), wcat[...]).reshape(12, 64, WIDE)[:, 8:56].reshape(576, WIDE)
+    lhs = jnp.concatenate([pool3[r : r + 12].reshape(768, 3 * CH) for r in range(3)], axis=1)
+    pre = dot_nt(lhs, wcat[...]).reshape(12, 64, WIDE)[:, 8:56].reshape(576, WIDE)
     sigma = sigmoid(pre)
     coarse_act = pre * sigma
     act_grad = dot_nt(proj_in_bf, proj_w)
@@ -317,12 +359,10 @@
         keep[:, first:last, :] = jnp.where(core == 0, even, odd).astype(BF)
         send[:, first:last, :] = jnp.where(core == 0, odd, even).astype(BF)
 
-    for r in range(3):
-        source = pool3[2 + r : 10 + r, 16:48, :].reshape(256, 3 * CH)
-        part = dot_tn(own_grad, source)
-        for s in range(3):
-            t = 3 * r + s
-            emit(16 * t, 16 * t + 16, part[:, s * CH : (s + 1) * CH])
+    source = [pool3[2 + r : 10 + r, 16:48, :].reshape(256, 3 * CH) for r in range(3)]
+    part = dot_tn(own_grad, jnp.concatenate(source, axis=1))
+    for t in range(9):
+        emit(16 * t, 16 * t + 16, part[:, t * CH : (t + 1) * CH])
     emit(144, 160, dot_tn(own_act, own_in))
     total = None
     for r in range(3):
@@ -367,45 +407,33 @@
     top, left, height, breadth = (meta[0], meta[1], meta[2], meta[3])
     mask = column_mask(left - 4, 96, breadth)
 
-    def second_rows(k, both):
+    def second_pair(k, both):
         wide = 0.25 * repeated(pooled_grad[k])
-        rows = []
         for e in range(2):
             value = rounded((both[e].astype(F32) + wide) * slope2[2 * k + e])
-            rows.append(value * (mask * row_ok(top - 2 + 2 * k + e, height)))
-        second3[pl.ds(2 * k, 2)] = three(jnp.concatenate(rows, axis=0)).reshape(2, 96, 3 * CH)
+            second3[2 * k + e] = three(value * (mask * row_ok(top - 2 + 2 * k + e, height)))
 
     first_core = meta[4] % 2 == 0
-    second_rows(0, lax.select(first_core, outer[10:12, 0:96, :], inner[10:12, 0:96, :]))
-    second_rows(9, lax.select(first_core, inner[8:10, 0:96, :], outer[8:10, 0:96, :]))
-
-    @pl.loop(0, 8)
-    def _(k):
-        rows = pl.ds(2 * k, 2)
+    second_pair(0, lax.select(first_core, outer[2:4], inner[2:4]))
+    second_pair(9, lax.select(first_core, inner[0:2], outer[0:2]))
+    for k in range(8):
+        rows = slice(2 * k, 2 * k + 2)
         before, after = sides(meta, pair[rows, 32:48, :], other[rows, 32:48, :])
-        second_rows(k + 1, jnp.concatenate([before, cot[rows], after], axis=1))
-
-    def weight_grad(source, grad):
-        return [dot_tn(source[r : r + 16].reshape(1024, 3 * CH), grad) for r in range(3)]
+        second_pair(k + 1, jnp.concatenate([before, cot[rows], after], axis=1))
 
     def emit(base, parts):
         for r in range(3):
             grads[base + 384 * r : base + 384 * (r + 1), :] = parts[r].astype(BF)
 
-    second_own = second3[2:18, 16:80, CH : 2 * CH].reshape(1024, CH)
-    emit(1152, weight_grad(act3, second_own))
-    back_w = flipped(w2)
-
-    @pl.loop(0, 3)
-    def _(b):
-        value = dot_nt(taps(second3, 6 * b, 6), back_w).reshape(6, 96, CH)
-        value = rounded(value * slope1[pl.ds(6 * b, 6)])
-        value = masked(value, mask, top - 1 + 6 * b, height)
-        out = three(value.reshape(576, CH)).reshape(6, 96, 3 * CH)
-        first3[pl.ds(6 * b, 6)] = out[:, 16:80, :]
-
-    first_own = first3[1:17, :, CH : 2 * CH].reshape(1024, CH)
-    emit(0, weight_grad(feat3, first_own))
+    back_w = paired(flipped(w2), 1)
+    for starts in ([0, 2, 4, 6], [8, 10, 12, 14, 16]):
+        value = dot_nt(four_rows(lambda h: second3[h], starts), back_w)
+        for k, row in enumerate(split_rows(value, starts)):
+            h = starts[k // 2] + k % 2
+            row = rounded(row * slope1[h]) * (mask * row_ok(top - 1 + h, height))
+            first3[h] = three(row)[16:80]
+    emit(1152, weight_grad(act3[...], second3[2:18, 16:80, CH : 2 * CH]))
+    emit(0, weight_grad(feat3[...], first3[1:17, :, CH : 2 * CH]))
     core = meta[4] % 2
     for k in range(8):
         keep[k] = grads[pl.ds(pl.multiple_of((2 * k + core) * 144, 16), 144), :]
@@ -425,11 +453,11 @@
 
 
 def feature_kernel(first3, w1, out):
-    back_w = flipped(w1)
-
-    @pl.loop(0, 2)
-    def _(b):
-        out[pl.ds(8 * b, 8)] = dot_nt(taps(first3, 8 * b, 8), back_w).astype(BF).reshape(8, 64, CH)
+    back_w = paired(flipped(w1), 1)
+    for starts in ([0, 2, 4, 6], [8, 10, 12, 14]):
+        value = dot_nt(four_rows(lambda h: first3[h], starts), back_w)
+        for k, row in enumerate(split_rows(value, starts)):
+            out[starts[0] + k] = row.astype(BF)
 
 
 def feature_step(first3, w1):
@@ -531,30 +559,31 @@
     )
     pair = swap(pair, "col", 1)
     other = swap_outer(other, "col")
-    own_far = swap(own, "row", 8)
-    edge = ((12, 128, CH), BF)
-    inner, outer = call(
+    near0 = call(stack_kernel, "stack_two", (((2, 160, CH), BF),), (own, swap(own, "row", 8)))[0]
+    edge, edge_cot = (((8, 128, CH), BF), ((4, 96, CH), BF))
+    inner, outer, inner_cot, outer_cot = call(
         pack_rows_kernel,
         "pack_rows",
-        (edge, edge),
+        (edge, edge, edge_cot, edge_cot),
         (meta, feat, cot, pair, other),
         (pltpu.SemaphoreType.DMA((4,)),),
         far=(1, 2),
     )
+    inner, outer, near0 = lax.optimization_barrier((inner, outer, near0))
     inner = swap(inner, "row", 1)
     outer = swap_outer(outer, "row")
-    halo = (pair, other, inner, outer)
     w1, w2 = (conv_first.reshape(1152, CH), conv_second.reshape(1152, CH))
-    act3w, slope1, feat3 = first_step(meta, feat, halo, w1)
-    near0 = call(stack_kernel, "stack_two", (((2, 160, CH), BF),), (own, after_all(own_far, slope1)))[0]
+    pair_in = after_all(pair, near0)
     near = [near0] + [swap(near0, "row", 2 * k) for k in range(1, 4)]
-    pool3, slope2, act, act3 = second_step(meta, act3w, w2)
-    near = list(lax.optimization_barrier((slope2, *near)))[1:]
+    halo_cot = (pair, other, swap(inner_cot, "row", 1), swap_outer(outer_cot, "row"))
+    parts = inner_step(meta, feat, pair_in, other, w1, w2)
+    parts, near = lax.optimization_barrier((parts, near))
     far = swap(call(stack_kernel, "stack_eight", (((4, 2, 160, CH), BF),), near)[0], "row", 1)
-    blended, keep_c, send_c, pooled_grad = coarse_step(meta, pool3, cot, halo, near, far, act)
+    pool3, slope1, slope2, act, feat3, act3 = outer_step(meta, inner, outer, parts)
+    blended, keep_c, send_c, pooled_grad = coarse_step(meta, pool3, cot, halo_cot, near, far, act)
     got_c = swap(send_c, "row", 1)
     keep_f, send_f, first3 = fine_backward(
-        meta, pooled_grad, cot, halo, slope1, slope2, feat3, act3, conv_second.reshape(9, CH, CH)
+        meta, pooled_grad, cot, halo_cot, slope1, slope2, feat3, act3, conv_second.reshape(9, CH, CH)
     )
     got_f = swap(send_f, "row", 1)
     feature_grad = feature_step(first3, conv_first.reshape(9, CH, CH))

time: 120 us -> 111 us (0.925)
  waiting for transfers between devices: 9.39 us -> 3.77 us
  Pallas kernels: 26.8 us -> 21.7 us
  blocking collectives: 57.4 us -> 59.6 us
    pallas_call x14, Pallas kernels: 26.8 us -> 21.7 us  [call(): pl.pallas_call(kernel, name=name, out_shape=shapes, in_specs=[HBM if k in...]
    ppermute x2 -> x3, waiting for transfers between devices: 3.64 us -> 0.01 us  [swap_outer(): return lax.ppermute(value, axis, pairs)]
    ppermute x2 -> x3, starting transfers between devices: 3.09 us -> 6.02 us  [swap_outer(): return lax.ppermute(value, axis, pairs)]
    ppermute x10 -> x11, starting transfers between devices: 21.8 us -> 19 us  [swap(): return lax.ppermute(value, axis, [(i, i ^ mask) for i in range(count)])]
    all_to_all x2, blocking collectives: 27.6 us -> 30.3 us  [exchange_row(): lax.all_to_all(value, 'row', 0, 0, axis_index_groups=groups, tiled=True)]
    ppermute x10 -> x11, waiting for transfers between devices: 5.74 us -> 3.76 us  [swap(): return lax.ppermute(value, axis, [(i, i ^ mask) for i in range(count)])]
  transfers between devices with their start and end apart: 12 -> 14, of which waited for: 4 -> 4; matrix products, arithmetic and copies ran while one was open for 0% -> 0% of each run, Pallas kernels for 14% -> 11%
where the time goes in v6:
time: 111 us
  blocking collectives  59.6 us (54%)
  starting transfers between devices  25 us (23%)
  Pallas kernels  21.7 us (20%)
  waiting for transfers between devices  3.77 us (3%)
    all_to_all x2, blocking collectives, exchange_row(): lax.all_to_all(value, 'row', 0, 0, axis_index_groups=groups, tiled=True)  30.3 us
    all_to_all x2, blocking collectives, exchange_column(): return lax.all_to_all(value, 'col', 0, 0, tiled=True)  29.3 us
    pallas_call x14, Pallas kernels, call(): pl.pallas_call(kernel, name=name, out_shape=shapes, in_specs=[HBM if k in...  21.7 us
    ppermute x11, starting transfers between devices, swap(): return lax.ppermute(value, axis, [(i, i ^ mask) for i in range(count)])  19 us
    ppermute x3, starting transfers between devices, swap_outer(): return lax.ppermute(value, axis, pairs)  6.02 us
    ppermute x11, waiting for transfers between devices, swap(): return lax.ppermute(value, axis, [(i, i ^ mask) for i in range(count)])  3.76 us
  transfers between devices with their start and end apart: 14, of which 4 were waited for; matrix products, arithmetic and copies ran while one was open for 0% of the time, Pallas kernels for 11%

profile of v6, /device:TPU:1, one launch (start us, length us, event | category | flops | bytes accessed | tf_op | source)
XLA Modules:
  0.0 111.0 jit_solution(6330848532723439908)
XLA Ops:
  0.6 0.1 stack.19.meta
  0.7 1.7 %pack_columns.1 = (bf16[16,48,128]{2,1,0:T(8,128)(2,1)S(1)}, bf16[16,48,128]{2,1,0:T(8,128)(2,1)S(1)}, bf16[160,128]{1,0:T(8,128)(2,1)S(1)}) custom-call(s32[6]{0:T(128)S(1)} %stack.19.meta, bf16[16,64,128]{2,1,0:T(8,128)(2,1)} %bitcast.28, bf16[16,64,128]{2,1,0:T(8,128)(2,1)} %bitcast.20, bf16[9,16,128]{2,1,0:T(8,128)(2,1)} %bitcast.31, bf16[16,128]{1,0:T(8,128)(2,1)} %proj.1), custom_call_target="tpu_custom_call" | custom-call | tf_op jit(solution)/shard_map/pack_columns/pallas_call | solution.py:23
  2.4 2.6 %collective-permute-start = (bf16[16,48,128]{2,1,0:T(8,128)(2,1)S(1)}, bf16[16,48,128]{2,1,0:T(8,128)(2,1)S(1)}, u32[]{:S(2)}, u32[]{:S(2)}) collective-permute-start(bf16[16,48,128]{2,1,0:T(8,128)(2,1)S(1)} %get-tuple-element.56), channel_id=1, source_target_pairs={{0,1},{1,0},{2,3},{3,2},{4,5},{5,4},{6,7},{7,6},{8,9},{9,8},{10,11... | collective-permute-start | bytes 589832 | tf_op jit(solution)/shard_map/ppermute | solution.py:515
  5.0 0.7 collective-permute-start.1
  5.7 3.0 %collective-permute-start.2 = (bf16[160,128]{1,0:T(8,128)(2,1)S(1)}, bf16[160,128]{1,0:T(8,128)(2,1)S(1)}, u32[]{:S(2)}, u32[]{:S(2)}) collective-permute-start(bf16[160,128]{1,0:T(8,128)(2,1)S(1)} %get-tuple-element.60.refs_0_), channel_id=1, source_target_pairs={{0,128},{16,144},{32,160},{48,176},{64,192},{80,208},{96,224},{112... | collective-permute-start | bytes 122888 | tf_op jit(solution)/shard_map/ppermute | solution.py:515
  8.7 1.4 %collective-permute-done.2.refs_1_ = bf16[160,128]{1,0:T(8,128)(2,1)S(1)} collective-permute-done((bf16[160,128]{1,0:T(8,128)(2,1)S(1)}, bf16[160,128]{1,0:T(8,128)(2,1)S(1)}, u32[]{:S(2)}, u32[]{:S(2)}) %collective-permute-start.2) | collective-permute-done | bytes 40992 | tf_op jit(solution)/shard_map/ppermute | solution.py:515
  10.1 1.6 %pack_rows.1 = (bf16[8,128,128]{2,1,0:T(8,128)(2,1)S(1)}, bf16[8,128,128]{2,1,0:T(8,128)(2,1)S(1)}, bf16[4,96,128]{2,1,0:T(8,128)(2,1)S(1)}, bf16[4,96,128]{2,1,0:T(8,128)(2,1)S(1)}) custom-call(s32[6]{0:T(128)S(1)} %stack.19.meta, bf16[16,64,128]{2,1,0:T(8,128)(2,1)} %bitcast.29, bf16[16,64,128]{2,1,0:T(8,128)(2,1)} %bitcast.21, ...), custom_call_target="tpu_custom_call" | custom-call | tf_op jit(solution)/shard_map/pack_rows/pallas_call | solution.py:23
  11.7 2.2 %collective-permute-start.3 = (bf16[8,128,128]{2,1,0:T(8,128)(2,1)S(1)}, bf16[8,128,128]{2,1,0:T(8,128)(2,1)S(1)}, u32[]{:S(2)}, u32[]{:S(2)}) collective-permute-start(bf16[8,128,128]{2,1,0:T(8,128)(2,1)S(1)} %get-tuple-element.61), channel_id=1, source_target_pairs={{0,16},{16,0},{32,48},{48,32},{64,80},{80,64},{96,112},{112,96},{1... | collective-permute-start | bytes 786440 | tf_op jit(solution)/shard_map/ppermute | solution.py:515
  13.9 3.0 %collective-permute-start.4 = (bf16[8,128,128]{2,1,0:T(8,128)(2,1)S(1)}, bf16[8,128,128]{2,1,0:T(8,128)(2,1)S(1)}, u32[]{:S(2)}, u32[]{:S(2)}) collective-permute-start(bf16[8,128,128]{2,1,0:T(8,128)(2,1)S(1)} %get-tuple-element.62), channel_id=1, source_target_pairs={{16,32},{32,16},{48,64},{64,48},{80,96},{96,80},{112,128},{128,112... | collective-permute-start | bytes 786440 | tf_op jit(solution)/shard_map/ppermute | solution.py:521
  16.9 4.2 %collective-permute-start.7 = (bf16[2,160,128]{2,1,0:T(8,128)(2,1)S(1)}, bf16[2,160,128]{2,1,0:T(8,128)(2,1)S(1)}, u32[]{:S(2)}, u32[]{:S(2)}) collective-permute-start(bf16[2,160,128]{2,1,0:T(8,128)(2,1)S(1)} %stack_two.1.refs_0_.near0), channel_id=1, source_target_pairs={{0,96},{16,112},{32,64},{48,80},{64,32},{80,48},{96,0},{112,16},{1... | collective-permute-start | bytes 245768 | tf_op jit(solution)/shard_map/ppermute | solution.py:515
  21.1 0.7 collective-permute-start.5
  21.8 4.8 %forward_inner.1 = (bf16[16,128,384]{2,1,0:T(8,128)(2,1)S(1)}, bf16[14,128,384]{2,1,0:T(8,128)(2,1)S(1)}, f32[14,96,128]{2,1,0:T(8,128)S(1)}, bf16[6,64,384]{2,1...) custom-call(s32[6]{0:T(128)S(1)} %stack.19.meta, ...), custom_call_target="tpu_custom_call" | custom-call | tf_op jit(solution)/shard_map/forward_inner/pallas_call | solution.py:23
  26.6 0.8 collective-permute-done.7.refs_3_.near3
  27.4 2.3 %collective-permute-start.9 = (bf16[4,96,128]{2,1,0:T(8,128)(2,1)S(1)}, bf16[4,96,128]{2,1,0:T(8,128)(2,1)S(1)}, u32[]{:S(2)}, u32[]{:S(2)}) collective-permute-start(bf16[4,96,128]{2,1,0:T(8,128)(2,1)S(1)} %get-tuple-element.83), channel_id=1, source_target_pairs={{16,32},{32,16},{48,64},{64,48},{80,96},{96,80},{112,128},{128,112... | collective-permute-start | bytes 294920 | tf_op jit(solution)/shard_map/ppermute | solution.py:521
  29.8 0.1 collective-permute-start.10
  29.9 3.4 %forward_outer.1 = (bf16[14,64,384]{2,1,0:T(8,128)(2,1)S(1)}, f32[18,96,128]{2,1,0:T(8,128)S(1)}, f32[20,96,128]{2,1,0:T(8,128)S(1)}, bf16[16,64,128]{2,1,0:T(8,...) custom-call(s32[6]{0:T(128)S(1)} %stack.19.meta, ...), custom_call_target="tpu_custom_call" | custom-call | flops 4000000000 | tf_op jit(solution)/shard_map/forward_outer/pallas_call | solution.py:23
  33.4 3.7 %coarse_step.1 = (bf16[16,64,128]{2,1,0:T(8,128)(2,1)}, bf16[8,160,128]{2,1,0:T(8,128)(2,1)S(1)}, bf16[8,160,128]{2,1,0:T(8,128)(2,1)S(1)}, f32[10,48,128]{2,1,0:T(8,128)S(1)}) custom-call(s32[6]{0:T(128)S(1)} %stack.19.meta, bf16[14,64,384]{2,1,0:T(8,128)(2,1)S(1)} %get-tuple-element.81.pool3, bf16[16,64,128]{2,1,0:T(8,128)(2,1)S(1)} %bitcast.22, ...), custom_call_target="tpu_custom_call" | custom-call | flops 2000000000 | tf_op jit(solution)/shard_map/coarse_step/pallas_call | solution.py:23
  37.1 0.7 collective-permute-start.11
  37.9 2.7 %fine_backward.1 = (bf16[8,144,128]{2,1,0:T(8,128)(2,1)S(1)}, bf16[8,144,128]{2,1,0:T(8,128)(2,1)S(1)}, bf16[18,64,384]{2,1,0:T(8,128)(2,1)S(1)}) custom-call(s32[6]{0:T(128)S(1)} %stack.19.meta, f32[10,48,128]{2,1,0:T(8,128)S(1)} %get-tuple-element.90.pooled_grad, bf16[16,64,128]{2,1,0:T(8,128)(2,1)S(1)} %bitcast.23, ...), custom_call_target="tpu_custom_call" | custom-call | flops 2000000000 | tf_op jit(solution)/shard_map/fine_backward/pallas_call | solution.py:23
  40.5 0.1 collective-permute-start.12
  40.7 1.3 %feature_step.1 = bf16[16,64,128]{2,1,0:T(8,128)(2,1)} custom-call(bf16[18,64,384]{2,1,0:T(8,128)(2,1)S(1)} %get-tuple-element.95.first3, bf16[9,128,128]{2,1,0:T(8,128)(2,1)S(1)} %bitcast.27), custom_call_target="tpu_custom_call" | custom-call | flops 1000000000 | tf_op jit(solution)/shard_map/feature_step/pallas_call | solution.py:23
  41.9 0.3 collective-permute-done.12.got_f
  42.2 0.1 scatter_core.1
  42.4 19.7 %all_to_all.20.got = bf16[8,304,128]{2,1,0:T(8,128)(2,1)S(1)} all-to-all(bf16[8,304,128]{2,1,0:T(8,128)(2,1)S(1)} %scatter_core.1), channel_id=1, replica_groups={{0,32,64,96,128,160,192,224},{16,48,80,112,144,176,208,240},{1,33,65,97..., dimensions={0} | all-to-all | bytes 1245184 | tf_op jit(solution)/shard_map/all_to_all | solution.py:527
  62.1 0.1 scatter_row.1
  62.2 18.8 %all_to_all.21.got = bf16[16,32,128]{2,1,0:T(8,128)(2,1)S(1)} all-to-all(bf16[16,32,128]{2,1,0:T(8,128)(2,1)S(1)} %scatter_row.1), channel_id=1, replica_groups=mesh['row'=16,'col'=16] {'col'}, dimensions={0} | all-to-all | bytes 262144 | tf_op jit(solution)/shard_map/all_to_all | solution.py:531
  81.1 10.5 %all_to_all.22.got = bf16[16,32,128]{2,1,0:T(8,128)(2,1)S(1)} all-to-all(bf16[16,32,128]{2,1,0:T(8,128)(2,1)S(1)} %scatter_column.1), channel_id=1, replica_groups=mesh['row'=16,'col'=16] {'col'}, dimensions={0} | all-to-all | bytes 262144 | tf_op jit(solution)/shard_map/all_to_all | solution.py:531
  91.5 0.7 gather_column.1
  92.2 10.6 %all_to_all.23.mine = bf16[8,144,128]{2,1,0:T(8,128)(2,1)S(1)} all-to-all(bf16[8,144,128]{2,1,0:T(8,128)(2,1)S(1)} %get-tuple-element.101), channel_id=1, replica_groups={{0,32,64,96,128,160,192,224},{16,48,80,112,144,176,208,240},{1,33,65,97..., dimensions={0} | all-to-all | bytes 589824 | tf_op jit(solution)/shard_map/all_to_all | solution.py:527
  102.8 5.4 %collective-permute-start.13 = (bf16[8,144,128]{2,1,0:T(8,128)(2,1)S(1)}, bf16[8,144,128]{2,1,0:T(8,128)(2,1)S(1)}, u32[]{:S(2)}, u32[]{:S(2)}) collective-permute-start(bf16[8,144,128]{2,1,0:T(8,128)(2,1)S(1)} %all_to_all.23.mine), channel_id=1, source_target_pairs={{0,16},{16,0},{32,48},{48,32},{64,80},{80,64},{96,112},{112,96},{1... | collective-permute-start | bytes 884744 | tf_op jit(solution)/shard_map/ppermute | solution.py:515
  108.2 1.2 %collective-permute-done.13.other = bf16[8,144,128]{2,1,0:T(8,128)(2,1)S(1)} collective-permute-done((bf16[8,144,128]{2,1,0:T(8,128)(2,1)S(1)}, bf16[8,144,128]{2,1,0:T(8,128)(2,1)S(1)}, u32[]{:S(2)}, u32[]{:S(2)}) %collective-permute-start.13) | collective-permute-done | bytes 294944 | tf_op jit(solution)/shard_map/ppermute | solution.py:515
  109.4 1.6 %finish.1 = (f32[8,144,128]{2,1,0:T(8,128)}, f32[8,144,128]{2,1,0:T(8,128)}) custom-call(s32[6]{0:T(128)S(1)} %stack.19.meta, bf16[8,144,128]{2,1,0:T(8,128)(2,1)S(1)} %all_to_all.23.mine, bf16[8,144,128]{2,1,0:T(8,128)(2,1)S(1)} %collective-permute-done.13.other), custom_call_target="tpu_custom_call" | custom-call | tf_op jit(solution)/shard_map/finish/pallas_call | solution.py:23
  (22 shorter events, 0.1 us)
Async XLA Ops:
  2.4 7.7 %collective-permute-start = (bf16[16,48,128]{2,1,0:T(8,128)(2,1)S(1)}, bf16[16,48,128]{2,1,0:T(8,128)(2,1)S(1)}, u32[]{:S(2)}, u32[]{:S(2)}) collective-permute-start(bf16[16,48,128]{2,1,0:T(8,128)(2,1)S(1)} %get-tuple-element.56), channel_id=1, source_target_pairs={{0,1},{1,0},{2,3},{3,2},{4,5},{5,4},{6,7},{7,6},{8,9},{9,8},{10,11... | collective-permute-start | bytes 589832 | tf_op jit(solution)/shard_map/ppermute | solution.py:515
  5.0 5.1 %collective-permute-start.1 = (bf16[16,48,128]{2,1,0:T(8,128)(2,1)S(1)}, bf16[16,48,128]{2,1,0:T(8,128)(2,1)S(1)}, u32[]{:S(2)}, u32[]{:S(2)}) collective-permute-start(bf16[16,48,128]{2,1,0:T(8,128)(2,1)S(1)} %get-tuple-element.57), channel_id=1, source_target_pairs={{1,2},{2,1},{3,4},{4,3},{5,6},{6,5},{7,8},{8,7},{9,10},{10,9},{11,... | collective-permute-start | bytes 589832 | tf_op jit(solution)/shard_map/ppermute | solution.py:521
  5.7 4.4 %collective-permute-start.2 = (bf16[160,128]{1,0:T(8,128)(2,1)S(1)}, bf16[160,128]{1,0:T(8,128)(2,1)S(1)}, u32[]{:S(2)}, u32[]{:S(2)}) collective-permute-start(bf16[160,128]{1,0:T(8,128)(2,1)S(1)} %get-tuple-element.60.refs_0_), channel_id=1, source_target_pairs={{0,128},{16,144},{32,160},{48,176},{64,192},{80,208},{96,224},{112... | collective-permute-start | bytes 122888 | tf_op jit(solution)/shard_map/ppermute | solution.py:515
  11.7 18.2 %collective-permute-start.3 = (bf16[8,128,128]{2,1,0:T(8,128)(2,1)S(1)}, bf16[8,128,128]{2,1,0:T(8,128)(2,1)S(1)}, u32[]{:S(2)}, u32[]{:S(2)}) collective-permute-start(bf16[8,128,128]{2,1,0:T(8,128)(2,1)S(1)} %get-tuple-element.61), channel_id=1, source_target_pairs={{0,16},{16,0},{32,48},{48,32},{64,80},{80,64},{96,112},{112,96},{1... | collective-permute-start | bytes 786440 | tf_op jit(solution)/shard_map/ppermute | solution.py:515
  13.9 16.0 %collective-permute-start.4 = (bf16[8,128,128]{2,1,0:T(8,128)(2,1)S(1)}, bf16[8,128,128]{2,1,0:T(8,128)(2,1)S(1)}, u32[]{:S(2)}, u32[]{:S(2)}) collective-permute-start(bf16[8,128,128]{2,1,0:T(8,128)(2,1)S(1)} %get-tuple-element.62), channel_id=1, source_target_pairs={{16,32},{32,16},{48,64},{64,48},{80,96},{96,80},{112,128},{128,112... | collective-permute-start | bytes 786440 | tf_op jit(solution)/shard_map/ppermute | solution.py:521
  16.9 10.5 %collective-permute-start.7 = (bf16[2,160,128]{2,1,0:T(8,128)(2,1)S(1)}, bf16[2,160,128]{2,1,0:T(8,128)(2,1)S(1)}, u32[]{:S(2)}, u32[]{:S(2)}) collective-permute-start(bf16[2,160,128]{2,1,0:T(8,128)(2,1)S(1)} %stack_two.1.refs_0_.near0), channel_id=1, source_target_pairs={{0,96},{16,112},{32,64},{48,80},{64,32},{80,48},{96,0},{112,16},{1... | collective-permute-start | bytes 245768 | tf_op jit(solution)/shard_map/ppermute | solution.py:515
  21.1 6.3 %collective-permute-start.6 = (bf16[2,160,128]{2,1,0:T(8,128)(2,1)S(1)}, bf16[2,160,128]{2,1,0:T(8,128)(2,1)S(1)}, u32[]{:S(2)}, u32[]{:S(2)}) collective-permute-start(bf16[2,160,128]{2,1,0:T(8,128)(2,1)S(1)} %stack_two.1.refs_0_.near0), channel_id=1, source_target_pairs={{0,64},{16,80},{32,96},{48,112},{64,0},{80,16},{96,32},{112,48},{1... | collective-permute-start | bytes 245768 | tf_op jit(solution)/shard_map/ppermute | solution.py:515
  21.1 8.6 %collective-permute-start.5 = (bf16[2,160,128]{2,1,0:T(8,128)(2,1)S(1)}, bf16[2,160,128]{2,1,0:T(8,128)(2,1)S(1)}, u32[]{:S(2)}, u32[]{:S(2)}) collective-permute-start(bf16[2,160,128]{2,1,0:T(8,128)(2,1)S(1)} %stack_two.1.refs_0_.near0), channel_id=1, source_target_pairs={{0,32},{16,48},{32,0},{48,16},{64,96},{80,112},{96,64},{112,80},{1... | collective-permute-start | bytes 245768 | tf_op jit(solution)/shard_map/ppermute | solution.py:515
  27.4 6.0 %collective-permute-start.8 = (bf16[4,96,128]{2,1,0:T(8,128)(2,1)S(1)}, bf16[4,96,128]{2,1,0:T(8,128)(2,1)S(1)}, u32[]{:S(2)}, u32[]{:S(2)}) collective-permute-start(bf16[4,96,128]{2,1,0:T(8,128)(2,1)S(1)} %get-tuple-element.82), channel_id=1, source_target_pairs={{0,16},{16,0},{32,48},{48,32},{64,80},{80,64},{96,112},{112,96},{1... | collective-permute-start | bytes 294920 | tf_op jit(solution)/shard_map/ppermute | solution.py:515
  27.4 6.0 %collective-permute-start.9 = (bf16[4,96,128]{2,1,0:T(8,128)(2,1)S(1)}, bf16[4,96,128]{2,1,0:T(8,128)(2,1)S(1)}, u32[]{:S(2)}, u32[]{:S(2)}) collective-permute-start(bf16[4,96,128]{2,1,0:T(8,128)(2,1)S(1)} %get-tuple-element.83), channel_id=1, source_target_pairs={{16,32},{32,16},{48,64},{64,48},{80,96},{96,80},{112,128},{128,112... | collective-permute-start | bytes 294920 | tf_op jit(solution)/shard_map/ppermute | solution.py:521
  29.8 3.6 %copy-start = (bf16[16,16,4,128]{3,2,1,0:T(4,128)(2,1)S(1)}, bf16[16,16,4,128]{3,2,1,0:T(4,128)(2,1)}, u32[]{:S(2)}) copy-start(bf16[16,16,4,128]{3,2,1,0:T(4,128)(2,1)} %param.11) | copy-start | bytes 786436
  29.8 3.6 %collective-permute-start.10 = (bf16[4,2,160,128]{3,2,1,0:T(8,128)(2,1)S(1)}, bf16[4,2,160,128]{3,2,1,0:T(8,128)(2,1)S(1)}, u32[]{:S(2)}, u32[]{:S(2)}) collective-permute-start(bf16[4,2,160,128]{3,2,1,0:T(8,128)(2,1)S(1)} %stack_eight.1), channel_id=1, source_target_pairs={{0,16},{16,0},{32,48},{48,32},{64,80},{80,64},{96,112},{112,96},{1... | collective-permute-start | bytes 983048 | tf_op jit(solution)/shard_map/ppermute | solution.py:515
  33.4 4.4 %copy-start.1 = (bf16[3,3,128,128]{3,2,1,0:T(8,128)(2,1)S(1)}, bf16[3,3,128,128]{3,2,1,0:T(8,128)(2,1)}, u32[]{:S(2)}) copy-start(bf16[3,3,128,128]{3,2,1,0:T(8,128)(2,1)} %param.8) | copy-start | bytes 884740
  37.1 5.1 %collective-permute-start.11 = (bf16[8,160,128]{2,1,0:T(8,128)(2,1)S(1)}, bf16[8,160,128]{2,1,0:T(8,128)(2,1)S(1)}, u32[]{:S(2)}, u32[]{:S(2)}) collective-permute-start(bf16[8,160,128]{2,1,0:T(8,128)(2,1)S(1)} %get-tuple-element.98), channel_id=1, source_target_pairs={{0,16},{16,0},{32,48},{48,32},{64,80},{80,64},{96,112},{112,96},{1... | collective-permute-start | bytes 983048 | tf_op jit(solution)/shard_map/ppermute | solution.py:515
  37.9 2.8 %copy-start.2 = (bf16[3,3,128,128]{3,2,1,0:T(8,128)(2,1)S(1)}, bf16[3,3,128,128]{3,2,1,0:T(8,128)(2,1)}, u32[]{:S(2)}) copy-start(bf16[3,3,128,128]{3,2,1,0:T(8,128)(2,1)} %param.7) | copy-start | bytes 884740
  40.5 1.7 %collective-permute-start.12 = (bf16[8,144,128]{2,1,0:T(8,128)(2,1)S(1)}, bf16[8,144,128]{2,1,0:T(8,128)(2,1)S(1)}, u32[]{:S(2)}, u32[]{:S(2)}) collective-permute-start(bf16[8,144,128]{2,1,0:T(8,128)(2,1)S(1)} %get-tuple-element.99), channel_id=1, source_target_pairs={{0,16},{16,0},{32,48},{48,32},{64,80},{80,64},{96,112},{112,96},{1... | collective-permute-start | bytes 884744 | tf_op jit(solution)/shard_map/ppermute | solution.py:515
  102.8 6.6 %collective-permute-start.13 = (bf16[8,144,128]{2,1,0:T(8,128)(2,1)S(1)}, bf16[8,144,128]{2,1,0:T(8,128)(2,1)S(1)}, u32[]{:S(2)}, u32[]{:S(2)}) collective-permute-start(bf16[8,144,128]{2,1,0:T(8,128)(2,1)S(1)} %all_to_all.23.mine), channel_id=1, source_target_pairs={{0,16},{16,0},{32,48},{48,32},{64,80},{80,64},{96,112},{112,96},{1... | collective-permute-start | bytes 884744 | tf_op jit(solution)/shard_map/ppermute | solution.py:515

commit v7 on v6

--- a/solution.py
+++ b/solution.py
@@ -150,20 +150,28 @@
         copy.wait()
 
 
-def pack_rows_kernel(meta, feat, cot, pair, other, inner, outer, inner_cot, outer_cot, done):
+EDGE = 8 * 128 + 4 * 96
+
+
+def cot_edge(ref, first, count=1):
+    value = ref[1024 + 96 * first : 1024 + 96 * (first + count), :]
+    return value if count == 1 else value.reshape(count, 96, CH)
+
+
+def pack_rows_kernel(meta, feat, cot, pair, other, inner, outer, done):
     core = meta[4] % 2
     jobs = []
-    for low, first, second in ((1 - core, inner, inner_cot), (core, outer, outer_cot)):
-        jobs.append((first, feat, pl.ds(8 * low, 8), 0, 32))
-        jobs.append((second, cot, pl.ds(12 * low, 4), 32, 16))
+    for low, out in ((1 - core, inner), (core, outer)):
+        jobs += [(out, 128 * k, feat, 8 * low + k, 0, 32) for k in range(8)]
+        jobs += [(out, 1024 + 96 * k, cot, 12 * low + k, 32, 16) for k in range(4)]
     copies = []
-    for k, (out, middle, rows, _, width) in enumerate(jobs):
-        copies.append(pltpu.make_async_copy(middle.at[rows], out.at[:, width : width + 64, :], done.at[k]))
+    for k, (out, base, middle, row, _, width) in enumerate(jobs):
+        copies.append(pltpu.make_async_copy(middle.at[row], out.at[base + width : base + width + 64, :], done.at[k]))
         copies[k].start()
-    for out, _, rows, first, width in jobs:
-        before, after = sides(meta, pair[rows, first : first + width, :], other[rows, first : first + width, :])
-        out[:, 0:width, :] = before
-        out[:, width + 64 :, :] = after
+    for out, base, _, row, first, width in jobs:
+        before, after = sides(meta, pair[row, first : first + width, :], other[row, first : first + width, :])
+        out[base : base + width, :] = before
+        out[base + width + 64 : base + 2 * width + 64, :] = after
     for copy in copies:
         copy.wait()
 
@@ -236,8 +244,8 @@
 ):
     below_at = 24 * (meta[4] % 2)
     for k in range(8):
-        feat3[k + below_at] = three(outer[k].astype(F32))
-        feat3[k + 24 - below_at] = three(inner[k].astype(F32))
+        feat3[k + below_at] = three(outer[128 * k : 128 * k + 128, :].astype(F32))
+        feat3[k + 24 - below_at] = three(inner[128 * k : 128 * k + 128, :].astype(F32))
     feat3[8:24] = feat3i[...]
     for starts in ([1, 3, 5, 7], [23, 25, 27, 29]):
         for h, (pre, wide) in first_rows(meta, lambda h: feat3[h], starts, weight1[...]).items():
@@ -328,8 +336,8 @@
 
     below_at = 10 * core
     for k in range(2):
-        projin[k + below_at] = pair_sum(outer[2 * k], outer[2 * k + 1])
-        projin[k + 10 - below_at] = pair_sum(inner[2 * k], inner[2 * k + 1])
+        projin[k + below_at] = pair_sum(cot_edge(outer, 2 * k), cot_edge(outer, 2 * k + 1))
+        projin[k + 10 - below_at] = pair_sum(cot_edge(inner, 2 * k), cot_edge(inner, 2 * k + 1))
 
     for k in range(8):
         rows = slice(2 * k, 2 * k + 2)
@@ -414,8 +422,8 @@
             second3[2 * k + e] = three(value * (mask * row_ok(top - 2 + 2 * k + e, height)))
 
     first_core = meta[4] % 2 == 0
-    second_pair(0, lax.select(first_core, outer[2:4], inner[2:4]))
-    second_pair(9, lax.select(first_core, inner[0:2], outer[0:2]))
+    second_pair(0, lax.select(first_core, cot_edge(outer, 2, 2), cot_edge(inner, 2, 2)))
+    second_pair(9, lax.select(first_core, cot_edge(inner, 0, 2), cot_edge(outer, 0, 2)))
     for k in range(8):
         rows = slice(2 * k, 2 * k + 2)
         before, after = sides(meta, pair[rows, 32:48, :], other[rows, 32:48, :])
@@ -560,13 +568,13 @@
     pair = swap(pair, "col", 1)
     other = swap_outer(other, "col")
     near0 = call(stack_kernel, "stack_two", (((2, 160, CH), BF),), (own, swap(own, "row", 8)))[0]
-    edge, edge_cot = (((8, 128, CH), BF), ((4, 96, CH), BF))
-    inner, outer, inner_cot, outer_cot = call(
+    edge = ((EDGE, CH), BF)
+    inner, outer = call(
         pack_rows_kernel,
         "pack_rows",
-        (edge, edge, edge_cot, edge_cot),
+        (edge, edge),
         (meta, feat, cot, pair, other),
-        (pltpu.SemaphoreType.DMA((4,)),),
+        (pltpu.SemaphoreType.DMA((24,)),),
         far=(1, 2),
     )
     inner, outer, near0 = lax.optimization_barrier((inner, outer, near0))
@@ -575,15 +583,14 @@
     w1, w2 = (conv_first.reshape(1152, CH), conv_second.reshape(1152, CH))
     pair_in = after_all(pair, near0)
     near = [near0] + [swap(near0, "row", 2 * k) for k in range(1, 4)]
-    halo_cot = (pair, other, swap(inner_cot, "row", 1), swap_outer(outer_cot, "row"))
     parts = inner_step(meta, feat, pair_in, other, w1, w2)
     parts, near = lax.optimization_barrier((parts, near))
     far = swap(call(stack_kernel, "stack_eight", (((4, 2, 160, CH), BF),), near)[0], "row", 1)
     pool3, slope1, slope2, act, feat3, act3 = outer_step(meta, inner, outer, parts)
-    blended, keep_c, send_c, pooled_grad = coarse_step(meta, pool3, cot, halo_cot, near, far, act)
+    blended, keep_c, send_c, pooled_grad = coarse_step(meta, pool3, cot, (pair, other, inner, outer), near, far, act)
     got_c = swap(send_c, "row", 1)
     keep_f, send_f, first3 = fine_backward(
-        meta, pooled_grad, cot, halo_cot, slope1, slope2, feat3, act3, conv_second.reshape(9, CH, CH)
+        meta, pooled_grad, cot, (pair, other, inner, outer), slope1, slope2, feat3, act3, conv_second.reshape(9, CH, CH)
     )
     got_f = swap(send_f, "row", 1)
     feature_grad = feature_step(first3, conv_first.reshape(9, CH, CH))

time: 111 us -> 107 us (0.964)
  blocking collectives: 59.6 us -> 56.7 us
  starting transfers between devices: 25 us -> 22.7 us
    all_to_all x2, blocking collectives: 30.3 us -> 27.5 us  [exchange_row(): lax.all_to_all(value, 'row', 0, 0, axis_index_groups=groups, tiled=True)]
    ppermute x3 -> x2, starting transfers between devices: 6.02 us -> 3.68 us  [swap_outer(): return lax.ppermute(value, axis, pairs)]
    ppermute x11 -> x10, waiting for transfers between devices: 3.76 us -> 4.82 us  [swap(): return lax.ppermute(value, axis, [(i, i ^ mask) for i in range(count)])]
    ppermute x11 -> x10, starting transfers between devices: 19 us -> 19 us  [swap(): return lax.ppermute(value, axis, [(i, i ^ mask) for i in range(count)])]
  transfers between devices with their start and end apart: 14 -> 12, of which waited for: 4 -> 4; matrix products, arithmetic and copies ran while one was open for 0% -> 0% of each run, Pallas kernels for 11% -> 11%
where the time goes in v7:
time: 107 us
  blocking collectives  56.7 us (53%)
  starting transfers between devices  22.7 us (21%)
  Pallas kernels  21.8 us (20%)
  waiting for transfers between devices  4.82 us (5%)
    all_to_all x2, blocking collectives, exchange_column(): return lax.all_to_all(value, 'col', 0, 0, tiled=True)  29.2 us
    all_to_all x2, blocking collectives, exchange_row(): lax.all_to_all(value, 'row', 0, 0, axis_index_groups=groups, tiled=True)  27.5 us
    pallas_call x14, Pallas kernels, call(): pl.pallas_call(kernel, name=name, out_shape=shapes, in_specs=[HBM if k in...  21.8 us
    ppermute x10, starting transfers between devices, swap(): return lax.ppermute(value, axis, [(i, i ^ mask) for i in range(count)])  19 us
    ppermute x10, waiting for transfers between devices, swap(): return lax.ppermute(value, axis, [(i, i ^ mask) for i in range(count)])  4.82 us
    ppermute x2, starting transfers between devices, swap_outer(): return lax.ppermute(value, axis, pairs)  3.68 us
  transfers between devices with their start and end apart: 12, of which 4 were waited for; matrix products, arithmetic and copies ran while one was open for 0% of the time, Pallas kernels for 11%

profile of v7, /device:TPU:1, one launch (start us, length us, event | category | flops | bytes accessed | tf_op | source)
XLA Modules:
  0.0 106.9 jit_solution(5312535898215670668)
XLA Ops:
  0.6 0.1 stack.19.meta
  0.7 1.7 %pack_columns.1 = (bf16[16,48,128]{2,1,0:T(8,128)(2,1)S(1)}, bf16[16,48,128]{2,1,0:T(8,128)(2,1)S(1)}, bf16[160,128]{1,0:T(8,128)(2,1)S(1)}) custom-call(s32[6]{0:T(128)S(1)} %stack.19.meta, bf16[16,64,128]{2,1,0:T(8,128)(2,1)} %bitcast.28, bf16[16,64,128]{2,1,0:T(8,128)(2,1)} %bitcast.20, bf16[9,16,128]{2,1,0:T(8,128)(2,1)} %bitcast.31, bf16[16,128]{1,0:T(8,128)(2,1)} %proj.1), custom_call_target="tpu_custom_call" | custom-call | tf_op jit(solution)/shard_map/pack_columns/pallas_call | solution.py:23
  2.4 2.6 %collective-permute-start = (bf16[16,48,128]{2,1,0:T(8,128)(2,1)S(1)}, bf16[16,48,128]{2,1,0:T(8,128)(2,1)S(1)}, u32[]{:S(2)}, u32[]{:S(2)}) collective-permute-start(bf16[16,48,128]{2,1,0:T(8,128)(2,1)S(1)} %get-tuple-element.54), channel_id=1, source_target_pairs={{0,1},{1,0},{2,3},{3,2},{4,5},{5,4},{6,7},{7,6},{8,9},{9,8},{10,11... | collective-permute-start | bytes 589832 | tf_op jit(solution)/shard_map/ppermute | solution.py:523
  5.0 0.7 collective-permute-start.1
  5.7 3.0 %collective-permute-start.2 = (bf16[160,128]{1,0:T(8,128)(2,1)S(1)}, bf16[160,128]{1,0:T(8,128)(2,1)S(1)}, u32[]{:S(2)}, u32[]{:S(2)}) collective-permute-start(bf16[160,128]{1,0:T(8,128)(2,1)S(1)} %get-tuple-element.58.refs_0_), channel_id=1, source_target_pairs={{0,128},{16,144},{32,160},{48,176},{64,192},{80,208},{96,224},{112... | collective-permute-start | bytes 122888 | tf_op jit(solution)/shard_map/ppermute | solution.py:523
  8.7 1.4 %collective-permute-done.2.refs_1_ = bf16[160,128]{1,0:T(8,128)(2,1)S(1)} collective-permute-done((bf16[160,128]{1,0:T(8,128)(2,1)S(1)}, bf16[160,128]{1,0:T(8,128)(2,1)S(1)}, u32[]{:S(2)}, u32[]{:S(2)}) %collective-permute-start.2) | collective-permute-done | bytes 40992 | tf_op jit(solution)/shard_map/ppermute | solution.py:523
  10.1 1.7 %pack_rows.1 = (bf16[1408,128]{1,0:T(8,128)(2,1)S(1)}, bf16[1408,128]{1,0:T(8,128)(2,1)S(1)}) custom-call(s32[6]{0:T(128)S(1)} %stack.19.meta, bf16[16,64,128]{2,1,0:T(8,128)(2,1)} %bitcast.29, bf16[16,64,128]{2,1,0:T(8,128)(2,1)} %bitcast.21, bf16[16,48,128]{2,1,0:T(8,128)(2,1)S(1)} %collective-permute-done.pair, ...), custom_call_target="tpu_custom_call" | custom-call | tf_op jit(solution)/shard_map/pack_rows/pallas_call | solution.py:23
  11.8 2.2 %collective-permute-start.3 = (bf16[1408,128]{1,0:T(8,128)(2,1)S(1)}, bf16[1408,128]{1,0:T(8,128)(2,1)S(1)}, u32[]{:S(2)}, u32[]{:S(2)}) collective-permute-start(bf16[1408,128]{1,0:T(8,128)(2,1)S(1)} %get-tuple-element.59), channel_id=1, source_target_pairs={{0,16},{16,0},{32,48},{48,32},{64,80},{80,64},{96,112},{112,96},{1... | collective-permute-start | bytes 1081352 | tf_op jit(solution)/shard_map/ppermute | solution.py:523
  14.0 3.0 %collective-permute-start.4 = (bf16[1408,128]{1,0:T(8,128)(2,1)S(1)}, bf16[1408,128]{1,0:T(8,128)(2,1)S(1)}, u32[]{:S(2)}, u32[]{:S(2)}) collective-permute-start(bf16[1408,128]{1,0:T(8,128)(2,1)S(1)} %get-tuple-element.60), channel_id=1, source_target_pairs={{16,32},{32,16},{48,64},{64,48},{80,96},{96,80},{112,128},{128,112... | collective-permute-start | bytes 1081352 | tf_op jit(solution)/shard_map/ppermute | solution.py:529
  17.1 4.2 %collective-permute-start.7 = (bf16[2,160,128]{2,1,0:T(8,128)(2,1)S(1)}, bf16[2,160,128]{2,1,0:T(8,128)(2,1)S(1)}, u32[]{:S(2)}, u32[]{:S(2)}) collective-permute-start(bf16[2,160,128]{2,1,0:T(8,128)(2,1)S(1)} %stack_two.1.refs_0_.near0), channel_id=1, source_target_pairs={{0,96},{16,112},{32,64},{48,80},{64,32},{80,48},{96,0},{112,16},{1... | collective-permute-start | bytes 245768 | tf_op jit(solution)/shard_map/ppermute | solution.py:523
  21.2 0.7 collective-permute-start.5
  21.9 4.8 %forward_inner.1 = (bf16[16,128,384]{2,1,0:T(8,128)(2,1)S(1)}, bf16[14,128,384]{2,1,0:T(8,128)(2,1)S(1)}, f32[14,96,128]{2,1,0:T(8,128)S(1)}, bf16[6,64,384]{2,1...) custom-call(s32[6]{0:T(128)S(1)} %stack.19.meta, ...), custom_call_target="tpu_custom_call" | custom-call | tf_op jit(solution)/shard_map/forward_inner/pallas_call | solution.py:23
  26.7 1.9 %collective-permute-done.7.refs_3_.near3 = bf16[2,160,128]{2,1,0:T(8,128)(2,1)S(1)} collective-permute-done((bf16[2,160,128]{2,1,0:T(8,128)(2,1)S(1)}, bf16[2,160,128]{2,1,0:T(8,128)(2,1)S(1)}, u32[]{:S(2)}, u32[]{:S(2)}) %collective-permute-start.7) | collective-permute-done | bytes 81952 | tf_op jit(solution)/shard_map/ppermute | solution.py:523
  28.6 0.1 collective-permute-start.8
  28.7 3.4 %forward_outer.1 = (bf16[14,64,384]{2,1,0:T(8,128)(2,1)S(1)}, f32[18,96,128]{2,1,0:T(8,128)S(1)}, f32[20,96,128]{2,1,0:T(8,128)S(1)}, bf16[16,64,128]{2,1,0:T(8,...) custom-call(s32[6]{0:T(128)S(1)} %stack.19.meta, ...), custom_call_target="tpu_custom_call" | custom-call | flops 4000000000 | tf_op jit(solution)/shard_map/forward_outer/pallas_call | solution.py:23
  32.2 0.0 copy-start.1
  32.2 3.7 %coarse_step.1 = (bf16[16,64,128]{2,1,0:T(8,128)(2,1)}, bf16[8,160,128]{2,1,0:T(8,128)(2,1)S(1)}, bf16[8,160,128]{2,1,0:T(8,128)(2,1)S(1)}, f32[10,48,128]{2,1,0:T(8,128)S(1)}) custom-call(s32[6]{0:T(128)S(1)} %stack.19.meta, bf16[14,64,384]{2,1,0:T(8,128)(2,1)S(1)} %get-tuple-element.79.pool3, bf16[16,64,128]{2,1,0:T(8,128)(2,1)S(1)} %bitcast.22, ...), custom_call_target="tpu_custom_call" | custom-call | flops 2000000000 | tf_op jit(solution)/shard_map/coarse_step/pallas_call | solution.py:23
  35.9 0.7 collective-permute-start.9
  36.6 2.7 %fine_backward.1 = (bf16[8,144,128]{2,1,0:T(8,128)(2,1)S(1)}, bf16[8,144,128]{2,1,0:T(8,128)(2,1)S(1)}, bf16[18,64,384]{2,1,0:T(8,128)(2,1)S(1)}) custom-call(s32[6]{0:T(128)S(1)} %stack.19.meta, f32[10,48,128]{2,1,0:T(8,128)S(1)} %get-tuple-element.86.pooled_grad, bf16[16,64,128]{2,1,0:T(8,128)(2,1)S(1)} %bitcast.23, ...), custom_call_target="tpu_custom_call" | custom-call | flops 2000000000 | tf_op jit(solution)/shard_map/fine_backward/pallas_call | solution.py:23
  39.3 0.1 collective-permute-start.10
  39.5 1.3 %feature_step.1 = bf16[16,64,128]{2,1,0:T(8,128)(2,1)} custom-call(bf16[18,64,384]{2,1,0:T(8,128)(2,1)S(1)} %get-tuple-element.91.first3, bf16[9,128,128]{2,1,0:T(8,128)(2,1)S(1)} %bitcast.27), custom_call_target="tpu_custom_call" | custom-call | flops 1000000000 | tf_op jit(solution)/shard_map/feature_step/pallas_call | solution.py:23
  40.7 0.3 collective-permute-done.10.got_f
  41.0 0.1 scatter_core.1
  41.1 17.1 %all_to_all.20.got = bf16[8,304,128]{2,1,0:T(8,128)(2,1)S(1)} all-to-all(bf16[8,304,128]{2,1,0:T(8,128)(2,1)S(1)} %scatter_core.1), channel_id=1, replica_groups={{0,32,64,96,128,160,192,224},{16,48,80,112,144,176,208,240},{1,33,65,97..., dimensions={0} | all-to-all | bytes 1245184 | tf_op jit(solution)/shard_map/all_to_all | solution.py:535
  58.2 0.1 scatter_row.1
  58.3 18.7 %all_to_all.21.got = bf16[16,32,128]{2,1,0:T(8,128)(2,1)S(1)} all-to-all(bf16[16,32,128]{2,1,0:T(8,128)(2,1)S(1)} %scatter_row.1), channel_id=1, replica_groups=mesh['row'=16,'col'=16] {'col'}, dimensions={0} | all-to-all | bytes 262144 | tf_op jit(solution)/shard_map/all_to_all | solution.py:539
  77.0 10.5 %all_to_all.22.got = bf16[16,32,128]{2,1,0:T(8,128)(2,1)S(1)} all-to-all(bf16[16,32,128]{2,1,0:T(8,128)(2,1)S(1)} %scatter_column.1), channel_id=1, replica_groups=mesh['row'=16,'col'=16] {'col'}, dimensions={0} | all-to-all | bytes 262144 | tf_op jit(solution)/shard_map/all_to_all | solution.py:539
  87.5 0.7 gather_column.1
  88.2 10.4 %all_to_all.23.mine = bf16[8,144,128]{2,1,0:T(8,128)(2,1)S(1)} all-to-all(bf16[8,144,128]{2,1,0:T(8,128)(2,1)S(1)} %get-tuple-element.97), channel_id=1, replica_groups={{0,32,64,96,128,160,192,224},{16,48,80,112,144,176,208,240},{1,33,65,97..., dimensions={0} | all-to-all | bytes 589824 | tf_op jit(solution)/shard_map/all_to_all | solution.py:535
  98.6 5.4 %collective-permute-start.11 = (bf16[8,144,128]{2,1,0:T(8,128)(2,1)S(1)}, bf16[8,144,128]{2,1,0:T(8,128)(2,1)S(1)}, u32[]{:S(2)}, u32[]{:S(2)}) collective-permute-start(bf16[8,144,128]{2,1,0:T(8,128)(2,1)S(1)} %all_to_all.23.mine), channel_id=1, source_target_pairs={{0,16},{16,0},{32,48},{48,32},{64,80},{80,64},{96,112},{112,96},{1... | collective-permute-start | bytes 884744 | tf_op jit(solution)/shard_map/ppermute | solution.py:523
  104.1 1.2 %collective-permute-done.11.other = bf16[8,144,128]{2,1,0:T(8,128)(2,1)S(1)} collective-permute-done((bf16[8,144,128]{2,1,0:T(8,128)(2,1)S(1)}, bf16[8,144,128]{2,1,0:T(8,128)(2,1)S(1)}, u32[]{:S(2)}, u32[]{:S(2)}) %collective-permute-start.11) | collective-permute-done | bytes 294944 | tf_op jit(solution)/shard_map/ppermute | solution.py:523
  105.3 1.6 %finish.1 = (f32[8,144,128]{2,1,0:T(8,128)}, f32[8,144,128]{2,1,0:T(8,128)}) custom-call(s32[6]{0:T(128)S(1)} %stack.19.meta, bf16[8,144,128]{2,1,0:T(8,128)(2,1)S(1)} %all_to_all.23.mine, bf16[8,144,128]{2,1,0:T(8,128)(2,1)S(1)} %collective-permute-done.11.other), custom_call_target="tpu_custom_call" | custom-call | tf_op jit(solution)/shard_map/finish/pallas_call | solution.py:23
  (18 shorter events, 0.1 us)
Async XLA Ops:
  2.4 7.7 %collective-permute-start = (bf16[16,48,128]{2,1,0:T(8,128)(2,1)S(1)}, bf16[16,48,128]{2,1,0:T(8,128)(2,1)S(1)}, u32[]{:S(2)}, u32[]{:S(2)}) collective-permute-start(bf16[16,48,128]{2,1,0:T(8,128)(2,1)S(1)} %get-tuple-element.54), channel_id=1, source_target_pairs={{0,1},{1,0},{2,3},{3,2},{4,5},{5,4},{6,7},{7,6},{8,9},{9,8},{10,11... | collective-permute-start | bytes 589832 | tf_op jit(solution)/shard_map/ppermute | solution.py:523
  5.0 5.1 %collective-permute-start.1 = (bf16[16,48,128]{2,1,0:T(8,128)(2,1)S(1)}, bf16[16,48,128]{2,1,0:T(8,128)(2,1)S(1)}, u32[]{:S(2)}, u32[]{:S(2)}) collective-permute-start(bf16[16,48,128]{2,1,0:T(8,128)(2,1)S(1)} %get-tuple-element.55), channel_id=1, source_target_pairs={{1,2},{2,1},{3,4},{4,3},{5,6},{6,5},{7,8},{8,7},{9,10},{10,9},{11,... | collective-permute-start | bytes 589832 | tf_op jit(solution)/shard_map/ppermute | solution.py:529
  5.7 4.4 %collective-permute-start.2 = (bf16[160,128]{1,0:T(8,128)(2,1)S(1)}, bf16[160,128]{1,0:T(8,128)(2,1)S(1)}, u32[]{:S(2)}, u32[]{:S(2)}) collective-permute-start(bf16[160,128]{1,0:T(8,128)(2,1)S(1)} %get-tuple-element.58.refs_0_), channel_id=1, source_target_pairs={{0,128},{16,144},{32,160},{48,176},{64,192},{80,208},{96,224},{112... | collective-permute-start | bytes 122888 | tf_op jit(solution)/shard_map/ppermute | solution.py:523
  11.8 16.9 %collective-permute-start.3 = (bf16[1408,128]{1,0:T(8,128)(2,1)S(1)}, bf16[1408,128]{1,0:T(8,128)(2,1)S(1)}, u32[]{:S(2)}, u32[]{:S(2)}) collective-permute-start(bf16[1408,128]{1,0:T(8,128)(2,1)S(1)} %get-tuple-element.59), channel_id=1, source_target_pairs={{0,16},{16,0},{32,48},{48,32},{64,80},{80,64},{96,112},{112,96},{1... | collective-permute-start | bytes 1081352 | tf_op jit(solution)/shard_map/ppermute | solution.py:523
  14.0 14.7 %collective-permute-start.4 = (bf16[1408,128]{1,0:T(8,128)(2,1)S(1)}, bf16[1408,128]{1,0:T(8,128)(2,1)S(1)}, u32[]{:S(2)}, u32[]{:S(2)}) collective-permute-start(bf16[1408,128]{1,0:T(8,128)(2,1)S(1)} %get-tuple-element.60), channel_id=1, source_target_pairs={{16,32},{32,16},{48,64},{64,48},{80,96},{96,80},{112,128},{128,112... | collective-permute-start | bytes 1081352 | tf_op jit(solution)/shard_map/ppermute | solution.py:529
  17.1 11.5 %collective-permute-start.7 = (bf16[2,160,128]{2,1,0:T(8,128)(2,1)S(1)}, bf16[2,160,128]{2,1,0:T(8,128)(2,1)S(1)}, u32[]{:S(2)}, u32[]{:S(2)}) collective-permute-start(bf16[2,160,128]{2,1,0:T(8,128)(2,1)S(1)} %stack_two.1.refs_0_.near0), channel_id=1, source_target_pairs={{0,96},{16,112},{32,64},{48,80},{64,32},{80,48},{96,0},{112,16},{1... | collective-permute-start | bytes 245768 | tf_op jit(solution)/shard_map/ppermute | solution.py:523
  21.2 7.3 %collective-permute-start.6 = (bf16[2,160,128]{2,1,0:T(8,128)(2,1)S(1)}, bf16[2,160,128]{2,1,0:T(8,128)(2,1)S(1)}, u32[]{:S(2)}, u32[]{:S(2)}) collective-permute-start(bf16[2,160,128]{2,1,0:T(8,128)(2,1)S(1)} %stack_two.1.refs_0_.near0), channel_id=1, source_target_pairs={{0,64},{16,80},{32,96},{48,112},{64,0},{80,16},{96,32},{112,48},{1... | collective-permute-start | bytes 245768 | tf_op jit(solution)/shard_map/ppermute | solution.py:523
  21.2 7.3 %collective-permute-start.5 = (bf16[2,160,128]{2,1,0:T(8,128)(2,1)S(1)}, bf16[2,160,128]{2,1,0:T(8,128)(2,1)S(1)}, u32[]{:S(2)}, u32[]{:S(2)}) collective-permute-start(bf16[2,160,128]{2,1,0:T(8,128)(2,1)S(1)} %stack_two.1.refs_0_.near0), channel_id=1, source_target_pairs={{0,32},{16,48},{32,0},{48,16},{64,96},{80,112},{96,64},{112,80},{1... | collective-permute-start | bytes 245768 | tf_op jit(solution)/shard_map/ppermute | solution.py:523
  28.6 3.6 %copy-start = (bf16[16,16,4,128]{3,2,1,0:T(4,128)(2,1)S(1)}, bf16[16,16,4,128]{3,2,1,0:T(4,128)(2,1)}, u32[]{:S(2)}) copy-start(bf16[16,16,4,128]{3,2,1,0:T(4,128)(2,1)} %param.11) | copy-start | bytes 786436
  28.6 3.6 %collective-permute-start.8 = (bf16[4,2,160,128]{3,2,1,0:T(8,128)(2,1)S(1)}, bf16[4,2,160,128]{3,2,1,0:T(8,128)(2,1)S(1)}, u32[]{:S(2)}, u32[]{:S(2)}) collective-permute-start(bf16[4,2,160,128]{3,2,1,0:T(8,128)(2,1)S(1)} %stack_eight.1), channel_id=1, source_target_pairs={{0,16},{16,0},{32,48},{48,32},{64,80},{80,64},{96,112},{112,96},{1... | collective-permute-start | bytes 983048 | tf_op jit(solution)/shard_map/ppermute | solution.py:523
  32.2 4.4 %copy-start.1 = (bf16[3,3,128,128]{3,2,1,0:T(8,128)(2,1)S(1)}, bf16[3,3,128,128]{3,2,1,0:T(8,128)(2,1)}, u32[]{:S(2)}) copy-start(bf16[3,3,128,128]{3,2,1,0:T(8,128)(2,1)} %param.8) | copy-start | bytes 884740
  35.9 5.1 %collective-permute-start.9 = (bf16[8,160,128]{2,1,0:T(8,128)(2,1)S(1)}, bf16[8,160,128]{2,1,0:T(8,128)(2,1)S(1)}, u32[]{:S(2)}, u32[]{:S(2)}) collective-permute-start(bf16[8,160,128]{2,1,0:T(8,128)(2,1)S(1)} %get-tuple-element.94), channel_id=1, source_target_pairs={{0,16},{16,0},{32,48},{48,32},{64,80},{80,64},{96,112},{112,96},{1... | collective-permute-start | bytes 983048 | tf_op jit(solution)/shard_map/ppermute | solution.py:523
  36.6 2.8 %copy-start.2 = (bf16[3,3,128,128]{3,2,1,0:T(8,128)(2,1)S(1)}, bf16[3,3,128,128]{3,2,1,0:T(8,128)(2,1)}, u32[]{:S(2)}) copy-start(bf16[3,3,128,128]{3,2,1,0:T(8,128)(2,1)} %param.7) | copy-start | bytes 884740
  39.3 1.7 %collective-permute-start.10 = (bf16[8,144,128]{2,1,0:T(8,128)(2,1)S(1)}, bf16[8,144,128]{2,1,0:T(8,128)(2,1)S(1)}, u32[]{:S(2)}, u32[]{:S(2)}) collective-permute-start(bf16[8,144,128]{2,1,0:T(8,128)(2,1)S(1)} %get-tuple-element.95), channel_id=1, source_target_pairs={{0,16},{16,0},{32,48},{48,32},{64,80},{80,64},{96,112},{112,96},{1... | collective-permute-start | bytes 884744 | tf_op jit(solution)/shard_map/ppermute | solution.py:523
  98.6 6.7 %collective-permute-start.11 = (bf16[8,144,128]{2,1,0:T(8,128)(2,1)S(1)}, bf16[8,144,128]{2,1,0:T(8,128)(2,1)S(1)}, u32[]{:S(2)}, u32[]{:S(2)}) collective-permute-start(bf16[8,144,128]{2,1,0:T(8,128)(2,1)S(1)} %all_to_all.23.mine), channel_id=1, source_target_pairs={{0,16},{16,0},{32,48},{48,32},{64,80},{80,64},{96,112},{112,96},{1... | collective-permute-start | bytes 884744 | tf_op jit(solution)/shard_map/ppermute | solution.py:523

commit v8 on v7

--- a/solution.py
+++ b/solution.py
@@ -69,6 +69,10 @@
     return jnp.concatenate(
         [jnp.concatenate([weight, pad], axis=axis), jnp.concatenate([pad, weight], axis=axis)], axis=1 - axis
     )
+
+
+def flipped(weight):
+    return jnp.concatenate([weight[(8 - t) * CH : (9 - t) * CH, :] for t in range(9)], axis=1)
 
 
 def four_rows(row, starts):
@@ -158,22 +162,29 @@
     return value if count == 1 else value.reshape(count, 96, CH)
 
 
-def pack_rows_kernel(meta, feat, cot, pair, other, inner, outer, done):
+def prepare_kernel(feat_far, cot_far, w1_far, w2_far, feat, cot, weight1, weight2, back1, back2, w1, w2, done):
+    pairs = ((w1_far, w1), (w2_far, w2), (feat_far, feat), (cot_far, cot))
+    copies = [pltpu.make_async_copy(a, b, done.at[k]) for k, (a, b) in enumerate(pairs)]
+    for copy in copies:
+        copy.start()
+    for k, (w, weight, back) in enumerate(((w1, weight1, back1), (w2, weight2, back2))):
+        copies[k].wait()
+        weight[...] = paired(w[...], 0)
+        back[...] = paired(flipped(w), 1)
+    for copy in copies[2:]:
+        copy.wait()
+
+
+def pack_rows_kernel(meta, feat, cot, pair, other, inner, outer):
     core = meta[4] % 2
-    jobs = []
     for low, out in ((1 - core, inner), (core, outer)):
-        jobs += [(out, 128 * k, feat, 8 * low + k, 0, 32) for k in range(8)]
-        jobs += [(out, 1024 + 96 * k, cot, 12 * low + k, 32, 16) for k in range(4)]
-    copies = []
-    for k, (out, base, middle, row, _, width) in enumerate(jobs):
-        copies.append(pltpu.make_async_copy(middle.at[row], out.at[base + width : base + width + 64, :], done.at[k]))
-        copies[k].start()
-    for out, base, _, row, first, width in jobs:
-        before, after = sides(meta, pair[row, first : first + width, :], other[row, first : first + width, :])
-        out[base : base + width, :] = before
-        out[base + width + 64 : base + 2 * width + 64, :] = after
-    for copy in copies:
-        copy.wait()
+        jobs = [(128 * k, feat, 8 * low + k, 0, 32) for k in range(8)]
+        jobs += [(1024 + 96 * k, cot, 12 * low + k, 32, 16) for k in range(4)]
+        for base, middle, row, first, width in jobs:
+            before, after = sides(meta, pair[row, first : first + width, :], other[row, first : first + width, :])
+            out[base : base + width, :] = before
+            out[base + width : base + width + 64, :] = middle[row]
+            out[base + width + 64 : base + 2 * width + 64, :] = after
 
 
 def stack_kernel(*refs):
@@ -212,19 +223,7 @@
 INNER_SECOND = [10, 12, 14, 16, 18, 20]
 
 
-def inner_kernel(
-    meta, feat_far, pair, other, w1_far, w2_far,
-    feat3, act3, slope1, pool3, slope2, act, weight1, weight2, feat, w1, w2, done,
-):
-    copies = [
-        pltpu.make_async_copy(a, b, done.at[k]) for k, (a, b) in enumerate(((feat_far, feat), (w1_far, w1), (w2_far, w2)))
-    ]
-    for copy in copies:
-        copy.start()
-    for copy in copies:
-        copy.wait()
-    weight1[...] = paired(w1[...], 0)
-    weight2[...] = paired(w2[...], 0)
+def inner_kernel(meta, feat, pair, other, weight1, weight2, feat3, act3, slope1, pool3, slope2, act):
     for k in range(16):
         before, after = sides(meta, pair[k, 0:32, :], other[k, 0:32, :])
         feat3[k] = three(jnp.concatenate([before, feat[k], after], axis=0).astype(F32))
@@ -269,7 +268,7 @@
     act3o[...] = act3[6:24, 32:96, :]
 
 
-def inner_step(meta, feat, pair, other, w1, w2):
+def inner_step(meta, feat, pair, other, weight1, weight2):
     return call(
         inner_kernel,
         "forward_inner",
@@ -280,23 +279,14 @@
             ((6, 64, 384), BF),
             ((12, 96, CH), F32),
             ((12, 64, CH), BF),
-            ((1536, 256), BF),
-            ((1536, 256), BF),
         ),
-        (meta, feat, pair, other, w1, w2),
-        (
-            ((16, 64, CH), BF),
-            ((1152, CH), BF),
-            ((1152, CH), BF),
-            pltpu.SemaphoreType.DMA((3,)),
-        ),
-        far=(1, 4, 5),
+        (meta, feat, pair, other, weight1, weight2),
         limit=24,
         flops=0,
     )
 
 
-def outer_step(meta, inner, outer, parts):
+def outer_step(meta, inner, outer, parts, weight1, weight2):
     return call(
         outer_kernel,
         "forward_outer",
@@ -308,7 +298,7 @@
             ((18, 64, 384), BF),
             ((18, 64, 384), BF),
         ),
-        (meta, inner, outer) + tuple(parts),
+        (meta, inner, outer) + tuple(parts) + (weight1, weight2),
         (((32, 128, 384), BF), ((30, 128, 384), BF)),
         limit=24,
         flops=4 * 10**9,
@@ -316,8 +306,8 @@
 
 
 def coarse_kernel(
-    meta, pool3, cot, pair, other, inner, outer, near0, near1, near2, near3, far, act,
-    blended, keep, send, pooled_grad, wcat, projs, wide3, projin,
+    meta, pool3, cot, pair, other, inner, outer, near0, near1, near2, near3, far,
+    own, projs_out, keep, send, pooled_grad, wcat, projs, wide3, projin,
 ):
     top, left, height, breadth, me = (meta[0], meta[1], meta[2], meta[3], meta[4])
     core = me % 2
@@ -380,19 +370,24 @@
         part = dot_nn(lhs, rhs)
         total = part if total is None else total + part
     pooled_grad[...] = total.reshape(10, 48, CH)
-    projected = dot_nn(own_act, proj_w).reshape(8, 32, CH)
+    own[...] = own_act
+    projs_out[...] = proj_w
+
+
+def blend_kernel(own, proj, act, blended):
+    projected = dot_nn(own[...], proj[...]).reshape(8, 32, CH)
     for k in range(8):
         row = repeated(projected[k])
         for e in range(2):
             blended[2 * k + e] = (act[2 * k + e].astype(F32) + row).astype(BF)
 
 
-def coarse_step(meta, pool3, cot, halo, near, far, act):
+def coarse_step(meta, pool3, cot, halo, near, far):
     return call(
         coarse_kernel,
         "coarse_step",
-        (((16, 64, CH), BF), ((8, 160, CH), BF), ((8, 160, CH), BF), ((10, 48, CH), F32)),
-        (meta, pool3, cot) + halo + tuple(near) + (far, act),
+        (((256, WIDE), BF), ((WIDE, CH), BF), ((8, 160, CH), BF), ((8, 160, CH), BF), ((10, 48, CH), F32)),
+        (meta, pool3, cot) + halo + tuple(near) + (far,),
         (
             ((WIDE, 9 * CH), BF),
             ((WIDE, CH), BF),
@@ -404,12 +399,8 @@
     )
 
 
-def flipped(weight):
-    return jnp.concatenate([weight[8 - t] for t in range(9)], axis=1)
-
-
 def backward_kernel(
-    meta, pooled_grad, cot, pair, other, inner, outer, slope1, slope2, feat3, act3, w2,
+    meta, pooled_grad, cot, pair, other, inner, outer, slope1, slope2, feat3, act3, back_w,
     keep, send, first3, second3, grads,
 ):
     top, left, height, breadth = (meta[0], meta[1], meta[2], meta[3])
@@ -433,9 +424,8 @@
         for r in range(3):
             grads[base + 384 * r : base + 384 * (r + 1), :] = parts[r].astype(BF)
 
-    back_w = paired(flipped(w2), 1)
     for starts in ([0, 2, 4, 6], [8, 10, 12, 14, 16]):
-        value = dot_nt(four_rows(lambda h: second3[h], starts), back_w)
+        value = dot_nt(four_rows(lambda h: second3[h], starts), back_w[...])
         for k, row in enumerate(split_rows(value, starts)):
             h = starts[k // 2] + k % 2
             row = rounded(row * slope1[h]) * (mask * row_ok(top - 1 + h, height))
@@ -448,28 +438,27 @@
         send[k] = grads[pl.ds(pl.multiple_of((2 * k + 1 - core) * 144, 16), 144), :]
 
 
-def fine_backward(meta, pooled_grad, cot, halo, slope1, slope2, feat3, act3, w2):
+def fine_backward(meta, pooled_grad, cot, halo, slope1, slope2, feat3, act3, back_w):
     return call(
         backward_kernel,
         "fine_backward",
         (((8, 144, CH), BF), ((8, 144, CH), BF), ((18, 64, 384), BF)),
-        (meta, pooled_grad, cot) + halo + (slope1, slope2, feat3, act3, w2),
+        (meta, pooled_grad, cot) + halo + (slope1, slope2, feat3, act3, back_w),
         (((20, 96, 384), BF), ((2304, CH), BF)),
         limit=20,
         flops=2 * 10**9,
     )
 
 
-def feature_kernel(first3, w1, out):
-    back_w = paired(flipped(w1), 1)
+def feature_kernel(first3, back_w, out):
     for starts in ([0, 2, 4, 6], [8, 10, 12, 14]):
-        value = dot_nt(four_rows(lambda h: first3[h], starts), back_w)
+        value = dot_nt(four_rows(lambda h: first3[h], starts), back_w[...])
         for k, row in enumerate(split_rows(value, starts)):
             out[starts[0] + k] = row.astype(BF)
 
 
-def feature_step(first3, w1):
-    return call(feature_kernel, "feature_step", (((16, 64, CH), BF),), (first3, w1), limit=12, flops=10**9)[0]
+def feature_step(first3, back_w):
+    return call(feature_kernel, "feature_step", (((16, 64, CH), BF),), (first3, back_w), limit=12, flops=10**9)[0]
 
 
 def scatter_core_kernel(keep_c, keep_f, got_c, got_f, out):
@@ -565,35 +554,40 @@
         (pltpu.SemaphoreType.DMA((14,)),),
         far=(1, 2, 3, 4),
     )
+    w1, w2 = (conv_first.reshape(1152, CH), conv_second.reshape(1152, CH))
+    big, wide = (((16, 64, CH), BF), ((1536, 256), BF))
+    feat_in, cot_in, weight1, weight2, back1, back2 = call(
+        prepare_kernel,
+        "prepare",
+        (big, big, wide, wide, ((256, 1536), BF), ((256, 1536), BF)),
+        (after_all(feat, own), cot, w1, w2),
+        (((1152, CH), BF), ((1152, CH), BF), pltpu.SemaphoreType.DMA((4,))),
+        far=(0, 1, 2, 3),
+        flops=4 * 10**9,
+    )
     pair = swap(pair, "col", 1)
     other = swap_outer(other, "col")
     near0 = call(stack_kernel, "stack_two", (((2, 160, CH), BF),), (own, swap(own, "row", 8)))[0]
-    edge = ((EDGE, CH), BF)
     inner, outer = call(
-        pack_rows_kernel,
-        "pack_rows",
-        (edge, edge),
-        (meta, feat, cot, pair, other),
-        (pltpu.SemaphoreType.DMA((24,)),),
-        far=(1, 2),
+        pack_rows_kernel, "pack_rows", (((EDGE, CH), BF),) * 2, (meta, feat_in, cot_in, pair, other)
     )
     inner, outer, near0 = lax.optimization_barrier((inner, outer, near0))
     inner = swap(inner, "row", 1)
     outer = swap_outer(outer, "row")
-    w1, w2 = (conv_first.reshape(1152, CH), conv_second.reshape(1152, CH))
     pair_in = after_all(pair, near0)
     near = [near0] + [swap(near0, "row", 2 * k) for k in range(1, 4)]
-    parts = inner_step(meta, feat, pair_in, other, w1, w2)
+    parts = inner_step(meta, feat_in, pair_in, other, weight1, weight2)
     parts, near = lax.optimization_barrier((parts, near))
     far = swap(call(stack_kernel, "stack_eight", (((4, 2, 160, CH), BF),), near)[0], "row", 1)
-    pool3, slope1, slope2, act, feat3, act3 = outer_step(meta, inner, outer, parts)
-    blended, keep_c, send_c, pooled_grad = coarse_step(meta, pool3, cot, (pair, other, inner, outer), near, far, act)
+    pool3, slope1, slope2, act, feat3, act3 = outer_step(meta, inner, outer, parts, weight1, weight2)
+    halo = (pair, other, inner, outer)
+    own_act, proj, keep_c, send_c, pooled_grad = coarse_step(meta, pool3, cot_in, halo, near, far)
     got_c = swap(send_c, "row", 1)
     keep_f, send_f, first3 = fine_backward(
-        meta, pooled_grad, cot, (pair, other, inner, outer), slope1, slope2, feat3, act3, conv_second.reshape(9, CH, CH)
+        meta, pooled_grad, cot_in, halo, slope1, slope2, feat3, act3, back2
     )
     got_f = swap(send_f, "row", 1)
-    feature_grad = feature_step(first3, conv_first.reshape(9, CH, CH))
+    feature_grad = feature_step(first3, back1)
 
     got_f = after_all(got_f, feature_grad)
     part = call(scatter_core_kernel, "scatter_core", (((8, 304, CH), BF),), (keep_c, keep_f, got_c, got_f))[0]
@@ -609,11 +603,13 @@
         (((336, CH), F32),),
     )
     fine = exchange_row(fine)
+    blended = call(blend_kernel, "blend", (((16, 64, CH), BF),), (after_all(own_act, fine), proj, act), flops=10**9)[0]
+    other = after_all(swap(fine, "row", 1), blended)
     first, second = call(
         functools.partial(finish_kernel, fine_scale),
         "finish",
         (((8, 144, CH), F32), ((8, 144, CH), F32)),
-        (meta, fine, swap(fine, "row", 1)),
+        (meta, fine, other),
     )
     shape = features.shape
     return (

time: 107 us -> 108 us (level)
  starting transfers between devices: 22.7 us -> 20.6 us
  waiting for transfers between devices: 4.82 us -> 6.24 us
  blocking collectives: 56.7 us -> 58.1 us
    ppermute x10, starting transfers between devices: 19 us -> 16.9 us  [swap(): return lax.ppermute(value, axis, [(i, i ^ mask) for i in range(count)])]
    ppermute x10, waiting for transfers between devices: 4.82 us -> 6.23 us  [swap(): return lax.ppermute(value, axis, [(i, i ^ mask) for i in range(count)])]
    pallas_call x14 -> x16, Pallas kernels: 21.8 us -> 21.7 us  [call(): pl.pallas_call(kernel, name=name, out_shape=shapes, in_specs=[HBM if k in...]
  transfers between devices with their start and end apart: 12 -> 12, of which waited for: 4 -> 4; matrix products, arithmetic and copies ran while one was open for 0% -> 0% of each run, Pallas kernels for 11% -> 12%
where the time goes in v8:
time: 108 us
  blocking collectives  58.1 us (54%)
  Pallas kernels  21.7 us (20%)
  starting transfers between devices  20.6 us (19%)
  waiting for transfers between devices  6.24 us (6%)
    all_to_all x2, blocking collectives, exchange_column(): return lax.all_to_all(value, 'col', 0, 0, tiled=True)  30.2 us
    all_to_all x2, blocking collectives, exchange_row(): lax.all_to_all(value, 'row', 0, 0, axis_index_groups=groups, tiled=True)  27.9 us
    pallas_call x16, Pallas kernels, call(): pl.pallas_call(kernel, name=name, out_shape=shapes, in_specs=[HBM if k in...  21.7 us
    ppermute x10, starting transfers between devices, swap(): return lax.ppermute(value, axis, [(i, i ^ mask) for i in range(count)])  16.9 us
    ppermute x10, waiting for transfers between devices, swap(): return lax.ppermute(value, axis, [(i, i ^ mask) for i in range(count)])  6.23 us
    ppermute x2, starting transfers between devices, swap_outer(): return lax.ppermute(value, axis, pairs)  3.68 us
  transfers between devices with their start and end apart: 12, of which 4 were waited for; matrix products, arithmetic and copies ran while one was open for 0% of the time, Pallas kernels for 12%

profile of v8, /device:TPU:1, one launch (start us, length us, event | category | flops | bytes accessed | tf_op | source)
XLA Modules:
  0.0 107.5 jit_solution(8388690325073295962)
XLA Ops:
  0.7 1.7 %pack_columns.1 = (bf16[16,48,128]{2,1,0:T(8,128)(2,1)S(1)}, bf16[16,48,128]{2,1,0:T(8,128)(2,1)S(1)}, bf16[160,128]{1,0:T(8,128)(2,1)S(1)}) custom-call(s32[6]{0:T(128)S(1)} %stack.19.meta, bf16[16,64,128]{2,1,0:T(8,128)(2,1)} %bitcast.18, bf16[16,64,128]{2,1,0:T(8,128)(2,1)} %bitcast.20, bf16[9,16,128]{2,1,0:T(8,128)(2,1)} %bitcast.22, bf16[16,128]{1,0:T(8,128)(2,1)} %proj.1), custom_call_target="tpu_custom_call" | custom-call | tf_op jit(solution)/shard_map/pack_columns/pallas_call | solution.py:23
  2.4 3.8 %collective-permute-start.2 = (bf16[160,128]{1,0:T(8,128)(2,1)S(1)}, bf16[160,128]{1,0:T(8,128)(2,1)S(1)}, u32[]{:S(2)}, u32[]{:S(2)}) collective-permute-start(bf16[160,128]{1,0:T(8,128)(2,1)S(1)} %get-tuple-element.60.refs_0_), channel_id=1, source_target_pairs={{0,128},{16,144},{32,160},{48,176},{64,192},{80,208},{96,224},{112... | collective-permute-start | bytes 122888 | tf_op jit(solution)/shard_map/ppermute | solution.py:512
  6.3 1.6 %collective-permute-start = (bf16[16,48,128]{2,1,0:T(8,128)(2,1)S(1)}, bf16[16,48,128]{2,1,0:T(8,128)(2,1)S(1)}, u32[]{:S(2)}, u32[]{:S(2)}) collective-permute-start(bf16[16,48,128]{2,1,0:T(8,128)(2,1)S(1)} %get-tuple-element.64), channel_id=1, source_target_pairs={{0,1},{1,0},{2,3},{3,2},{4,5},{5,4},{6,7},{7,6},{8,9},{9,8},{10,11... | collective-permute-start | bytes 589832 | tf_op jit(solution)/shard_map/ppermute | solution.py:512
  7.9 0.7 collective-permute-start.1
  8.6 1.2 %prepare.1 = (bf16[16,64,128]{2,1,0:T(8,128)(2,1)S(1)}, bf16[16,64,128]{2,1,0:T(8,128)(2,1)S(1)}, bf16[1536,256]{1,0:T(8,128)(2,1)S(1)}, bf16[1536,256]{1,0:T(8,...) custom-call(bf16[16,64,128]{2,1,0:T(8,128)(2,1)} %bitcast.19, bf16[16,64,128]{2,1,0:T(8,128)(2,1)} %bitcast.21, ...), custom_call_target="tpu_custom_call" | custom-call | flops 4000000000 | tf_op jit(solution)/shard_map/prepare/pallas_call | solution.py:23
  9.9 2.2 %collective-permute-done.pair = bf16[16,48,128]{2,1,0:T(8,128)(2,1)S(1)} collective-permute-done((bf16[16,48,128]{2,1,0:T(8,128)(2,1)S(1)}, bf16[16,48,128]{2,1,0:T(8,128)(2,1)S(1)}, u32[]{:S(2)}, u32[]{:S(2)}) %collective-permute-start) | collective-permute-done | bytes 196640 | tf_op jit(solution)/shard_map/ppermute | solution.py:512
  12.1 0.6 pack_rows.1
  12.7 1.8 %collective-permute-start.3 = (bf16[1408,128]{1,0:T(8,128)(2,1)S(1)}, bf16[1408,128]{1,0:T(8,128)(2,1)S(1)}, u32[]{:S(2)}, u32[]{:S(2)}) collective-permute-start(bf16[1408,128]{1,0:T(8,128)(2,1)S(1)} %get-tuple-element.68), channel_id=1, source_target_pairs={{0,16},{16,0},{32,48},{48,32},{64,80},{80,64},{96,112},{112,96},{1... | collective-permute-start | bytes 1081352 | tf_op jit(solution)/shard_map/ppermute | solution.py:512
  14.5 3.0 %collective-permute-start.4 = (bf16[1408,128]{1,0:T(8,128)(2,1)S(1)}, bf16[1408,128]{1,0:T(8,128)(2,1)S(1)}, u32[]{:S(2)}, u32[]{:S(2)}) collective-permute-start(bf16[1408,128]{1,0:T(8,128)(2,1)S(1)} %get-tuple-element.69), channel_id=1, source_target_pairs={{16,32},{32,16},{48,64},{64,48},{80,96},{96,80},{112,128},{128,112... | collective-permute-start | bytes 1081352 | tf_op jit(solution)/shard_map/ppermute | solution.py:518
  17.5 2.2 %collective-permute-start.7 = (bf16[2,160,128]{2,1,0:T(8,128)(2,1)S(1)}, bf16[2,160,128]{2,1,0:T(8,128)(2,1)S(1)}, u32[]{:S(2)}, u32[]{:S(2)}) collective-permute-start(bf16[2,160,128]{2,1,0:T(8,128)(2,1)S(1)} %stack_two.1.refs_0_.near0), channel_id=1, source_target_pairs={{0,96},{16,112},{32,64},{48,80},{64,32},{80,48},{96,0},{112,16},{1... | collective-permute-start | bytes 245768 | tf_op jit(solution)/shard_map/ppermute | solution.py:512
  19.7 0.9 collective-permute-start.6
  20.6 0.3 collective-permute-start.5
  20.9 3.6 %forward_inner.1 = (bf16[16,128,384]{2,1,0:T(8,128)(2,1)S(1)}, bf16[14,128,384]{2,1,0:T(8,128)(2,1)S(1)}, f32[14,96,128]{2,1,0:T(8,128)S(1)}, bf16[6,64,384]{2,1...) custom-call(s32[6]{0:T(128)S(1)} %stack.19.meta, ...), custom_call_target="tpu_custom_call" | custom-call | tf_op jit(solution)/shard_map/forward_inner/pallas_call | solution.py:23
  24.5 3.5 %collective-permute-done.7.refs_3_.near3 = bf16[2,160,128]{2,1,0:T(8,128)(2,1)S(1)} collective-permute-done((bf16[2,160,128]{2,1,0:T(8,128)(2,1)S(1)}, bf16[2,160,128]{2,1,0:T(8,128)(2,1)S(1)}, u32[]{:S(2)}, u32[]{:S(2)}) %collective-permute-start.7) | collective-permute-done | bytes 81952 | tf_op jit(solution)/shard_map/ppermute | solution.py:512
  28.1 3.4 %forward_outer.1 = (bf16[14,64,384]{2,1,0:T(8,128)(2,1)S(1)}, f32[18,96,128]{2,1,0:T(8,128)S(1)}, f32[20,96,128]{2,1,0:T(8,128)S(1)}, bf16[16,64,128]{2,1,0:T(8,...) custom-call(s32[6]{0:T(128)S(1)} %stack.19.meta, ...), custom_call_target="tpu_custom_call" | custom-call | flops 4000000000 | tf_op jit(solution)/shard_map/forward_outer/pallas_call | solution.py:23
  31.5 3.6 %coarse_step.1 = (bf16[256,256]{1,0:T(8,128)(2,1)S(1)}, bf16[256,128]{1,0:T(8,128)(2,1)S(1)}, bf16[8,160,128]{2,1,0:T(8,128)(2,1)S(1)}, bf16[8,160,128]{2,1,0:T(8,128)(2,1)S(1)}, f32[10,48,128]{2,1,0:T(8,128)S(1)}) custom-call(s32[6]{0:T(128)S(1)} %stack.19.meta, bf16[14,64,384]{2,1,0:T(8,128)(2,1)S(1)} %get-tuple-element.86.pool3, ...), custom_call_target="tpu_custom_call" | custom-call | flops 2000000000 | tf_op jit(solution)/shard_map/coarse_step/pallas_call | solution.py:23
  35.1 0.7 collective-permute-start.9
  35.9 2.7 %fine_backward.1 = (bf16[8,144,128]{2,1,0:T(8,128)(2,1)S(1)}, bf16[8,144,128]{2,1,0:T(8,128)(2,1)S(1)}, bf16[18,64,384]{2,1,0:T(8,128)(2,1)S(1)}) custom-call(s32[6]{0:T(128)S(1)} %stack.19.meta, f32[10,48,128]{2,1,0:T(8,128)S(1)} %get-tuple-element.93.pooled_grad, bf16[16,64,128]{2,1,0:T(8,128)(2,1)S(1)} %get-tuple-element.63.cot, ...), custom_call_target="tpu_custom_call" | custom-call | flops 2000000000 | tf_op jit(solution)/shard_map/fine_backward/pallas_call | solution.py:23
  38.6 0.1 collective-permute-start.10
  38.7 1.3 %feature_step.1 = bf16[16,64,128]{2,1,0:T(8,128)(2,1)} custom-call(bf16[18,64,384]{2,1,0:T(8,128)(2,1)S(1)} %get-tuple-element.102.first3, bf16[256,1536]{1,0:T(8,128)(2,1)S(1)} %get-tuple-element.103.back_w), custom_call_target="tpu_custom_call" | custom-call | flops 1000000000 | tf_op jit(solution)/shard_map/feature_step/pallas_call | solution.py:23
  40.0 0.2 collective-permute-done.10.got_f
  40.2 0.1 scatter_core.1
  40.4 17.4 %all_to_all.20.got = bf16[8,304,128]{2,1,0:T(8,128)(2,1)S(1)} all-to-all(bf16[8,304,128]{2,1,0:T(8,128)(2,1)S(1)} %scatter_core.1), channel_id=1, replica_groups={{0,32,64,96,128,160,192,224},{16,48,80,112,144,176,208,240},{1,33,65,97..., dimensions={0} | all-to-all | bytes 1245184 | tf_op jit(solution)/shard_map/all_to_all | solution.py:524
  57.8 0.1 scatter_row.1
  57.9 19.7 %all_to_all.21.got = bf16[16,32,128]{2,1,0:T(8,128)(2,1)S(1)} all-to-all(bf16[16,32,128]{2,1,0:T(8,128)(2,1)S(1)} %scatter_row.1), channel_id=1, replica_groups=mesh['row'=16,'col'=16] {'col'}, dimensions={0} | all-to-all | bytes 262144 | tf_op jit(solution)/shard_map/all_to_all | solution.py:528
  77.7 10.5 %all_to_all.22.got = bf16[16,32,128]{2,1,0:T(8,128)(2,1)S(1)} all-to-all(bf16[16,32,128]{2,1,0:T(8,128)(2,1)S(1)} %scatter_column.1), channel_id=1, replica_groups=mesh['row'=16,'col'=16] {'col'}, dimensions={0} | all-to-all | bytes 262144 | tf_op jit(solution)/shard_map/all_to_all | solution.py:528
  88.1 0.7 gather_column.1
  88.8 10.5 %all_to_all.23.mine = bf16[8,144,128]{2,1,0:T(8,128)(2,1)S(1)} all-to-all(bf16[8,144,128]{2,1,0:T(8,128)(2,1)S(1)} %get-tuple-element.105), channel_id=1, replica_groups={{0,32,64,96,128,160,192,224},{16,48,80,112,144,176,208,240},{1,33,65,97..., dimensions={0} | all-to-all | bytes 589824 | tf_op jit(solution)/shard_map/all_to_all | solution.py:524
  99.3 5.4 %collective-permute-start.11 = (bf16[8,144,128]{2,1,0:T(8,128)(2,1)S(1)}, bf16[8,144,128]{2,1,0:T(8,128)(2,1)S(1)}, u32[]{:S(2)}, u32[]{:S(2)}) collective-permute-start(bf16[8,144,128]{2,1,0:T(8,128)(2,1)S(1)} %all_to_all.23.mine), channel_id=1, source_target_pairs={{0,16},{16,0},{32,48},{48,32},{64,80},{80,64},{96,112},{112,96},{1... | collective-permute-start | bytes 884744 | tf_op jit(solution)/shard_map/ppermute | solution.py:512
  104.7 0.9 blend.1
  105.6 0.3 collective-permute-done.11.other
  105.9 1.6 %finish.1 = (f32[8,144,128]{2,1,0:T(8,128)}, f32[8,144,128]{2,1,0:T(8,128)}) custom-call(s32[6]{0:T(128)S(1)} %stack.19.meta, bf16[8,144,128]{2,1,0:T(8,128)(2,1)S(1)} %all_to_all.23.mine, bf16[8,144,128]{2,1,0:T(8,128)(2,1)S(1)} %collective-permute-done.11.other), custom_call_target="tpu_custom_call" | custom-call | tf_op jit(solution)/shard_map/finish/pallas_call | solution.py:23
  (14 shorter events, 0.3 us)
Async XLA Ops:
  2.4 7.4 %collective-permute-start.2 = (bf16[160,128]{1,0:T(8,128)(2,1)S(1)}, bf16[160,128]{1,0:T(8,128)(2,1)S(1)}, u32[]{:S(2)}, u32[]{:S(2)}) collective-permute-start(bf16[160,128]{1,0:T(8,128)(2,1)S(1)} %get-tuple-element.60.refs_0_), channel_id=1, source_target_pairs={{0,128},{16,144},{32,160},{48,176},{64,192},{80,208},{96,224},{112... | collective-permute-start | bytes 122888 | tf_op jit(solution)/shard_map/ppermute | solution.py:512
  6.3 5.8 %collective-permute-start = (bf16[16,48,128]{2,1,0:T(8,128)(2,1)S(1)}, bf16[16,48,128]{2,1,0:T(8,128)(2,1)S(1)}, u32[]{:S(2)}, u32[]{:S(2)}) collective-permute-start(bf16[16,48,128]{2,1,0:T(8,128)(2,1)S(1)} %get-tuple-element.64), channel_id=1, source_target_pairs={{0,1},{1,0},{2,3},{3,2},{4,5},{5,4},{6,7},{7,6},{8,9},{9,8},{10,11... | collective-permute-start | bytes 589832 | tf_op jit(solution)/shard_map/ppermute | solution.py:512
  7.9 4.2 %collective-permute-start.1 = (bf16[16,48,128]{2,1,0:T(8,128)(2,1)S(1)}, bf16[16,48,128]{2,1,0:T(8,128)(2,1)S(1)}, u32[]{:S(2)}, u32[]{:S(2)}) collective-permute-start(bf16[16,48,128]{2,1,0:T(8,128)(2,1)S(1)} %get-tuple-element.65), channel_id=1, source_target_pairs={{1,2},{2,1},{3,4},{4,3},{5,6},{6,5},{7,8},{8,7},{9,10},{10,9},{11,... | collective-permute-start | bytes 589832 | tf_op jit(solution)/shard_map/ppermute | solution.py:518
  12.7 15.3 %collective-permute-start.3 = (bf16[1408,128]{1,0:T(8,128)(2,1)S(1)}, bf16[1408,128]{1,0:T(8,128)(2,1)S(1)}, u32[]{:S(2)}, u32[]{:S(2)}) collective-permute-start(bf16[1408,128]{1,0:T(8,128)(2,1)S(1)} %get-tuple-element.68), channel_id=1, source_target_pairs={{0,16},{16,0},{32,48},{48,32},{64,80},{80,64},{96,112},{112,96},{1... | collective-permute-start | bytes 1081352 | tf_op jit(solution)/shard_map/ppermute | solution.py:512
  14.5 13.6 %collective-permute-start.4 = (bf16[1408,128]{1,0:T(8,128)(2,1)S(1)}, bf16[1408,128]{1,0:T(8,128)(2,1)S(1)}, u32[]{:S(2)}, u32[]{:S(2)}) collective-permute-start(bf16[1408,128]{1,0:T(8,128)(2,1)S(1)} %get-tuple-element.69), channel_id=1, source_target_pairs={{16,32},{32,16},{48,64},{64,48},{80,96},{96,80},{112,128},{128,112... | collective-permute-start | bytes 1081352 | tf_op jit(solution)/shard_map/ppermute | solution.py:518
  17.5 10.4 %collective-permute-start.7 = (bf16[2,160,128]{2,1,0:T(8,128)(2,1)S(1)}, bf16[2,160,128]{2,1,0:T(8,128)(2,1)S(1)}, u32[]{:S(2)}, u32[]{:S(2)}) collective-permute-start(bf16[2,160,128]{2,1,0:T(8,128)(2,1)S(1)} %stack_two.1.refs_0_.near0), channel_id=1, source_target_pairs={{0,96},{16,112},{32,64},{48,80},{64,32},{80,48},{96,0},{112,16},{1... | collective-permute-start | bytes 245768 | tf_op jit(solution)/shard_map/ppermute | solution.py:512
  19.7 8.2 %collective-permute-start.6 = (bf16[2,160,128]{2,1,0:T(8,128)(2,1)S(1)}, bf16[2,160,128]{2,1,0:T(8,128)(2,1)S(1)}, u32[]{:S(2)}, u32[]{:S(2)}) collective-permute-start(bf16[2,160,128]{2,1,0:T(8,128)(2,1)S(1)} %stack_two.1.refs_0_.near0), channel_id=1, source_target_pairs={{0,64},{16,80},{32,96},{48,112},{64,0},{80,16},{96,32},{112,48},{1... | collective-permute-start | bytes 245768 | tf_op jit(solution)/shard_map/ppermute | solution.py:512
  20.6 7.3 %collective-permute-start.5 = (bf16[2,160,128]{2,1,0:T(8,128)(2,1)S(1)}, bf16[2,160,128]{2,1,0:T(8,128)(2,1)S(1)}, u32[]{:S(2)}, u32[]{:S(2)}) collective-permute-start(bf16[2,160,128]{2,1,0:T(8,128)(2,1)S(1)} %stack_two.1.refs_0_.near0), channel_id=1, source_target_pairs={{0,32},{16,48},{32,0},{48,16},{64,96},{80,112},{96,64},{112,80},{1... | collective-permute-start | bytes 245768 | tf_op jit(solution)/shard_map/ppermute | solution.py:512
  28.0 3.6 %collective-permute-start.8 = (bf16[4,2,160,128]{3,2,1,0:T(8,128)(2,1)S(1)}, bf16[4,2,160,128]{3,2,1,0:T(8,128)(2,1)S(1)}, u32[]{:S(2)}, u32[]{:S(2)}) collective-permute-start(bf16[4,2,160,128]{3,2,1,0:T(8,128)(2,1)S(1)} %stack_eight.1), channel_id=1, source_target_pairs={{0,16},{16,0},{32,48},{48,32},{64,80},{80,64},{96,112},{112,96},{1... | collective-permute-start | bytes 983048 | tf_op jit(solution)/shard_map/ppermute | solution.py:512
  35.1 5.1 %collective-permute-start.9 = (bf16[8,160,128]{2,1,0:T(8,128)(2,1)S(1)}, bf16[8,160,128]{2,1,0:T(8,128)(2,1)S(1)}, u32[]{:S(2)}, u32[]{:S(2)}) collective-permute-start(bf16[8,160,128]{2,1,0:T(8,128)(2,1)S(1)} %get-tuple-element.100), channel_id=1, source_target_pairs={{0,16},{16,0},{32,48},{48,32},{64,80},{80,64},{96,112},{112,96},{1... | collective-permute-start | bytes 983048 | tf_op jit(solution)/shard_map/ppermute | solution.py:512
  38.6 1.7 %collective-permute-start.10 = (bf16[8,144,128]{2,1,0:T(8,128)(2,1)S(1)}, bf16[8,144,128]{2,1,0:T(8,128)(2,1)S(1)}, u32[]{:S(2)}, u32[]{:S(2)}) collective-permute-start(bf16[8,144,128]{2,1,0:T(8,128)(2,1)S(1)} %get-tuple-element.101), channel_id=1, source_target_pairs={{0,16},{16,0},{32,48},{48,32},{64,80},{80,64},{96,112},{112,96},{1... | collective-permute-start | bytes 884744 | tf_op jit(solution)/shard_map/ppermute | solution.py:512
  99.3 6.6 %collective-permute-start.11 = (bf16[8,144,128]{2,1,0:T(8,128)(2,1)S(1)}, bf16[8,144,128]{2,1,0:T(8,128)(2,1)S(1)}, u32[]{:S(2)}, u32[]{:S(2)}) collective-permute-start(bf16[8,144,128]{2,1,0:T(8,128)(2,1)S(1)} %all_to_all.23.mine), channel_id=1, source_target_pairs={{0,16},{16,0},{32,48},{48,32},{64,80},{80,64},{96,112},{112,96},{1... | collective-permute-start | bytes 884744 | tf_op jit(solution)/shard_map/ppermute | solution.py:512

commit v9 on v8

--- a/solution.py
+++ b/solution.py
@@ -162,20 +162,27 @@
     return value if count == 1 else value.reshape(count, 96, CH)
 
 
-def prepare_kernel(feat_far, cot_far, w1_far, w2_far, feat, cot, weight1, weight2, back1, back2, w1, w2, done):
-    pairs = ((w1_far, w1), (w2_far, w2), (feat_far, feat), (cot_far, cot))
-    copies = [pltpu.make_async_copy(a, b, done.at[k]) for k, (a, b) in enumerate(pairs)]
+def bring_kernel(feat_far, cot_far, feat, cot, done):
+    copies = [
+        pltpu.make_async_copy(a, b, done.at[k]) for k, (a, b) in enumerate(((feat_far, feat), (cot_far, cot)))
+    ]
     for copy in copies:
         copy.start()
-    for k, (w, weight, back) in enumerate(((w1, weight1, back1), (w2, weight2, back2))):
-        copies[k].wait()
+    for copy in copies:
+        copy.wait()
+
+
+def weights_kernel(w1_far, w2_far, weight1, weight2, back1, back2, w1, w2, done):
+    copies = [pltpu.make_async_copy(a, b, done.at[k]) for k, (a, b) in enumerate(((w1_far, w1), (w2_far, w2)))]
+    for copy in copies:
+        copy.start()
+    for copy, w, weight, back in zip(copies, (w1, w2), (weight1, weight2), (back1, back2)):
+        copy.wait()
         weight[...] = paired(w[...], 0)
         back[...] = paired(flipped(w), 1)
-    for copy in copies[2:]:
-        copy.wait()
-
-
-def pack_rows_kernel(meta, feat, cot, pair, other, inner, outer):
+
+
+def pack_rows_kernel(meta, feat, cot, pair, other, own, far, inner, outer, both):
     core = meta[4] % 2
     for low, out in ((1 - core, inner), (core, outer)):
         jobs = [(128 * k, feat, 8 * low + k, 0, 32) for k in range(8)]
@@ -185,6 +192,8 @@
             out[base : base + width, :] = before
             out[base + width : base + width + 64, :] = middle[row]
             out[base + width + 64 : base + 2 * width + 64, :] = after
+    both[0] = own[...]
+    both[1] = far[...]
 
 
 def stack_kernel(*refs):
@@ -556,22 +565,34 @@
     )
     w1, w2 = (conv_first.reshape(1152, CH), conv_second.reshape(1152, CH))
     big, wide = (((16, 64, CH), BF), ((1536, 256), BF))
-    feat_in, cot_in, weight1, weight2, back1, back2 = call(
-        prepare_kernel,
-        "prepare",
-        (big, big, wide, wide, ((256, 1536), BF), ((256, 1536), BF)),
-        (after_all(feat, own), cot, w1, w2),
-        (((1152, CH), BF), ((1152, CH), BF), pltpu.SemaphoreType.DMA((4,))),
-        far=(0, 1, 2, 3),
+    feat_in, cot_in = call(
+        bring_kernel,
+        "bring",
+        (big, big),
+        (after_all(feat, own), cot),
+        (pltpu.SemaphoreType.DMA((2,)),),
+        far=(0, 1),
+        flops=4 * 10**9,
+    )
+    own_far = swap(after_all(own, feat_in), "row", 8)
+    weight1, weight2, back1, back2 = call(
+        weights_kernel,
+        "weights",
+        (wide, wide, ((256, 1536), BF), ((256, 1536), BF)),
+        (after_all(w1, feat_in), w2),
+        (((1152, CH), BF), ((1152, CH), BF), pltpu.SemaphoreType.DMA((2,))),
+        far=(0, 1),
         flops=4 * 10**9,
     )
     pair = swap(pair, "col", 1)
     other = swap_outer(other, "col")
-    near0 = call(stack_kernel, "stack_two", (((2, 160, CH), BF),), (own, swap(own, "row", 8)))[0]
-    inner, outer = call(
-        pack_rows_kernel, "pack_rows", (((EDGE, CH), BF),) * 2, (meta, feat_in, cot_in, pair, other)
-    )
-    inner, outer, near0 = lax.optimization_barrier((inner, outer, near0))
+    edge = ((EDGE, CH), BF)
+    inner, outer, near0 = call(
+        pack_rows_kernel,
+        "pack_rows",
+        (edge, edge, ((2, 160, CH), BF)),
+        (meta, feat_in, cot_in, pair, after_all(other, weight1), own, own_far),
+    )
     inner = swap(inner, "row", 1)
     outer = swap_outer(outer, "row")
     pair_in = after_all(pair, near0)

time: 108 us -> 107 us (level)
  starting transfers between devices: 20.6 us -> 26.9 us
  blocking collectives: 58.1 us -> 52 us
  waiting for transfers between devices: 6.24 us -> 3.79 us
  Pallas kernels: 21.7 us -> 22.8 us
    ppermute x10, starting transfers between devices: 16.9 us -> 23.2 us  [swap(): return lax.ppermute(value, axis, [(i, i ^ mask) for i in range(count)])]
    all_to_all x2, blocking collectives: 30.2 us -> 24.4 us  [exchange_column(): return lax.all_to_all(value, 'col', 0, 0, tiled=True)]
    ppermute x10, waiting for transfers between devices: 6.23 us -> 3.79 us  [swap(): return lax.ppermute(value, axis, [(i, i ^ mask) for i in range(count)])]
  transfers between devices with their start and end apart: 12 -> 12, of which waited for: 4 -> 4; matrix products, arithmetic and copies ran while one was open for 0% -> 0% of each run, Pallas kernels for 12% -> 13%
where the time goes in v9:
time: 107 us; the launch traced here: 106 us
  blocking collectives  52 us (49%)
  starting transfers between devices  26.9 us (25%)
  Pallas kernels  22.8 us (21%)
  waiting for transfers between devices  3.79 us (4%)
    all_to_all x2, blocking collectives, exchange_row(): lax.all_to_all(value, 'row', 0, 0, axis_index_groups=groups, tiled=True)  27.6 us
    all_to_all x2, blocking collectives, exchange_column(): return lax.all_to_all(value, 'col', 0, 0, tiled=True)  24.4 us
    ppermute x10, starting transfers between devices, swap(): return lax.ppermute(value, axis, [(i, i ^ mask) for i in range(count)])  23.2 us
    pallas_call x16, Pallas kernels, call(): pl.pallas_call(kernel, name=name, out_shape=shapes, in_specs=[HBM if k in...  22.8 us
    ppermute x10, waiting for transfers between devices, swap(): return lax.ppermute(value, axis, [(i, i ^ mask) for i in range(count)])  3.79 us
    ppermute x2, starting transfers between devices, swap_outer(): return lax.ppermute(value, axis, pairs)  3.68 us
  transfers between devices with their start and end apart: 12, of which 4 were waited for; matrix products, arithmetic and copies ran while one was open for 0% of the time, Pallas kernels for 13%

profile of v9, /device:TPU:1, one launch (start us, length us, event | category | flops | bytes accessed | tf_op | source)
XLA Modules:
  0.0 106.3 jit_solution(15574980480508845894)
XLA Ops:
  0.7 1.7 %pack_columns.1 = (bf16[16,48,128]{2,1,0:T(8,128)(2,1)S(1)}, bf16[16,48,128]{2,1,0:T(8,128)(2,1)S(1)}, bf16[160,128]{1,0:T(8,128)(2,1)S(1)}) custom-call(s32[6]{0:T(128)S(1)} %stack.19.meta, bf16[16,64,128]{2,1,0:T(8,128)(2,1)} %bitcast.18, bf16[16,64,128]{2,1,0:T(8,128)(2,1)} %bitcast.20, bf16[9,16,128]{2,1,0:T(8,128)(2,1)} %bitcast.22, bf16[16,128]{1,0:T(8,128)(2,1)} %proj.1), custom_call_target="tpu_custom_call" | custom-call | tf_op jit(solution)/shard_map/pack_columns/pallas_call | solution.py:23
  2.4 2.6 %collective-permute-start = (bf16[16,48,128]{2,1,0:T(8,128)(2,1)S(1)}, bf16[16,48,128]{2,1,0:T(8,128)(2,1)S(1)}, u32[]{:S(2)}, u32[]{:S(2)}) collective-permute-start(bf16[16,48,128]{2,1,0:T(8,128)(2,1)S(1)} %get-tuple-element.65), channel_id=1, source_target_pairs={{0,1},{1,0},{2,3},{3,2},{4,5},{5,4},{6,7},{7,6},{8,9},{9,8},{10,11... | collective-permute-start | bytes 589832 | tf_op jit(solution)/shard_map/ppermute | solution.py:521
  5.0 0.7 collective-permute-start.1
  5.7 1.0 bring.1
  6.7 3.0 %collective-permute-start.2 = (bf16[160,128]{1,0:T(8,128)(2,1)S(1)}, bf16[160,128]{1,0:T(8,128)(2,1)S(1)}, u32[]{:S(2)}, u32[]{:S(2)}) collective-permute-start(bf16[160,128]{1,0:T(8,128)(2,1)S(1)} %get-tuple-element.70.own), channel_id=1, source_target_pairs={{0,128},{16,144},{32,160},{48,176},{64,192},{80,208},{96,224},{112... | collective-permute-start | bytes 122888 | tf_op jit(solution)/shard_map/ppermute | solution.py:521
  9.7 1.2 %weights.1 = (bf16[1536,256]{1,0:T(8,128)(2,1)S(1)}, bf16[1536,256]{1,0:T(8,128)(2,1)S(1)}, bf16[256,1536]{1,0:T(8,128)(2,1)S(1)}, bf16[256,1536]{1,0:T(8,128)(2,1)S(1)}) custom-call(bf16[1152,128]{1,0:T(8,128)(2,1)} %bitcast.25, bf16[1152,128]{1,0:T(8,128)(2,1)} %bitcast.26), custom_call_target="tpu_custom_call" | custom-call | flops 4000000000 | tf_op jit(solution)/shard_map/weights/pallas_call | solution.py:23
  11.0 0.2 collective-permute-done.2.far
  11.2 0.6 pack_rows.1
  11.8 5.6 %collective-permute-start.3 = (bf16[1408,128]{1,0:T(8,128)(2,1)S(1)}, bf16[1408,128]{1,0:T(8,128)(2,1)S(1)}, u32[]{:S(2)}, u32[]{:S(2)}) collective-permute-start(bf16[1408,128]{1,0:T(8,128)(2,1)S(1)} %get-tuple-element.71), channel_id=1, source_target_pairs={{0,16},{16,0},{32,48},{48,32},{64,80},{80,64},{96,112},{112,96},{1... | collective-permute-start | bytes 1081352 | tf_op jit(solution)/shard_map/ppermute | solution.py:521
  17.4 3.0 %collective-permute-start.4 = (bf16[1408,128]{1,0:T(8,128)(2,1)S(1)}, bf16[1408,128]{1,0:T(8,128)(2,1)S(1)}, u32[]{:S(2)}, u32[]{:S(2)}) collective-permute-start(bf16[1408,128]{1,0:T(8,128)(2,1)S(1)} %get-tuple-element.72), channel_id=1, source_target_pairs={{16,32},{32,16},{48,64},{64,48},{80,96},{96,80},{112,128},{128,112... | collective-permute-start | bytes 1081352 | tf_op jit(solution)/shard_map/ppermute | solution.py:527
  20.5 4.9 %collective-permute-start.7 = (bf16[2,160,128]{2,1,0:T(8,128)(2,1)S(1)}, bf16[2,160,128]{2,1,0:T(8,128)(2,1)S(1)}, u32[]{:S(2)}, u32[]{:S(2)}) collective-permute-start(bf16[2,160,128]{2,1,0:T(8,128)(2,1)S(1)} %get-tuple-element.89.refs_0_.near0), channel_id=1, source_target_pairs={{0,96},{16,112},{32,64},{48,80},{64,32},{80,48},{96,0},{112,16},{1... | collective-permute-start | bytes 245768 | tf_op jit(solution)/shard_map/ppermute | solution.py:521
  25.4 0.7 collective-permute-start.5
  26.1 3.6 %forward_inner.1 = (bf16[16,128,384]{2,1,0:T(8,128)(2,1)S(1)}, bf16[14,128,384]{2,1,0:T(8,128)(2,1)S(1)}, f32[14,96,128]{2,1,0:T(8,128)S(1)}, bf16[6,64,384]{2,1...) custom-call(s32[6]{0:T(128)S(1)} %stack.19.meta, ...), custom_call_target="tpu_custom_call" | custom-call | tf_op jit(solution)/shard_map/forward_inner/pallas_call | solution.py:23
  29.7 3.0 %collective-permute-done.7.refs_3_.near3 = bf16[2,160,128]{2,1,0:T(8,128)(2,1)S(1)} collective-permute-done((bf16[2,160,128]{2,1,0:T(8,128)(2,1)S(1)}, bf16[2,160,128]{2,1,0:T(8,128)(2,1)S(1)}, u32[]{:S(2)}, u32[]{:S(2)}) %collective-permute-start.7) | collective-permute-done | bytes 81952 | tf_op jit(solution)/shard_map/ppermute | solution.py:521
  32.9 3.5 %forward_outer.1 = (bf16[14,64,384]{2,1,0:T(8,128)(2,1)S(1)}, f32[18,96,128]{2,1,0:T(8,128)S(1)}, f32[20,96,128]{2,1,0:T(8,128)S(1)}, bf16[16,64,128]{2,1,0:T(8,...) custom-call(s32[6]{0:T(128)S(1)} %stack.19.meta, ...), custom_call_target="tpu_custom_call" | custom-call | flops 4000000000 | tf_op jit(solution)/shard_map/forward_outer/pallas_call | solution.py:23
  36.4 3.6 %coarse_step.1 = (bf16[256,256]{1,0:T(8,128)(2,1)S(1)}, bf16[256,128]{1,0:T(8,128)(2,1)S(1)}, bf16[8,160,128]{2,1,0:T(8,128)(2,1)S(1)}, bf16[8,160,128]{2,1,0:T(8,128)(2,1)S(1)}, f32[10,48,128]{2,1,0:T(8,128)S(1)}) custom-call(s32[6]{0:T(128)S(1)} %stack.19.meta, bf16[14,64,384]{2,1,0:T(8,128)(2,1)S(1)} %get-tuple-element.88.pool3, ...), custom_call_target="tpu_custom_call" | custom-call | flops 2000000000 | tf_op jit(solution)/shard_map/coarse_step/pallas_call | solution.py:23
  40.0 0.7 collective-permute-start.9
  40.7 2.7 %fine_backward.1 = (bf16[8,144,128]{2,1,0:T(8,128)(2,1)S(1)}, bf16[8,144,128]{2,1,0:T(8,128)(2,1)S(1)}, bf16[18,64,384]{2,1,0:T(8,128)(2,1)S(1)}) custom-call(s32[6]{0:T(128)S(1)} %stack.19.meta, f32[10,48,128]{2,1,0:T(8,128)S(1)} %get-tuple-element.95.pooled_grad, bf16[16,64,128]{2,1,0:T(8,128)(2,1)S(1)} %get-tuple-element.64.cot, ...), custom_call_target="tpu_custom_call" | custom-call | flops 2000000000 | tf_op jit(solution)/shard_map/fine_backward/pallas_call | solution.py:23
  43.4 0.1 collective-permute-start.10
  43.6 1.3 %feature_step.1 = bf16[16,64,128]{2,1,0:T(8,128)(2,1)} custom-call(bf16[18,64,384]{2,1,0:T(8,128)(2,1)S(1)} %get-tuple-element.104.first3, bf16[256,1536]{1,0:T(8,128)(2,1)S(1)} %get-tuple-element.105.back_w), custom_call_target="tpu_custom_call" | custom-call | flops 1000000000 | tf_op jit(solution)/shard_map/feature_step/pallas_call | solution.py:23
  44.9 0.2 collective-permute-done.10.got_f
  45.1 0.1 scatter_core.1
  45.3 17.1 %all_to_all.20.got = bf16[8,304,128]{2,1,0:T(8,128)(2,1)S(1)} all-to-all(bf16[8,304,128]{2,1,0:T(8,128)(2,1)S(1)} %scatter_core.1), channel_id=1, replica_groups={{0,32,64,96,128,160,192,224},{16,48,80,112,144,176,208,240},{1,33,65,97..., dimensions={0} | all-to-all | bytes 1245184 | tf_op jit(solution)/shard_map/all_to_all | solution.py:533
  62.4 0.1 scatter_row.1
  62.5 13.9 %all_to_all.21.got = bf16[16,32,128]{2,1,0:T(8,128)(2,1)S(1)} all-to-all(bf16[16,32,128]{2,1,0:T(8,128)(2,1)S(1)} %scatter_row.1), channel_id=1, replica_groups=mesh['row'=16,'col'=16] {'col'}, dimensions={0} | all-to-all | bytes 262144 | tf_op jit(solution)/shard_map/all_to_all | solution.py:537
  76.4 10.5 %all_to_all.22.got = bf16[16,32,128]{2,1,0:T(8,128)(2,1)S(1)} all-to-all(bf16[16,32,128]{2,1,0:T(8,128)(2,1)S(1)} %scatter_column.1), channel_id=1, replica_groups=mesh['row'=16,'col'=16] {'col'}, dimensions={0} | all-to-all | bytes 262144 | tf_op jit(solution)/shard_map/all_to_all | solution.py:537
  86.9 0.7 gather_column.1
  87.6 10.5 %all_to_all.23.mine = bf16[8,144,128]{2,1,0:T(8,128)(2,1)S(1)} all-to-all(bf16[8,144,128]{2,1,0:T(8,128)(2,1)S(1)} %get-tuple-element.107), channel_id=1, replica_groups={{0,32,64,96,128,160,192,224},{16,48,80,112,144,176,208,240},{1,33,65,97..., dimensions={0} | all-to-all | bytes 589824 | tf_op jit(solution)/shard_map/all_to_all | solution.py:533
  98.1 5.4 %collective-permute-start.11 = (bf16[8,144,128]{2,1,0:T(8,128)(2,1)S(1)}, bf16[8,144,128]{2,1,0:T(8,128)(2,1)S(1)}, u32[]{:S(2)}, u32[]{:S(2)}) collective-permute-start(bf16[8,144,128]{2,1,0:T(8,128)(2,1)S(1)} %all_to_all.23.mine), channel_id=1, source_target_pairs={{0,16},{16,0},{32,48},{48,32},{64,80},{80,64},{96,112},{112,96},{1... | collective-permute-start | bytes 884744 | tf_op jit(solution)/shard_map/ppermute | solution.py:521
  103.5 0.9 blend.1
  104.4 0.3 collective-permute-done.11.other
  104.7 1.6 %finish.1 = (f32[8,144,128]{2,1,0:T(8,128)}, f32[8,144,128]{2,1,0:T(8,128)}) custom-call(s32[6]{0:T(128)S(1)} %stack.19.meta, bf16[8,144,128]{2,1,0:T(8,128)(2,1)S(1)} %all_to_all.23.mine, bf16[8,144,128]{2,1,0:T(8,128)(2,1)S(1)} %collective-permute-done.11.other), custom_call_target="tpu_custom_call" | custom-call | tf_op jit(solution)/shard_map/finish/pallas_call | solution.py:23
  (14 shorter events, 0.3 us)
Async XLA Ops:
  2.4 8.7 %collective-permute-start = (bf16[16,48,128]{2,1,0:T(8,128)(2,1)S(1)}, bf16[16,48,128]{2,1,0:T(8,128)(2,1)S(1)}, u32[]{:S(2)}, u32[]{:S(2)}) collective-permute-start(bf16[16,48,128]{2,1,0:T(8,128)(2,1)S(1)} %get-tuple-element.65), channel_id=1, source_target_pairs={{0,1},{1,0},{2,3},{3,2},{4,5},{5,4},{6,7},{7,6},{8,9},{9,8},{10,11... | collective-permute-start | bytes 589832 | tf_op jit(solution)/shard_map/ppermute | solution.py:521
  5.0 6.0 %collective-permute-start.1 = (bf16[16,48,128]{2,1,0:T(8,128)(2,1)S(1)}, bf16[16,48,128]{2,1,0:T(8,128)(2,1)S(1)}, u32[]{:S(2)}, u32[]{:S(2)}) collective-permute-start(bf16[16,48,128]{2,1,0:T(8,128)(2,1)S(1)} %get-tuple-element.66), channel_id=1, source_target_pairs={{1,2},{2,1},{3,4},{4,3},{5,6},{6,5},{7,8},{8,7},{9,10},{10,9},{11,... | collective-permute-start | bytes 589832 | tf_op jit(solution)/shard_map/ppermute | solution.py:527
  6.7 4.4 %collective-permute-start.2 = (bf16[160,128]{1,0:T(8,128)(2,1)S(1)}, bf16[160,128]{1,0:T(8,128)(2,1)S(1)}, u32[]{:S(2)}, u32[]{:S(2)}) collective-permute-start(bf16[160,128]{1,0:T(8,128)(2,1)S(1)} %get-tuple-element.70.own), channel_id=1, source_target_pairs={{0,128},{16,144},{32,160},{48,176},{64,192},{80,208},{96,224},{112... | collective-permute-start | bytes 122888 | tf_op jit(solution)/shard_map/ppermute | solution.py:521
  11.8 21.1 %collective-permute-start.3 = (bf16[1408,128]{1,0:T(8,128)(2,1)S(1)}, bf16[1408,128]{1,0:T(8,128)(2,1)S(1)}, u32[]{:S(2)}, u32[]{:S(2)}) collective-permute-start(bf16[1408,128]{1,0:T(8,128)(2,1)S(1)} %get-tuple-element.71), channel_id=1, source_target_pairs={{0,16},{16,0},{32,48},{48,32},{64,80},{80,64},{96,112},{112,96},{1... | collective-permute-start | bytes 1081352 | tf_op jit(solution)/shard_map/ppermute | solution.py:521
  17.4 15.5 %collective-permute-start.4 = (bf16[1408,128]{1,0:T(8,128)(2,1)S(1)}, bf16[1408,128]{1,0:T(8,128)(2,1)S(1)}, u32[]{:S(2)}, u32[]{:S(2)}) collective-permute-start(bf16[1408,128]{1,0:T(8,128)(2,1)S(1)} %get-tuple-element.72), channel_id=1, source_target_pairs={{16,32},{32,16},{48,64},{64,48},{80,96},{96,80},{112,128},{128,112... | collective-permute-start | bytes 1081352 | tf_op jit(solution)/shard_map/ppermute | solution.py:527
  20.5 12.3 %collective-permute-start.7 = (bf16[2,160,128]{2,1,0:T(8,128)(2,1)S(1)}, bf16[2,160,128]{2,1,0:T(8,128)(2,1)S(1)}, u32[]{:S(2)}, u32[]{:S(2)}) collective-permute-start(bf16[2,160,128]{2,1,0:T(8,128)(2,1)S(1)} %get-tuple-element.89.refs_0_.near0), channel_id=1, source_target_pairs={{0,96},{16,112},{32,64},{48,80},{64,32},{80,48},{96,0},{112,16},{1... | collective-permute-start | bytes 245768 | tf_op jit(solution)/shard_map/ppermute | solution.py:521
  25.4 7.3 %collective-permute-start.6 = (bf16[2,160,128]{2,1,0:T(8,128)(2,1)S(1)}, bf16[2,160,128]{2,1,0:T(8,128)(2,1)S(1)}, u32[]{:S(2)}, u32[]{:S(2)}) collective-permute-start(bf16[2,160,128]{2,1,0:T(8,128)(2,1)S(1)} %get-tuple-element.89.refs_0_.near0), channel_id=1, source_target_pairs={{0,64},{16,80},{32,96},{48,112},{64,0},{80,16},{96,32},{112,48},{1... | collective-permute-start | bytes 245768 | tf_op jit(solution)/shard_map/ppermute | solution.py:521
  25.4 7.3 %collective-permute-start.5 = (bf16[2,160,128]{2,1,0:T(8,128)(2,1)S(1)}, bf16[2,160,128]{2,1,0:T(8,128)(2,1)S(1)}, u32[]{:S(2)}, u32[]{:S(2)}) collective-permute-start(bf16[2,160,128]{2,1,0:T(8,128)(2,1)S(1)} %get-tuple-element.89.refs_0_.near0), channel_id=1, source_target_pairs={{0,32},{16,48},{32,0},{48,16},{64,96},{80,112},{96,64},{112,80},{1... | collective-permute-start | bytes 245768 | tf_op jit(solution)/shard_map/ppermute | solution.py:521
  32.8 3.6 %collective-permute-start.8 = (bf16[4,2,160,128]{3,2,1,0:T(8,128)(2,1)S(1)}, bf16[4,2,160,128]{3,2,1,0:T(8,128)(2,1)S(1)}, u32[]{:S(2)}, u32[]{:S(2)}) collective-permute-start(bf16[4,2,160,128]{3,2,1,0:T(8,128)(2,1)S(1)} %stack_eight.1), channel_id=1, source_target_pairs={{0,16},{16,0},{32,48},{48,32},{64,80},{80,64},{96,112},{112,96},{1... | collective-permute-start | bytes 983048 | tf_op jit(solution)/shard_map/ppermute | solution.py:521
  40.0 5.1 %collective-permute-start.9 = (bf16[8,160,128]{2,1,0:T(8,128)(2,1)S(1)}, bf16[8,160,128]{2,1,0:T(8,128)(2,1)S(1)}, u32[]{:S(2)}, u32[]{:S(2)}) collective-permute-start(bf16[8,160,128]{2,1,0:T(8,128)(2,1)S(1)} %get-tuple-element.102), channel_id=1, source_target_pairs={{0,16},{16,0},{32,48},{48,32},{64,80},{80,64},{96,112},{112,96},{1... | collective-permute-start | bytes 983048 | tf_op jit(solution)/shard_map/ppermute | solution.py:521
  43.4 1.7 %collective-permute-start.10 = (bf16[8,144,128]{2,1,0:T(8,128)(2,1)S(1)}, bf16[8,144,128]{2,1,0:T(8,128)(2,1)S(1)}, u32[]{:S(2)}, u32[]{:S(2)}) collective-permute-start(bf16[8,144,128]{2,1,0:T(8,128)(2,1)S(1)} %get-tuple-element.103), channel_id=1, source_target_pairs={{0,16},{16,0},{32,48},{48,32},{64,80},{80,64},{96,112},{112,96},{1... | collective-permute-start | bytes 884744 | tf_op jit(solution)/shard_map/ppermute | solution.py:521
  98.1 6.6 %collective-permute-start.11 = (bf16[8,144,128]{2,1,0:T(8,128)(2,1)S(1)}, bf16[8,144,128]{2,1,0:T(8,128)(2,1)S(1)}, u32[]{:S(2)}, u32[]{:S(2)}) collective-permute-start(bf16[8,144,128]{2,1,0:T(8,128)(2,1)S(1)} %all_to_all.23.mine), channel_id=1, source_target_pairs={{0,16},{16,0},{32,48},{48,32},{64,80},{80,64},{96,112},{112,96},{1... | collective-permute-start | bytes 884744 | tf_op jit(solution)/shard_map/ppermute | solution.py:521

commit v10 on v9

--- a/solution.py
+++ b/solution.py
@@ -17,7 +17,7 @@
 HBM = pl.BlockSpec(memory_space=pltpu.HBM)
 
 
-def call(kernel, name, outs, ins, scratch=(), limit=16, flops=0, moved=0, far=()):
+def call(kernel, name, outs, ins, scratch=(), limit=16, flops=0, moved=0, far=(), far_out=False):
     ins = [pltpu.with_memory_space_constraint(v, pltpu.HBM) if k in far else v for k, v in enumerate(ins)]
     shapes = tuple(jax.ShapeDtypeStruct(shape, dtype) for shape, dtype in outs)
     return pl.pallas_call(
@@ -25,7 +25,7 @@
         name=name,
         out_shape=shapes,
         in_specs=[HBM if k in far else SM if v.ndim == 1 else VM for k, v in enumerate(ins)],
-        out_specs=tuple(VM for _ in outs),
+        out_specs=tuple(HBM if far_out else VM for _ in outs),
         scratch_shapes=[pltpu.VMEM(*v) if isinstance(v, tuple) else v for v in scratch],
         compiler_params=pltpu.CompilerParams(vmem_limit_bytes=limit * MIB),
         cost_estimate=pl.CostEstimate(flops=flops, bytes_accessed=moved, transcendentals=0),
@@ -138,15 +138,14 @@
     return lax.select(even, other, pair), lax.select(even, pair, other)
 
 
-def pack_columns_kernel(meta, feat, cot, conv, proj, pair, other, weights, done):
+def pack_columns_kernel(meta, feat, cot, pair, other, done):
     odd = meta[5] % 2
     pairs = [
         (feat.at[:, aligned(32 - 32 * odd, 32), :], pair.at[:, 0:32, :]),
         (cot.at[:, aligned(48 - 48 * odd, 16), :], pair.at[:, 32:48, :]),
         (feat.at[:, aligned(32 * odd, 32), :], other.at[:, 0:32, :]),
         (cot.at[:, aligned(48 * odd, 16), :], other.at[:, 32:48, :]),
-        (proj, weights.at[144:160, :]),
-    ] + [(conv.at[t], weights.at[16 * t : 16 * t + 16, :]) for t in range(9)]
+    ]
     copies = [pltpu.make_async_copy(a, b, done.at[k]) for k, (a, b) in enumerate(pairs)]
     for copy in copies:
         copy.start()
@@ -162,10 +161,10 @@
     return value if count == 1 else value.reshape(count, 96, CH)
 
 
-def bring_kernel(feat_far, cot_far, feat, cot, done):
-    copies = [
-        pltpu.make_async_copy(a, b, done.at[k]) for k, (a, b) in enumerate(((feat_far, feat), (cot_far, cot)))
-    ]
+def bring_kernel(feat_far, cot_far, conv, proj, feat, cot, weights, done):
+    pairs = [(feat_far, feat), (cot_far, cot), (proj, weights.at[144:160, :])]
+    pairs += [(conv.at[t], weights.at[16 * t : 16 * t + 16, :]) for t in range(9)]
+    copies = [pltpu.make_async_copy(a, b, done.at[k]) for k, (a, b) in enumerate(pairs)]
     for copy in copies:
         copy.start()
     for copy in copies:
@@ -246,9 +245,8 @@
             act[h - 10 + e] = value[e][32:96]
 
 
-def outer_kernel(
-    meta, inner, outer, feat3i, act3i, slope1i, pool3i, slope2i, acti, weight1, weight2,
-    pool3, slope1, slope2, act, feat3o, act3o, feat3, act3,
+def outer_first_kernel(
+    meta, inner, outer, feat3i, act3i, slope1i, weight1, act3, slope1, feat3o, act3o, feat3
 ):
     below_at = 24 * (meta[4] % 2)
     for k in range(8):
@@ -262,6 +260,11 @@
                 slope1[h - 7] = slope_of(pre[16:112])
     slope1[2:16] = slope1i[...]
     act3[8:22] = act3i[...]
+    feat3o[...] = feat3[7:25, 32:96, :]
+    act3o[...] = act3[6:24, 32:96, :]
+
+
+def outer_second_kernel(meta, act3, pool3i, slope2i, acti, weight2, pool3, slope2, act):
     for starts in ([2, 4, 6, 8], [22, 24, 26, 28]):
         for h, (pre, value, small) in second_rows(meta, lambda h: act3[h - 1], starts, weight2[...]).items():
             pool3[h // 2 - 1] = small
@@ -273,8 +276,6 @@
     pool3[4:10] = pool3i[...]
     slope2[4:16] = slope2i[...]
     act[2:14] = acti[...]
-    feat3o[...] = feat3[7:25, 32:96, :]
-    act3o[...] = act3[6:24, 32:96, :]
 
 
 def inner_step(meta, feat, pair, other, weight1, weight2):
@@ -295,21 +296,25 @@
     )
 
 
-def outer_step(meta, inner, outer, parts, weight1, weight2):
+def outer_first_step(meta, inner, outer, feat3, act3, slope1, weight1):
     return call(
-        outer_kernel,
-        "forward_outer",
-        (
-            ((14, 64, 384), BF),
-            ((18, 96, CH), F32),
-            ((20, 96, CH), F32),
-            ((16, 64, CH), BF),
-            ((18, 64, 384), BF),
-            ((18, 64, 384), BF),
-        ),
-        (meta, inner, outer) + tuple(parts) + (weight1, weight2),
-        (((32, 128, 384), BF), ((30, 128, 384), BF)),
-        limit=24,
+        outer_first_kernel,
+        "outer_first",
+        (((30, 128, 384), BF), ((18, 96, CH), F32), ((18, 64, 384), BF), ((18, 64, 384), BF)),
+        (meta, inner, outer, feat3, act3, slope1, weight1),
+        (((32, 128, 384), BF),),
+        limit=20,
+        flops=2 * 10**9,
+    )
+
+
+def outer_second_step(meta, act3, pool3, slope2, act, weight2):
+    return call(
+        outer_second_kernel,
+        "outer_second",
+        (((14, 64, 384), BF), ((20, 96, CH), F32), ((16, 64, CH), BF)),
+        (meta, act3, pool3, slope2, act, weight2),
+        limit=16,
         flops=4 * 10**9,
     )
 
@@ -506,14 +511,20 @@
         fine[k] = value
 
 
-def finish_kernel(scale, meta, mine, other, first, second):
+def finish_kernel(scale, meta, mine, other, first, second, slabs, done):
     core = meta[4] % 2
+    copies = []
     for at in range(8):
         out = first if at < 4 else second
         a = mine[at].astype(F32) * scale
         b = other[at].astype(F32) * scale
-        out[2 * (at % 4)] = jnp.where(core == 0, a, b)
-        out[2 * (at % 4) + 1] = jnp.where(core == 0, b, a)
+        slabs[2 * at] = jnp.where(core == 0, a, b)
+        slabs[2 * at + 1] = jnp.where(core == 0, b, a)
+        pair = slabs.at[2 * at : 2 * at + 2]
+        copies.append(pltpu.make_async_copy(pair, out.at[2 * (at % 4) : 2 * (at % 4) + 2], done.at[at]))
+        copies[at].start()
+    for copy in copies:
+        copy.wait()
 
 
 def swap(value, axis, mask):
@@ -555,26 +566,26 @@
     slab = ((160, CH), BF)
 
     side = ((16, 48, CH), BF)
-    pair, other, own = call(
+    pair, other = call(
         pack_columns_kernel,
         "pack_columns",
-        (side, side, slab),
-        (meta, feat, cot, conv, coarse_proj),
-        (pltpu.SemaphoreType.DMA((14,)),),
-        far=(1, 2, 3, 4),
+        (side, side),
+        (meta, feat, cot),
+        (pltpu.SemaphoreType.DMA((4,)),),
+        far=(1, 2),
     )
     w1, w2 = (conv_first.reshape(1152, CH), conv_second.reshape(1152, CH))
     big, wide = (((16, 64, CH), BF), ((1536, 256), BF))
-    feat_in, cot_in = call(
+    feat_in, cot_in, own = call(
         bring_kernel,
         "bring",
-        (big, big),
-        (after_all(feat, own), cot),
-        (pltpu.SemaphoreType.DMA((2,)),),
-        far=(0, 1),
+        (big, big, slab),
+        (after_all(feat, pair), cot, conv, coarse_proj),
+        (pltpu.SemaphoreType.DMA((12,)),),
+        far=(0, 1, 2, 3),
         flops=4 * 10**9,
     )
-    own_far = swap(after_all(own, feat_in), "row", 8)
+    own_far = swap(own, "row", 8)
     weight1, weight2, back1, back2 = call(
         weights_kernel,
         "weights",
@@ -597,15 +608,16 @@
     outer = swap_outer(outer, "row")
     pair_in = after_all(pair, near0)
     near = [near0] + [swap(near0, "row", 2 * k) for k in range(1, 4)]
-    parts = inner_step(meta, feat_in, pair_in, other, weight1, weight2)
-    parts, near = lax.optimization_barrier((parts, near))
+    feat3, act3, slope1, pool3, slope2, act = inner_step(meta, feat_in, pair_in, other, weight1, weight2)
+    act3, slope1, feat3, act3o = outer_first_step(meta, inner, outer, feat3, act3, slope1, weight1)
+    near = list(lax.optimization_barrier((slope1, *near)))[1:]
     far = swap(call(stack_kernel, "stack_eight", (((4, 2, 160, CH), BF),), near)[0], "row", 1)
-    pool3, slope1, slope2, act, feat3, act3 = outer_step(meta, inner, outer, parts, weight1, weight2)
+    pool3, slope2, act = outer_second_step(meta, act3, pool3, slope2, act, weight2)
     halo = (pair, other, inner, outer)
     own_act, proj, keep_c, send_c, pooled_grad = coarse_step(meta, pool3, cot_in, halo, near, far)
     got_c = swap(send_c, "row", 1)
     keep_f, send_f, first3 = fine_backward(
-        meta, pooled_grad, cot_in, halo, slope1, slope2, feat3, act3, back2
+        meta, pooled_grad, cot_in, halo, slope1, slope2, feat3, act3o, back2
     )
     got_f = swap(send_f, "row", 1)
     feature_grad = feature_step(first3, back1)
@@ -631,6 +643,8 @@
         "finish",
         (((8, 144, CH), F32), ((8, 144, CH), F32)),
         (meta, fine, other),
+        (((16, 144, CH), F32), pltpu.SemaphoreType.DMA((8,))),
+        far_out=True,
     )
     shape = features.shape
     return (

time: 107 us -> 107 us (level)
    all_to_all x2, blocking collectives: 27.6 us -> 29.7 us  [exchange_row(): lax.all_to_all(value, 'row', 0, 0, axis_index_groups=groups, tiled=True)]
    all_to_all x2, blocking collectives: 24.4 us -> 22.7 us  [exchange_column(): return lax.all_to_all(value, 'col', 0, 0, tiled=True)]
    pallas_call x16 -> x17, Pallas kernels: 22.8 us -> 23.5 us  [call(): pl.pallas_call(kernel, name=name, out_shape=shapes, in_specs=[HBM if k in...]
  transfers between devices with their start and end apart: 12 -> 12, of which waited for: 4 -> 5; matrix products, arithmetic and copies ran while one was open for 0% -> 0% of each run, Pallas kernels for 13% -> 14%
where the time goes in v10:
time: 107 us
  blocking collectives  52.4 us (49%)
  starting transfers between devices  26.4 us (25%)
  Pallas kernels  23.5 us (22%)
  waiting for transfers between devices  3.24 us (3%)
    all_to_all x2, blocking collectives, exchange_row(): lax.all_to_all(value, 'row', 0, 0, axis_index_groups=groups, tiled=True)  29.7 us
    pallas_call x17, Pallas kernels, call(): pl.pallas_call(kernel, name=name, out_shape=shapes, in_specs=[HBM if k in...  23.5 us
    ppermute x10, starting transfers between devices, swap(): return lax.ppermute(value, axis, [(i, i ^ mask) for i in range(count)])  22.7 us
    all_to_all x2, blocking collectives, exchange_column(): return lax.all_to_all(value, 'col', 0, 0, tiled=True)  22.7 us
    ppermute x2, starting transfers between devices, swap_outer(): return lax.ppermute(value, axis, pairs)  3.69 us
    ppermute x10, waiting for transfers between devices, swap(): return lax.ppermute(value, axis, [(i, i ^ mask) for i in range(count)])  3.05 us
  transfers between devices with their start and end apart: 12, of which 5 were waited for; matrix products, arithmetic and copies ran while one was open for 0% of the time, Pallas kernels for 14%

profile of v10, /device:TPU:1, one launch (start us, length us, event | category | flops | bytes accessed | tf_op | source)
XLA Modules:
  0.0 106.6 jit_solution(7738949296332136785)
XLA Ops:
  0.7 1.6 %pack_columns.1 = (bf16[16,48,128]{2,1,0:T(8,128)(2,1)S(1)}, bf16[16,48,128]{2,1,0:T(8,128)(2,1)S(1)}) custom-call(s32[6]{0:T(128)S(1)} %stack.19.meta, bf16[16,64,128]{2,1,0:T(8,128)(2,1)} %bitcast.18, bf16[16,64,128]{2,1,0:T(8,128)(2,1)} %bitcast.20), custom_call_target="tpu_custom_call" | custom-call | tf_op jit(solution)/shard_map/pack_columns/pallas_call | solution.py:23
  2.3 0.7 collective-permute-start.1
  3.0 5.4 %collective-permute-start = (bf16[16,48,128]{2,1,0:T(8,128)(2,1)S(1)}, bf16[16,48,128]{2,1,0:T(8,128)(2,1)S(1)}, u32[]{:S(2)}, u32[]{:S(2)}) collective-permute-start(bf16[16,48,128]{2,1,0:T(8,128)(2,1)S(1)} %get-tuple-element.55), channel_id=1, source_target_pairs={{0,1},{1,0},{2,3},{3,2},{4,5},{5,4},{6,7},{7,6},{8,9},{9,8},{10,11... | collective-permute-start | bytes 589832 | tf_op jit(solution)/shard_map/ppermute | solution.py:532
  8.4 1.1 %bring.1 = (bf16[16,64,128]{2,1,0:T(8,128)(2,1)S(1)}, bf16[16,64,128]{2,1,0:T(8,128)(2,1)S(1)}, bf16[160,128]{1,0:T(8,128)(2,1)S(1)}) custom-call(bf16[16,64,128]{2,1,0:T(8,128)(2,1)} %bitcast.19, bf16[16,64,128]{2,1,0:T(8,128)(2,1)} %bitcast.21, bf16[9,16,128]{2,1,0:T(8,128)(2,1)} %bitcast.27, bf16[16,128]{1,0:T(8,128)(2,1)} %proj.1), custom_call_target="tpu_custom_call" | custom-call | flops 4000000000 | tf_op jit(solution)/shard_map/bring/pallas_call | solution.py:23
  9.6 3.0 %collective-permute-start.2 = (bf16[160,128]{1,0:T(8,128)(2,1)S(1)}, bf16[160,128]{1,0:T(8,128)(2,1)S(1)}, u32[]{:S(2)}, u32[]{:S(2)}) collective-permute-start(bf16[160,128]{1,0:T(8,128)(2,1)S(1)} %get-tuple-element.63.own), channel_id=1, source_target_pairs={{0,128},{16,144},{32,160},{48,176},{64,192},{80,208},{96,224},{112... | collective-permute-start | bytes 122888 | tf_op jit(solution)/shard_map/ppermute | solution.py:532
  12.6 1.2 %weights.1 = (bf16[1536,256]{1,0:T(8,128)(2,1)S(1)}, bf16[1536,256]{1,0:T(8,128)(2,1)S(1)}, bf16[256,1536]{1,0:T(8,128)(2,1)S(1)}, bf16[256,1536]{1,0:T(8,128)(2,1)S(1)}) custom-call(bf16[1152,128]{1,0:T(8,128)(2,1)} %bitcast.24, bf16[1152,128]{1,0:T(8,128)(2,1)} %bitcast.25), custom_call_target="tpu_custom_call" | custom-call | flops 4000000000 | tf_op jit(solution)/shard_map/weights/pallas_call | solution.py:23
  13.8 1.9 %collective-permute-done.2.far = bf16[160,128]{1,0:T(8,128)(2,1)S(1)} collective-permute-done((bf16[160,128]{1,0:T(8,128)(2,1)S(1)}, bf16[160,128]{1,0:T(8,128)(2,1)S(1)}, u32[]{:S(2)}, u32[]{:S(2)}) %collective-permute-start.2) | collective-permute-done | bytes 40992 | tf_op jit(solution)/shard_map/ppermute | solution.py:532
  15.7 0.6 pack_rows.1
  16.4 3.9 %collective-permute-start.3 = (bf16[1408,128]{1,0:T(8,128)(2,1)S(1)}, bf16[1408,128]{1,0:T(8,128)(2,1)S(1)}, u32[]{:S(2)}, u32[]{:S(2)}) collective-permute-start(bf16[1408,128]{1,0:T(8,128)(2,1)S(1)} %get-tuple-element.64), channel_id=1, source_target_pairs={{0,16},{16,0},{32,48},{48,32},{64,80},{80,64},{96,112},{112,96},{1... | collective-permute-start | bytes 1081352 | tf_op jit(solution)/shard_map/ppermute | solution.py:532
  20.3 3.0 %collective-permute-start.4 = (bf16[1408,128]{1,0:T(8,128)(2,1)S(1)}, bf16[1408,128]{1,0:T(8,128)(2,1)S(1)}, u32[]{:S(2)}, u32[]{:S(2)}) collective-permute-start(bf16[1408,128]{1,0:T(8,128)(2,1)S(1)} %get-tuple-element.65), channel_id=1, source_target_pairs={{16,32},{32,16},{48,64},{64,48},{80,96},{96,80},{112,128},{128,112... | collective-permute-start | bytes 1081352 | tf_op jit(solution)/shard_map/ppermute | solution.py:538
  23.3 1.3 %collective-permute-start.5 = (bf16[2,160,128]{2,1,0:T(8,128)(2,1)S(1)}, bf16[2,160,128]{2,1,0:T(8,128)(2,1)S(1)}, u32[]{:S(2)}, u32[]{:S(2)}) collective-permute-start(bf16[2,160,128]{2,1,0:T(8,128)(2,1)S(1)} %get-tuple-element.78.refs_0_.near0), channel_id=1, source_target_pairs={{0,32},{16,48},{32,0},{48,16},{64,96},{80,112},{96,64},{112,80},{1... | collective-permute-start | bytes 245768 | tf_op jit(solution)/shard_map/ppermute | solution.py:532
  24.6 1.6 %collective-permute-start.6 = (bf16[2,160,128]{2,1,0:T(8,128)(2,1)S(1)}, bf16[2,160,128]{2,1,0:T(8,128)(2,1)S(1)}, u32[]{:S(2)}, u32[]{:S(2)}) collective-permute-start(bf16[2,160,128]{2,1,0:T(8,128)(2,1)S(1)} %get-tuple-element.78.refs_0_.near0), channel_id=1, source_target_pairs={{0,64},{16,80},{32,96},{48,112},{64,0},{80,16},{96,32},{112,48},{1... | collective-permute-start | bytes 245768 | tf_op jit(solution)/shard_map/ppermute | solution.py:532
  26.3 1.0 collective-permute-start.7
  27.3 3.6 %forward_inner.1 = (bf16[16,128,384]{2,1,0:T(8,128)(2,1)S(1)}, bf16[14,128,384]{2,1,0:T(8,128)(2,1)S(1)}, f32[14,96,128]{2,1,0:T(8,128)S(1)}, bf16[6,64,384]{2,1...) custom-call(s32[6]{0:T(128)S(1)} %stack.19.meta, ...), custom_call_target="tpu_custom_call" | custom-call | tf_op jit(solution)/shard_map/forward_inner/pallas_call | solution.py:23
  30.9 0.2 collective-permute-done.4.outer
  31.1 2.4 %outer_first.1 = (bf16[30,128,384]{2,1,0:T(8,128)(2,1)S(1)}, f32[18,96,128]{2,1,0:T(8,128)S(1)}, bf16[18,64,384]{2,1,0:T(8,128)(2,1)S(1)}, bf16[18,64,384]{2,1,0:T(8,128)(2,1)S(1)}) custom-call(s32[6]{0:T(128)S(1)} %stack.19.meta, bf16[1408,128]{1,0:T(8,128)(2,1)S(1)} %collective-permute-done.3.inner, bf16[1408,128]{1,0:T(8,128)(2,1)S(1)} %collective-permute-done.4.outer, ...), custom_call_target="tpu_custom_call" | custom-call | flops 2000000000 | tf_op jit(solution)/shard_map/outer_first/pallas_call | solution.py:23
  33.5 0.6 collective-permute-done.6.refs_2_.near2
  34.2 1.9 %outer_second.1 = (bf16[14,64,384]{2,1,0:T(8,128)(2,1)S(1)}, f32[20,96,128]{2,1,0:T(8,128)S(1)}, bf16[16,64,128]{2,1,0:T(8,128)(2,1)S(1)}) custom-call(s32[6]{0:T(128)S(1)} %stack.19.meta, bf16[30,128,384]{2,1,0:T(8,128)(2,1)S(1)} %get-tuple-element.72.act3, bf16[6,64,384]{2,1,0:T(8,128)(2,1)S(1)} %get-tuple-element.73.pool3i, ...), custom_call_target="tpu_custom_call" | custom-call | flops 4000000000 | tf_op jit(solution)/shard_map/outer_second/pallas_call | solution.py:23
  36.1 3.6 %coarse_step.1 = (bf16[256,256]{1,0:T(8,128)(2,1)S(1)}, bf16[256,128]{1,0:T(8,128)(2,1)S(1)}, bf16[8,160,128]{2,1,0:T(8,128)(2,1)S(1)}, bf16[8,160,128]{2,1,0:T(8,128)(2,1)S(1)}, f32[10,48,128]{2,1,0:T(8,128)S(1)}) custom-call(s32[6]{0:T(128)S(1)} %stack.19.meta, bf16[14,64,384]{2,1,0:T(8,128)(2,1)S(1)} %get-tuple-element.76.pool3, ...), custom_call_target="tpu_custom_call" | custom-call | flops 2000000000 | tf_op jit(solution)/shard_map/coarse_step/pallas_call | solution.py:23
  39.7 0.8 collective-permute-start.9
  40.4 2.7 %fine_backward.1 = (bf16[8,144,128]{2,1,0:T(8,128)(2,1)S(1)}, bf16[8,144,128]{2,1,0:T(8,128)(2,1)S(1)}, bf16[18,64,384]{2,1,0:T(8,128)(2,1)S(1)}) custom-call(s32[6]{0:T(128)S(1)} %stack.19.meta, f32[10,48,128]{2,1,0:T(8,128)S(1)} %get-tuple-element.84.pooled_grad, bf16[16,64,128]{2,1,0:T(8,128)(2,1)S(1)} %get-tuple-element.58.cot, ...), custom_call_target="tpu_custom_call" | custom-call | flops 2000000000 | tf_op jit(solution)/shard_map/fine_backward/pallas_call | solution.py:23
  43.2 1.3 %feature_step.1 = bf16[16,64,128]{2,1,0:T(8,128)(2,1)} custom-call(bf16[18,64,384]{2,1,0:T(8,128)(2,1)S(1)} %get-tuple-element.92.first3, bf16[256,1536]{1,0:T(8,128)(2,1)S(1)} %get-tuple-element.93.back_w), custom_call_target="tpu_custom_call" | custom-call | flops 1000000000 | tf_op jit(solution)/shard_map/feature_step/pallas_call | solution.py:23
  44.5 0.3 collective-permute-done.10.got_f
  44.9 19.2 %all_to_all.20.got = bf16[8,304,128]{2,1,0:T(8,128)(2,1)S(1)} all-to-all(bf16[8,304,128]{2,1,0:T(8,128)(2,1)S(1)} %scatter_core.1), channel_id=1, replica_groups={{0,32,64,96,128,160,192,224},{16,48,80,112,144,176,208,240},{1,33,65,97..., dimensions={0} | all-to-all | bytes 1245184 | tf_op jit(solution)/shard_map/all_to_all | solution.py:544
  64.3 12.2 %all_to_all.21.got = bf16[16,32,128]{2,1,0:T(8,128)(2,1)S(1)} all-to-all(bf16[16,32,128]{2,1,0:T(8,128)(2,1)S(1)} %scatter_row.1), channel_id=1, replica_groups=mesh['row'=16,'col'=16] {'col'}, dimensions={0} | all-to-all | bytes 262144 | tf_op jit(solution)/shard_map/all_to_all | solution.py:548
  76.5 10.5 %all_to_all.22.got = bf16[16,32,128]{2,1,0:T(8,128)(2,1)S(1)} all-to-all(bf16[16,32,128]{2,1,0:T(8,128)(2,1)S(1)} %scatter_column.1), channel_id=1, replica_groups=mesh['row'=16,'col'=16] {'col'}, dimensions={0} | all-to-all | bytes 262144 | tf_op jit(solution)/shard_map/all_to_all | solution.py:548
  87.0 0.7 gather_column.1
  87.6 10.5 %all_to_all.23.mine = bf16[8,144,128]{2,1,0:T(8,128)(2,1)S(1)} all-to-all(bf16[8,144,128]{2,1,0:T(8,128)(2,1)S(1)} %get-tuple-element.95), channel_id=1, replica_groups={{0,32,64,96,128,160,192,224},{16,48,80,112,144,176,208,240},{1,33,65,97..., dimensions={0} | all-to-all | bytes 589824 | tf_op jit(solution)/shard_map/all_to_all | solution.py:544
  98.1 5.5 %collective-permute-start.11 = (bf16[8,144,128]{2,1,0:T(8,128)(2,1)S(1)}, bf16[8,144,128]{2,1,0:T(8,128)(2,1)S(1)}, u32[]{:S(2)}, u32[]{:S(2)}) collective-permute-start(bf16[8,144,128]{2,1,0:T(8,128)(2,1)S(1)} %all_to_all.23.mine), channel_id=1, source_target_pairs={{0,16},{16,0},{32,48},{48,32},{64,80},{80,64},{96,112},{112,96},{1... | collective-permute-start | bytes 884744 | tf_op jit(solution)/shard_map/ppermute | solution.py:532
  103.6 0.9 blend.1
  104.5 0.3 collective-permute-done.11.other
  104.8 1.6 %finish.1 = (f32[8,144,128]{2,1,0:T(8,128)}, f32[8,144,128]{2,1,0:T(8,128)}) custom-call(s32[6]{0:T(128)S(1)} %stack.19.meta, bf16[8,144,128]{2,1,0:T(8,128)(2,1)S(1)} %all_to_all.23.mine, bf16[8,144,128]{2,1,0:T(8,128)(2,1)S(1)} %collective-permute-done.11.other), custom_call_target="tpu_custom_call" | custom-call | tf_op jit(solution)/shard_map/finish/pallas_call | solution.py:23
  (15 shorter events, 0.6 us)
Async XLA Ops:
  2.3 11.5 %collective-permute-start.1 = (bf16[16,48,128]{2,1,0:T(8,128)(2,1)S(1)}, bf16[16,48,128]{2,1,0:T(8,128)(2,1)S(1)}, u32[]{:S(2)}, u32[]{:S(2)}) collective-permute-start(bf16[16,48,128]{2,1,0:T(8,128)(2,1)S(1)} %get-tuple-element.59), channel_id=1, source_target_pairs={{1,2},{2,1},{3,4},{4,3},{5,6},{6,5},{7,8},{8,7},{9,10},{10,9},{11,... | collective-permute-start | bytes 589832 | tf_op jit(solution)/shard_map/ppermute | solution.py:538
  3.0 12.7 %collective-permute-start = (bf16[16,48,128]{2,1,0:T(8,128)(2,1)S(1)}, bf16[16,48,128]{2,1,0:T(8,128)(2,1)S(1)}, u32[]{:S(2)}, u32[]{:S(2)}) collective-permute-start(bf16[16,48,128]{2,1,0:T(8,128)(2,1)S(1)} %get-tuple-element.55), channel_id=1, source_target_pairs={{0,1},{1,0},{2,3},{3,2},{4,5},{5,4},{6,7},{7,6},{8,9},{9,8},{10,11... | collective-permute-start | bytes 589832 | tf_op jit(solution)/shard_map/ppermute | solution.py:532
  9.6 6.1 %collective-permute-start.2 = (bf16[160,128]{1,0:T(8,128)(2,1)S(1)}, bf16[160,128]{1,0:T(8,128)(2,1)S(1)}, u32[]{:S(2)}, u32[]{:S(2)}) collective-permute-start(bf16[160,128]{1,0:T(8,128)(2,1)S(1)} %get-tuple-element.63.own), channel_id=1, source_target_pairs={{0,128},{16,144},{32,160},{48,176},{64,192},{80,208},{96,224},{112... | collective-permute-start | bytes 122888 | tf_op jit(solution)/shard_map/ppermute | solution.py:532
  16.4 14.5 %collective-permute-start.3 = (bf16[1408,128]{1,0:T(8,128)(2,1)S(1)}, bf16[1408,128]{1,0:T(8,128)(2,1)S(1)}, u32[]{:S(2)}, u32[]{:S(2)}) collective-permute-start(bf16[1408,128]{1,0:T(8,128)(2,1)S(1)} %get-tuple-element.64), channel_id=1, source_target_pairs={{0,16},{16,0},{32,48},{48,32},{64,80},{80,64},{96,112},{112,96},{1... | collective-permute-start | bytes 1081352 | tf_op jit(solution)/shard_map/ppermute | solution.py:532
  20.3 10.8 %collective-permute-start.4 = (bf16[1408,128]{1,0:T(8,128)(2,1)S(1)}, bf16[1408,128]{1,0:T(8,128)(2,1)S(1)}, u32[]{:S(2)}, u32[]{:S(2)}) collective-permute-start(bf16[1408,128]{1,0:T(8,128)(2,1)S(1)} %get-tuple-element.65), channel_id=1, source_target_pairs={{16,32},{32,16},{48,64},{64,48},{80,96},{96,80},{112,128},{128,112... | collective-permute-start | bytes 1081352 | tf_op jit(solution)/shard_map/ppermute | solution.py:538
  23.3 10.1 %collective-permute-start.5 = (bf16[2,160,128]{2,1,0:T(8,128)(2,1)S(1)}, bf16[2,160,128]{2,1,0:T(8,128)(2,1)S(1)}, u32[]{:S(2)}, u32[]{:S(2)}) collective-permute-start(bf16[2,160,128]{2,1,0:T(8,128)(2,1)S(1)} %get-tuple-element.78.refs_0_.near0), channel_id=1, source_target_pairs={{0,32},{16,48},{32,0},{48,16},{64,96},{80,112},{96,64},{112,80},{1... | collective-permute-start | bytes 245768 | tf_op jit(solution)/shard_map/ppermute | solution.py:532
  24.6 9.5 %collective-permute-start.6 = (bf16[2,160,128]{2,1,0:T(8,128)(2,1)S(1)}, bf16[2,160,128]{2,1,0:T(8,128)(2,1)S(1)}, u32[]{:S(2)}, u32[]{:S(2)}) collective-permute-start(bf16[2,160,128]{2,1,0:T(8,128)(2,1)S(1)} %get-tuple-element.78.refs_0_.near0), channel_id=1, source_target_pairs={{0,64},{16,80},{32,96},{48,112},{64,0},{80,16},{96,32},{112,48},{1... | collective-permute-start | bytes 245768 | tf_op jit(solution)/shard_map/ppermute | solution.py:532
  26.3 7.8 %collective-permute-start.7 = (bf16[2,160,128]{2,1,0:T(8,128)(2,1)S(1)}, bf16[2,160,128]{2,1,0:T(8,128)(2,1)S(1)}, u32[]{:S(2)}, u32[]{:S(2)}) collective-permute-start(bf16[2,160,128]{2,1,0:T(8,128)(2,1)S(1)} %get-tuple-element.78.refs_0_.near0), channel_id=1, source_target_pairs={{0,96},{16,112},{32,64},{48,80},{64,32},{80,48},{96,0},{112,16},{1... | collective-permute-start | bytes 245768 | tf_op jit(solution)/shard_map/ppermute | solution.py:532
  34.1 2.0 %collective-permute-start.8 = (bf16[4,2,160,128]{3,2,1,0:T(8,128)(2,1)S(1)}, bf16[4,2,160,128]{3,2,1,0:T(8,128)(2,1)S(1)}, u32[]{:S(2)}, u32[]{:S(2)}) collective-permute-start(bf16[4,2,160,128]{3,2,1,0:T(8,128)(2,1)S(1)} %stack_eight.1), channel_id=1, source_target_pairs={{0,16},{16,0},{32,48},{48,32},{64,80},{80,64},{96,112},{112,96},{1... | collective-permute-start | bytes 983048 | tf_op jit(solution)/shard_map/ppermute | solution.py:532
  39.7 5.1 %collective-permute-start.9 = (bf16[8,160,128]{2,1,0:T(8,128)(2,1)S(1)}, bf16[8,160,128]{2,1,0:T(8,128)(2,1)S(1)}, u32[]{:S(2)}, u32[]{:S(2)}) collective-permute-start(bf16[8,160,128]{2,1,0:T(8,128)(2,1)S(1)} %get-tuple-element.90), channel_id=1, source_target_pairs={{0,16},{16,0},{32,48},{48,32},{64,80},{80,64},{96,112},{112,96},{1... | collective-permute-start | bytes 983048 | tf_op jit(solution)/shard_map/ppermute | solution.py:532
  43.1 1.7 %collective-permute-start.10 = (bf16[8,144,128]{2,1,0:T(8,128)(2,1)S(1)}, bf16[8,144,128]{2,1,0:T(8,128)(2,1)S(1)}, u32[]{:S(2)}, u32[]{:S(2)}) collective-permute-start(bf16[8,144,128]{2,1,0:T(8,128)(2,1)S(1)} %get-tuple-element.91), channel_id=1, source_target_pairs={{0,16},{16,0},{32,48},{48,32},{64,80},{80,64},{96,112},{112,96},{1... | collective-permute-start | bytes 884744 | tf_op jit(solution)/shard_map/ppermute | solution.py:532
  98.1 6.7 %collective-permute-start.11 = (bf16[8,144,128]{2,1,0:T(8,128)(2,1)S(1)}, bf16[8,144,128]{2,1,0:T(8,128)(2,1)S(1)}, u32[]{:S(2)}, u32[]{:S(2)}) collective-permute-start(bf16[8,144,128]{2,1,0:T(8,128)(2,1)S(1)} %all_to_all.23.mine), channel_id=1, source_target_pairs={{0,16},{16,0},{32,48},{48,32},{64,80},{80,64},{96,112},{112,96},{1... | collective-permute-start | bytes 884744 | tf_op jit(solution)/shard_map/ppermute | solution.py:532

commit v11 on v10

--- a/solution.py
+++ b/solution.py
@@ -606,9 +606,9 @@
     )
     inner = swap(inner, "row", 1)
     outer = swap_outer(outer, "row")
-    pair_in = after_all(pair, near0)
+    feat3, act3, slope1, pool3, slope2, act = inner_step(meta, feat_in, pair, other, weight1, weight2)
+    near0 = after_all(near0, slope1)
     near = [near0] + [swap(near0, "row", 2 * k) for k in range(1, 4)]
-    feat3, act3, slope1, pool3, slope2, act = inner_step(meta, feat_in, pair_in, other, weight1, weight2)
     act3, slope1, feat3, act3o = outer_first_step(meta, inner, outer, feat3, act3, slope1, weight1)
     near = list(lax.optimization_barrier((slope1, *near)))[1:]
     far = swap(call(stack_kernel, "stack_eight", (((4, 2, 160, CH), BF),), near)[0], "row", 1)

time: 107 us -> 108 us (level)
  waiting for transfers between devices: 3.24 us -> 4.83 us
  blocking collectives: 52.4 us -> 50.9 us
    ppermute x10, waiting for transfers between devices: 3.05 us -> 4.83 us  [swap(): return lax.ppermute(value, axis, [(i, i ^ mask) for i in range(count)])]
    all_to_all x2, blocking collectives: 29.7 us -> 28.4 us  [exchange_row(): lax.all_to_all(value, 'row', 0, 0, axis_index_groups=groups, tiled=True)]
  transfers between devices with their start and end apart: 12 -> 12, of which waited for: 5 -> 4; matrix products, arithmetic and copies ran while one was open for 0% -> 0% of each run, Pallas kernels for 14% -> 14%
where the time goes in v11:
time: 108 us
  blocking collectives  50.9 us (47%)
  starting transfers between devices  27.4 us (25%)
  Pallas kernels  23.6 us (22%)
  waiting for transfers between devices  4.83 us (4%)
    all_to_all x2, blocking collectives, exchange_row(): lax.all_to_all(value, 'row', 0, 0, axis_index_groups=groups, tiled=True)  28.4 us
    ppermute x10, starting transfers between devices, swap(): return lax.ppermute(value, axis, [(i, i ^ mask) for i in range(count)])  23.7 us
    pallas_call x17, Pallas kernels, call(): pl.pallas_call(kernel, name=name, out_shape=shapes, in_specs=[HBM if k in...  23.6 us
    all_to_all x2, blocking collectives, exchange_column(): return lax.all_to_all(value, 'col', 0, 0, tiled=True)  22.5 us
    ppermute x10, waiting for transfers between devices, swap(): return lax.ppermute(value, axis, [(i, i ^ mask) for i in range(count)])  4.83 us
    ppermute x2, starting transfers between devices, swap_outer(): return lax.ppermute(value, axis, pairs)  3.69 us
  transfers between devices with their start and end apart: 12, of which 4 were waited for; matrix products, arithmetic and copies ran while one was open for 0% of the time, Pallas kernels for 14%

profile of v11, /device:TPU:1, one launch (start us, length us, event | category | flops | bytes accessed | tf_op | source)
XLA Modules:
  0.0 107.7 jit_solution(15340409276560635125)
XLA Ops:
  0.7 1.6 %pack_columns.1 = (bf16[16,48,128]{2,1,0:T(8,128)(2,1)S(1)}, bf16[16,48,128]{2,1,0:T(8,128)(2,1)S(1)}) custom-call(s32[6]{0:T(128)S(1)} %stack.19.meta, bf16[16,64,128]{2,1,0:T(8,128)(2,1)} %bitcast.18, bf16[16,64,128]{2,1,0:T(8,128)(2,1)} %bitcast.20), custom_call_target="tpu_custom_call" | custom-call | tf_op jit(solution)/shard_map/pack_columns/pallas_call | solution.py:23
  2.3 0.7 collective-permute-start.1
  3.0 5.4 %collective-permute-start = (bf16[16,48,128]{2,1,0:T(8,128)(2,1)S(1)}, bf16[16,48,128]{2,1,0:T(8,128)(2,1)S(1)}, u32[]{:S(2)}, u32[]{:S(2)}) collective-permute-start(bf16[16,48,128]{2,1,0:T(8,128)(2,1)S(1)} %get-tuple-element.55), channel_id=1, source_target_pairs={{0,1},{1,0},{2,3},{3,2},{4,5},{5,4},{6,7},{7,6},{8,9},{9,8},{10,11... | collective-permute-start | bytes 589832 | tf_op jit(solution)/shard_map/ppermute | solution.py:532
  8.4 1.1 %bring.1 = (bf16[16,64,128]{2,1,0:T(8,128)(2,1)S(1)}, bf16[16,64,128]{2,1,0:T(8,128)(2,1)S(1)}, bf16[160,128]{1,0:T(8,128)(2,1)S(1)}) custom-call(bf16[16,64,128]{2,1,0:T(8,128)(2,1)} %bitcast.19, bf16[16,64,128]{2,1,0:T(8,128)(2,1)} %bitcast.21, bf16[9,16,128]{2,1,0:T(8,128)(2,1)} %bitcast.27, bf16[16,128]{1,0:T(8,128)(2,1)} %proj.1), custom_call_target="tpu_custom_call" | custom-call | flops 4000000000 | tf_op jit(solution)/shard_map/bring/pallas_call | solution.py:23
  9.6 3.0 %collective-permute-start.2 = (bf16[160,128]{1,0:T(8,128)(2,1)S(1)}, bf16[160,128]{1,0:T(8,128)(2,1)S(1)}, u32[]{:S(2)}, u32[]{:S(2)}) collective-permute-start(bf16[160,128]{1,0:T(8,128)(2,1)S(1)} %get-tuple-element.63.own), channel_id=1, source_target_pairs={{0,128},{16,144},{32,160},{48,176},{64,192},{80,208},{96,224},{112... | collective-permute-start | bytes 122888 | tf_op jit(solution)/shard_map/ppermute | solution.py:532
  12.6 1.2 %weights.1 = (bf16[1536,256]{1,0:T(8,128)(2,1)S(1)}, bf16[1536,256]{1,0:T(8,128)(2,1)S(1)}, bf16[256,1536]{1,0:T(8,128)(2,1)S(1)}, bf16[256,1536]{1,0:T(8,128)(2,1)S(1)}) custom-call(bf16[1152,128]{1,0:T(8,128)(2,1)} %bitcast.24, bf16[1152,128]{1,0:T(8,128)(2,1)} %bitcast.25), custom_call_target="tpu_custom_call" | custom-call | flops 4000000000 | tf_op jit(solution)/shard_map/weights/pallas_call | solution.py:23
  13.8 1.9 %collective-permute-done.2.far = bf16[160,128]{1,0:T(8,128)(2,1)S(1)} collective-permute-done((bf16[160,128]{1,0:T(8,128)(2,1)S(1)}, bf16[160,128]{1,0:T(8,128)(2,1)S(1)}, u32[]{:S(2)}, u32[]{:S(2)}) %collective-permute-start.2) | collective-permute-done | bytes 40992 | tf_op jit(solution)/shard_map/ppermute | solution.py:532
  15.7 0.6 pack_rows.1
  16.4 3.9 %collective-permute-start.3 = (bf16[1408,128]{1,0:T(8,128)(2,1)S(1)}, bf16[1408,128]{1,0:T(8,128)(2,1)S(1)}, u32[]{:S(2)}, u32[]{:S(2)}) collective-permute-start(bf16[1408,128]{1,0:T(8,128)(2,1)S(1)} %get-tuple-element.64), channel_id=1, source_target_pairs={{0,16},{16,0},{32,48},{48,32},{64,80},{80,64},{96,112},{112,96},{1... | collective-permute-start | bytes 1081352 | tf_op jit(solution)/shard_map/ppermute | solution.py:532
  20.3 3.0 %collective-permute-start.4 = (bf16[1408,128]{1,0:T(8,128)(2,1)S(1)}, bf16[1408,128]{1,0:T(8,128)(2,1)S(1)}, u32[]{:S(2)}, u32[]{:S(2)}) collective-permute-start(bf16[1408,128]{1,0:T(8,128)(2,1)S(1)} %get-tuple-element.65), channel_id=1, source_target_pairs={{16,32},{32,16},{48,64},{64,48},{80,96},{96,80},{112,128},{128,112... | collective-permute-start | bytes 1081352 | tf_op jit(solution)/shard_map/ppermute | solution.py:538
  23.3 3.6 %forward_inner.1 = (bf16[16,128,384]{2,1,0:T(8,128)(2,1)S(1)}, bf16[14,128,384]{2,1,0:T(8,128)(2,1)S(1)}, f32[14,96,128]{2,1,0:T(8,128)S(1)}, bf16[6,64,384]{2,1...) custom-call(s32[6]{0:T(128)S(1)} %stack.19.meta, ...), custom_call_target="tpu_custom_call" | custom-call | tf_op jit(solution)/shard_map/forward_inner/pallas_call | solution.py:23
  26.9 1.3 %collective-permute-start.5 = (bf16[2,160,128]{2,1,0:T(8,128)(2,1)S(1)}, bf16[2,160,128]{2,1,0:T(8,128)(2,1)S(1)}, u32[]{:S(2)}, u32[]{:S(2)}) collective-permute-start(bf16[2,160,128]{2,1,0:T(8,128)(2,1)S(1)} %get-tuple-element.78.refs_0_.near0), channel_id=1, source_target_pairs={{0,32},{16,48},{32,0},{48,16},{64,96},{80,112},{96,64},{112,80},{1... | collective-permute-start | bytes 245768 | tf_op jit(solution)/shard_map/ppermute | solution.py:532
  28.2 1.6 %collective-permute-start.6 = (bf16[2,160,128]{2,1,0:T(8,128)(2,1)S(1)}, bf16[2,160,128]{2,1,0:T(8,128)(2,1)S(1)}, u32[]{:S(2)}, u32[]{:S(2)}) collective-permute-start(bf16[2,160,128]{2,1,0:T(8,128)(2,1)S(1)} %get-tuple-element.78.refs_0_.near0), channel_id=1, source_target_pairs={{0,64},{16,80},{32,96},{48,112},{64,0},{80,16},{96,32},{112,48},{1... | collective-permute-start | bytes 245768 | tf_op jit(solution)/shard_map/ppermute | solution.py:532
  29.9 1.0 collective-permute-start.7
  30.9 2.4 %outer_first.1 = (bf16[30,128,384]{2,1,0:T(8,128)(2,1)S(1)}, f32[18,96,128]{2,1,0:T(8,128)S(1)}, bf16[18,64,384]{2,1,0:T(8,128)(2,1)S(1)}, bf16[18,64,384]{2,1,0:T(8,128)(2,1)S(1)}) custom-call(s32[6]{0:T(128)S(1)} %stack.19.meta, bf16[1408,128]{1,0:T(8,128)(2,1)S(1)} %collective-permute-done.3.inner, bf16[1408,128]{1,0:T(8,128)(2,1)S(1)} %collective-permute-done.4.outer, ...), custom_call_target="tpu_custom_call" | custom-call | flops 2000000000 | tf_op jit(solution)/shard_map/outer_first/pallas_call | solution.py:23
  33.3 0.9 collective-permute-done.6.refs_2_.near2
  34.2 1.7 %collective-permute-done.7.refs_3_.near3 = bf16[2,160,128]{2,1,0:T(8,128)(2,1)S(1)} collective-permute-done((bf16[2,160,128]{2,1,0:T(8,128)(2,1)S(1)}, bf16[2,160,128]{2,1,0:T(8,128)(2,1)S(1)}, u32[]{:S(2)}, u32[]{:S(2)}) %collective-permute-start.7) | collective-permute-done | bytes 81952 | tf_op jit(solution)/shard_map/ppermute | solution.py:532
  35.9 1.2 %collective-permute-start.8 = (bf16[4,2,160,128]{3,2,1,0:T(8,128)(2,1)S(1)}, bf16[4,2,160,128]{3,2,1,0:T(8,128)(2,1)S(1)}, u32[]{:S(2)}, u32[]{:S(2)}) collective-permute-start(bf16[4,2,160,128]{3,2,1,0:T(8,128)(2,1)S(1)} %stack_eight.1), channel_id=1, source_target_pairs={{0,16},{16,0},{32,48},{48,32},{64,80},{80,64},{96,112},{112,96},{1... | collective-permute-start | bytes 983048 | tf_op jit(solution)/shard_map/ppermute | solution.py:532
  37.1 1.9 %outer_second.1 = (bf16[14,64,384]{2,1,0:T(8,128)(2,1)S(1)}, f32[20,96,128]{2,1,0:T(8,128)S(1)}, bf16[16,64,128]{2,1,0:T(8,128)(2,1)S(1)}) custom-call(s32[6]{0:T(128)S(1)} %stack.19.meta, bf16[30,128,384]{2,1,0:T(8,128)(2,1)S(1)} %get-tuple-element.70.act3, bf16[6,64,384]{2,1,0:T(8,128)(2,1)S(1)} %get-tuple-element.71.pool3i, ...), custom_call_target="tpu_custom_call" | custom-call | flops 4000000000 | tf_op jit(solution)/shard_map/outer_second/pallas_call | solution.py:23
  39.0 3.6 %coarse_step.1 = (bf16[256,256]{1,0:T(8,128)(2,1)S(1)}, bf16[256,128]{1,0:T(8,128)(2,1)S(1)}, bf16[8,160,128]{2,1,0:T(8,128)(2,1)S(1)}, bf16[8,160,128]{2,1,0:T(8,128)(2,1)S(1)}, f32[10,48,128]{2,1,0:T(8,128)S(1)}) custom-call(s32[6]{0:T(128)S(1)} %stack.19.meta, bf16[14,64,384]{2,1,0:T(8,128)(2,1)S(1)} %get-tuple-element.74.pool3, ...), custom_call_target="tpu_custom_call" | custom-call | flops 2000000000 | tf_op jit(solution)/shard_map/coarse_step/pallas_call | solution.py:23
  42.9 2.7 %fine_backward.1 = (bf16[8,144,128]{2,1,0:T(8,128)(2,1)S(1)}, bf16[8,144,128]{2,1,0:T(8,128)(2,1)S(1)}, bf16[18,64,384]{2,1,0:T(8,128)(2,1)S(1)}) custom-call(s32[6]{0:T(128)S(1)} %stack.19.meta, f32[10,48,128]{2,1,0:T(8,128)S(1)} %get-tuple-element.84.pooled_grad, bf16[16,64,128]{2,1,0:T(8,128)(2,1)S(1)} %get-tuple-element.58.cot, ...), custom_call_target="tpu_custom_call" | custom-call | flops 2000000000 | tf_op jit(solution)/shard_map/fine_backward/pallas_call | solution.py:23
  45.6 0.6 collective-permute-start.10
  46.2 1.3 %feature_step.1 = bf16[16,64,128]{2,1,0:T(8,128)(2,1)} custom-call(bf16[18,64,384]{2,1,0:T(8,128)(2,1)S(1)} %get-tuple-element.92.first3, bf16[256,1536]{1,0:T(8,128)(2,1)S(1)} %get-tuple-element.93.back_w), custom_call_target="tpu_custom_call" | custom-call | flops 1000000000 | tf_op jit(solution)/shard_map/feature_step/pallas_call | solution.py:23
  47.6 17.9 %all_to_all.20.got = bf16[8,304,128]{2,1,0:T(8,128)(2,1)S(1)} all-to-all(bf16[8,304,128]{2,1,0:T(8,128)(2,1)S(1)} %scatter_core.1), channel_id=1, replica_groups={{0,32,64,96,128,160,192,224},{16,48,80,112,144,176,208,240},{1,33,65,97..., dimensions={0} | all-to-all | bytes 1245184 | tf_op jit(solution)/shard_map/all_to_all | solution.py:544
  65.6 12.0 %all_to_all.21.got = bf16[16,32,128]{2,1,0:T(8,128)(2,1)S(1)} all-to-all(bf16[16,32,128]{2,1,0:T(8,128)(2,1)S(1)} %scatter_row.1), channel_id=1, replica_groups=mesh['row'=16,'col'=16] {'col'}, dimensions={0} | all-to-all | bytes 262144 | tf_op jit(solution)/shard_map/all_to_all | solution.py:548
  77.7 10.5 %all_to_all.22.got = bf16[16,32,128]{2,1,0:T(8,128)(2,1)S(1)} all-to-all(bf16[16,32,128]{2,1,0:T(8,128)(2,1)S(1)} %scatter_column.1), channel_id=1, replica_groups=mesh['row'=16,'col'=16] {'col'}, dimensions={0} | all-to-all | bytes 262144 | tf_op jit(solution)/shard_map/all_to_all | solution.py:548
  88.2 0.7 gather_column.1
  88.8 10.5 %all_to_all.23.mine = bf16[8,144,128]{2,1,0:T(8,128)(2,1)S(1)} all-to-all(bf16[8,144,128]{2,1,0:T(8,128)(2,1)S(1)} %get-tuple-element.95), channel_id=1, replica_groups={{0,32,64,96,128,160,192,224},{16,48,80,112,144,176,208,240},{1,33,65,97..., dimensions={0} | all-to-all | bytes 589824 | tf_op jit(solution)/shard_map/all_to_all | solution.py:544
  99.3 5.4 %collective-permute-start.11 = (bf16[8,144,128]{2,1,0:T(8,128)(2,1)S(1)}, bf16[8,144,128]{2,1,0:T(8,128)(2,1)S(1)}, u32[]{:S(2)}, u32[]{:S(2)}) collective-permute-start(bf16[8,144,128]{2,1,0:T(8,128)(2,1)S(1)} %all_to_all.23.mine), channel_id=1, source_target_pairs={{0,16},{16,0},{32,48},{48,32},{64,80},{80,64},{96,112},{112,96},{1... | collective-permute-start | bytes 884744 | tf_op jit(solution)/shard_map/ppermute | solution.py:532
  104.7 0.9 blend.1
  105.6 0.3 collective-permute-done.11.other
  105.9 1.6 %finish.1 = (f32[8,144,128]{2,1,0:T(8,128)}, f32[8,144,128]{2,1,0:T(8,128)}) custom-call(s32[6]{0:T(128)S(1)} %stack.19.meta, bf16[8,144,128]{2,1,0:T(8,128)(2,1)S(1)} %all_to_all.23.mine, bf16[8,144,128]{2,1,0:T(8,128)(2,1)S(1)} %collective-permute-done.11.other), custom_call_target="tpu_custom_call" | custom-call | tf_op jit(solution)/shard_map/finish/pallas_call | solution.py:23
  (15 shorter events, 0.7 us)
Async XLA Ops:
  2.3 11.5 %collective-permute-start.1 = (bf16[16,48,128]{2,1,0:T(8,128)(2,1)S(1)}, bf16[16,48,128]{2,1,0:T(8,128)(2,1)S(1)}, u32[]{:S(2)}, u32[]{:S(2)}) collective-permute-start(bf16[16,48,128]{2,1,0:T(8,128)(2,1)S(1)} %get-tuple-element.59), channel_id=1, source_target_pairs={{1,2},{2,1},{3,4},{4,3},{5,6},{6,5},{7,8},{8,7},{9,10},{10,9},{11,... | collective-permute-start | bytes 589832 | tf_op jit(solution)/shard_map/ppermute | solution.py:538
  3.0 12.7 %collective-permute-start = (bf16[16,48,128]{2,1,0:T(8,128)(2,1)S(1)}, bf16[16,48,128]{2,1,0:T(8,128)(2,1)S(1)}, u32[]{:S(2)}, u32[]{:S(2)}) collective-permute-start(bf16[16,48,128]{2,1,0:T(8,128)(2,1)S(1)} %get-tuple-element.55), channel_id=1, source_target_pairs={{0,1},{1,0},{2,3},{3,2},{4,5},{5,4},{6,7},{7,6},{8,9},{9,8},{10,11... | collective-permute-start | bytes 589832 | tf_op jit(solution)/shard_map/ppermute | solution.py:532
  9.6 6.1 %collective-permute-start.2 = (bf16[160,128]{1,0:T(8,128)(2,1)S(1)}, bf16[160,128]{1,0:T(8,128)(2,1)S(1)}, u32[]{:S(2)}, u32[]{:S(2)}) collective-permute-start(bf16[160,128]{1,0:T(8,128)(2,1)S(1)} %get-tuple-element.63.own), channel_id=1, source_target_pairs={{0,128},{16,144},{32,160},{48,176},{64,192},{80,208},{96,224},{112... | collective-permute-start | bytes 122888 | tf_op jit(solution)/shard_map/ppermute | solution.py:532
  16.4 14.5 %collective-permute-start.3 = (bf16[1408,128]{1,0:T(8,128)(2,1)S(1)}, bf16[1408,128]{1,0:T(8,128)(2,1)S(1)}, u32[]{:S(2)}, u32[]{:S(2)}) collective-permute-start(bf16[1408,128]{1,0:T(8,128)(2,1)S(1)} %get-tuple-element.64), channel_id=1, source_target_pairs={{0,16},{16,0},{32,48},{48,32},{64,80},{80,64},{96,112},{112,96},{1... | collective-permute-start | bytes 1081352 | tf_op jit(solution)/shard_map/ppermute | solution.py:532
  20.3 10.6 %collective-permute-start.4 = (bf16[1408,128]{1,0:T(8,128)(2,1)S(1)}, bf16[1408,128]{1,0:T(8,128)(2,1)S(1)}, u32[]{:S(2)}, u32[]{:S(2)}) collective-permute-start(bf16[1408,128]{1,0:T(8,128)(2,1)S(1)} %get-tuple-element.65), channel_id=1, source_target_pairs={{16,32},{32,16},{48,64},{64,48},{80,96},{96,80},{112,128},{128,112... | collective-permute-start | bytes 1081352 | tf_op jit(solution)/shard_map/ppermute | solution.py:538
  26.9 6.3 %collective-permute-start.5 = (bf16[2,160,128]{2,1,0:T(8,128)(2,1)S(1)}, bf16[2,160,128]{2,1,0:T(8,128)(2,1)S(1)}, u32[]{:S(2)}, u32[]{:S(2)}) collective-permute-start(bf16[2,160,128]{2,1,0:T(8,128)(2,1)S(1)} %get-tuple-element.78.refs_0_.near0), channel_id=1, source_target_pairs={{0,32},{16,48},{32,0},{48,16},{64,96},{80,112},{96,64},{112,80},{1... | collective-permute-start | bytes 245768 | tf_op jit(solution)/shard_map/ppermute | solution.py:532
  28.2 6.0 %collective-permute-start.6 = (bf16[2,160,128]{2,1,0:T(8,128)(2,1)S(1)}, bf16[2,160,128]{2,1,0:T(8,128)(2,1)S(1)}, u32[]{:S(2)}, u32[]{:S(2)}) collective-permute-start(bf16[2,160,128]{2,1,0:T(8,128)(2,1)S(1)} %get-tuple-element.78.refs_0_.near0), channel_id=1, source_target_pairs={{0,64},{16,80},{32,96},{48,112},{64,0},{80,16},{96,32},{112,48},{1... | collective-permute-start | bytes 245768 | tf_op jit(solution)/shard_map/ppermute | solution.py:532
  29.9 6.0 %collective-permute-start.7 = (bf16[2,160,128]{2,1,0:T(8,128)(2,1)S(1)}, bf16[2,160,128]{2,1,0:T(8,128)(2,1)S(1)}, u32[]{:S(2)}, u32[]{:S(2)}) collective-permute-start(bf16[2,160,128]{2,1,0:T(8,128)(2,1)S(1)} %get-tuple-element.78.refs_0_.near0), channel_id=1, source_target_pairs={{0,96},{16,112},{32,64},{48,80},{64,32},{80,48},{96,0},{112,16},{1... | collective-permute-start | bytes 245768 | tf_op jit(solution)/shard_map/ppermute | solution.py:532
  35.9 3.0 %collective-permute-start.8 = (bf16[4,2,160,128]{3,2,1,0:T(8,128)(2,1)S(1)}, bf16[4,2,160,128]{3,2,1,0:T(8,128)(2,1)S(1)}, u32[]{:S(2)}, u32[]{:S(2)}) collective-permute-start(bf16[4,2,160,128]{3,2,1,0:T(8,128)(2,1)S(1)} %stack_eight.1), channel_id=1, source_target_pairs={{0,16},{16,0},{32,48},{48,32},{64,80},{80,64},{96,112},{112,96},{1... | collective-permute-start | bytes 983048 | tf_op jit(solution)/shard_map/ppermute | solution.py:532
  42.6 4.9 %collective-permute-start.9 = (bf16[8,160,128]{2,1,0:T(8,128)(2,1)S(1)}, bf16[8,160,128]{2,1,0:T(8,128)(2,1)S(1)}, u32[]{:S(2)}, u32[]{:S(2)}) collective-permute-start(bf16[8,160,128]{2,1,0:T(8,128)(2,1)S(1)} %get-tuple-element.90), channel_id=1, source_target_pairs={{0,16},{16,0},{32,48},{48,32},{64,80},{80,64},{96,112},{112,96},{1... | collective-permute-start | bytes 983048 | tf_op jit(solution)/shard_map/ppermute | solution.py:532
  45.6 1.9 %collective-permute-start.10 = (bf16[8,144,128]{2,1,0:T(8,128)(2,1)S(1)}, bf16[8,144,128]{2,1,0:T(8,128)(2,1)S(1)}, u32[]{:S(2)}, u32[]{:S(2)}) collective-permute-start(bf16[8,144,128]{2,1,0:T(8,128)(2,1)S(1)} %get-tuple-element.91), channel_id=1, source_target_pairs={{0,16},{16,0},{32,48},{48,32},{64,80},{80,64},{96,112},{112,96},{1... | collective-permute-start | bytes 884744 | tf_op jit(solution)/shard_map/ppermute | solution.py:532
  99.3 6.6 %collective-permute-start.11 = (bf16[8,144,128]{2,1,0:T(8,128)(2,1)S(1)}, bf16[8,144,128]{2,1,0:T(8,128)(2,1)S(1)}, u32[]{:S(2)}, u32[]{:S(2)}) collective-permute-start(bf16[8,144,128]{2,1,0:T(8,128)(2,1)S(1)} %all_to_all.23.mine), channel_id=1, source_target_pairs={{0,16},{16,0},{32,48},{48,32},{64,80},{80,64},{96,112},{112,96},{1... | collective-permute-start | bytes 884744 | tf_op jit(solution)/shard_map/ppermute | solution.py:532

commit v12 on v9

--- a/solution.py
+++ b/solution.py
@@ -138,15 +138,14 @@
     return lax.select(even, other, pair), lax.select(even, pair, other)
 
 
-def pack_columns_kernel(meta, feat, cot, conv, proj, pair, other, weights, done):
+def pack_columns_kernel(meta, feat, cot, pair, other, done):
     odd = meta[5] % 2
     pairs = [
         (feat.at[:, aligned(32 - 32 * odd, 32), :], pair.at[:, 0:32, :]),
         (cot.at[:, aligned(48 - 48 * odd, 16), :], pair.at[:, 32:48, :]),
         (feat.at[:, aligned(32 * odd, 32), :], other.at[:, 0:32, :]),
         (cot.at[:, aligned(48 * odd, 16), :], other.at[:, 32:48, :]),
-        (proj, weights.at[144:160, :]),
-    ] + [(conv.at[t], weights.at[16 * t : 16 * t + 16, :]) for t in range(9)]
+    ]
     copies = [pltpu.make_async_copy(a, b, done.at[k]) for k, (a, b) in enumerate(pairs)]
     for copy in copies:
         copy.start()
@@ -162,10 +161,10 @@
     return value if count == 1 else value.reshape(count, 96, CH)
 
 
-def bring_kernel(feat_far, cot_far, feat, cot, done):
-    copies = [
-        pltpu.make_async_copy(a, b, done.at[k]) for k, (a, b) in enumerate(((feat_far, feat), (cot_far, cot)))
-    ]
+def bring_kernel(feat_far, cot_far, conv, proj, feat, cot, weights, done):
+    pairs = [(feat_far, feat), (cot_far, cot), (proj, weights.at[144:160, :])]
+    pairs += [(conv.at[t], weights.at[16 * t : 16 * t + 16, :]) for t in range(9)]
+    copies = [pltpu.make_async_copy(a, b, done.at[k]) for k, (a, b) in enumerate(pairs)]
     for copy in copies:
         copy.start()
     for copy in copies:
@@ -483,7 +482,7 @@
     total[0:304, :] = value
     total[304:336, :] = jnp.zeros((32, CH), F32)
     for k in range(16):
-        out[k] = total[20 * k : 20 * k + 32, :].astype(BF)
+        out[k] = total[20 * k : 20 * k + 24, :].astype(BF)
 
 
 def scatter_column_kernel(got, out):
@@ -497,7 +496,7 @@
 
 def gather_column_kernel(scale, got, conv, proj, fine, total):
     for k in range(16):
-        total[20 * k : 20 * k + 32, :] = got[k].astype(F32)
+        total[20 * k : 20 * k + 24, :] = got[k].astype(F32)
     for k in range(9):
         conv[k] = total[16 * k : 16 * k + 16, :] * scale
     proj[...] = total[144:160, :] * scale
@@ -555,26 +554,26 @@
     slab = ((160, CH), BF)
 
     side = ((16, 48, CH), BF)
-    pair, other, own = call(
+    pair, other = call(
         pack_columns_kernel,
         "pack_columns",
-        (side, side, slab),
-        (meta, feat, cot, conv, coarse_proj),
-        (pltpu.SemaphoreType.DMA((14,)),),
-        far=(1, 2, 3, 4),
+        (side, side),
+        (meta, feat, cot),
+        (pltpu.SemaphoreType.DMA((4,)),),
+        far=(1, 2),
     )
     w1, w2 = (conv_first.reshape(1152, CH), conv_second.reshape(1152, CH))
     big, wide = (((16, 64, CH), BF), ((1536, 256), BF))
-    feat_in, cot_in = call(
+    feat_in, cot_in, own = call(
         bring_kernel,
         "bring",
-        (big, big),
-        (after_all(feat, own), cot),
-        (pltpu.SemaphoreType.DMA((2,)),),
-        far=(0, 1),
+        (big, big, slab),
+        (after_all(feat, pair), cot, conv, coarse_proj),
+        (pltpu.SemaphoreType.DMA((12,)),),
+        far=(0, 1, 2, 3),
         flops=4 * 10**9,
     )
-    own_far = swap(after_all(own, feat_in), "row", 8)
+    own_far = swap(own, "row", 8)
     weight1, weight2, back1, back2 = call(
         weights_kernel,
         "weights",
@@ -593,8 +592,8 @@
         (edge, edge, ((2, 160, CH), BF)),
         (meta, feat_in, cot_in, pair, after_all(other, weight1), own, own_far),
     )
+    outer = swap_outer(outer, "row")
     inner = swap(inner, "row", 1)
-    outer = swap_outer(outer, "row")
     pair_in = after_all(pair, near0)
     near = [near0] + [swap(near0, "row", 2 * k) for k in range(1, 4)]
     parts = inner_step(meta, feat_in, pair_in, other, weight1, weight2)
@@ -613,9 +612,9 @@
     got_f = after_all(got_f, feature_grad)
     part = call(scatter_core_kernel, "scatter_core", (((8, 304, CH), BF),), (keep_c, keep_f, got_c, got_f))[0]
     part = call(
-        scatter_row_kernel, "scatter_row", (((16, 32, CH), BF),), (exchange_row(part),), (((336, CH), F32),)
+        scatter_row_kernel, "scatter_row", (((16, 24, CH), BF),), (exchange_row(part),), (((336, CH), F32),)
     )[0]
-    part = call(scatter_column_kernel, "scatter_column", (((16, 32, CH), BF),), (exchange_column(part),))[0]
+    part = call(scatter_column_kernel, "scatter_column", (((16, 24, CH), BF),), (exchange_column(part),))[0]
     conv_grad, proj_grad, fine = call(
         functools.partial(gather_column_kernel, coarse_scale),
         "gather_column",

time: 107 us -> 106 us (level)
  waiting for transfers between devices: 3.79 us -> 5.45 us
  blocking collectives: 52 us -> 50.7 us
    all_to_all x2, blocking collectives: 24.4 us -> 22.2 us  [exchange_column(): return lax.all_to_all(value, 'col', 0, 0, tiled=True)]
    ppermute x10, waiting for transfers between devices: 3.79 us -> 5.45 us  [swap(): return lax.ppermute(value, axis, [(i, i ^ mask) for i in range(count)])]
  transfers between devices with their start and end apart: 12 -> 12, of which waited for: 4 -> 4; matrix products, arithmetic and copies ran while one was open for 0% -> 0% of each run, Pallas kernels for 13% -> 14%
where the time goes in v12:
time: 106 us
  blocking collectives  50.7 us (48%)
  starting transfers between devices  25.9 us (24%)
  Pallas kernels  22.7 us (21%)
  waiting for transfers between devices  5.45 us (5%)
    all_to_all x2, blocking collectives, exchange_row(): lax.all_to_all(value, 'row', 0, 0, axis_index_groups=groups, tiled=True)  28.5 us
    pallas_call x16, Pallas kernels, call(): pl.pallas_call(kernel, name=name, out_shape=shapes, in_specs=[HBM if k in...  22.7 us
    all_to_all x2, blocking collectives, exchange_column(): return lax.all_to_all(value, 'col', 0, 0, tiled=True)  22.2 us
    ppermute x10, starting transfers between devices, swap(): return lax.ppermute(value, axis, [(i, i ^ mask) for i in range(count)])  22.2 us
    ppermute x10, waiting for transfers between devices, swap(): return lax.ppermute(value, axis, [(i, i ^ mask) for i in range(count)])  5.45 us
    ppermute x2, starting transfers between devices, swap_outer(): return lax.ppermute(value, axis, pairs)  3.69 us
  transfers between devices with their start and end apart: 12, of which 4 were waited for; matrix products, arithmetic and copies ran while one was open for 0% of the time, Pallas kernels for 14%

profile of v12, /device:TPU:1, one launch (start us, length us, event | category | flops | bytes accessed | tf_op | source)
XLA Modules:
  0.0 105.7 jit_solution(6467853557530444862)
XLA Ops:
  0.7 1.6 %pack_columns.1 = (bf16[16,48,128]{2,1,0:T(8,128)(2,1)S(1)}, bf16[16,48,128]{2,1,0:T(8,128)(2,1)S(1)}) custom-call(s32[6]{0:T(128)S(1)} %stack.19.meta, bf16[16,64,128]{2,1,0:T(8,128)(2,1)} %bitcast.18, bf16[16,64,128]{2,1,0:T(8,128)(2,1)} %bitcast.20), custom_call_target="tpu_custom_call" | custom-call | tf_op jit(solution)/shard_map/pack_columns/pallas_call | solution.py:23
  2.3 0.7 collective-permute-start.1
  3.0 5.4 %collective-permute-start = (bf16[16,48,128]{2,1,0:T(8,128)(2,1)S(1)}, bf16[16,48,128]{2,1,0:T(8,128)(2,1)S(1)}, u32[]{:S(2)}, u32[]{:S(2)}) collective-permute-start(bf16[16,48,128]{2,1,0:T(8,128)(2,1)S(1)} %get-tuple-element.60), channel_id=1, source_target_pairs={{0,1},{1,0},{2,3},{3,2},{4,5},{5,4},{6,7},{7,6},{8,9},{9,8},{10,11... | collective-permute-start | bytes 589832 | tf_op jit(solution)/shard_map/ppermute | solution.py:520
  8.4 1.1 %bring.1 = (bf16[16,64,128]{2,1,0:T(8,128)(2,1)S(1)}, bf16[16,64,128]{2,1,0:T(8,128)(2,1)S(1)}, bf16[160,128]{1,0:T(8,128)(2,1)S(1)}) custom-call(bf16[16,64,128]{2,1,0:T(8,128)(2,1)} %bitcast.19, bf16[16,64,128]{2,1,0:T(8,128)(2,1)} %bitcast.21, bf16[9,16,128]{2,1,0:T(8,128)(2,1)} %bitcast.27, bf16[16,128]{1,0:T(8,128)(2,1)} %proj.1), custom_call_target="tpu_custom_call" | custom-call | flops 4000000000 | tf_op jit(solution)/shard_map/bring/pallas_call | solution.py:23
  9.6 3.0 %collective-permute-start.2 = (bf16[160,128]{1,0:T(8,128)(2,1)S(1)}, bf16[160,128]{1,0:T(8,128)(2,1)S(1)}, u32[]{:S(2)}, u32[]{:S(2)}) collective-permute-start(bf16[160,128]{1,0:T(8,128)(2,1)S(1)} %get-tuple-element.68.own), channel_id=1, source_target_pairs={{0,128},{16,144},{32,160},{48,176},{64,192},{80,208},{96,224},{112... | collective-permute-start | bytes 122888 | tf_op jit(solution)/shard_map/ppermute | solution.py:520
  12.6 1.2 %weights.1 = (bf16[1536,256]{1,0:T(8,128)(2,1)S(1)}, bf16[1536,256]{1,0:T(8,128)(2,1)S(1)}, bf16[256,1536]{1,0:T(8,128)(2,1)S(1)}, bf16[256,1536]{1,0:T(8,128)(2,1)S(1)}) custom-call(bf16[1152,128]{1,0:T(8,128)(2,1)} %bitcast.24, bf16[1152,128]{1,0:T(8,128)(2,1)} %bitcast.25), custom_call_target="tpu_custom_call" | custom-call | flops 4000000000 | tf_op jit(solution)/shard_map/weights/pallas_call | solution.py:23
  13.8 1.9 %collective-permute-done.2.far = bf16[160,128]{1,0:T(8,128)(2,1)S(1)} collective-permute-done((bf16[160,128]{1,0:T(8,128)(2,1)S(1)}, bf16[160,128]{1,0:T(8,128)(2,1)S(1)}, u32[]{:S(2)}, u32[]{:S(2)}) %collective-permute-start.2) | collective-permute-done | bytes 40992 | tf_op jit(solution)/shard_map/ppermute | solution.py:520
  15.7 0.6 pack_rows.1
  16.4 3.9 %collective-permute-start.3 = (bf16[1408,128]{1,0:T(8,128)(2,1)S(1)}, bf16[1408,128]{1,0:T(8,128)(2,1)S(1)}, u32[]{:S(2)}, u32[]{:S(2)}) collective-permute-start(bf16[1408,128]{1,0:T(8,128)(2,1)S(1)} %get-tuple-element.69), channel_id=1, source_target_pairs={{0,16},{16,0},{32,48},{48,32},{64,80},{80,64},{96,112},{112,96},{1... | collective-permute-start | bytes 1081352 | tf_op jit(solution)/shard_map/ppermute | solution.py:520
  20.3 3.0 %collective-permute-start.4 = (bf16[1408,128]{1,0:T(8,128)(2,1)S(1)}, bf16[1408,128]{1,0:T(8,128)(2,1)S(1)}, u32[]{:S(2)}, u32[]{:S(2)}) collective-permute-start(bf16[1408,128]{1,0:T(8,128)(2,1)S(1)} %get-tuple-element.70), channel_id=1, source_target_pairs={{16,32},{32,16},{48,64},{64,48},{80,96},{96,80},{112,128},{128,112... | collective-permute-start | bytes 1081352 | tf_op jit(solution)/shard_map/ppermute | solution.py:526
  23.3 1.8 %collective-permute-start.7 = (bf16[2,160,128]{2,1,0:T(8,128)(2,1)S(1)}, bf16[2,160,128]{2,1,0:T(8,128)(2,1)S(1)}, u32[]{:S(2)}, u32[]{:S(2)}) collective-permute-start(bf16[2,160,128]{2,1,0:T(8,128)(2,1)S(1)} %get-tuple-element.87.refs_0_.near0), channel_id=1, source_target_pairs={{0,96},{16,112},{32,64},{48,80},{64,32},{80,48},{96,0},{112,16},{1... | collective-permute-start | bytes 245768 | tf_op jit(solution)/shard_map/ppermute | solution.py:520
  25.1 1.3 %collective-permute-start.6 = (bf16[2,160,128]{2,1,0:T(8,128)(2,1)S(1)}, bf16[2,160,128]{2,1,0:T(8,128)(2,1)S(1)}, u32[]{:S(2)}, u32[]{:S(2)}) collective-permute-start(bf16[2,160,128]{2,1,0:T(8,128)(2,1)S(1)} %get-tuple-element.87.refs_0_.near0), channel_id=1, source_target_pairs={{0,64},{16,80},{32,96},{48,112},{64,0},{80,16},{96,32},{112,48},{1... | collective-permute-start | bytes 245768 | tf_op jit(solution)/shard_map/ppermute | solution.py:520
  26.4 0.3 collective-permute-start.5
  26.7 3.6 %forward_inner.1 = (bf16[16,128,384]{2,1,0:T(8,128)(2,1)S(1)}, bf16[14,128,384]{2,1,0:T(8,128)(2,1)S(1)}, f32[14,96,128]{2,1,0:T(8,128)S(1)}, bf16[6,64,384]{2,1...) custom-call(s32[6]{0:T(128)S(1)} %stack.19.meta, ...), custom_call_target="tpu_custom_call" | custom-call | tf_op jit(solution)/shard_map/forward_inner/pallas_call | solution.py:23
  30.3 3.0 %collective-permute-done.7.refs_3_.near3 = bf16[2,160,128]{2,1,0:T(8,128)(2,1)S(1)} collective-permute-done((bf16[2,160,128]{2,1,0:T(8,128)(2,1)S(1)}, bf16[2,160,128]{2,1,0:T(8,128)(2,1)S(1)}, u32[]{:S(2)}, u32[]{:S(2)}) %collective-permute-start.7) | collective-permute-done | bytes 81952 | tf_op jit(solution)/shard_map/ppermute | solution.py:520
  33.4 3.5 %forward_outer.1 = (bf16[14,64,384]{2,1,0:T(8,128)(2,1)S(1)}, f32[18,96,128]{2,1,0:T(8,128)S(1)}, f32[20,96,128]{2,1,0:T(8,128)S(1)}, bf16[16,64,128]{2,1,0:T(8,...) custom-call(s32[6]{0:T(128)S(1)} %stack.19.meta, ...), custom_call_target="tpu_custom_call" | custom-call | flops 4000000000 | tf_op jit(solution)/shard_map/forward_outer/pallas_call | solution.py:23
  36.9 3.6 %coarse_step.1 = (bf16[256,256]{1,0:T(8,128)(2,1)S(1)}, bf16[256,128]{1,0:T(8,128)(2,1)S(1)}, bf16[8,160,128]{2,1,0:T(8,128)(2,1)S(1)}, bf16[8,160,128]{2,1,0:T(8,128)(2,1)S(1)}, f32[10,48,128]{2,1,0:T(8,128)S(1)}) custom-call(s32[6]{0:T(128)S(1)} %stack.19.meta, bf16[14,64,384]{2,1,0:T(8,128)(2,1)S(1)} %get-tuple-element.86.pool3, ...), custom_call_target="tpu_custom_call" | custom-call | flops 2000000000 | tf_op jit(solution)/shard_map/coarse_step/pallas_call | solution.py:23
  40.5 0.7 collective-permute-start.9
  41.3 2.7 %fine_backward.1 = (bf16[8,144,128]{2,1,0:T(8,128)(2,1)S(1)}, bf16[8,144,128]{2,1,0:T(8,128)(2,1)S(1)}, bf16[18,64,384]{2,1,0:T(8,128)(2,1)S(1)}) custom-call(s32[6]{0:T(128)S(1)} %stack.19.meta, f32[10,48,128]{2,1,0:T(8,128)S(1)} %get-tuple-element.93.pooled_grad, bf16[16,64,128]{2,1,0:T(8,128)(2,1)S(1)} %get-tuple-element.63.cot, ...), custom_call_target="tpu_custom_call" | custom-call | flops 2000000000 | tf_op jit(solution)/shard_map/fine_backward/pallas_call | solution.py:23
  44.0 0.1 collective-permute-start.10
  44.1 1.3 %feature_step.1 = bf16[16,64,128]{2,1,0:T(8,128)(2,1)} custom-call(bf16[18,64,384]{2,1,0:T(8,128)(2,1)S(1)} %get-tuple-element.102.first3, bf16[256,1536]{1,0:T(8,128)(2,1)S(1)} %get-tuple-element.103.back_w), custom_call_target="tpu_custom_call" | custom-call | flops 1000000000 | tf_op jit(solution)/shard_map/feature_step/pallas_call | solution.py:23
  45.4 0.2 collective-permute-done.10.got_f
  45.6 0.1 scatter_core.1
  45.8 18.0 %all_to_all.20.got = bf16[8,304,128]{2,1,0:T(8,128)(2,1)S(1)} all-to-all(bf16[8,304,128]{2,1,0:T(8,128)(2,1)S(1)} %scatter_core.1), channel_id=1, replica_groups={{0,32,64,96,128,160,192,224},{16,48,80,112,144,176,208,240},{1,33,65,97..., dimensions={0} | all-to-all | bytes 1245184 | tf_op jit(solution)/shard_map/all_to_all | solution.py:532
  63.9 12.1 %all_to_all.21.got = bf16[16,24,128]{2,1,0:T(8,128)(2,1)S(1)} all-to-all(bf16[16,24,128]{2,1,0:T(8,128)(2,1)S(1)} %scatter_row.1), channel_id=1, replica_groups=mesh['row'=16,'col'=16] {'col'}, dimensions={0} | all-to-all | bytes 196608 | tf_op jit(solution)/shard_map/all_to_all | solution.py:536
  76.0 10.1 %all_to_all.22.got = bf16[16,24,128]{2,1,0:T(8,128)(2,1)S(1)} all-to-all(bf16[16,24,128]{2,1,0:T(8,128)(2,1)S(1)} %scatter_column.1), channel_id=1, replica_groups=mesh['row'=16,'col'=16] {'col'}, dimensions={0} | all-to-all | bytes 196608 | tf_op jit(solution)/shard_map/all_to_all | solution.py:536
  86.2 0.7 gather_column.1
  86.8 10.5 %all_to_all.23.mine = bf16[8,144,128]{2,1,0:T(8,128)(2,1)S(1)} all-to-all(bf16[8,144,128]{2,1,0:T(8,128)(2,1)S(1)} %get-tuple-element.105), channel_id=1, replica_groups={{0,32,64,96,128,160,192,224},{16,48,80,112,144,176,208,240},{1,33,65,97..., dimensions={0} | all-to-all | bytes 589824 | tf_op jit(solution)/shard_map/all_to_all | solution.py:532
  97.3 5.5 %collective-permute-start.11 = (bf16[8,144,128]{2,1,0:T(8,128)(2,1)S(1)}, bf16[8,144,128]{2,1,0:T(8,128)(2,1)S(1)}, u32[]{:S(2)}, u32[]{:S(2)}) collective-permute-start(bf16[8,144,128]{2,1,0:T(8,128)(2,1)S(1)} %all_to_all.23.mine), channel_id=1, source_target_pairs={{0,16},{16,0},{32,48},{48,32},{64,80},{80,64},{96,112},{112,96},{1... | collective-permute-start | bytes 884744 | tf_op jit(solution)/shard_map/ppermute | solution.py:520
  102.9 0.9 blend.1
  103.8 0.3 collective-permute-done.11.other
  104.1 1.6 %finish.1 = (f32[8,144,128]{2,1,0:T(8,128)}, f32[8,144,128]{2,1,0:T(8,128)}) custom-call(s32[6]{0:T(128)S(1)} %stack.19.meta, bf16[8,144,128]{2,1,0:T(8,128)(2,1)S(1)} %all_to_all.23.mine, bf16[8,144,128]{2,1,0:T(8,128)(2,1)S(1)} %collective-permute-done.11.other), custom_call_target="tpu_custom_call" | custom-call | tf_op jit(solution)/shard_map/finish/pallas_call | solution.py:23
  (14 shorter events, 0.4 us)
Async XLA Ops:
  2.3 11.5 %collective-permute-start.1 = (bf16[16,48,128]{2,1,0:T(8,128)(2,1)S(1)}, bf16[16,48,128]{2,1,0:T(8,128)(2,1)S(1)}, u32[]{:S(2)}, u32[]{:S(2)}) collective-permute-start(bf16[16,48,128]{2,1,0:T(8,128)(2,1)S(1)} %get-tuple-element.64), channel_id=1, source_target_pairs={{1,2},{2,1},{3,4},{4,3},{5,6},{6,5},{7,8},{8,7},{9,10},{10,9},{11,... | collective-permute-start | bytes 589832 | tf_op jit(solution)/shard_map/ppermute | solution.py:526
  3.0 12.7 %collective-permute-start = (bf16[16,48,128]{2,1,0:T(8,128)(2,1)S(1)}, bf16[16,48,128]{2,1,0:T(8,128)(2,1)S(1)}, u32[]{:S(2)}, u32[]{:S(2)}) collective-permute-start(bf16[16,48,128]{2,1,0:T(8,128)(2,1)S(1)} %get-tuple-element.60), channel_id=1, source_target_pairs={{0,1},{1,0},{2,3},{3,2},{4,5},{5,4},{6,7},{7,6},{8,9},{9,8},{10,11... | collective-permute-start | bytes 589832 | tf_op jit(solution)/shard_map/ppermute | solution.py:520
  9.6 6.1 %collective-permute-start.2 = (bf16[160,128]{1,0:T(8,128)(2,1)S(1)}, bf16[160,128]{1,0:T(8,128)(2,1)S(1)}, u32[]{:S(2)}, u32[]{:S(2)}) collective-permute-start(bf16[160,128]{1,0:T(8,128)(2,1)S(1)} %get-tuple-element.68.own), channel_id=1, source_target_pairs={{0,128},{16,144},{32,160},{48,176},{64,192},{80,208},{96,224},{112... | collective-permute-start | bytes 122888 | tf_op jit(solution)/shard_map/ppermute | solution.py:520
  16.4 17.1 %collective-permute-start.3 = (bf16[1408,128]{1,0:T(8,128)(2,1)S(1)}, bf16[1408,128]{1,0:T(8,128)(2,1)S(1)}, u32[]{:S(2)}, u32[]{:S(2)}) collective-permute-start(bf16[1408,128]{1,0:T(8,128)(2,1)S(1)} %get-tuple-element.69), channel_id=1, source_target_pairs={{0,16},{16,0},{32,48},{48,32},{64,80},{80,64},{96,112},{112,96},{1... | collective-permute-start | bytes 1081352 | tf_op jit(solution)/shard_map/ppermute | solution.py:520
  20.3 13.1 %collective-permute-start.4 = (bf16[1408,128]{1,0:T(8,128)(2,1)S(1)}, bf16[1408,128]{1,0:T(8,128)(2,1)S(1)}, u32[]{:S(2)}, u32[]{:S(2)}) collective-permute-start(bf16[1408,128]{1,0:T(8,128)(2,1)S(1)} %get-tuple-element.70), channel_id=1, source_target_pairs={{16,32},{32,16},{48,64},{64,48},{80,96},{96,80},{112,128},{128,112... | collective-permute-start | bytes 1081352 | tf_op jit(solution)/shard_map/ppermute | solution.py:526
  23.3 10.0 %collective-permute-start.7 = (bf16[2,160,128]{2,1,0:T(8,128)(2,1)S(1)}, bf16[2,160,128]{2,1,0:T(8,128)(2,1)S(1)}, u32[]{:S(2)}, u32[]{:S(2)}) collective-permute-start(bf16[2,160,128]{2,1,0:T(8,128)(2,1)S(1)} %get-tuple-element.87.refs_0_.near0), channel_id=1, source_target_pairs={{0,96},{16,112},{32,64},{48,80},{64,32},{80,48},{96,0},{112,16},{1... | collective-permute-start | bytes 245768 | tf_op jit(solution)/shard_map/ppermute | solution.py:520
  25.1 8.2 %collective-permute-start.6 = (bf16[2,160,128]{2,1,0:T(8,128)(2,1)S(1)}, bf16[2,160,128]{2,1,0:T(8,128)(2,1)S(1)}, u32[]{:S(2)}, u32[]{:S(2)}) collective-permute-start(bf16[2,160,128]{2,1,0:T(8,128)(2,1)S(1)} %get-tuple-element.87.refs_0_.near0), channel_id=1, source_target_pairs={{0,64},{16,80},{32,96},{48,112},{64,0},{80,16},{96,32},{112,48},{1... | collective-permute-start | bytes 245768 | tf_op jit(solution)/shard_map/ppermute | solution.py:520
  26.4 6.9 %collective-permute-start.5 = (bf16[2,160,128]{2,1,0:T(8,128)(2,1)S(1)}, bf16[2,160,128]{2,1,0:T(8,128)(2,1)S(1)}, u32[]{:S(2)}, u32[]{:S(2)}) collective-permute-start(bf16[2,160,128]{2,1,0:T(8,128)(2,1)S(1)} %get-tuple-element.87.refs_0_.near0), channel_id=1, source_target_pairs={{0,32},{16,48},{32,0},{48,16},{64,96},{80,112},{96,64},{112,80},{1... | collective-permute-start | bytes 245768 | tf_op jit(solution)/shard_map/ppermute | solution.py:520
  33.3 3.6 %collective-permute-start.8 = (bf16[4,2,160,128]{3,2,1,0:T(8,128)(2,1)S(1)}, bf16[4,2,160,128]{3,2,1,0:T(8,128)(2,1)S(1)}, u32[]{:S(2)}, u32[]{:S(2)}) collective-permute-start(bf16[4,2,160,128]{3,2,1,0:T(8,128)(2,1)S(1)} %stack_eight.1), channel_id=1, source_target_pairs={{0,16},{16,0},{32,48},{48,32},{64,80},{80,64},{96,112},{112,96},{1... | collective-permute-start | bytes 983048 | tf_op jit(solution)/shard_map/ppermute | solution.py:520
  40.5 5.1 %collective-permute-start.9 = (bf16[8,160,128]{2,1,0:T(8,128)(2,1)S(1)}, bf16[8,160,128]{2,1,0:T(8,128)(2,1)S(1)}, u32[]{:S(2)}, u32[]{:S(2)}) collective-permute-start(bf16[8,160,128]{2,1,0:T(8,128)(2,1)S(1)} %get-tuple-element.100), channel_id=1, source_target_pairs={{0,16},{16,0},{32,48},{48,32},{64,80},{80,64},{96,112},{112,96},{1... | collective-permute-start | bytes 983048 | tf_op jit(solution)/shard_map/ppermute | solution.py:520
  44.0 1.7 %collective-permute-start.10 = (bf16[8,144,128]{2,1,0:T(8,128)(2,1)S(1)}, bf16[8,144,128]{2,1,0:T(8,128)(2,1)S(1)}, u32[]{:S(2)}, u32[]{:S(2)}) collective-permute-start(bf16[8,144,128]{2,1,0:T(8,128)(2,1)S(1)} %get-tuple-element.101), channel_id=1, source_target_pairs={{0,16},{16,0},{32,48},{48,32},{64,80},{80,64},{96,112},{112,96},{1... | collective-permute-start | bytes 884744 | tf_op jit(solution)/shard_map/ppermute | solution.py:520
  97.3 6.7 %collective-permute-start.11 = (bf16[8,144,128]{2,1,0:T(8,128)(2,1)S(1)}, bf16[8,144,128]{2,1,0:T(8,128)(2,1)S(1)}, u32[]{:S(2)}, u32[]{:S(2)}) collective-permute-start(bf16[8,144,128]{2,1,0:T(8,128)(2,1)S(1)} %all_to_all.23.mine), channel_id=1, source_target_pairs={{0,16},{16,0},{32,48},{48,32},{64,80},{80,64},{96,112},{112,96},{1... | collective-permute-start | bytes 884744 | tf_op jit(solution)/shard_map/ppermute | solution.py:520

commit v13 on v12

--- a/solution.py
+++ b/solution.py
@@ -471,23 +471,26 @@
 
 def scatter_core_kernel(keep_c, keep_f, got_c, got_f, out):
     for k in range(8):
-        out[k, 0:160, :] = (keep_c[k].astype(F32) + got_c[k].astype(F32)).astype(BF)
-        out[k, 160:304, :] = (keep_f[k].astype(F32) + got_f[k].astype(F32)).astype(BF)
-
-
-def scatter_row_kernel(got, out, total):
+        coarse = keep_c[k].astype(F32) + got_c[k].astype(F32)
+        fine = keep_f[k].astype(F32) + got_f[k].astype(F32)
+        for j in range(2):
+            out[2 * k + j, 0:80, :] = coarse[80 * j : 80 * j + 80].astype(BF)
+            out[2 * k + j, 80:152, :] = fine[72 * j : 72 * j + 72].astype(BF)
+
+
+def scatter_plane_kernel(got, out, total):
+    value = got[0].astype(F32)
+    for k in range(1, 16):
+        value = value + got[k].astype(F32)
+    total[0:152, :] = value
+    total[152:160, :] = jnp.zeros((8, CH), F32)
+    for k in range(8):
+        out[k] = total[19 * k : 19 * k + 24, :].astype(BF)
+
+
+def scatter_column_kernel(got, out):
     value = got[0].astype(F32)
     for k in range(1, 8):
-        value = value + got[k].astype(F32)
-    total[0:304, :] = value
-    total[304:336, :] = jnp.zeros((32, CH), F32)
-    for k in range(16):
-        out[k] = total[20 * k : 20 * k + 24, :].astype(BF)
-
-
-def scatter_column_kernel(got, out):
-    value = got[0].astype(F32)
-    for k in range(1, 16):
         value = value + got[k].astype(F32)
     value = value.astype(BF)
     for k in range(16):
@@ -495,12 +498,13 @@
 
 
 def gather_column_kernel(scale, got, conv, proj, fine, total):
-    for k in range(16):
-        total[20 * k : 20 * k + 24, :] = got[k].astype(F32)
+    for j in range(2):
+        for k in range(8):
+            total[j, 19 * k : 19 * k + 24, :] = got[8 * j + k].astype(F32)
     for k in range(9):
-        conv[k] = total[16 * k : 16 * k + 16, :] * scale
-    proj[...] = total[144:160, :] * scale
-    value = total[160:304, :].astype(BF)
+        conv[k] = total[k // 5, 16 * (k % 5) : 16 * (k % 5) + 16, :] * scale
+    proj[...] = total[1, 64:80, :] * scale
+    value = jnp.concatenate([total[0, 80:152, :], total[1, 80:152, :]], axis=0).astype(BF)
     for k in range(8):
         fine[k] = value
 
@@ -530,6 +534,21 @@
     count = lax.axis_size("row")
     groups = [list(range(c, count, 2)) for c in range(2)]
     return lax.all_to_all(value, "row", 0, 0, axis_index_groups=groups, tiled=True)
+
+
+def exchange_plane(value):
+    rows, cols = (lax.axis_size("row"), lax.axis_size("col"))
+    groups = []
+    for core in range(2):
+        for z in range(cols // 2):
+            groups.append([r * cols + c for r in range(core, rows, 2) for c in (z, z + cols // 2)])
+    return lax.all_to_all(value, ("row", "col"), 0, 0, axis_index_groups=groups, tiled=True)
+
+
+def exchange_depth(value):
+    count = lax.axis_size("col")
+    groups = [list(range(k, k + count // 2)) for k in (0, count // 2)]
+    return lax.all_to_all(value, "col", 0, 0, axis_index_groups=groups, tiled=True)
 
 
 def exchange_column(value):
@@ -610,17 +629,17 @@
     feature_grad = feature_step(first3, back1)
 
     got_f = after_all(got_f, feature_grad)
-    part = call(scatter_core_kernel, "scatter_core", (((8, 304, CH), BF),), (keep_c, keep_f, got_c, got_f))[0]
+    part = call(scatter_core_kernel, "scatter_core", (((16, 152, CH), BF),), (keep_c, keep_f, got_c, got_f))[0]
     part = call(
-        scatter_row_kernel, "scatter_row", (((16, 24, CH), BF),), (exchange_row(part),), (((336, CH), F32),)
+        scatter_plane_kernel, "scatter_plane", (((8, 24, CH), BF),), (exchange_plane(part),), (((160, CH), F32),)
     )[0]
-    part = call(scatter_column_kernel, "scatter_column", (((16, 24, CH), BF),), (exchange_column(part),))[0]
+    part = call(scatter_column_kernel, "scatter_column", (((16, 24, CH), BF),), (exchange_depth(part),))[0]
     conv_grad, proj_grad, fine = call(
         functools.partial(gather_column_kernel, coarse_scale),
         "gather_column",
         (((9, 16, CH), F32), ((16, CH), F32), ((8, 144, CH), BF)),
         (exchange_column(part),),
-        (((336, CH), F32),),
+        (((2, 160, CH), F32),),
     )
     fine = exchange_row(fine)
     blended = call(blend_kernel, "blend", (((16, 64, CH), BF),), (after_all(own_act, fine), proj, act), flops=10**9)[0]

time: 106 us -> 105 us (level)
    all_to_all x0 -> x2, blocking collectives: none -> 28.4 us  [the longest x1 17.1 us: exchange_plane(): lax.all_to_all(value, ('row', 'col'), 0, 0, axis_index_groups=groups, til...]
    all_to_all x2 -> x1, blocking collectives: 28.5 us -> 11.5 us  [exchange_row(): lax.all_to_all(value, 'row', 0, 0, axis_index_groups=groups, tiled=True)]
    all_to_all x2 -> x1, blocking collectives: 22.2 us -> 9.98 us  [exchange_column(): return lax.all_to_all(value, 'col', 0, 0, tiled=True)]
where the time goes in v13:
time: 105 us
  blocking collectives  49.9 us (48%)
  starting transfers between devices  25.7 us (24%)
  Pallas kernels  22.7 us (22%)
  waiting for transfers between devices  5.45 us (5%)
    pallas_call x16, Pallas kernels, call(): pl.pallas_call(kernel, name=name, out_shape=shapes, in_specs=[HBM if k in...  22.7 us
    ppermute x10, starting transfers between devices, swap(): return lax.ppermute(value, axis, [(i, i ^ mask) for i in range(count)])  22 us
    all_to_all x1, blocking collectives, exchange_plane(): lax.all_to_all(value, ('row', 'col'), 0, 0, axis_index_groups=groups, til...  17.1 us
    all_to_all x1, blocking collectives, exchange_row(): lax.all_to_all(value, 'row', 0, 0, axis_index_groups=groups, tiled=True)  11.5 us
    all_to_all x1, blocking collectives, exchange_depth(): lax.all_to_all(value, 'col', 0, 0, axis_index_groups=groups, tiled=True)  11.3 us
    all_to_all x1, blocking collectives, exchange_column(): return lax.all_to_all(value, 'col', 0, 0, tiled=True)  9.98 us
    ppermute x10, waiting for transfers between devices, swap(): return lax.ppermute(value, axis, [(i, i ^ mask) for i in range(count)])  5.45 us
    ppermute x2, starting transfers between devices, swap_outer(): return lax.ppermute(value, axis, pairs)  3.69 us
  transfers between devices with their start and end apart: 12, of which 4 were waited for; matrix products, arithmetic and copies ran while one was open for 0% of the time, Pallas kernels for 14%

profile of v13, /device:TPU:1, one launch (start us, length us, event | category | flops | bytes accessed | tf_op | source)
XLA Modules:
  0.0 104.7 jit_solution(2015145702088175522)
XLA Ops:
  0.7 1.6 %pack_columns.1 = (bf16[16,48,128]{2,1,0:T(8,128)(2,1)S(1)}, bf16[16,48,128]{2,1,0:T(8,128)(2,1)S(1)}) custom-call(s32[6]{0:T(128)S(1)} %stack.19.meta, bf16[16,64,128]{2,1,0:T(8,128)(2,1)} %bitcast.18, bf16[16,64,128]{2,1,0:T(8,128)(2,1)} %bitcast.20), custom_call_target="tpu_custom_call" | custom-call | tf_op jit(solution)/shard_map/pack_columns/pallas_call | solution.py:23
  2.3 0.7 collective-permute-start.1
  3.0 5.4 %collective-permute-start = (bf16[16,48,128]{2,1,0:T(8,128)(2,1)S(1)}, bf16[16,48,128]{2,1,0:T(8,128)(2,1)S(1)}, u32[]{:S(2)}, u32[]{:S(2)}) collective-permute-start(bf16[16,48,128]{2,1,0:T(8,128)(2,1)S(1)} %get-tuple-element.60), channel_id=1, source_target_pairs={{0,1},{1,0},{2,3},{3,2},{4,5},{5,4},{6,7},{7,6},{8,9},{9,8},{10,11... | collective-permute-start | bytes 589832 | tf_op jit(solution)/shard_map/ppermute | solution.py:524
  8.4 1.1 %bring.1 = (bf16[16,64,128]{2,1,0:T(8,128)(2,1)S(1)}, bf16[16,64,128]{2,1,0:T(8,128)(2,1)S(1)}, bf16[160,128]{1,0:T(8,128)(2,1)S(1)}) custom-call(bf16[16,64,128]{2,1,0:T(8,128)(2,1)} %bitcast.19, bf16[16,64,128]{2,1,0:T(8,128)(2,1)} %bitcast.21, bf16[9,16,128]{2,1,0:T(8,128)(2,1)} %bitcast.27, bf16[16,128]{1,0:T(8,128)(2,1)} %proj.1), custom_call_target="tpu_custom_call" | custom-call | flops 4000000000 | tf_op jit(solution)/shard_map/bring/pallas_call | solution.py:23
  9.6 3.0 %collective-permute-start.2 = (bf16[160,128]{1,0:T(8,128)(2,1)S(1)}, bf16[160,128]{1,0:T(8,128)(2,1)S(1)}, u32[]{:S(2)}, u32[]{:S(2)}) collective-permute-start(bf16[160,128]{1,0:T(8,128)(2,1)S(1)} %get-tuple-element.68.own), channel_id=1, source_target_pairs={{0,128},{16,144},{32,160},{48,176},{64,192},{80,208},{96,224},{112... | collective-permute-start | bytes 122888 | tf_op jit(solution)/shard_map/ppermute | solution.py:524
  12.6 1.2 %weights.1 = (bf16[1536,256]{1,0:T(8,128)(2,1)S(1)}, bf16[1536,256]{1,0:T(8,128)(2,1)S(1)}, bf16[256,1536]{1,0:T(8,128)(2,1)S(1)}, bf16[256,1536]{1,0:T(8,128)(2,1)S(1)}) custom-call(bf16[1152,128]{1,0:T(8,128)(2,1)} %bitcast.24, bf16[1152,128]{1,0:T(8,128)(2,1)} %bitcast.25), custom_call_target="tpu_custom_call" | custom-call | flops 4000000000 | tf_op jit(solution)/shard_map/weights/pallas_call | solution.py:23
  13.8 1.9 %collective-permute-done.2.far = bf16[160,128]{1,0:T(8,128)(2,1)S(1)} collective-permute-done((bf16[160,128]{1,0:T(8,128)(2,1)S(1)}, bf16[160,128]{1,0:T(8,128)(2,1)S(1)}, u32[]{:S(2)}, u32[]{:S(2)}) %collective-permute-start.2) | collective-permute-done | bytes 40992 | tf_op jit(solution)/shard_map/ppermute | solution.py:524
  15.7 0.6 pack_rows.1
  16.4 3.9 %collective-permute-start.3 = (bf16[1408,128]{1,0:T(8,128)(2,1)S(1)}, bf16[1408,128]{1,0:T(8,128)(2,1)S(1)}, u32[]{:S(2)}, u32[]{:S(2)}) collective-permute-start(bf16[1408,128]{1,0:T(8,128)(2,1)S(1)} %get-tuple-element.69), channel_id=1, source_target_pairs={{0,16},{16,0},{32,48},{48,32},{64,80},{80,64},{96,112},{112,96},{1... | collective-permute-start | bytes 1081352 | tf_op jit(solution)/shard_map/ppermute | solution.py:524
  20.3 3.0 %collective-permute-start.4 = (bf16[1408,128]{1,0:T(8,128)(2,1)S(1)}, bf16[1408,128]{1,0:T(8,128)(2,1)S(1)}, u32[]{:S(2)}, u32[]{:S(2)}) collective-permute-start(bf16[1408,128]{1,0:T(8,128)(2,1)S(1)} %get-tuple-element.70), channel_id=1, source_target_pairs={{16,32},{32,16},{48,64},{64,48},{80,96},{96,80},{112,128},{128,112... | collective-permute-start | bytes 1081352 | tf_op jit(solution)/shard_map/ppermute | solution.py:530
  23.3 1.8 %collective-permute-start.7 = (bf16[2,160,128]{2,1,0:T(8,128)(2,1)S(1)}, bf16[2,160,128]{2,1,0:T(8,128)(2,1)S(1)}, u32[]{:S(2)}, u32[]{:S(2)}) collective-permute-start(bf16[2,160,128]{2,1,0:T(8,128)(2,1)S(1)} %get-tuple-element.87.refs_0_.near0), channel_id=1, source_target_pairs={{0,96},{16,112},{32,64},{48,80},{64,32},{80,48},{96,0},{112,16},{1... | collective-permute-start | bytes 245768 | tf_op jit(solution)/shard_map/ppermute | solution.py:524
  25.1 1.3 %collective-permute-start.6 = (bf16[2,160,128]{2,1,0:T(8,128)(2,1)S(1)}, bf16[2,160,128]{2,1,0:T(8,128)(2,1)S(1)}, u32[]{:S(2)}, u32[]{:S(2)}) collective-permute-start(bf16[2,160,128]{2,1,0:T(8,128)(2,1)S(1)} %get-tuple-element.87.refs_0_.near0), channel_id=1, source_target_pairs={{0,64},{16,80},{32,96},{48,112},{64,0},{80,16},{96,32},{112,48},{1... | collective-permute-start | bytes 245768 | tf_op jit(solution)/shard_map/ppermute | solution.py:524
  26.4 0.3 collective-permute-start.5
  26.7 3.6 %forward_inner.1 = (bf16[16,128,384]{2,1,0:T(8,128)(2,1)S(1)}, bf16[14,128,384]{2,1,0:T(8,128)(2,1)S(1)}, f32[14,96,128]{2,1,0:T(8,128)S(1)}, bf16[6,64,384]{2,1...) custom-call(s32[6]{0:T(128)S(1)} %stack.19.meta, ...), custom_call_target="tpu_custom_call" | custom-call | tf_op jit(solution)/shard_map/forward_inner/pallas_call | solution.py:23
  30.3 3.0 %collective-permute-done.7.refs_3_.near3 = bf16[2,160,128]{2,1,0:T(8,128)(2,1)S(1)} collective-permute-done((bf16[2,160,128]{2,1,0:T(8,128)(2,1)S(1)}, bf16[2,160,128]{2,1,0:T(8,128)(2,1)S(1)}, u32[]{:S(2)}, u32[]{:S(2)}) %collective-permute-start.7) | collective-permute-done | bytes 81952 | tf_op jit(solution)/shard_map/ppermute | solution.py:524
  33.4 3.5 %forward_outer.1 = (bf16[14,64,384]{2,1,0:T(8,128)(2,1)S(1)}, f32[18,96,128]{2,1,0:T(8,128)S(1)}, f32[20,96,128]{2,1,0:T(8,128)S(1)}, bf16[16,64,128]{2,1,0:T(8,...) custom-call(s32[6]{0:T(128)S(1)} %stack.19.meta, ...), custom_call_target="tpu_custom_call" | custom-call | flops 4000000000 | tf_op jit(solution)/shard_map/forward_outer/pallas_call | solution.py:23
  36.9 3.6 %coarse_step.1 = (bf16[256,256]{1,0:T(8,128)(2,1)S(1)}, bf16[256,128]{1,0:T(8,128)(2,1)S(1)}, bf16[8,160,128]{2,1,0:T(8,128)(2,1)S(1)}, bf16[8,160,128]{2,1,0:T(8,128)(2,1)S(1)}, f32[10,48,128]{2,1,0:T(8,128)S(1)}) custom-call(s32[6]{0:T(128)S(1)} %stack.19.meta, bf16[14,64,384]{2,1,0:T(8,128)(2,1)S(1)} %get-tuple-element.86.pool3, ...), custom_call_target="tpu_custom_call" | custom-call | flops 2000000000 | tf_op jit(solution)/shard_map/coarse_step/pallas_call | solution.py:23
  40.5 0.7 collective-permute-start.9
  41.3 2.7 %fine_backward.1 = (bf16[8,144,128]{2,1,0:T(8,128)(2,1)S(1)}, bf16[8,144,128]{2,1,0:T(8,128)(2,1)S(1)}, bf16[18,64,384]{2,1,0:T(8,128)(2,1)S(1)}) custom-call(s32[6]{0:T(128)S(1)} %stack.19.meta, f32[10,48,128]{2,1,0:T(8,128)S(1)} %get-tuple-element.93.pooled_grad, bf16[16,64,128]{2,1,0:T(8,128)(2,1)S(1)} %get-tuple-element.63.cot, ...), custom_call_target="tpu_custom_call" | custom-call | flops 2000000000 | tf_op jit(solution)/shard_map/fine_backward/pallas_call | solution.py:23
  44.0 0.1 collective-permute-start.10
  44.1 1.3 %feature_step.1 = bf16[16,64,128]{2,1,0:T(8,128)(2,1)} custom-call(bf16[18,64,384]{2,1,0:T(8,128)(2,1)S(1)} %get-tuple-element.102.first3, bf16[256,1536]{1,0:T(8,128)(2,1)S(1)} %get-tuple-element.103.back_w), custom_call_target="tpu_custom_call" | custom-call | flops 1000000000 | tf_op jit(solution)/shard_map/feature_step/pallas_call | solution.py:23
  45.4 0.2 collective-permute-done.10.got_f
  45.6 0.1 scatter_core.1
  45.8 17.1 %all_to_all.20.got = bf16[16,152,128]{2,1,0:T(8,128)(2,1)S(1)} all-to-all(bf16[16,152,128]{2,1,0:T(8,128)(2,1)S(1)} %scatter_core.1), channel_id=1, replica_groups={{0,8,32,40,64,72,96,104,128,136,160,168,192,200,224,232},{1,9,33,41,65,..., dimensions={0} | all-to-all | bytes 1245184 | tf_op jit(solution)/shard_map/all_to_all | solution.py:545
  63.0 11.3 %all_to_all.21.got = bf16[8,24,128]{2,1,0:T(8,128)(2,1)S(1)} all-to-all(bf16[8,24,128]{2,1,0:T(8,128)(2,1)S(1)} %scatter_plane.1), channel_id=1, replica_groups={{0,1,2,3,4,5,6,7},{8,9,10,11,12,13,14,15},{16,17,18,19,20,21,22,23},{24..., dimensions={0} | all-to-all | bytes 98304 | tf_op jit(solution)/shard_map/all_to_all | solution.py:551
  74.4 10.0 %all_to_all.22.got = bf16[16,24,128]{2,1,0:T(8,128)(2,1)S(1)} all-to-all(bf16[16,24,128]{2,1,0:T(8,128)(2,1)S(1)} %scatter_column.1), channel_id=1, replica_groups=mesh['row'=16,'col'=16] {'col'}, dimensions={0} | all-to-all | bytes 196608 | tf_op jit(solution)/shard_map/all_to_all | solution.py:555
  84.3 0.7 gather_column.1
  85.0 11.5 %all_to_all.23.mine = bf16[8,144,128]{2,1,0:T(8,128)(2,1)S(1)} all-to-all(bf16[8,144,128]{2,1,0:T(8,128)(2,1)S(1)} %get-tuple-element.105), channel_id=1, replica_groups={{0,32,64,96,128,160,192,224},{16,48,80,112,144,176,208,240},{1,33,65,97..., dimensions={0} | all-to-all | bytes 589824 | tf_op jit(solution)/shard_map/all_to_all | solution.py:536
  96.5 5.4 %collective-permute-start.11 = (bf16[8,144,128]{2,1,0:T(8,128)(2,1)S(1)}, bf16[8,144,128]{2,1,0:T(8,128)(2,1)S(1)}, u32[]{:S(2)}, u32[]{:S(2)}) collective-permute-start(bf16[8,144,128]{2,1,0:T(8,128)(2,1)S(1)} %all_to_all.23.mine), channel_id=1, source_target_pairs={{0,16},{16,0},{32,48},{48,32},{64,80},{80,64},{96,112},{112,96},{1... | collective-permute-start | bytes 884744 | tf_op jit(solution)/shard_map/ppermute | solution.py:524
  101.9 0.9 blend.1
  102.8 0.3 collective-permute-done.11.other
  103.1 1.6 %finish.1 = (f32[8,144,128]{2,1,0:T(8,128)}, f32[8,144,128]{2,1,0:T(8,128)}) custom-call(s32[6]{0:T(128)S(1)} %stack.19.meta, bf16[8,144,128]{2,1,0:T(8,128)(2,1)S(1)} %all_to_all.23.mine, bf16[8,144,128]{2,1,0:T(8,128)(2,1)S(1)} %collective-permute-done.11.other), custom_call_target="tpu_custom_call" | custom-call | tf_op jit(solution)/shard_map/finish/pallas_call | solution.py:23
  (14 shorter events, 0.3 us)
Async XLA Ops:
  2.3 11.5 %collective-permute-start.1 = (bf16[16,48,128]{2,1,0:T(8,128)(2,1)S(1)}, bf16[16,48,128]{2,1,0:T(8,128)(2,1)S(1)}, u32[]{:S(2)}, u32[]{:S(2)}) collective-permute-start(bf16[16,48,128]{2,1,0:T(8,128)(2,1)S(1)} %get-tuple-element.64), channel_id=1, source_target_pairs={{1,2},{2,1},{3,4},{4,3},{5,6},{6,5},{7,8},{8,7},{9,10},{10,9},{11,... | collective-permute-start | bytes 589832 | tf_op jit(solution)/shard_map/ppermute | solution.py:530
  3.0 12.7 %collective-permute-start = (bf16[16,48,128]{2,1,0:T(8,128)(2,1)S(1)}, bf16[16,48,128]{2,1,0:T(8,128)(2,1)S(1)}, u32[]{:S(2)}, u32[]{:S(2)}) collective-permute-start(bf16[16,48,128]{2,1,0:T(8,128)(2,1)S(1)} %get-tuple-element.60), channel_id=1, source_target_pairs={{0,1},{1,0},{2,3},{3,2},{4,5},{5,4},{6,7},{7,6},{8,9},{9,8},{10,11... | collective-permute-start | bytes 589832 | tf_op jit(solution)/shard_map/ppermute | solution.py:524
  9.6 6.1 %collective-permute-start.2 = (bf16[160,128]{1,0:T(8,128)(2,1)S(1)}, bf16[160,128]{1,0:T(8,128)(2,1)S(1)}, u32[]{:S(2)}, u32[]{:S(2)}) collective-permute-start(bf16[160,128]{1,0:T(8,128)(2,1)S(1)} %get-tuple-element.68.own), channel_id=1, source_target_pairs={{0,128},{16,144},{32,160},{48,176},{64,192},{80,208},{96,224},{112... | collective-permute-start | bytes 122888 | tf_op jit(solution)/shard_map/ppermute | solution.py:524
  16.4 17.1 %collective-permute-start.3 = (bf16[1408,128]{1,0:T(8,128)(2,1)S(1)}, bf16[1408,128]{1,0:T(8,128)(2,1)S(1)}, u32[]{:S(2)}, u32[]{:S(2)}) collective-permute-start(bf16[1408,128]{1,0:T(8,128)(2,1)S(1)} %get-tuple-element.69), channel_id=1, source_target_pairs={{0,16},{16,0},{32,48},{48,32},{64,80},{80,64},{96,112},{112,96},{1... | collective-permute-start | bytes 1081352 | tf_op jit(solution)/shard_map/ppermute | solution.py:524
  20.3 13.1 %collective-permute-start.4 = (bf16[1408,128]{1,0:T(8,128)(2,1)S(1)}, bf16[1408,128]{1,0:T(8,128)(2,1)S(1)}, u32[]{:S(2)}, u32[]{:S(2)}) collective-permute-start(bf16[1408,128]{1,0:T(8,128)(2,1)S(1)} %get-tuple-element.70), channel_id=1, source_target_pairs={{16,32},{32,16},{48,64},{64,48},{80,96},{96,80},{112,128},{128,112... | collective-permute-start | bytes 1081352 | tf_op jit(solution)/shard_map/ppermute | solution.py:530
  23.3 10.0 %collective-permute-start.7 = (bf16[2,160,128]{2,1,0:T(8,128)(2,1)S(1)}, bf16[2,160,128]{2,1,0:T(8,128)(2,1)S(1)}, u32[]{:S(2)}, u32[]{:S(2)}) collective-permute-start(bf16[2,160,128]{2,1,0:T(8,128)(2,1)S(1)} %get-tuple-element.87.refs_0_.near0), channel_id=1, source_target_pairs={{0,96},{16,112},{32,64},{48,80},{64,32},{80,48},{96,0},{112,16},{1... | collective-permute-start | bytes 245768 | tf_op jit(solution)/shard_map/ppermute | solution.py:524
  25.1 8.2 %collective-permute-start.6 = (bf16[2,160,128]{2,1,0:T(8,128)(2,1)S(1)}, bf16[2,160,128]{2,1,0:T(8,128)(2,1)S(1)}, u32[]{:S(2)}, u32[]{:S(2)}) collective-permute-start(bf16[2,160,128]{2,1,0:T(8,128)(2,1)S(1)} %get-tuple-element.87.refs_0_.near0), channel_id=1, source_target_pairs={{0,64},{16,80},{32,96},{48,112},{64,0},{80,16},{96,32},{112,48},{1... | collective-permute-start | bytes 245768 | tf_op jit(solution)/shard_map/ppermute | solution.py:524
  26.4 6.9 %collective-permute-start.5 = (bf16[2,160,128]{2,1,0:T(8,128)(2,1)S(1)}, bf16[2,160,128]{2,1,0:T(8,128)(2,1)S(1)}, u32[]{:S(2)}, u32[]{:S(2)}) collective-permute-start(bf16[2,160,128]{2,1,0:T(8,128)(2,1)S(1)} %get-tuple-element.87.refs_0_.near0), channel_id=1, source_target_pairs={{0,32},{16,48},{32,0},{48,16},{64,96},{80,112},{96,64},{112,80},{1... | collective-permute-start | bytes 245768 | tf_op jit(solution)/shard_map/ppermute | solution.py:524
  33.3 3.6 %collective-permute-start.8 = (bf16[4,2,160,128]{3,2,1,0:T(8,128)(2,1)S(1)}, bf16[4,2,160,128]{3,2,1,0:T(8,128)(2,1)S(1)}, u32[]{:S(2)}, u32[]{:S(2)}) collective-permute-start(bf16[4,2,160,128]{3,2,1,0:T(8,128)(2,1)S(1)} %stack_eight.1), channel_id=1, source_target_pairs={{0,16},{16,0},{32,48},{48,32},{64,80},{80,64},{96,112},{112,96},{1... | collective-permute-start | bytes 983048 | tf_op jit(solution)/shard_map/ppermute | solution.py:524
  40.5 5.1 %collective-permute-start.9 = (bf16[8,160,128]{2,1,0:T(8,128)(2,1)S(1)}, bf16[8,160,128]{2,1,0:T(8,128)(2,1)S(1)}, u32[]{:S(2)}, u32[]{:S(2)}) collective-permute-start(bf16[8,160,128]{2,1,0:T(8,128)(2,1)S(1)} %get-tuple-element.100), channel_id=1, source_target_pairs={{0,16},{16,0},{32,48},{48,32},{64,80},{80,64},{96,112},{112,96},{1... | collective-permute-start | bytes 983048 | tf_op jit(solution)/shard_map/ppermute | solution.py:524
  44.0 1.7 %collective-permute-start.10 = (bf16[8,144,128]{2,1,0:T(8,128)(2,1)S(1)}, bf16[8,144,128]{2,1,0:T(8,128)(2,1)S(1)}, u32[]{:S(2)}, u32[]{:S(2)}) collective-permute-start(bf16[8,144,128]{2,1,0:T(8,128)(2,1)S(1)} %get-tuple-element.101), channel_id=1, source_target_pairs={{0,16},{16,0},{32,48},{48,32},{64,80},{80,64},{96,112},{112,96},{1... | collective-permute-start | bytes 884744 | tf_op jit(solution)/shard_map/ppermute | solution.py:524
  96.5 6.6 %collective-permute-start.11 = (bf16[8,144,128]{2,1,0:T(8,128)(2,1)S(1)}, bf16[8,144,128]{2,1,0:T(8,128)(2,1)S(1)}, u32[]{:S(2)}, u32[]{:S(2)}) collective-permute-start(bf16[8,144,128]{2,1,0:T(8,128)(2,1)S(1)} %all_to_all.23.mine), channel_id=1, source_target_pairs={{0,16},{16,0},{32,48},{48,32},{64,80},{80,64},{96,112},{112,96},{1... | collective-permute-start | bytes 884744 | tf_op jit(solution)/shard_map/ppermute | solution.py:524

commit v14 on v13

--- a/solution.py
+++ b/solution.py
@@ -382,7 +382,10 @@
     projs_out[...] = proj_w
 
 
-def blend_kernel(own, proj, act, blended):
+def blend_kernel(scale, own, proj, act, coarse, blended, conv, proj_grad):
+    for k in range(9):
+        conv[k] = coarse[k // 5, 16 * (k % 5) : 16 * (k % 5) + 16, :].astype(F32) * scale
+    proj_grad[...] = coarse[1, 64:80, :].astype(F32) * scale
     projected = dot_nn(own[...], proj[...]).reshape(8, 32, CH)
     for k in range(8):
         row = repeated(projected[k])
@@ -497,15 +500,13 @@
         out[k] = value
 
 
-def gather_column_kernel(scale, got, conv, proj, fine, total):
+def gather_column_kernel(meta, got, coarse, fine, total):
     for j in range(2):
         for k in range(8):
             total[j, 19 * k : 19 * k + 24, :] = got[8 * j + k].astype(F32)
-    for k in range(9):
-        conv[k] = total[k // 5, 16 * (k % 5) : 16 * (k % 5) + 16, :] * scale
-    proj[...] = total[1, 64:80, :] * scale
-    value = jnp.concatenate([total[0, 80:152, :], total[1, 80:152, :]], axis=0).astype(BF)
-    for k in range(8):
+    coarse[...] = total[:, 0:80, :].astype(BF)
+    value = total[meta[5] // 8, 80:152, :].astype(BF)
+    for k in range(16):
         fine[k] = value
 
 
@@ -513,10 +514,12 @@
     core = meta[4] % 2
     for at in range(8):
         out = first if at < 4 else second
-        a = mine[at].astype(F32) * scale
-        b = other[at].astype(F32) * scale
-        out[2 * (at % 4)] = jnp.where(core == 0, a, b)
-        out[2 * (at % 4) + 1] = jnp.where(core == 0, b, a)
+        for j in range(2):
+            rows = slice(72 * j, 72 * j + 72)
+            a = mine[2 * at + j].astype(F32) * scale
+            b = other[2 * at + j].astype(F32) * scale
+            out[2 * (at % 4), rows, :] = jnp.where(core == 0, a, b)
+            out[2 * (at % 4) + 1, rows, :] = jnp.where(core == 0, b, a)
 
 
 def swap(value, axis, mask):
@@ -528,12 +531,6 @@
     count = lax.axis_size(axis)
     pairs = [(i, i + 1 if i % 2 else i - 1) for i in range(1, count - 1)]
     return lax.ppermute(value, axis, pairs)
-
-
-def exchange_row(value):
-    count = lax.axis_size("row")
-    groups = [list(range(c, count, 2)) for c in range(2)]
-    return lax.all_to_all(value, "row", 0, 0, axis_index_groups=groups, tiled=True)
 
 
 def exchange_plane(value):
@@ -634,15 +631,21 @@
         scatter_plane_kernel, "scatter_plane", (((8, 24, CH), BF),), (exchange_plane(part),), (((160, CH), F32),)
     )[0]
     part = call(scatter_column_kernel, "scatter_column", (((16, 24, CH), BF),), (exchange_depth(part),))[0]
-    conv_grad, proj_grad, fine = call(
-        functools.partial(gather_column_kernel, coarse_scale),
+    coarse, fine = call(
+        gather_column_kernel,
         "gather_column",
-        (((9, 16, CH), F32), ((16, CH), F32), ((8, 144, CH), BF)),
-        (exchange_column(part),),
+        (((2, 80, CH), BF), ((16, 72, CH), BF)),
+        (meta, exchange_column(part)),
         (((2, 160, CH), F32),),
     )
-    fine = exchange_row(fine)
-    blended = call(blend_kernel, "blend", (((16, 64, CH), BF),), (after_all(own_act, fine), proj, act), flops=10**9)[0]
+    fine = exchange_plane(fine)
+    blended, conv_grad, proj_grad = call(
+        functools.partial(blend_kernel, coarse_scale),
+        "blend",
+        (((16, 64, CH), BF), ((9, 16, CH), F32), ((16, CH), F32)),
+        (after_all(own_act, fine), proj, act, coarse),
+        flops=10**9,
+    )
     other = after_all(swap(fine, "row", 1), blended)
     first, second = call(
         functools.partial(finish_kernel, fine_scale),

time: 105 us -> 105 us (level)
    all_to_all x1 -> x0, blocking collectives: 11.5 us -> none  [exchange_row(): lax.all_to_all(value, 'row', 0, 0, axis_index_groups=groups, tiled=True)]
    all_to_all x1 -> x2, blocking collectives: 17.1 us -> 28.3 us  [exchange_plane(): lax.all_to_all(value, ('row', 'col'), 0, 0, axis_index_groups=groups, til...]
where the time goes in v14:
time: 105 us; the launch traced here: 104 us
  blocking collectives  49.5 us (47%)
  starting transfers between devices  25.7 us (24%)
  Pallas kernels  22.7 us (22%)
  waiting for transfers between devices  5.45 us (5%)
    all_to_all x2, blocking collectives, exchange_plane(): lax.all_to_all(value, ('row', 'col'), 0, 0, axis_index_groups=groups, til...  28.3 us
    pallas_call x16, Pallas kernels, call(): pl.pallas_call(kernel, name=name, out_shape=shapes, in_specs=[HBM if k in...  22.7 us
    ppermute x10, starting transfers between devices, swap(): return lax.ppermute(value, axis, [(i, i ^ mask) for i in range(count)])  22 us
    all_to_all x1, blocking collectives, exchange_depth(): lax.all_to_all(value, 'col', 0, 0, axis_index_groups=groups, tiled=True)  11.3 us
    all_to_all x1, blocking collectives, exchange_column(): return lax.all_to_all(value, 'col', 0, 0, tiled=True)  9.98 us
    ppermute x10, waiting for transfers between devices, swap(): return lax.ppermute(value, axis, [(i, i ^ mask) for i in range(count)])  5.44 us
    ppermute x2, starting transfers between devices, swap_outer(): return lax.ppermute(value, axis, pairs)  3.69 us
  transfers between devices with their start and end apart: 12, of which 4 were waited for; matrix products, arithmetic and copies ran while one was open for 0% of the time, Pallas kernels for 14%

profile of v14, /device:TPU:1, one launch (start us, length us, event | category | flops | bytes accessed | tf_op | source)
XLA Modules:
  0.0 104.2 jit_solution(16099642841042850606)
XLA Ops:
  0.7 1.6 %pack_columns.1 = (bf16[16,48,128]{2,1,0:T(8,128)(2,1)S(1)}, bf16[16,48,128]{2,1,0:T(8,128)(2,1)S(1)}) custom-call(s32[6]{0:T(128)S(1)} %stack.19.meta, bf16[16,64,128]{2,1,0:T(8,128)(2,1)} %bitcast.18, bf16[16,64,128]{2,1,0:T(8,128)(2,1)} %bitcast.20), custom_call_target="tpu_custom_call" | custom-call | tf_op jit(solution)/shard_map/pack_columns/pallas_call | solution.py:23
  2.3 0.7 collective-permute-start.1
  3.0 5.4 %collective-permute-start = (bf16[16,48,128]{2,1,0:T(8,128)(2,1)S(1)}, bf16[16,48,128]{2,1,0:T(8,128)(2,1)S(1)}, u32[]{:S(2)}, u32[]{:S(2)}) collective-permute-start(bf16[16,48,128]{2,1,0:T(8,128)(2,1)S(1)} %get-tuple-element.62), channel_id=1, source_target_pairs={{0,1},{1,0},{2,3},{3,2},{4,5},{5,4},{6,7},{7,6},{8,9},{9,8},{10,11... | collective-permute-start | bytes 589832 | tf_op jit(solution)/shard_map/ppermute | solution.py:527
  8.4 1.1 %bring.1 = (bf16[16,64,128]{2,1,0:T(8,128)(2,1)S(1)}, bf16[16,64,128]{2,1,0:T(8,128)(2,1)S(1)}, bf16[160,128]{1,0:T(8,128)(2,1)S(1)}) custom-call(bf16[16,64,128]{2,1,0:T(8,128)(2,1)} %bitcast.19, bf16[16,64,128]{2,1,0:T(8,128)(2,1)} %bitcast.21, bf16[9,16,128]{2,1,0:T(8,128)(2,1)} %bitcast.26, bf16[16,128]{1,0:T(8,128)(2,1)} %proj.1), custom_call_target="tpu_custom_call" | custom-call | flops 4000000000 | tf_op jit(solution)/shard_map/bring/pallas_call | solution.py:23
  9.6 3.0 %collective-permute-start.2 = (bf16[160,128]{1,0:T(8,128)(2,1)S(1)}, bf16[160,128]{1,0:T(8,128)(2,1)S(1)}, u32[]{:S(2)}, u32[]{:S(2)}) collective-permute-start(bf16[160,128]{1,0:T(8,128)(2,1)S(1)} %get-tuple-element.70.own), channel_id=1, source_target_pairs={{0,128},{16,144},{32,160},{48,176},{64,192},{80,208},{96,224},{112... | collective-permute-start | bytes 122888 | tf_op jit(solution)/shard_map/ppermute | solution.py:527
  12.6 1.2 %weights.1 = (bf16[1536,256]{1,0:T(8,128)(2,1)S(1)}, bf16[1536,256]{1,0:T(8,128)(2,1)S(1)}, bf16[256,1536]{1,0:T(8,128)(2,1)S(1)}, bf16[256,1536]{1,0:T(8,128)(2,1)S(1)}) custom-call(bf16[1152,128]{1,0:T(8,128)(2,1)} %bitcast.24, bf16[1152,128]{1,0:T(8,128)(2,1)} %bitcast.25), custom_call_target="tpu_custom_call" | custom-call | flops 4000000000 | tf_op jit(solution)/shard_map/weights/pallas_call | solution.py:23
  13.8 1.9 %collective-permute-done.2.far = bf16[160,128]{1,0:T(8,128)(2,1)S(1)} collective-permute-done((bf16[160,128]{1,0:T(8,128)(2,1)S(1)}, bf16[160,128]{1,0:T(8,128)(2,1)S(1)}, u32[]{:S(2)}, u32[]{:S(2)}) %collective-permute-start.2) | collective-permute-done | bytes 40992 | tf_op jit(solution)/shard_map/ppermute | solution.py:527
  15.7 0.6 pack_rows.1
  16.4 3.9 %collective-permute-start.3 = (bf16[1408,128]{1,0:T(8,128)(2,1)S(1)}, bf16[1408,128]{1,0:T(8,128)(2,1)S(1)}, u32[]{:S(2)}, u32[]{:S(2)}) collective-permute-start(bf16[1408,128]{1,0:T(8,128)(2,1)S(1)} %get-tuple-element.71), channel_id=1, source_target_pairs={{0,16},{16,0},{32,48},{48,32},{64,80},{80,64},{96,112},{112,96},{1... | collective-permute-start | bytes 1081352 | tf_op jit(solution)/shard_map/ppermute | solution.py:527
  20.3 3.0 %collective-permute-start.4 = (bf16[1408,128]{1,0:T(8,128)(2,1)S(1)}, bf16[1408,128]{1,0:T(8,128)(2,1)S(1)}, u32[]{:S(2)}, u32[]{:S(2)}) collective-permute-start(bf16[1408,128]{1,0:T(8,128)(2,1)S(1)} %get-tuple-element.72), channel_id=1, source_target_pairs={{16,32},{32,16},{48,64},{64,48},{80,96},{96,80},{112,128},{128,112... | collective-permute-start | bytes 1081352 | tf_op jit(solution)/shard_map/ppermute | solution.py:533
  23.3 1.8 %collective-permute-start.7 = (bf16[2,160,128]{2,1,0:T(8,128)(2,1)S(1)}, bf16[2,160,128]{2,1,0:T(8,128)(2,1)S(1)}, u32[]{:S(2)}, u32[]{:S(2)}) collective-permute-start(bf16[2,160,128]{2,1,0:T(8,128)(2,1)S(1)} %get-tuple-element.89.refs_0_.near0), channel_id=1, source_target_pairs={{0,96},{16,112},{32,64},{48,80},{64,32},{80,48},{96,0},{112,16},{1... | collective-permute-start | bytes 245768 | tf_op jit(solution)/shard_map/ppermute | solution.py:527
  25.1 1.3 %collective-permute-start.6 = (bf16[2,160,128]{2,1,0:T(8,128)(2,1)S(1)}, bf16[2,160,128]{2,1,0:T(8,128)(2,1)S(1)}, u32[]{:S(2)}, u32[]{:S(2)}) collective-permute-start(bf16[2,160,128]{2,1,0:T(8,128)(2,1)S(1)} %get-tuple-element.89.refs_0_.near0), channel_id=1, source_target_pairs={{0,64},{16,80},{32,96},{48,112},{64,0},{80,16},{96,32},{112,48},{1... | collective-permute-start | bytes 245768 | tf_op jit(solution)/shard_map/ppermute | solution.py:527
  26.4 0.3 collective-permute-start.5
  26.7 3.6 %forward_inner.1 = (bf16[16,128,384]{2,1,0:T(8,128)(2,1)S(1)}, bf16[14,128,384]{2,1,0:T(8,128)(2,1)S(1)}, f32[14,96,128]{2,1,0:T(8,128)S(1)}, bf16[6,64,384]{2,1...) custom-call(s32[6]{0:T(128)S(1)} %stack.19.meta, ...), custom_call_target="tpu_custom_call" | custom-call | tf_op jit(solution)/shard_map/forward_inner/pallas_call | solution.py:23
  30.3 3.0 %collective-permute-done.7.refs_3_.near3 = bf16[2,160,128]{2,1,0:T(8,128)(2,1)S(1)} collective-permute-done((bf16[2,160,128]{2,1,0:T(8,128)(2,1)S(1)}, bf16[2,160,128]{2,1,0:T(8,128)(2,1)S(1)}, u32[]{:S(2)}, u32[]{:S(2)}) %collective-permute-start.7) | collective-permute-done | bytes 81952 | tf_op jit(solution)/shard_map/ppermute | solution.py:527
  33.4 3.5 %forward_outer.1 = (bf16[14,64,384]{2,1,0:T(8,128)(2,1)S(1)}, f32[18,96,128]{2,1,0:T(8,128)S(1)}, f32[20,96,128]{2,1,0:T(8,128)S(1)}, bf16[16,64,128]{2,1,0:T(8,...) custom-call(s32[6]{0:T(128)S(1)} %stack.19.meta, ...), custom_call_target="tpu_custom_call" | custom-call | flops 4000000000 | tf_op jit(solution)/shard_map/forward_outer/pallas_call | solution.py:23
  36.9 3.6 %coarse_step.1 = (bf16[256,256]{1,0:T(8,128)(2,1)S(1)}, bf16[256,128]{1,0:T(8,128)(2,1)S(1)}, bf16[8,160,128]{2,1,0:T(8,128)(2,1)S(1)}, bf16[8,160,128]{2,1,0:T(8,128)(2,1)S(1)}, f32[10,48,128]{2,1,0:T(8,128)S(1)}) custom-call(s32[6]{0:T(128)S(1)} %stack.19.meta, bf16[14,64,384]{2,1,0:T(8,128)(2,1)S(1)} %get-tuple-element.88.pool3, ...), custom_call_target="tpu_custom_call" | custom-call | flops 2000000000 | tf_op jit(solution)/shard_map/coarse_step/pallas_call | solution.py:23
  40.5 0.7 collective-permute-start.9
  41.3 2.7 %fine_backward.1 = (bf16[8,144,128]{2,1,0:T(8,128)(2,1)S(1)}, bf16[8,144,128]{2,1,0:T(8,128)(2,1)S(1)}, bf16[18,64,384]{2,1,0:T(8,128)(2,1)S(1)}) custom-call(s32[6]{0:T(128)S(1)} %stack.19.meta, f32[10,48,128]{2,1,0:T(8,128)S(1)} %get-tuple-element.95.pooled_grad, bf16[16,64,128]{2,1,0:T(8,128)(2,1)S(1)} %get-tuple-element.65.cot, ...), custom_call_target="tpu_custom_call" | custom-call | flops 2000000000 | tf_op jit(solution)/shard_map/fine_backward/pallas_call | solution.py:23
  44.0 0.1 collective-permute-start.10
  44.1 1.3 %feature_step.1 = bf16[16,64,128]{2,1,0:T(8,128)(2,1)} custom-call(bf16[18,64,384]{2,1,0:T(8,128)(2,1)S(1)} %get-tuple-element.104.first3, bf16[256,1536]{1,0:T(8,128)(2,1)S(1)} %get-tuple-element.105.back_w), custom_call_target="tpu_custom_call" | custom-call | flops 1000000000 | tf_op jit(solution)/shard_map/feature_step/pallas_call | solution.py:23
  45.4 0.2 collective-permute-done.10.got_f
  45.6 0.1 scatter_core.1
  45.8 17.1 %all_to_all.20.got = bf16[16,152,128]{2,1,0:T(8,128)(2,1)S(1)} all-to-all(bf16[16,152,128]{2,1,0:T(8,128)(2,1)S(1)} %scatter_core.1), channel_id=1, replica_groups={{0,8,32,40,64,72,96,104,128,136,160,168,192,200,224,232},{1,9,33,41,65,..., dimensions={0} | all-to-all | bytes 1245184 | tf_op jit(solution)/shard_map/all_to_all | solution.py:542
  63.0 11.3 %all_to_all.21.got = bf16[8,24,128]{2,1,0:T(8,128)(2,1)S(1)} all-to-all(bf16[8,24,128]{2,1,0:T(8,128)(2,1)S(1)} %scatter_plane.1), channel_id=1, replica_groups={{0,1,2,3,4,5,6,7},{8,9,10,11,12,13,14,15},{16,17,18,19,20,21,22,23},{24..., dimensions={0} | all-to-all | bytes 98304 | tf_op jit(solution)/shard_map/all_to_all | solution.py:548
  74.4 10.0 %all_to_all.22.got = bf16[16,24,128]{2,1,0:T(8,128)(2,1)S(1)} all-to-all(bf16[16,24,128]{2,1,0:T(8,128)(2,1)S(1)} %scatter_column.1), channel_id=1, replica_groups=mesh['row'=16,'col'=16] {'col'}, dimensions={0} | all-to-all | bytes 196608 | tf_op jit(solution)/shard_map/all_to_all | solution.py:552
  84.3 0.6 gather_column.1
  84.9 11.1 %all_to_all.23.mine = bf16[16,72,128]{2,1,0:T(8,128)(2,1)S(1)} all-to-all(bf16[16,72,128]{2,1,0:T(8,128)(2,1)S(1)} %get-tuple-element.107), channel_id=1, replica_groups={{0,8,32,40,64,72,96,104,128,136,160,168,192,200,224,232},{1,9,33,41,65,..., dimensions={0} | all-to-all | bytes 589824 | tf_op jit(solution)/shard_map/all_to_all | solution.py:542
  96.1 5.4 %collective-permute-start.11 = (bf16[16,72,128]{2,1,0:T(8,128)(2,1)S(1)}, bf16[16,72,128]{2,1,0:T(8,128)(2,1)S(1)}, u32[]{:S(2)}, u32[]{:S(2)}) collective-permute-start(bf16[16,72,128]{2,1,0:T(8,128)(2,1)S(1)} %all_to_all.23.mine), channel_id=1, source_target_pairs={{0,16},{16,0},{32,48},{48,32},{64,80},{80,64},{96,112},{112,96},{1... | collective-permute-start | bytes 884744 | tf_op jit(solution)/shard_map/ppermute | solution.py:527
  101.4 0.9 blend.1
  102.3 0.3 collective-permute-done.11.other
  102.6 1.6 %finish.1 = (f32[8,144,128]{2,1,0:T(8,128)}, f32[8,144,128]{2,1,0:T(8,128)}) custom-call(s32[6]{0:T(128)S(1)} %stack.19.meta, bf16[16,72,128]{2,1,0:T(8,128)(2,1)S(1)} %all_to_all.23.mine, bf16[16,72,128]{2,1,0:T(8,128)(2,1)S(1)} %collective-permute-done.11.other), custom_call_target="tpu_custom_call" | custom-call | tf_op jit(solution)/shard_map/finish/pallas_call | solution.py:23
  (14 shorter events, 0.3 us)
Async XLA Ops:
  2.3 11.5 %collective-permute-start.1 = (bf16[16,48,128]{2,1,0:T(8,128)(2,1)S(1)}, bf16[16,48,128]{2,1,0:T(8,128)(2,1)S(1)}, u32[]{:S(2)}, u32[]{:S(2)}) collective-permute-start(bf16[16,48,128]{2,1,0:T(8,128)(2,1)S(1)} %get-tuple-element.66), channel_id=1, source_target_pairs={{1,2},{2,1},{3,4},{4,3},{5,6},{6,5},{7,8},{8,7},{9,10},{10,9},{11,... | collective-permute-start | bytes 589832 | tf_op jit(solution)/shard_map/ppermute | solution.py:533
  3.0 12.7 %collective-permute-start = (bf16[16,48,128]{2,1,0:T(8,128)(2,1)S(1)}, bf16[16,48,128]{2,1,0:T(8,128)(2,1)S(1)}, u32[]{:S(2)}, u32[]{:S(2)}) collective-permute-start(bf16[16,48,128]{2,1,0:T(8,128)(2,1)S(1)} %get-tuple-element.62), channel_id=1, source_target_pairs={{0,1},{1,0},{2,3},{3,2},{4,5},{5,4},{6,7},{7,6},{8,9},{9,8},{10,11... | collective-permute-start | bytes 589832 | tf_op jit(solution)/shard_map/ppermute | solution.py:527
  9.6 6.1 %collective-permute-start.2 = (bf16[160,128]{1,0:T(8,128)(2,1)S(1)}, bf16[160,128]{1,0:T(8,128)(2,1)S(1)}, u32[]{:S(2)}, u32[]{:S(2)}) collective-permute-start(bf16[160,128]{1,0:T(8,128)(2,1)S(1)} %get-tuple-element.70.own), channel_id=1, source_target_pairs={{0,128},{16,144},{32,160},{48,176},{64,192},{80,208},{96,224},{112... | collective-permute-start | bytes 122888 | tf_op jit(solution)/shard_map/ppermute | solution.py:527
  16.4 17.1 %collective-permute-start.3 = (bf16[1408,128]{1,0:T(8,128)(2,1)S(1)}, bf16[1408,128]{1,0:T(8,128)(2,1)S(1)}, u32[]{:S(2)}, u32[]{:S(2)}) collective-permute-start(bf16[1408,128]{1,0:T(8,128)(2,1)S(1)} %get-tuple-element.71), channel_id=1, source_target_pairs={{0,16},{16,0},{32,48},{48,32},{64,80},{80,64},{96,112},{112,96},{1... | collective-permute-start | bytes 1081352 | tf_op jit(solution)/shard_map/ppermute | solution.py:527
  20.3 13.1 %collective-permute-start.4 = (bf16[1408,128]{1,0:T(8,128)(2,1)S(1)}, bf16[1408,128]{1,0:T(8,128)(2,1)S(1)}, u32[]{:S(2)}, u32[]{:S(2)}) collective-permute-start(bf16[1408,128]{1,0:T(8,128)(2,1)S(1)} %get-tuple-element.72), channel_id=1, source_target_pairs={{16,32},{32,16},{48,64},{64,48},{80,96},{96,80},{112,128},{128,112... | collective-permute-start | bytes 1081352 | tf_op jit(solution)/shard_map/ppermute | solution.py:533
  23.3 10.0 %collective-permute-start.7 = (bf16[2,160,128]{2,1,0:T(8,128)(2,1)S(1)}, bf16[2,160,128]{2,1,0:T(8,128)(2,1)S(1)}, u32[]{:S(2)}, u32[]{:S(2)}) collective-permute-start(bf16[2,160,128]{2,1,0:T(8,128)(2,1)S(1)} %get-tuple-element.89.refs_0_.near0), channel_id=1, source_target_pairs={{0,96},{16,112},{32,64},{48,80},{64,32},{80,48},{96,0},{112,16},{1... | collective-permute-start | bytes 245768 | tf_op jit(solution)/shard_map/ppermute | solution.py:527
  25.1 8.2 %collective-permute-start.6 = (bf16[2,160,128]{2,1,0:T(8,128)(2,1)S(1)}, bf16[2,160,128]{2,1,0:T(8,128)(2,1)S(1)}, u32[]{:S(2)}, u32[]{:S(2)}) collective-permute-start(bf16[2,160,128]{2,1,0:T(8,128)(2,1)S(1)} %get-tuple-element.89.refs_0_.near0), channel_id=1, source_target_pairs={{0,64},{16,80},{32,96},{48,112},{64,0},{80,16},{96,32},{112,48},{1... | collective-permute-start | bytes 245768 | tf_op jit(solution)/shard_map/ppermute | solution.py:527
  26.4 6.9 %collective-permute-start.5 = (bf16[2,160,128]{2,1,0:T(8,128)(2,1)S(1)}, bf16[2,160,128]{2,1,0:T(8,128)(2,1)S(1)}, u32[]{:S(2)}, u32[]{:S(2)}) collective-permute-start(bf16[2,160,128]{2,1,0:T(8,128)(2,1)S(1)} %get-tuple-element.89.refs_0_.near0), channel_id=1, source_target_pairs={{0,32},{16,48},{32,0},{48,16},{64,96},{80,112},{96,64},{112,80},{1... | collective-permute-start | bytes 245768 | tf_op jit(solution)/shard_map/ppermute | solution.py:527
  33.3 3.6 %collective-permute-start.8 = (bf16[4,2,160,128]{3,2,1,0:T(8,128)(2,1)S(1)}, bf16[4,2,160,128]{3,2,1,0:T(8,128)(2,1)S(1)}, u32[]{:S(2)}, u32[]{:S(2)}) collective-permute-start(bf16[4,2,160,128]{3,2,1,0:T(8,128)(2,1)S(1)} %stack_eight.1), channel_id=1, source_target_pairs={{0,16},{16,0},{32,48},{48,32},{64,80},{80,64},{96,112},{112,96},{1... | collective-permute-start | bytes 983048 | tf_op jit(solution)/shard_map/ppermute | solution.py:527
  40.5 5.1 %collective-permute-start.9 = (bf16[8,160,128]{2,1,0:T(8,128)(2,1)S(1)}, bf16[8,160,128]{2,1,0:T(8,128)(2,1)S(1)}, u32[]{:S(2)}, u32[]{:S(2)}) collective-permute-start(bf16[8,160,128]{2,1,0:T(8,128)(2,1)S(1)} %get-tuple-element.102), channel_id=1, source_target_pairs={{0,16},{16,0},{32,48},{48,32},{64,80},{80,64},{96,112},{112,96},{1... | collective-permute-start | bytes 983048 | tf_op jit(solution)/shard_map/ppermute | solution.py:527
  44.0 1.7 %collective-permute-start.10 = (bf16[8,144,128]{2,1,0:T(8,128)(2,1)S(1)}, bf16[8,144,128]{2,1,0:T(8,128)(2,1)S(1)}, u32[]{:S(2)}, u32[]{:S(2)}) collective-permute-start(bf16[8,144,128]{2,1,0:T(8,128)(2,1)S(1)} %get-tuple-element.103), channel_id=1, source_target_pairs={{0,16},{16,0},{32,48},{48,32},{64,80},{80,64},{96,112},{112,96},{1... | collective-permute-start | bytes 884744 | tf_op jit(solution)/shard_map/ppermute | solution.py:527
  96.1 6.6 %collective-permute-start.11 = (bf16[16,72,128]{2,1,0:T(8,128)(2,1)S(1)}, bf16[16,72,128]{2,1,0:T(8,128)(2,1)S(1)}, u32[]{:S(2)}, u32[]{:S(2)}) collective-permute-start(bf16[16,72,128]{2,1,0:T(8,128)(2,1)S(1)} %all_to_all.23.mine), channel_id=1, source_target_pairs={{0,16},{16,0},{32,48},{48,32},{64,80},{80,64},{96,112},{112,96},{1... | collective-permute-start | bytes 884744 | tf_op jit(solution)/shard_map/ppermute | solution.py:527

commit v15 on v14

--- a/solution.py
+++ b/solution.py
@@ -153,12 +153,11 @@
         copy.wait()
 
 
-EDGE = 8 * 128 + 4 * 96
-
-
-def cot_edge(ref, first, count=1):
-    value = ref[1024 + 96 * first : 1024 + 96 * (first + count), :]
-    return value if count == 1 else value.reshape(count, 96, CH)
+EDGE = 8 * 128 + 2 * 96 + 48
+
+
+def cot_edge(ref):
+    return ref[1024:1216, :].reshape(2, 96, CH)
 
 
 def bring_kernel(feat_far, cot_far, conv, proj, feat, cot, weights, done):
@@ -183,14 +182,23 @@
 
 def pack_rows_kernel(meta, feat, cot, pair, other, own, far, inner, outer, both):
     core = meta[4] % 2
+
+    def cot_row(row):
+        before, after = sides(meta, pair[row, 32:48, :], other[row, 32:48, :])
+        return jnp.concatenate([before, cot[row], after], axis=0)
+
     for low, out in ((1 - core, inner), (core, outer)):
-        jobs = [(128 * k, feat, 8 * low + k, 0, 32) for k in range(8)]
-        jobs += [(1024 + 96 * k, cot, 12 * low + k, 32, 16) for k in range(4)]
-        for base, middle, row, first, width in jobs:
-            before, after = sides(meta, pair[row, first : first + width, :], other[row, first : first + width, :])
-            out[base : base + width, :] = before
-            out[base + width : base + width + 64, :] = middle[row]
-            out[base + width + 64 : base + 2 * width + 64, :] = after
+        for k in range(8):
+            row = 8 * low + k
+            before, after = sides(meta, pair[row, 0:32, :], other[row, 0:32, :])
+            out[128 * k : 128 * k + 32, :] = before
+            out[128 * k + 32 : 128 * k + 96, :] = feat[row]
+            out[128 * k + 96 : 128 * k + 128, :] = after
+        for k in range(2):
+            out[1024 + 96 * k : 1120 + 96 * k, :] = cot_row(14 * low + k)
+        away = 2 + 10 * low
+        both_rows = cot_row(away).astype(F32) + cot_row(away + 1).astype(F32)
+        out[1216:1264, :] = pooled_pair(both_rows).astype(BF)
     both[0] = own[...]
     both[1] = far[...]
 
@@ -249,20 +257,25 @@
     meta, inner, outer, feat3i, act3i, slope1i, pool3i, slope2i, acti, weight1, weight2,
     pool3, slope1, slope2, act, feat3o, act3o, feat3, act3,
 ):
-    below_at = 24 * (meta[4] % 2)
+    below_at = 8 * (meta[4] % 2)
     for k in range(8):
         feat3[k + below_at] = three(outer[128 * k : 128 * k + 128, :].astype(F32))
-        feat3[k + 24 - below_at] = three(inner[128 * k : 128 * k + 128, :].astype(F32))
-    feat3[8:24] = feat3i[...]
+        feat3[k + 8 - below_at] = three(inner[128 * k : 128 * k + 128, :].astype(F32))
+
+    def feat_row(h):
+        return feat3i[h - 8] if 8 <= h < 24 else feat3[h if h < 8 else h - 16]
+
+    def act_row(h):
+        return act3i[h - 9] if 9 <= h < 23 else act3[h - 1 if h < 9 else h - 15]
+
     for starts in ([1, 3, 5, 7], [23, 25, 27, 29]):
-        for h, (pre, wide) in first_rows(meta, lambda h: feat3[h], starts, weight1[...]).items():
-            act3[h - 1] = wide
+        for h, (pre, wide) in first_rows(meta, feat_row, starts, weight1[...]).items():
+            act3[h - 1 if h < 9 else h - 15] = wide
             if 7 <= h <= 24:
                 slope1[h - 7] = slope_of(pre[16:112])
     slope1[2:16] = slope1i[...]
-    act3[8:22] = act3i[...]
     for starts in ([2, 4, 6, 8], [22, 24, 26, 28]):
-        for h, (pre, value, small) in second_rows(meta, lambda h: act3[h - 1], starts, weight2[...]).items():
+        for h, (pre, value, small) in second_rows(meta, act_row, starts, weight2[...]).items():
             pool3[h // 2 - 1] = small
             for e in range(2):
                 if 6 <= h + e < 26:
@@ -272,8 +285,9 @@
     pool3[4:10] = pool3i[...]
     slope2[4:16] = slope2i[...]
     act[2:14] = acti[...]
-    feat3o[...] = feat3[7:25, 32:96, :]
-    act3o[...] = act3[6:24, 32:96, :]
+    for k in range(18):
+        feat3o[k] = feat_row(k + 7)[32:96]
+        act3o[k] = act_row(k + 7)[32:96]
 
 
 def inner_step(meta, feat, pair, other, weight1, weight2):
@@ -307,7 +321,7 @@
             ((18, 64, 384), BF),
         ),
         (meta, inner, outer) + tuple(parts) + (weight1, weight2),
-        (((32, 128, 384), BF), ((30, 128, 384), BF)),
+        (((16, 128, 384), BF),) * 2,
         limit=24,
         flops=4 * 10**9,
     )
@@ -332,10 +346,10 @@
     def pair_sum(a, b):
         return pooled_pair(a.astype(F32) + b.astype(F32))
 
-    below_at = 10 * core
-    for k in range(2):
-        projin[k + below_at] = pair_sum(cot_edge(outer, 2 * k), cot_edge(outer, 2 * k + 1))
-        projin[k + 10 - below_at] = pair_sum(cot_edge(inner, 2 * k), cot_edge(inner, 2 * k + 1))
+    for ref, far_at, near_at in ((outer, 11 * core, 1 + 9 * core), (inner, 11 - 11 * core, 10 - 9 * core)):
+        projin[far_at] = ref[1216:1264, :].astype(F32)
+        near_rows = cot_edge(ref)
+        projin[near_at] = pair_sum(near_rows[0], near_rows[1])
 
     for k in range(8):
         rows = slice(2 * k, 2 * k + 2)
@@ -424,8 +438,8 @@
             second3[2 * k + e] = three(value * (mask * row_ok(top - 2 + 2 * k + e, height)))
 
     first_core = meta[4] % 2 == 0
-    second_pair(0, lax.select(first_core, cot_edge(outer, 2, 2), cot_edge(inner, 2, 2)))
-    second_pair(9, lax.select(first_core, cot_edge(inner, 0, 2), cot_edge(outer, 0, 2)))
+    second_pair(0, lax.select(first_core, cot_edge(outer), cot_edge(inner)))
+    second_pair(9, lax.select(first_core, cot_edge(inner), cot_edge(outer)))
     for k in range(8):
         rows = slice(2 * k, 2 * k + 2)
         before, after = sides(meta, pair[rows, 32:48, :], other[rows, 32:48, :])

time: 105 us -> 104 us (level)
  no operation moved by 1% of the time
where the time goes in v15:
time: 104 us
  blocking collectives  49.5 us (48%)
  starting transfers between devices  25.7 us (25%)
  Pallas kernels  22.6 us (22%)
  waiting for transfers between devices  5.04 us (5%)
    all_to_all x2, blocking collectives, exchange_plane(): lax.all_to_all(value, ('row', 'col'), 0, 0, axis_index_groups=groups, til...  28.3 us
    pallas_call x16, Pallas kernels, call(): pl.pallas_call(kernel, name=name, out_shape=shapes, in_specs=[HBM if k in...  22.6 us
    ppermute x10, starting transfers between devices, swap(): return lax.ppermute(value, axis, [(i, i ^ mask) for i in range(count)])  22 us
    all_to_all x1, blocking collectives, exchange_depth(): lax.all_to_all(value, 'col', 0, 0, axis_index_groups=groups, tiled=True)  11.3 us
    all_to_all x1, blocking collectives, exchange_column(): return lax.all_to_all(value, 'col', 0, 0, tiled=True)  9.98 us
    ppermute x10, waiting for transfers between devices, swap(): return lax.ppermute(value, axis, [(i, i ^ mask) for i in range(count)])  5.04 us
    ppermute x2, starting transfers between devices, swap_outer(): return lax.ppermute(value, axis, pairs)  3.69 us
  transfers between devices with their start and end apart: 12, of which 4 were waited for; matrix products, arithmetic and copies ran while one was open for 0% of the time, Pallas kernels for 14%

profile of v15, /device:TPU:1, one launch (start us, length us, event | category | flops | bytes accessed | tf_op | source)
XLA Modules:
  0.0 103.7 jit_solution(7677066664865293943)
XLA Ops:
  0.7 1.6 %pack_columns.1 = (bf16[16,48,128]{2,1,0:T(8,128)(2,1)S(1)}, bf16[16,48,128]{2,1,0:T(8,128)(2,1)S(1)}) custom-call(s32[6]{0:T(128)S(1)} %stack.19.meta, bf16[16,64,128]{2,1,0:T(8,128)(2,1)} %bitcast.18, bf16[16,64,128]{2,1,0:T(8,128)(2,1)} %bitcast.20), custom_call_target="tpu_custom_call" | custom-call | tf_op jit(solution)/shard_map/pack_columns/pallas_call | solution.py:23
  2.3 0.7 collective-permute-start.1
  3.0 5.4 %collective-permute-start = (bf16[16,48,128]{2,1,0:T(8,128)(2,1)S(1)}, bf16[16,48,128]{2,1,0:T(8,128)(2,1)S(1)}, u32[]{:S(2)}, u32[]{:S(2)}) collective-permute-start(bf16[16,48,128]{2,1,0:T(8,128)(2,1)S(1)} %get-tuple-element.62), channel_id=1, source_target_pairs={{0,1},{1,0},{2,3},{3,2},{4,5},{5,4},{6,7},{7,6},{8,9},{9,8},{10,11... | collective-permute-start | bytes 589832 | tf_op jit(solution)/shard_map/ppermute | solution.py:541
  8.4 1.1 %bring.1 = (bf16[16,64,128]{2,1,0:T(8,128)(2,1)S(1)}, bf16[16,64,128]{2,1,0:T(8,128)(2,1)S(1)}, bf16[160,128]{1,0:T(8,128)(2,1)S(1)}) custom-call(bf16[16,64,128]{2,1,0:T(8,128)(2,1)} %bitcast.19, bf16[16,64,128]{2,1,0:T(8,128)(2,1)} %bitcast.21, bf16[9,16,128]{2,1,0:T(8,128)(2,1)} %bitcast.26, bf16[16,128]{1,0:T(8,128)(2,1)} %proj.1), custom_call_target="tpu_custom_call" | custom-call | flops 4000000000 | tf_op jit(solution)/shard_map/bring/pallas_call | solution.py:23
  9.6 3.0 %collective-permute-start.2 = (bf16[160,128]{1,0:T(8,128)(2,1)S(1)}, bf16[160,128]{1,0:T(8,128)(2,1)S(1)}, u32[]{:S(2)}, u32[]{:S(2)}) collective-permute-start(bf16[160,128]{1,0:T(8,128)(2,1)S(1)} %get-tuple-element.70.own), channel_id=1, source_target_pairs={{0,128},{16,144},{32,160},{48,176},{64,192},{80,208},{96,224},{112... | collective-permute-start | bytes 122888 | tf_op jit(solution)/shard_map/ppermute | solution.py:541
  12.6 1.2 %weights.1 = (bf16[1536,256]{1,0:T(8,128)(2,1)S(1)}, bf16[1536,256]{1,0:T(8,128)(2,1)S(1)}, bf16[256,1536]{1,0:T(8,128)(2,1)S(1)}, bf16[256,1536]{1,0:T(8,128)(2,1)S(1)}) custom-call(bf16[1152,128]{1,0:T(8,128)(2,1)} %bitcast.24, bf16[1152,128]{1,0:T(8,128)(2,1)} %bitcast.25), custom_call_target="tpu_custom_call" | custom-call | flops 4000000000 | tf_op jit(solution)/shard_map/weights/pallas_call | solution.py:23
  13.8 1.9 %collective-permute-done.2.far = bf16[160,128]{1,0:T(8,128)(2,1)S(1)} collective-permute-done((bf16[160,128]{1,0:T(8,128)(2,1)S(1)}, bf16[160,128]{1,0:T(8,128)(2,1)S(1)}, u32[]{:S(2)}, u32[]{:S(2)}) %collective-permute-start.2) | collective-permute-done | bytes 40992 | tf_op jit(solution)/shard_map/ppermute | solution.py:541
  15.7 0.7 pack_rows.1
  16.4 3.9 %collective-permute-start.3 = (bf16[1264,128]{1,0:T(8,128)(2,1)S(1)}, bf16[1264,128]{1,0:T(8,128)(2,1)S(1)}, u32[]{:S(2)}, u32[]{:S(2)}) collective-permute-start(bf16[1264,128]{1,0:T(8,128)(2,1)S(1)} %get-tuple-element.71), channel_id=1, source_target_pairs={{0,16},{16,0},{32,48},{48,32},{64,80},{80,64},{96,112},{112,96},{1... | collective-permute-start | bytes 970760 | tf_op jit(solution)/shard_map/ppermute | solution.py:541
  20.3 3.0 %collective-permute-start.4 = (bf16[1264,128]{1,0:T(8,128)(2,1)S(1)}, bf16[1264,128]{1,0:T(8,128)(2,1)S(1)}, u32[]{:S(2)}, u32[]{:S(2)}) collective-permute-start(bf16[1264,128]{1,0:T(8,128)(2,1)S(1)} %get-tuple-element.72), channel_id=1, source_target_pairs={{16,32},{32,16},{48,64},{64,48},{80,96},{96,80},{112,128},{128,112... | collective-permute-start | bytes 970760 | tf_op jit(solution)/shard_map/ppermute | solution.py:547
  23.3 1.8 %collective-permute-start.7 = (bf16[2,160,128]{2,1,0:T(8,128)(2,1)S(1)}, bf16[2,160,128]{2,1,0:T(8,128)(2,1)S(1)}, u32[]{:S(2)}, u32[]{:S(2)}) collective-permute-start(bf16[2,160,128]{2,1,0:T(8,128)(2,1)S(1)} %get-tuple-element.89.refs_0_.near0), channel_id=1, source_target_pairs={{0,96},{16,112},{32,64},{48,80},{64,32},{80,48},{96,0},{112,16},{1... | collective-permute-start | bytes 245768 | tf_op jit(solution)/shard_map/ppermute | solution.py:541
  25.1 1.3 %collective-permute-start.6 = (bf16[2,160,128]{2,1,0:T(8,128)(2,1)S(1)}, bf16[2,160,128]{2,1,0:T(8,128)(2,1)S(1)}, u32[]{:S(2)}, u32[]{:S(2)}) collective-permute-start(bf16[2,160,128]{2,1,0:T(8,128)(2,1)S(1)} %get-tuple-element.89.refs_0_.near0), channel_id=1, source_target_pairs={{0,64},{16,80},{32,96},{48,112},{64,0},{80,16},{96,32},{112,48},{1... | collective-permute-start | bytes 245768 | tf_op jit(solution)/shard_map/ppermute | solution.py:541
  26.4 0.3 collective-permute-start.5
  26.7 3.6 %forward_inner.1 = (bf16[16,128,384]{2,1,0:T(8,128)(2,1)S(1)}, bf16[14,128,384]{2,1,0:T(8,128)(2,1)S(1)}, f32[14,96,128]{2,1,0:T(8,128)S(1)}, bf16[6,64,384]{2,1...) custom-call(s32[6]{0:T(128)S(1)} %stack.19.meta, ...), custom_call_target="tpu_custom_call" | custom-call | tf_op jit(solution)/shard_map/forward_inner/pallas_call | solution.py:23
  30.3 2.6 %collective-permute-done.7.refs_3_.near3 = bf16[2,160,128]{2,1,0:T(8,128)(2,1)S(1)} collective-permute-done((bf16[2,160,128]{2,1,0:T(8,128)(2,1)S(1)}, bf16[2,160,128]{2,1,0:T(8,128)(2,1)S(1)}, u32[]{:S(2)}, u32[]{:S(2)}) %collective-permute-start.7) | collective-permute-done | bytes 81952 | tf_op jit(solution)/shard_map/ppermute | solution.py:541
  33.1 3.4 %forward_outer.1 = (bf16[14,64,384]{2,1,0:T(8,128)(2,1)S(1)}, f32[18,96,128]{2,1,0:T(8,128)S(1)}, f32[20,96,128]{2,1,0:T(8,128)S(1)}, bf16[16,64,128]{2,1,0:T(8,...) custom-call(s32[6]{0:T(128)S(1)} %stack.19.meta, ...), custom_call_target="tpu_custom_call" | custom-call | flops 4000000000 | tf_op jit(solution)/shard_map/forward_outer/pallas_call | solution.py:23
  36.4 3.6 %coarse_step.1 = (bf16[256,256]{1,0:T(8,128)(2,1)S(1)}, bf16[256,128]{1,0:T(8,128)(2,1)S(1)}, bf16[8,160,128]{2,1,0:T(8,128)(2,1)S(1)}, bf16[8,160,128]{2,1,0:T(8,128)(2,1)S(1)}, f32[10,48,128]{2,1,0:T(8,128)S(1)}) custom-call(s32[6]{0:T(128)S(1)} %stack.19.meta, bf16[14,64,384]{2,1,0:T(8,128)(2,1)S(1)} %get-tuple-element.88.pool3, ...), custom_call_target="tpu_custom_call" | custom-call | flops 2000000000 | tf_op jit(solution)/shard_map/coarse_step/pallas_call | solution.py:23
  40.0 0.7 collective-permute-start.9
  40.8 2.7 %fine_backward.1 = (bf16[8,144,128]{2,1,0:T(8,128)(2,1)S(1)}, bf16[8,144,128]{2,1,0:T(8,128)(2,1)S(1)}, bf16[18,64,384]{2,1,0:T(8,128)(2,1)S(1)}) custom-call(s32[6]{0:T(128)S(1)} %stack.19.meta, f32[10,48,128]{2,1,0:T(8,128)S(1)} %get-tuple-element.95.pooled_grad, bf16[16,64,128]{2,1,0:T(8,128)(2,1)S(1)} %get-tuple-element.65.cot, ...), custom_call_target="tpu_custom_call" | custom-call | flops 2000000000 | tf_op jit(solution)/shard_map/fine_backward/pallas_call | solution.py:23
  43.5 0.1 collective-permute-start.10
  43.6 1.3 %feature_step.1 = bf16[16,64,128]{2,1,0:T(8,128)(2,1)} custom-call(bf16[18,64,384]{2,1,0:T(8,128)(2,1)S(1)} %get-tuple-element.104.first3, bf16[256,1536]{1,0:T(8,128)(2,1)S(1)} %get-tuple-element.105.back_w), custom_call_target="tpu_custom_call" | custom-call | flops 1000000000 | tf_op jit(solution)/shard_map/feature_step/pallas_call | solution.py:23
  44.9 0.2 collective-permute-done.10.got_f
  45.1 0.2 scatter_core.1
  45.3 17.1 %all_to_all.20.got = bf16[16,152,128]{2,1,0:T(8,128)(2,1)S(1)} all-to-all(bf16[16,152,128]{2,1,0:T(8,128)(2,1)S(1)} %scatter_core.1), channel_id=1, replica_groups={{0,8,32,40,64,72,96,104,128,136,160,168,192,200,224,232},{1,9,33,41,65,..., dimensions={0} | all-to-all | bytes 1245184 | tf_op jit(solution)/shard_map/all_to_all | solution.py:556
  62.5 11.3 %all_to_all.21.got = bf16[8,24,128]{2,1,0:T(8,128)(2,1)S(1)} all-to-all(bf16[8,24,128]{2,1,0:T(8,128)(2,1)S(1)} %scatter_plane.1), channel_id=1, replica_groups={{0,1,2,3,4,5,6,7},{8,9,10,11,12,13,14,15},{16,17,18,19,20,21,22,23},{24..., dimensions={0} | all-to-all | bytes 98304 | tf_op jit(solution)/shard_map/all_to_all | solution.py:562
  73.9 10.0 %all_to_all.22.got = bf16[16,24,128]{2,1,0:T(8,128)(2,1)S(1)} all-to-all(bf16[16,24,128]{2,1,0:T(8,128)(2,1)S(1)} %scatter_column.1), channel_id=1, replica_groups=mesh['row'=16,'col'=16] {'col'}, dimensions={0} | all-to-all | bytes 196608 | tf_op jit(solution)/shard_map/all_to_all | solution.py:566
  83.8 0.6 gather_column.1
  84.4 11.1 %all_to_all.23.mine = bf16[16,72,128]{2,1,0:T(8,128)(2,1)S(1)} all-to-all(bf16[16,72,128]{2,1,0:T(8,128)(2,1)S(1)} %get-tuple-element.107), channel_id=1, replica_groups={{0,8,32,40,64,72,96,104,128,136,160,168,192,200,224,232},{1,9,33,41,65,..., dimensions={0} | all-to-all | bytes 589824 | tf_op jit(solution)/shard_map/all_to_all | solution.py:556
  95.5 5.4 %collective-permute-start.11 = (bf16[16,72,128]{2,1,0:T(8,128)(2,1)S(1)}, bf16[16,72,128]{2,1,0:T(8,128)(2,1)S(1)}, u32[]{:S(2)}, u32[]{:S(2)}) collective-permute-start(bf16[16,72,128]{2,1,0:T(8,128)(2,1)S(1)} %all_to_all.23.mine), channel_id=1, source_target_pairs={{0,16},{16,0},{32,48},{48,32},{64,80},{80,64},{96,112},{112,96},{1... | collective-permute-start | bytes 884744 | tf_op jit(solution)/shard_map/ppermute | solution.py:541
  100.9 0.9 blend.1
  101.8 0.3 collective-permute-done.11.other
  102.1 1.6 %finish.1 = (f32[8,144,128]{2,1,0:T(8,128)}, f32[8,144,128]{2,1,0:T(8,128)}) custom-call(s32[6]{0:T(128)S(1)} %stack.19.meta, bf16[16,72,128]{2,1,0:T(8,128)(2,1)S(1)} %all_to_all.23.mine, bf16[16,72,128]{2,1,0:T(8,128)(2,1)S(1)} %collective-permute-done.11.other), custom_call_target="tpu_custom_call" | custom-call | tf_op jit(solution)/shard_map/finish/pallas_call | solution.py:23
  (14 shorter events, 0.3 us)
Async XLA Ops:
  2.3 11.5 %collective-permute-start.1 = (bf16[16,48,128]{2,1,0:T(8,128)(2,1)S(1)}, bf16[16,48,128]{2,1,0:T(8,128)(2,1)S(1)}, u32[]{:S(2)}, u32[]{:S(2)}) collective-permute-start(bf16[16,48,128]{2,1,0:T(8,128)(2,1)S(1)} %get-tuple-element.66), channel_id=1, source_target_pairs={{1,2},{2,1},{3,4},{4,3},{5,6},{6,5},{7,8},{8,7},{9,10},{10,9},{11,... | collective-permute-start | bytes 589832 | tf_op jit(solution)/shard_map/ppermute | solution.py:547
  3.0 12.7 %collective-permute-start = (bf16[16,48,128]{2,1,0:T(8,128)(2,1)S(1)}, bf16[16,48,128]{2,1,0:T(8,128)(2,1)S(1)}, u32[]{:S(2)}, u32[]{:S(2)}) collective-permute-start(bf16[16,48,128]{2,1,0:T(8,128)(2,1)S(1)} %get-tuple-element.62), channel_id=1, source_target_pairs={{0,1},{1,0},{2,3},{3,2},{4,5},{5,4},{6,7},{7,6},{8,9},{9,8},{10,11... | collective-permute-start | bytes 589832 | tf_op jit(solution)/shard_map/ppermute | solution.py:541
  9.6 6.1 %collective-permute-start.2 = (bf16[160,128]{1,0:T(8,128)(2,1)S(1)}, bf16[160,128]{1,0:T(8,128)(2,1)S(1)}, u32[]{:S(2)}, u32[]{:S(2)}) collective-permute-start(bf16[160,128]{1,0:T(8,128)(2,1)S(1)} %get-tuple-element.70.own), channel_id=1, source_target_pairs={{0,128},{16,144},{32,160},{48,176},{64,192},{80,208},{96,224},{112... | collective-permute-start | bytes 122888 | tf_op jit(solution)/shard_map/ppermute | solution.py:541
  16.4 16.7 %collective-permute-start.3 = (bf16[1264,128]{1,0:T(8,128)(2,1)S(1)}, bf16[1264,128]{1,0:T(8,128)(2,1)S(1)}, u32[]{:S(2)}, u32[]{:S(2)}) collective-permute-start(bf16[1264,128]{1,0:T(8,128)(2,1)S(1)} %get-tuple-element.71), channel_id=1, source_target_pairs={{0,16},{16,0},{32,48},{48,32},{64,80},{80,64},{96,112},{112,96},{1... | collective-permute-start | bytes 970760 | tf_op jit(solution)/shard_map/ppermute | solution.py:541
  20.3 12.8 %collective-permute-start.4 = (bf16[1264,128]{1,0:T(8,128)(2,1)S(1)}, bf16[1264,128]{1,0:T(8,128)(2,1)S(1)}, u32[]{:S(2)}, u32[]{:S(2)}) collective-permute-start(bf16[1264,128]{1,0:T(8,128)(2,1)S(1)} %get-tuple-element.72), channel_id=1, source_target_pairs={{16,32},{32,16},{48,64},{64,48},{80,96},{96,80},{112,128},{128,112... | collective-permute-start | bytes 970760 | tf_op jit(solution)/shard_map/ppermute | solution.py:547
  23.3 9.6 %collective-permute-start.7 = (bf16[2,160,128]{2,1,0:T(8,128)(2,1)S(1)}, bf16[2,160,128]{2,1,0:T(8,128)(2,1)S(1)}, u32[]{:S(2)}, u32[]{:S(2)}) collective-permute-start(bf16[2,160,128]{2,1,0:T(8,128)(2,1)S(1)} %get-tuple-element.89.refs_0_.near0), channel_id=1, source_target_pairs={{0,96},{16,112},{32,64},{48,80},{64,32},{80,48},{96,0},{112,16},{1... | collective-permute-start | bytes 245768 | tf_op jit(solution)/shard_map/ppermute | solution.py:541
  25.1 7.8 %collective-permute-start.6 = (bf16[2,160,128]{2,1,0:T(8,128)(2,1)S(1)}, bf16[2,160,128]{2,1,0:T(8,128)(2,1)S(1)}, u32[]{:S(2)}, u32[]{:S(2)}) collective-permute-start(bf16[2,160,128]{2,1,0:T(8,128)(2,1)S(1)} %get-tuple-element.89.refs_0_.near0), channel_id=1, source_target_pairs={{0,64},{16,80},{32,96},{48,112},{64,0},{80,16},{96,32},{112,48},{1... | collective-permute-start | bytes 245768 | tf_op jit(solution)/shard_map/ppermute | solution.py:541
  26.4 6.5 %collective-permute-start.5 = (bf16[2,160,128]{2,1,0:T(8,128)(2,1)S(1)}, bf16[2,160,128]{2,1,0:T(8,128)(2,1)S(1)}, u32[]{:S(2)}, u32[]{:S(2)}) collective-permute-start(bf16[2,160,128]{2,1,0:T(8,128)(2,1)S(1)} %get-tuple-element.89.refs_0_.near0), channel_id=1, source_target_pairs={{0,32},{16,48},{32,0},{48,16},{64,96},{80,112},{96,64},{112,80},{1... | collective-permute-start | bytes 245768 | tf_op jit(solution)/shard_map/ppermute | solution.py:541
  33.0 3.5 %collective-permute-start.8 = (bf16[4,2,160,128]{3,2,1,0:T(8,128)(2,1)S(1)}, bf16[4,2,160,128]{3,2,1,0:T(8,128)(2,1)S(1)}, u32[]{:S(2)}, u32[]{:S(2)}) collective-permute-start(bf16[4,2,160,128]{3,2,1,0:T(8,128)(2,1)S(1)} %stack_eight.1), channel_id=1, source_target_pairs={{0,16},{16,0},{32,48},{48,32},{64,80},{80,64},{96,112},{112,96},{1... | collective-permute-start | bytes 983048 | tf_op jit(solution)/shard_map/ppermute | solution.py:541
  40.0 5.1 %collective-permute-start.9 = (bf16[8,160,128]{2,1,0:T(8,128)(2,1)S(1)}, bf16[8,160,128]{2,1,0:T(8,128)(2,1)S(1)}, u32[]{:S(2)}, u32[]{:S(2)}) collective-permute-start(bf16[8,160,128]{2,1,0:T(8,128)(2,1)S(1)} %get-tuple-element.102), channel_id=1, source_target_pairs={{0,16},{16,0},{32,48},{48,32},{64,80},{80,64},{96,112},{112,96},{1... | collective-permute-start | bytes 983048 | tf_op jit(solution)/shard_map/ppermute | solution.py:541
  43.5 1.7 %collective-permute-start.10 = (bf16[8,144,128]{2,1,0:T(8,128)(2,1)S(1)}, bf16[8,144,128]{2,1,0:T(8,128)(2,1)S(1)}, u32[]{:S(2)}, u32[]{:S(2)}) collective-permute-start(bf16[8,144,128]{2,1,0:T(8,128)(2,1)S(1)} %get-tuple-element.103), channel_id=1, source_target_pairs={{0,16},{16,0},{32,48},{48,32},{64,80},{80,64},{96,112},{112,96},{1... | collective-permute-start | bytes 884744 | tf_op jit(solution)/shard_map/ppermute | solution.py:541
  95.5 6.6 %collective-permute-start.11 = (bf16[16,72,128]{2,1,0:T(8,128)(2,1)S(1)}, bf16[16,72,128]{2,1,0:T(8,128)(2,1)S(1)}, u32[]{:S(2)}, u32[]{:S(2)}) collective-permute-start(bf16[16,72,128]{2,1,0:T(8,128)(2,1)S(1)} %all_to_all.23.mine), channel_id=1, source_target_pairs={{0,16},{16,0},{32,48},{48,32},{64,80},{80,64},{96,112},{112,96},{1... | collective-permute-start | bytes 884744 | tf_op jit(solution)/shard_map/ppermute | solution.py:541

commit v16 on v15

--- a/solution.py
+++ b/solution.py
@@ -138,14 +138,15 @@
     return lax.select(even, other, pair), lax.select(even, pair, other)
 
 
-def pack_columns_kernel(meta, feat, cot, pair, other, done):
+def pack_columns_kernel(meta, feat, cot, conv, proj, pair, other, weights, done):
     odd = meta[5] % 2
     pairs = [
         (feat.at[:, aligned(32 - 32 * odd, 32), :], pair.at[:, 0:32, :]),
         (cot.at[:, aligned(48 - 48 * odd, 16), :], pair.at[:, 32:48, :]),
         (feat.at[:, aligned(32 * odd, 32), :], other.at[:, 0:32, :]),
         (cot.at[:, aligned(48 * odd, 16), :], other.at[:, 32:48, :]),
-    ]
+        (proj, weights.at[144:160, :]),
+    ] + [(conv.at[t], weights.at[16 * t : 16 * t + 16, :]) for t in range(9)]
     copies = [pltpu.make_async_copy(a, b, done.at[k]) for k, (a, b) in enumerate(pairs)]
     for copy in copies:
         copy.start()
@@ -160,9 +161,12 @@
     return ref[1024:1216, :].reshape(2, 96, CH)
 
 
-def bring_kernel(feat_far, cot_far, conv, proj, feat, cot, weights, done):
-    pairs = [(feat_far, feat), (cot_far, cot), (proj, weights.at[144:160, :])]
-    pairs += [(conv.at[t], weights.at[16 * t : 16 * t + 16, :]) for t in range(9)]
+def copy_kernel(value, out):
+    out[...] = value[...]
+
+
+def bring_kernel(feat_far, cot_far, feat, cot, done):
+    pairs = [(feat_far, feat), (cot_far, cot)]
     copies = [pltpu.make_async_copy(a, b, done.at[k]) for k, (a, b) in enumerate(pairs)]
     for copy in copies:
         copy.start()
@@ -584,24 +588,25 @@
     slab = ((160, CH), BF)
 
     side = ((16, 48, CH), BF)
-    pair, other = call(
+    pair, other, own = call(
         pack_columns_kernel,
         "pack_columns",
-        (side, side),
-        (meta, feat, cot),
-        (pltpu.SemaphoreType.DMA((4,)),),
-        far=(1, 2),
-    )
+        (side, side, slab),
+        (meta, feat, cot, conv, coarse_proj),
+        (pltpu.SemaphoreType.DMA((14,)),),
+        far=(1, 2, 3, 4),
+    )
+    own = call(copy_kernel, "own_slab", (slab,), (own,), flops=4 * 10**9)[0]
     w1, w2 = (conv_first.reshape(1152, CH), conv_second.reshape(1152, CH))
     big, wide = (((16, 64, CH), BF), ((1536, 256), BF))
-    feat_in, cot_in, own = call(
+    feat_in, cot_in = call(
         bring_kernel,
         "bring",
-        (big, big, slab),
-        (after_all(feat, pair), cot, conv, coarse_proj),
-        (pltpu.SemaphoreType.DMA((12,)),),
-        far=(0, 1, 2, 3),
-        flops=4 * 10**9,
+        (big, big),
+        (after_all(feat, own), cot),
+        (pltpu.SemaphoreType.DMA((2,)),),
+        far=(0, 1),
+        flops=0,
     )
     own_far = swap(own, "row", 8)
     weight1, weight2, back1, back2 = call(
@@ -611,7 +616,7 @@
         (after_all(w1, feat_in), w2),
         (((1152, CH), BF), ((1152, CH), BF), pltpu.SemaphoreType.DMA((2,))),
         far=(0, 1),
-        flops=4 * 10**9,
+        flops=0,
     )
     pair = swap(pair, "col", 1)
     other = swap_outer(other, "col")

time: 104 us -> 104 us (level)
  blocking collectives: 49.5 us -> 55.2 us
  starting transfers between devices: 25.7 us -> 21.7 us
  waiting for transfers between devices: 5.04 us -> 3.19 us
    all_to_all x2, blocking collectives: 28.3 us -> 34 us  [exchange_plane(): lax.all_to_all(value, ('row', 'col'), 0, 0, axis_index_groups=groups, til...]
    ppermute x10, starting transfers between devices: 22 us -> 18.1 us  [swap(): return lax.ppermute(value, axis, [(i, i ^ mask) for i in range(count)])]
    ppermute x10, waiting for transfers between devices: 5.04 us -> 3.19 us  [swap(): return lax.ppermute(value, axis, [(i, i ^ mask) for i in range(count)])]
    pallas_call x16 -> x17, Pallas kernels: 22.6 us -> 22.6 us  [call(): pl.pallas_call(kernel, name=name, out_shape=shapes, in_specs=[HBM if k in...]
  transfers between devices with their start and end apart: 12 -> 12, of which waited for: 4 -> 3; matrix products, arithmetic and copies ran while one was open for 0% -> 0% of each run, Pallas kernels for 14% -> 14%
where the time goes in v16:
time: 104 us
  blocking collectives  55.2 us (53%)
  Pallas kernels  22.6 us (22%)
  starting transfers between devices  21.7 us (21%)
  waiting for transfers between devices  3.19 us (3%)
    all_to_all x2, blocking collectives, exchange_plane(): lax.all_to_all(value, ('row', 'col'), 0, 0, axis_index_groups=groups, til...  34 us
    pallas_call x17, Pallas kernels, call(): pl.pallas_call(kernel, name=name, out_shape=shapes, in_specs=[HBM if k in...  22.6 us
    ppermute x10, starting transfers between devices, swap(): return lax.ppermute(value, axis, [(i, i ^ mask) for i in range(count)])  18.1 us
    all_to_all x1, blocking collectives, exchange_depth(): lax.all_to_all(value, 'col', 0, 0, axis_index_groups=groups, tiled=True)  11.3 us
    all_to_all x1, blocking collectives, exchange_column(): return lax.all_to_all(value, 'col', 0, 0, tiled=True)  9.98 us
    ppermute x2, starting transfers between devices, swap_outer(): return lax.ppermute(value, axis, pairs)  3.68 us
    ppermute x10, waiting for transfers between devices, swap(): return lax.ppermute(value, axis, [(i, i ^ mask) for i in range(count)])  3.19 us
  transfers between devices with their start and end apart: 12, of which 3 were waited for; matrix products, arithmetic and copies ran while one was open for 0% of the time, Pallas kernels for 14%

profile of v16, /device:TPU:1, one launch (start us, length us, event | category | flops | bytes accessed | tf_op | source)
XLA Modules:
  0.0 103.6 jit_solution(18370020663649756789)
XLA Ops:
  0.7 1.7 %pack_columns.1 = (bf16[16,48,128]{2,1,0:T(8,128)(2,1)S(1)}, bf16[16,48,128]{2,1,0:T(8,128)(2,1)S(1)}, bf16[160,128]{1,0:T(8,128)(2,1)S(1)}) custom-call(s32[6]{0:T(128)S(1)} %stack.19.meta, bf16[16,64,128]{2,1,0:T(8,128)(2,1)} %bitcast.18, bf16[16,64,128]{2,1,0:T(8,128)(2,1)} %bitcast.20, bf16[9,16,128]{2,1,0:T(8,128)(2,1)} %bitcast.24, bf16[16,128]{1,0:T(8,128)(2,1)} %proj.1), custom_call_target="tpu_custom_call" | custom-call | tf_op jit(solution)/shard_map/pack_columns/pallas_call | solution.py:23
  2.4 2.6 %collective-permute-start = (bf16[16,48,128]{2,1,0:T(8,128)(2,1)S(1)}, bf16[16,48,128]{2,1,0:T(8,128)(2,1)S(1)}, u32[]{:S(2)}, u32[]{:S(2)}) collective-permute-start(bf16[16,48,128]{2,1,0:T(8,128)(2,1)S(1)} %get-tuple-element.66), channel_id=1, source_target_pairs={{0,1},{1,0},{2,3},{3,2},{4,5},{5,4},{6,7},{7,6},{8,9},{9,8},{10,11... | collective-permute-start | bytes 589832 | tf_op jit(solution)/shard_map/ppermute | solution.py:545
  5.0 0.7 collective-permute-start.1
  5.7 3.0 %collective-permute-start.2 = (bf16[160,128]{1,0:T(8,128)(2,1)S(1)}, bf16[160,128]{1,0:T(8,128)(2,1)S(1)}, u32[]{:S(2)}, u32[]{:S(2)}) collective-permute-start(bf16[160,128]{1,0:T(8,128)(2,1)S(1)} %own_slab.1.own), channel_id=1, source_target_pairs={{0,128},{16,144},{32,160},{48,176},{64,192},{80,208},{96,224},{112... | collective-permute-start | bytes 122888 | tf_op jit(solution)/shard_map/ppermute | solution.py:545
  8.7 1.0 %bring.1 = (bf16[16,64,128]{2,1,0:T(8,128)(2,1)S(1)}, bf16[16,64,128]{2,1,0:T(8,128)(2,1)S(1)}) custom-call(bf16[16,64,128]{2,1,0:T(8,128)(2,1)} %bitcast.19, bf16[16,64,128]{2,1,0:T(8,128)(2,1)} %bitcast.21), custom_call_target="tpu_custom_call" | custom-call | tf_op jit(solution)/shard_map/bring/pallas_call | solution.py:23
  9.7 1.2 %weights.1 = (bf16[1536,256]{1,0:T(8,128)(2,1)S(1)}, bf16[1536,256]{1,0:T(8,128)(2,1)S(1)}, bf16[256,1536]{1,0:T(8,128)(2,1)S(1)}, bf16[256,1536]{1,0:T(8,128)(2,1)S(1)}) custom-call(bf16[1152,128]{1,0:T(8,128)(2,1)} %bitcast.22, bf16[1152,128]{1,0:T(8,128)(2,1)} %bitcast.23), custom_call_target="tpu_custom_call" | custom-call | tf_op jit(solution)/shard_map/weights/pallas_call | solution.py:23
  11.0 0.7 pack_rows.1
  11.7 1.3 %collective-permute-start.3 = (bf16[1264,128]{1,0:T(8,128)(2,1)S(1)}, bf16[1264,128]{1,0:T(8,128)(2,1)S(1)}, u32[]{:S(2)}, u32[]{:S(2)}) collective-permute-start(bf16[1264,128]{1,0:T(8,128)(2,1)S(1)} %get-tuple-element.71), channel_id=1, source_target_pairs={{0,16},{16,0},{32,48},{48,32},{64,80},{80,64},{96,112},{112,96},{1... | collective-permute-start | bytes 970760 | tf_op jit(solution)/shard_map/ppermute | solution.py:545
  13.0 3.0 %collective-permute-start.4 = (bf16[1264,128]{1,0:T(8,128)(2,1)S(1)}, bf16[1264,128]{1,0:T(8,128)(2,1)S(1)}, u32[]{:S(2)}, u32[]{:S(2)}) collective-permute-start(bf16[1264,128]{1,0:T(8,128)(2,1)S(1)} %get-tuple-element.72), channel_id=1, source_target_pairs={{16,32},{32,16},{48,64},{64,48},{80,96},{96,80},{112,128},{128,112... | collective-permute-start | bytes 970760 | tf_op jit(solution)/shard_map/ppermute | solution.py:551
  16.0 4.2 %collective-permute-start.7 = (bf16[2,160,128]{2,1,0:T(8,128)(2,1)S(1)}, bf16[2,160,128]{2,1,0:T(8,128)(2,1)S(1)}, u32[]{:S(2)}, u32[]{:S(2)}) collective-permute-start(bf16[2,160,128]{2,1,0:T(8,128)(2,1)S(1)} %get-tuple-element.89.refs_0_.near0), channel_id=1, source_target_pairs={{0,96},{16,112},{32,64},{48,80},{64,32},{80,48},{96,0},{112,16},{1... | collective-permute-start | bytes 245768 | tf_op jit(solution)/shard_map/ppermute | solution.py:545
  20.2 0.7 collective-permute-start.5
  20.9 3.6 %forward_inner.1 = (bf16[16,128,384]{2,1,0:T(8,128)(2,1)S(1)}, bf16[14,128,384]{2,1,0:T(8,128)(2,1)S(1)}, f32[14,96,128]{2,1,0:T(8,128)S(1)}, bf16[6,64,384]{2,1...) custom-call(s32[6]{0:T(128)S(1)} %stack.19.meta, ...), custom_call_target="tpu_custom_call" | custom-call | tf_op jit(solution)/shard_map/forward_inner/pallas_call | solution.py:23
  24.5 2.6 %collective-permute-done.7.refs_3_.near3 = bf16[2,160,128]{2,1,0:T(8,128)(2,1)S(1)} collective-permute-done((bf16[2,160,128]{2,1,0:T(8,128)(2,1)S(1)}, bf16[2,160,128]{2,1,0:T(8,128)(2,1)S(1)}, u32[]{:S(2)}, u32[]{:S(2)}) %collective-permute-start.7) | collective-permute-done | bytes 81952 | tf_op jit(solution)/shard_map/ppermute | solution.py:545
  27.2 0.1 collective-permute-start.8
  27.3 3.3 %forward_outer.1 = (bf16[14,64,384]{2,1,0:T(8,128)(2,1)S(1)}, f32[18,96,128]{2,1,0:T(8,128)S(1)}, f32[20,96,128]{2,1,0:T(8,128)S(1)}, bf16[16,64,128]{2,1,0:T(8,...) custom-call(s32[6]{0:T(128)S(1)} %stack.19.meta, ...), custom_call_target="tpu_custom_call" | custom-call | flops 4000000000 | tf_op jit(solution)/shard_map/forward_outer/pallas_call | solution.py:23
  30.6 3.6 %coarse_step.1 = (bf16[256,256]{1,0:T(8,128)(2,1)S(1)}, bf16[256,128]{1,0:T(8,128)(2,1)S(1)}, bf16[8,160,128]{2,1,0:T(8,128)(2,1)S(1)}, bf16[8,160,128]{2,1,0:T(8,128)(2,1)S(1)}, f32[10,48,128]{2,1,0:T(8,128)S(1)}) custom-call(s32[6]{0:T(128)S(1)} %stack.19.meta, bf16[14,64,384]{2,1,0:T(8,128)(2,1)S(1)} %get-tuple-element.88.pool3, ...), custom_call_target="tpu_custom_call" | custom-call | flops 2000000000 | tf_op jit(solution)/shard_map/coarse_step/pallas_call | solution.py:23
  34.2 0.7 collective-permute-start.9
  35.0 2.7 %fine_backward.1 = (bf16[8,144,128]{2,1,0:T(8,128)(2,1)S(1)}, bf16[8,144,128]{2,1,0:T(8,128)(2,1)S(1)}, bf16[18,64,384]{2,1,0:T(8,128)(2,1)S(1)}) custom-call(s32[6]{0:T(128)S(1)} %stack.19.meta, f32[10,48,128]{2,1,0:T(8,128)S(1)} %get-tuple-element.95.pooled_grad, bf16[16,64,128]{2,1,0:T(8,128)(2,1)S(1)} %get-tuple-element.65.cot, ...), custom_call_target="tpu_custom_call" | custom-call | flops 2000000000 | tf_op jit(solution)/shard_map/fine_backward/pallas_call | solution.py:23
  37.7 0.1 collective-permute-start.10
  37.8 1.3 %feature_step.1 = bf16[16,64,128]{2,1,0:T(8,128)(2,1)} custom-call(bf16[18,64,384]{2,1,0:T(8,128)(2,1)S(1)} %get-tuple-element.104.first3, bf16[256,1536]{1,0:T(8,128)(2,1)S(1)} %get-tuple-element.105.back_w), custom_call_target="tpu_custom_call" | custom-call | flops 1000000000 | tf_op jit(solution)/shard_map/feature_step/pallas_call | solution.py:23
  39.1 0.2 collective-permute-done.10.got_f
  39.3 0.2 scatter_core.1
  39.5 22.9 %all_to_all.20.got = bf16[16,152,128]{2,1,0:T(8,128)(2,1)S(1)} all-to-all(bf16[16,152,128]{2,1,0:T(8,128)(2,1)S(1)} %scatter_core.1), channel_id=1, replica_groups={{0,8,32,40,64,72,96,104,128,136,160,168,192,200,224,232},{1,9,33,41,65,..., dimensions={0} | all-to-all | bytes 1245184 | tf_op jit(solution)/shard_map/all_to_all | solution.py:560
  62.4 0.1 scatter_plane.1
  62.4 11.3 %all_to_all.21.got = bf16[8,24,128]{2,1,0:T(8,128)(2,1)S(1)} all-to-all(bf16[8,24,128]{2,1,0:T(8,128)(2,1)S(1)} %scatter_plane.1), channel_id=1, replica_groups={{0,1,2,3,4,5,6,7},{8,9,10,11,12,13,14,15},{16,17,18,19,20,21,22,23},{24..., dimensions={0} | all-to-all | bytes 98304 | tf_op jit(solution)/shard_map/all_to_all | solution.py:566
  73.7 10.0 %all_to_all.22.got = bf16[16,24,128]{2,1,0:T(8,128)(2,1)S(1)} all-to-all(bf16[16,24,128]{2,1,0:T(8,128)(2,1)S(1)} %scatter_column.1), channel_id=1, replica_groups=mesh['row'=16,'col'=16] {'col'}, dimensions={0} | all-to-all | bytes 196608 | tf_op jit(solution)/shard_map/all_to_all | solution.py:570
  83.7 0.6 gather_column.1
  84.3 11.1 %all_to_all.23.mine = bf16[16,72,128]{2,1,0:T(8,128)(2,1)S(1)} all-to-all(bf16[16,72,128]{2,1,0:T(8,128)(2,1)S(1)} %get-tuple-element.107), channel_id=1, replica_groups={{0,8,32,40,64,72,96,104,128,136,160,168,192,200,224,232},{1,9,33,41,65,..., dimensions={0} | all-to-all | bytes 589824 | tf_op jit(solution)/shard_map/all_to_all | solution.py:560
  95.4 5.4 %collective-permute-start.11 = (bf16[16,72,128]{2,1,0:T(8,128)(2,1)S(1)}, bf16[16,72,128]{2,1,0:T(8,128)(2,1)S(1)}, u32[]{:S(2)}, u32[]{:S(2)}) collective-permute-start(bf16[16,72,128]{2,1,0:T(8,128)(2,1)S(1)} %all_to_all.23.mine), channel_id=1, source_target_pairs={{0,16},{16,0},{32,48},{48,32},{64,80},{80,64},{96,112},{112,96},{1... | collective-permute-start | bytes 884744 | tf_op jit(solution)/shard_map/ppermute | solution.py:545
  100.8 0.9 blend.1
  101.7 0.3 collective-permute-done.11.other
  102.0 1.6 %finish.1 = (f32[8,144,128]{2,1,0:T(8,128)}, f32[8,144,128]{2,1,0:T(8,128)}) custom-call(s32[6]{0:T(128)S(1)} %stack.19.meta, bf16[16,72,128]{2,1,0:T(8,128)(2,1)S(1)} %all_to_all.23.mine, bf16[16,72,128]{2,1,0:T(8,128)(2,1)S(1)} %collective-permute-done.11.other), custom_call_target="tpu_custom_call" | custom-call | tf_op jit(solution)/shard_map/finish/pallas_call | solution.py:23
  (15 shorter events, 0.2 us)
Async XLA Ops:
  2.4 8.5 %collective-permute-start = (bf16[16,48,128]{2,1,0:T(8,128)(2,1)S(1)}, bf16[16,48,128]{2,1,0:T(8,128)(2,1)S(1)}, u32[]{:S(2)}, u32[]{:S(2)}) collective-permute-start(bf16[16,48,128]{2,1,0:T(8,128)(2,1)S(1)} %get-tuple-element.66), channel_id=1, source_target_pairs={{0,1},{1,0},{2,3},{3,2},{4,5},{5,4},{6,7},{7,6},{8,9},{9,8},{10,11... | collective-permute-start | bytes 589832 | tf_op jit(solution)/shard_map/ppermute | solution.py:545
  5.0 6.0 %collective-permute-start.1 = (bf16[16,48,128]{2,1,0:T(8,128)(2,1)S(1)}, bf16[16,48,128]{2,1,0:T(8,128)(2,1)S(1)}, u32[]{:S(2)}, u32[]{:S(2)}) collective-permute-start(bf16[16,48,128]{2,1,0:T(8,128)(2,1)S(1)} %get-tuple-element.67), channel_id=1, source_target_pairs={{1,2},{2,1},{3,4},{4,3},{5,6},{6,5},{7,8},{8,7},{9,10},{10,9},{11,... | collective-permute-start | bytes 589832 | tf_op jit(solution)/shard_map/ppermute | solution.py:551
  5.7 5.3 %collective-permute-start.2 = (bf16[160,128]{1,0:T(8,128)(2,1)S(1)}, bf16[160,128]{1,0:T(8,128)(2,1)S(1)}, u32[]{:S(2)}, u32[]{:S(2)}) collective-permute-start(bf16[160,128]{1,0:T(8,128)(2,1)S(1)} %own_slab.1.own), channel_id=1, source_target_pairs={{0,128},{16,144},{32,160},{48,176},{64,192},{80,208},{96,224},{112... | collective-permute-start | bytes 122888 | tf_op jit(solution)/shard_map/ppermute | solution.py:545
  11.7 15.6 %collective-permute-start.3 = (bf16[1264,128]{1,0:T(8,128)(2,1)S(1)}, bf16[1264,128]{1,0:T(8,128)(2,1)S(1)}, u32[]{:S(2)}, u32[]{:S(2)}) collective-permute-start(bf16[1264,128]{1,0:T(8,128)(2,1)S(1)} %get-tuple-element.71), channel_id=1, source_target_pairs={{0,16},{16,0},{32,48},{48,32},{64,80},{80,64},{96,112},{112,96},{1... | collective-permute-start | bytes 970760 | tf_op jit(solution)/shard_map/ppermute | solution.py:545
  13.0 14.3 %collective-permute-start.4 = (bf16[1264,128]{1,0:T(8,128)(2,1)S(1)}, bf16[1264,128]{1,0:T(8,128)(2,1)S(1)}, u32[]{:S(2)}, u32[]{:S(2)}) collective-permute-start(bf16[1264,128]{1,0:T(8,128)(2,1)S(1)} %get-tuple-element.72), channel_id=1, source_target_pairs={{16,32},{32,16},{48,64},{64,48},{80,96},{96,80},{112,128},{128,112... | collective-permute-start | bytes 970760 | tf_op jit(solution)/shard_map/ppermute | solution.py:551
  16.0 11.1 %collective-permute-start.7 = (bf16[2,160,128]{2,1,0:T(8,128)(2,1)S(1)}, bf16[2,160,128]{2,1,0:T(8,128)(2,1)S(1)}, u32[]{:S(2)}, u32[]{:S(2)}) collective-permute-start(bf16[2,160,128]{2,1,0:T(8,128)(2,1)S(1)} %get-tuple-element.89.refs_0_.near0), channel_id=1, source_target_pairs={{0,96},{16,112},{32,64},{48,80},{64,32},{80,48},{96,0},{112,16},{1... | collective-permute-start | bytes 245768 | tf_op jit(solution)/shard_map/ppermute | solution.py:545
  20.2 6.9 %collective-permute-start.6 = (bf16[2,160,128]{2,1,0:T(8,128)(2,1)S(1)}, bf16[2,160,128]{2,1,0:T(8,128)(2,1)S(1)}, u32[]{:S(2)}, u32[]{:S(2)}) collective-permute-start(bf16[2,160,128]{2,1,0:T(8,128)(2,1)S(1)} %get-tuple-element.89.refs_0_.near0), channel_id=1, source_target_pairs={{0,64},{16,80},{32,96},{48,112},{64,0},{80,16},{96,32},{112,48},{1... | collective-permute-start | bytes 245768 | tf_op jit(solution)/shard_map/ppermute | solution.py:545
  20.2 6.9 %collective-permute-start.5 = (bf16[2,160,128]{2,1,0:T(8,128)(2,1)S(1)}, bf16[2,160,128]{2,1,0:T(8,128)(2,1)S(1)}, u32[]{:S(2)}, u32[]{:S(2)}) collective-permute-start(bf16[2,160,128]{2,1,0:T(8,128)(2,1)S(1)} %get-tuple-element.89.refs_0_.near0), channel_id=1, source_target_pairs={{0,32},{16,48},{32,0},{48,16},{64,96},{80,112},{96,64},{112,80},{1... | collective-permute-start | bytes 245768 | tf_op jit(solution)/shard_map/ppermute | solution.py:545
  27.2 3.5 %collective-permute-start.8 = (bf16[4,2,160,128]{3,2,1,0:T(8,128)(2,1)S(1)}, bf16[4,2,160,128]{3,2,1,0:T(8,128)(2,1)S(1)}, u32[]{:S(2)}, u32[]{:S(2)}) collective-permute-start(bf16[4,2,160,128]{3,2,1,0:T(8,128)(2,1)S(1)} %stack_eight.1), channel_id=1, source_target_pairs={{0,16},{16,0},{32,48},{48,32},{64,80},{80,64},{96,112},{112,96},{1... | collective-permute-start | bytes 983048 | tf_op jit(solution)/shard_map/ppermute | solution.py:545
  34.2 5.1 %collective-permute-start.9 = (bf16[8,160,128]{2,1,0:T(8,128)(2,1)S(1)}, bf16[8,160,128]{2,1,0:T(8,128)(2,1)S(1)}, u32[]{:S(2)}, u32[]{:S(2)}) collective-permute-start(bf16[8,160,128]{2,1,0:T(8,128)(2,1)S(1)} %get-tuple-element.102), channel_id=1, source_target_pairs={{0,16},{16,0},{32,48},{48,32},{64,80},{80,64},{96,112},{112,96},{1... | collective-permute-start | bytes 983048 | tf_op jit(solution)/shard_map/ppermute | solution.py:545
  37.7 1.7 %collective-permute-start.10 = (bf16[8,144,128]{2,1,0:T(8,128)(2,1)S(1)}, bf16[8,144,128]{2,1,0:T(8,128)(2,1)S(1)}, u32[]{:S(2)}, u32[]{:S(2)}) collective-permute-start(bf16[8,144,128]{2,1,0:T(8,128)(2,1)S(1)} %get-tuple-element.103), channel_id=1, source_target_pairs={{0,16},{16,0},{32,48},{48,32},{64,80},{80,64},{96,112},{112,96},{1... | collective-permute-start | bytes 884744 | tf_op jit(solution)/shard_map/ppermute | solution.py:545
  95.4 6.6 %collective-permute-start.11 = (bf16[16,72,128]{2,1,0:T(8,128)(2,1)S(1)}, bf16[16,72,128]{2,1,0:T(8,128)(2,1)S(1)}, u32[]{:S(2)}, u32[]{:S(2)}) collective-permute-start(bf16[16,72,128]{2,1,0:T(8,128)(2,1)S(1)} %all_to_all.23.mine), channel_id=1, source_target_pairs={{0,16},{16,0},{32,48},{48,32},{64,80},{80,64},{96,112},{112,96},{1... | collective-permute-start | bytes 884744 | tf_op jit(solution)/shard_map/ppermute | solution.py:545

commit v17 on v16

--- a/solution.py
+++ b/solution.py
@@ -243,7 +243,14 @@
 INNER_SECOND = [10, 12, 14, 16, 18, 20]
 
 
-def inner_kernel(meta, feat, pair, other, weight1, weight2, feat3, act3, slope1, pool3, slope2, act):
+def inner_kernel(
+    meta, feat, cot, pair, other, weight1, weight2, feat3, act3, slope1, pool3, slope2, act, sums
+):
+    for k in range(8):
+        rows = slice(2 * k, 2 * k + 2)
+        before, after = sides(meta, pair[rows, 32:48, :], other[rows, 32:48, :])
+        both = jnp.concatenate([before, cot[rows], after], axis=1).astype(F32)
+        sums[k] = pooled_pair(both[0] + both[1])
     for k in range(16):
         before, after = sides(meta, pair[k, 0:32, :], other[k, 0:32, :])
         feat3[k] = three(jnp.concatenate([before, feat[k], after], axis=0).astype(F32))
@@ -294,7 +301,7 @@
         act3o[k] = act_row(k + 7)[32:96]
 
 
-def inner_step(meta, feat, pair, other, weight1, weight2):
+def inner_step(meta, feat, cot, pair, other, weight1, weight2):
     return call(
         inner_kernel,
         "forward_inner",
@@ -305,8 +312,9 @@
             ((6, 64, 384), BF),
             ((12, 96, CH), F32),
             ((12, 64, CH), BF),
+            ((8, 48, CH), F32),
         ),
-        (meta, feat, pair, other, weight1, weight2),
+        (meta, feat, cot, pair, other, weight1, weight2),
         limit=24,
         flops=0,
     )
@@ -332,7 +340,7 @@
 
 
 def coarse_kernel(
-    meta, pool3, cot, pair, other, inner, outer, near0, near1, near2, near3, far,
+    meta, pool3, sums, inner, outer, near0, near1, near2, near3, far,
     own, projs_out, keep, send, pooled_grad, wcat, projs, wide3, projin,
 ):
     top, left, height, breadth, me = (meta[0], meta[1], meta[2], meta[3], meta[4])
@@ -355,12 +363,7 @@
         near_rows = cot_edge(ref)
         projin[near_at] = pair_sum(near_rows[0], near_rows[1])
 
-    for k in range(8):
-        rows = slice(2 * k, 2 * k + 2)
-        before, after = sides(meta, pair[rows, 32:48, :], other[rows, 32:48, :])
-        both = jnp.concatenate([before, cot[rows], after], axis=1)
-        projin[k + 2] = pair_sum(both[0], both[1])
-
+    projin[2:10] = sums[...]
     proj_in = projin[...].reshape(576, CH)
     proj_in_bf = proj_in.astype(BF)
     lhs = jnp.concatenate([pool3[r : r + 12].reshape(768, 3 * CH) for r in range(3)], axis=1)
@@ -411,12 +414,12 @@
             blended[2 * k + e] = (act[2 * k + e].astype(F32) + row).astype(BF)
 
 
-def coarse_step(meta, pool3, cot, halo, near, far):
+def coarse_step(meta, pool3, sums, halo, near, far):
     return call(
         coarse_kernel,
         "coarse_step",
         (((256, WIDE), BF), ((WIDE, CH), BF), ((8, 160, CH), BF), ((8, 160, CH), BF), ((10, 48, CH), F32)),
-        (meta, pool3, cot) + halo + tuple(near) + (far,),
+        (meta, pool3, sums) + halo[2:] + tuple(near) + (far,),
         (
             ((WIDE, 9 * CH), BF),
             ((WIDE, CH), BF),
@@ -631,12 +634,12 @@
     inner = swap(inner, "row", 1)
     pair_in = after_all(pair, near0)
     near = [near0] + [swap(near0, "row", 2 * k) for k in range(1, 4)]
-    parts = inner_step(meta, feat_in, pair_in, other, weight1, weight2)
+    *parts, sums = inner_step(meta, feat_in, cot_in, pair_in, other, weight1, weight2)
     parts, near = lax.optimization_barrier((parts, near))
     far = swap(call(stack_kernel, "stack_eight", (((4, 2, 160, CH), BF),), near)[0], "row", 1)
     pool3, slope1, slope2, act, feat3, act3 = outer_step(meta, inner, outer, parts, weight1, weight2)
     halo = (pair, other, inner, outer)
-    own_act, proj, keep_c, send_c, pooled_grad = coarse_step(meta, pool3, cot_in, halo, near, far)
+    own_act, proj, keep_c, send_c, pooled_grad = coarse_step(meta, pool3, sums, halo, near, far)
     got_c = swap(send_c, "row", 1)
     keep_f, send_f, first3 = fine_backward(
         meta, pooled_grad, cot_in, halo, slope1, slope2, feat3, act3, back2

time: 104 us -> 104 us (level)
  no operation moved by 1% of the time
where the time goes in v17:
time: 104 us
  blocking collectives  55.2 us (53%)
  Pallas kernels  22.6 us (22%)
  starting transfers between devices  21.7 us (21%)
  waiting for transfers between devices  3.15 us (3%)
    all_to_all x2, blocking collectives, exchange_plane(): lax.all_to_all(value, ('row', 'col'), 0, 0, axis_index_groups=groups, til...  34 us
    pallas_call x17, Pallas kernels, call(): pl.pallas_call(kernel, name=name, out_shape=shapes, in_specs=[HBM if k in...  22.6 us
    ppermute x10, starting transfers between devices, swap(): return lax.ppermute(value, axis, [(i, i ^ mask) for i in range(count)])  18 us
    all_to_all x1, blocking collectives, exchange_depth(): lax.all_to_all(value, 'col', 0, 0, axis_index_groups=groups, tiled=True)  11.3 us
    all_to_all x1, blocking collectives, exchange_column(): return lax.all_to_all(value, 'col', 0, 0, tiled=True)  9.98 us
    ppermute x2, starting transfers between devices, swap_outer(): return lax.ppermute(value, axis, pairs)  3.68 us
    ppermute x10, waiting for transfers between devices, swap(): return lax.ppermute(value, axis, [(i, i ^ mask) for i in range(count)])  3.14 us
  transfers between devices with their start and end apart: 12, of which 3 were waited for; matrix products, arithmetic and copies ran while one was open for 0% of the time, Pallas kernels for 14%

profile of v17, /device:TPU:1, one launch (start us, length us, event | category | flops | bytes accessed | tf_op | source)
XLA Modules:
  0.0 103.6 jit_solution(11291651679085631376)
XLA Ops:
  0.7 1.7 %pack_columns.1 = (bf16[16,48,128]{2,1,0:T(8,128)(2,1)S(1)}, bf16[16,48,128]{2,1,0:T(8,128)(2,1)S(1)}, bf16[160,128]{1,0:T(8,128)(2,1)S(1)}) custom-call(s32[6]{0:T(128)S(1)} %stack.19.meta, bf16[16,64,128]{2,1,0:T(8,128)(2,1)} %bitcast.18, bf16[16,64,128]{2,1,0:T(8,128)(2,1)} %bitcast.20, bf16[9,16,128]{2,1,0:T(8,128)(2,1)} %bitcast.24, bf16[16,128]{1,0:T(8,128)(2,1)} %proj.1), custom_call_target="tpu_custom_call" | custom-call | tf_op jit(solution)/shard_map/pack_columns/pallas_call | solution.py:23
  2.4 2.6 %collective-permute-start = (bf16[16,48,128]{2,1,0:T(8,128)(2,1)S(1)}, bf16[16,48,128]{2,1,0:T(8,128)(2,1)S(1)}, u32[]{:S(2)}, u32[]{:S(2)}) collective-permute-start(bf16[16,48,128]{2,1,0:T(8,128)(2,1)S(1)} %get-tuple-element.67), channel_id=1, source_target_pairs={{0,1},{1,0},{2,3},{3,2},{4,5},{5,4},{6,7},{7,6},{8,9},{9,8},{10,11... | collective-permute-start | bytes 589832 | tf_op jit(solution)/shard_map/ppermute | solution.py:548
  5.0 0.7 collective-permute-start.1
  5.7 3.0 %collective-permute-start.2 = (bf16[160,128]{1,0:T(8,128)(2,1)S(1)}, bf16[160,128]{1,0:T(8,128)(2,1)S(1)}, u32[]{:S(2)}, u32[]{:S(2)}) collective-permute-start(bf16[160,128]{1,0:T(8,128)(2,1)S(1)} %own_slab.1.own), channel_id=1, source_target_pairs={{0,128},{16,144},{32,160},{48,176},{64,192},{80,208},{96,224},{112... | collective-permute-start | bytes 122888 | tf_op jit(solution)/shard_map/ppermute | solution.py:548
  8.7 1.0 %bring.1 = (bf16[16,64,128]{2,1,0:T(8,128)(2,1)S(1)}, bf16[16,64,128]{2,1,0:T(8,128)(2,1)S(1)}) custom-call(bf16[16,64,128]{2,1,0:T(8,128)(2,1)} %bitcast.19, bf16[16,64,128]{2,1,0:T(8,128)(2,1)} %bitcast.21), custom_call_target="tpu_custom_call" | custom-call | tf_op jit(solution)/shard_map/bring/pallas_call | solution.py:23
  9.7 1.2 %weights.1 = (bf16[1536,256]{1,0:T(8,128)(2,1)S(1)}, bf16[1536,256]{1,0:T(8,128)(2,1)S(1)}, bf16[256,1536]{1,0:T(8,128)(2,1)S(1)}, bf16[256,1536]{1,0:T(8,128)(2,1)S(1)}) custom-call(bf16[1152,128]{1,0:T(8,128)(2,1)} %bitcast.22, bf16[1152,128]{1,0:T(8,128)(2,1)} %bitcast.23), custom_call_target="tpu_custom_call" | custom-call | tf_op jit(solution)/shard_map/weights/pallas_call | solution.py:23
  11.0 0.7 pack_rows.1
  11.7 1.3 %collective-permute-start.3 = (bf16[1264,128]{1,0:T(8,128)(2,1)S(1)}, bf16[1264,128]{1,0:T(8,128)(2,1)S(1)}, u32[]{:S(2)}, u32[]{:S(2)}) collective-permute-start(bf16[1264,128]{1,0:T(8,128)(2,1)S(1)} %get-tuple-element.72), channel_id=1, source_target_pairs={{0,16},{16,0},{32,48},{48,32},{64,80},{80,64},{96,112},{112,96},{1... | collective-permute-start | bytes 970760 | tf_op jit(solution)/shard_map/ppermute | solution.py:548
  13.0 3.0 %collective-permute-start.4 = (bf16[1264,128]{1,0:T(8,128)(2,1)S(1)}, bf16[1264,128]{1,0:T(8,128)(2,1)S(1)}, u32[]{:S(2)}, u32[]{:S(2)}) collective-permute-start(bf16[1264,128]{1,0:T(8,128)(2,1)S(1)} %get-tuple-element.73), channel_id=1, source_target_pairs={{16,32},{32,16},{48,64},{64,48},{80,96},{96,80},{112,128},{128,112... | collective-permute-start | bytes 970760 | tf_op jit(solution)/shard_map/ppermute | solution.py:554
  16.0 4.2 %collective-permute-start.7 = (bf16[2,160,128]{2,1,0:T(8,128)(2,1)S(1)}, bf16[2,160,128]{2,1,0:T(8,128)(2,1)S(1)}, u32[]{:S(2)}, u32[]{:S(2)}) collective-permute-start(bf16[2,160,128]{2,1,0:T(8,128)(2,1)S(1)} %get-tuple-element.91.refs_0_.near0), channel_id=1, source_target_pairs={{0,96},{16,112},{32,64},{48,80},{64,32},{80,48},{96,0},{112,16},{1... | collective-permute-start | bytes 245768 | tf_op jit(solution)/shard_map/ppermute | solution.py:548
  20.2 0.7 collective-permute-start.5
  20.9 3.6 %forward_inner.1 = (bf16[16,128,384]{2,1,0:T(8,128)(2,1)S(1)}, bf16[14,128,384]{2,1,0:T(8,128)(2,1)S(1)}, f32[14,96,128]{2,1,0:T(8,128)S(1)}, bf16[6,64,384]{2,1...) custom-call(s32[6]{0:T(128)S(1)} %stack.19.meta, ...), custom_call_target="tpu_custom_call" | custom-call | tf_op jit(solution)/shard_map/forward_inner/pallas_call | solution.py:23
  24.5 2.6 %collective-permute-done.7.refs_3_.near3 = bf16[2,160,128]{2,1,0:T(8,128)(2,1)S(1)} collective-permute-done((bf16[2,160,128]{2,1,0:T(8,128)(2,1)S(1)}, bf16[2,160,128]{2,1,0:T(8,128)(2,1)S(1)}, u32[]{:S(2)}, u32[]{:S(2)}) %collective-permute-start.7) | collective-permute-done | bytes 81952 | tf_op jit(solution)/shard_map/ppermute | solution.py:548
  27.2 0.1 collective-permute-start.8
  27.3 3.3 %forward_outer.1 = (bf16[14,64,384]{2,1,0:T(8,128)(2,1)S(1)}, f32[18,96,128]{2,1,0:T(8,128)S(1)}, f32[20,96,128]{2,1,0:T(8,128)S(1)}, bf16[16,64,128]{2,1,0:T(8,...) custom-call(s32[6]{0:T(128)S(1)} %stack.19.meta, ...), custom_call_target="tpu_custom_call" | custom-call | flops 4000000000 | tf_op jit(solution)/shard_map/forward_outer/pallas_call | solution.py:23
  30.6 3.5 %coarse_step.1 = (bf16[256,256]{1,0:T(8,128)(2,1)S(1)}, bf16[256,128]{1,0:T(8,128)(2,1)S(1)}, bf16[8,160,128]{2,1,0:T(8,128)(2,1)S(1)}, bf16[8,160,128]{2,1,0:T(8,128)(2,1)S(1)}, f32[10,48,128]{2,1,0:T(8,128)S(1)}) custom-call(s32[6]{0:T(128)S(1)} %stack.19.meta, bf16[14,64,384]{2,1,0:T(8,128)(2,1)S(1)} %get-tuple-element.89.pool3, ...), custom_call_target="tpu_custom_call" | custom-call | flops 2000000000 | tf_op jit(solution)/shard_map/coarse_step/pallas_call | solution.py:23
  34.2 0.7 collective-permute-start.9
  34.9 2.7 %fine_backward.1 = (bf16[8,144,128]{2,1,0:T(8,128)(2,1)S(1)}, bf16[8,144,128]{2,1,0:T(8,128)(2,1)S(1)}, bf16[18,64,384]{2,1,0:T(8,128)(2,1)S(1)}) custom-call(s32[6]{0:T(128)S(1)} %stack.19.meta, f32[10,48,128]{2,1,0:T(8,128)S(1)} %get-tuple-element.97.pooled_grad, bf16[16,64,128]{2,1,0:T(8,128)(2,1)S(1)} %get-tuple-element.66.cot, ...), custom_call_target="tpu_custom_call" | custom-call | flops 2000000000 | tf_op jit(solution)/shard_map/fine_backward/pallas_call | solution.py:23
  37.6 0.1 collective-permute-start.10
  37.8 1.3 %feature_step.1 = bf16[16,64,128]{2,1,0:T(8,128)(2,1)} custom-call(bf16[18,64,384]{2,1,0:T(8,128)(2,1)S(1)} %get-tuple-element.106.first3, bf16[256,1536]{1,0:T(8,128)(2,1)S(1)} %get-tuple-element.107.back_w), custom_call_target="tpu_custom_call" | custom-call | flops 1000000000 | tf_op jit(solution)/shard_map/feature_step/pallas_call | solution.py:23
  39.1 0.2 collective-permute-done.10.got_f
  39.3 0.2 scatter_core.1
  39.5 22.9 %all_to_all.20.got = bf16[16,152,128]{2,1,0:T(8,128)(2,1)S(1)} all-to-all(bf16[16,152,128]{2,1,0:T(8,128)(2,1)S(1)} %scatter_core.1), channel_id=1, replica_groups={{0,8,32,40,64,72,96,104,128,136,160,168,192,200,224,232},{1,9,33,41,65,..., dimensions={0} | all-to-all | bytes 1245184 | tf_op jit(solution)/shard_map/all_to_all | solution.py:563
  62.3 0.1 scatter_plane.1
  62.4 11.3 %all_to_all.21.got = bf16[8,24,128]{2,1,0:T(8,128)(2,1)S(1)} all-to-all(bf16[8,24,128]{2,1,0:T(8,128)(2,1)S(1)} %scatter_plane.1), channel_id=1, replica_groups={{0,1,2,3,4,5,6,7},{8,9,10,11,12,13,14,15},{16,17,18,19,20,21,22,23},{24..., dimensions={0} | all-to-all | bytes 98304 | tf_op jit(solution)/shard_map/all_to_all | solution.py:569
  73.7 10.0 %all_to_all.22.got = bf16[16,24,128]{2,1,0:T(8,128)(2,1)S(1)} all-to-all(bf16[16,24,128]{2,1,0:T(8,128)(2,1)S(1)} %scatter_column.1), channel_id=1, replica_groups=mesh['row'=16,'col'=16] {'col'}, dimensions={0} | all-to-all | bytes 196608 | tf_op jit(solution)/shard_map/all_to_all | solution.py:573
  83.7 0.6 gather_column.1
  84.3 11.1 %all_to_all.23.mine = bf16[16,72,128]{2,1,0:T(8,128)(2,1)S(1)} all-to-all(bf16[16,72,128]{2,1,0:T(8,128)(2,1)S(1)} %get-tuple-element.109), channel_id=1, replica_groups={{0,8,32,40,64,72,96,104,128,136,160,168,192,200,224,232},{1,9,33,41,65,..., dimensions={0} | all-to-all | bytes 589824 | tf_op jit(solution)/shard_map/all_to_all | solution.py:563
  95.4 5.4 %collective-permute-start.11 = (bf16[16,72,128]{2,1,0:T(8,128)(2,1)S(1)}, bf16[16,72,128]{2,1,0:T(8,128)(2,1)S(1)}, u32[]{:S(2)}, u32[]{:S(2)}) collective-permute-start(bf16[16,72,128]{2,1,0:T(8,128)(2,1)S(1)} %all_to_all.23.mine), channel_id=1, source_target_pairs={{0,16},{16,0},{32,48},{48,32},{64,80},{80,64},{96,112},{112,96},{1... | collective-permute-start | bytes 884744 | tf_op jit(solution)/shard_map/ppermute | solution.py:548
  100.8 0.9 blend.1
  101.7 0.3 collective-permute-done.11.other
  102.0 1.6 %finish.1 = (f32[8,144,128]{2,1,0:T(8,128)}, f32[8,144,128]{2,1,0:T(8,128)}) custom-call(s32[6]{0:T(128)S(1)} %stack.19.meta, bf16[16,72,128]{2,1,0:T(8,128)(2,1)S(1)} %all_to_all.23.mine, bf16[16,72,128]{2,1,0:T(8,128)(2,1)S(1)} %collective-permute-done.11.other), custom_call_target="tpu_custom_call" | custom-call | tf_op jit(solution)/shard_map/finish/pallas_call | solution.py:23
  (15 shorter events, 0.2 us)
Async XLA Ops:
  2.4 8.5 %collective-permute-start = (bf16[16,48,128]{2,1,0:T(8,128)(2,1)S(1)}, bf16[16,48,128]{2,1,0:T(8,128)(2,1)S(1)}, u32[]{:S(2)}, u32[]{:S(2)}) collective-permute-start(bf16[16,48,128]{2,1,0:T(8,128)(2,1)S(1)} %get-tuple-element.67), channel_id=1, source_target_pairs={{0,1},{1,0},{2,3},{3,2},{4,5},{5,4},{6,7},{7,6},{8,9},{9,8},{10,11... | collective-permute-start | bytes 589832 | tf_op jit(solution)/shard_map/ppermute | solution.py:548
  5.0 6.0 %collective-permute-start.1 = (bf16[16,48,128]{2,1,0:T(8,128)(2,1)S(1)}, bf16[16,48,128]{2,1,0:T(8,128)(2,1)S(1)}, u32[]{:S(2)}, u32[]{:S(2)}) collective-permute-start(bf16[16,48,128]{2,1,0:T(8,128)(2,1)S(1)} %get-tuple-element.68), channel_id=1, source_target_pairs={{1,2},{2,1},{3,4},{4,3},{5,6},{6,5},{7,8},{8,7},{9,10},{10,9},{11,... | collective-permute-start | bytes 589832 | tf_op jit(solution)/shard_map/ppermute | solution.py:554
  5.7 5.3 %collective-permute-start.2 = (bf16[160,128]{1,0:T(8,128)(2,1)S(1)}, bf16[160,128]{1,0:T(8,128)(2,1)S(1)}, u32[]{:S(2)}, u32[]{:S(2)}) collective-permute-start(bf16[160,128]{1,0:T(8,128)(2,1)S(1)} %own_slab.1.own), channel_id=1, source_target_pairs={{0,128},{16,144},{32,160},{48,176},{64,192},{80,208},{96,224},{112... | collective-permute-start | bytes 122888 | tf_op jit(solution)/shard_map/ppermute | solution.py:548
  11.7 15.6 %collective-permute-start.3 = (bf16[1264,128]{1,0:T(8,128)(2,1)S(1)}, bf16[1264,128]{1,0:T(8,128)(2,1)S(1)}, u32[]{:S(2)}, u32[]{:S(2)}) collective-permute-start(bf16[1264,128]{1,0:T(8,128)(2,1)S(1)} %get-tuple-element.72), channel_id=1, source_target_pairs={{0,16},{16,0},{32,48},{48,32},{64,80},{80,64},{96,112},{112,96},{1... | collective-permute-start | bytes 970760 | tf_op jit(solution)/shard_map/ppermute | solution.py:548
  13.0 14.3 %collective-permute-start.4 = (bf16[1264,128]{1,0:T(8,128)(2,1)S(1)}, bf16[1264,128]{1,0:T(8,128)(2,1)S(1)}, u32[]{:S(2)}, u32[]{:S(2)}) collective-permute-start(bf16[1264,128]{1,0:T(8,128)(2,1)S(1)} %get-tuple-element.73), channel_id=1, source_target_pairs={{16,32},{32,16},{48,64},{64,48},{80,96},{96,80},{112,128},{128,112... | collective-permute-start | bytes 970760 | tf_op jit(solution)/shard_map/ppermute | solution.py:554
  16.0 11.1 %collective-permute-start.7 = (bf16[2,160,128]{2,1,0:T(8,128)(2,1)S(1)}, bf16[2,160,128]{2,1,0:T(8,128)(2,1)S(1)}, u32[]{:S(2)}, u32[]{:S(2)}) collective-permute-start(bf16[2,160,128]{2,1,0:T(8,128)(2,1)S(1)} %get-tuple-element.91.refs_0_.near0), channel_id=1, source_target_pairs={{0,96},{16,112},{32,64},{48,80},{64,32},{80,48},{96,0},{112,16},{1... | collective-permute-start | bytes 245768 | tf_op jit(solution)/shard_map/ppermute | solution.py:548
  20.2 6.9 %collective-permute-start.6 = (bf16[2,160,128]{2,1,0:T(8,128)(2,1)S(1)}, bf16[2,160,128]{2,1,0:T(8,128)(2,1)S(1)}, u32[]{:S(2)}, u32[]{:S(2)}) collective-permute-start(bf16[2,160,128]{2,1,0:T(8,128)(2,1)S(1)} %get-tuple-element.91.refs_0_.near0), channel_id=1, source_target_pairs={{0,64},{16,80},{32,96},{48,112},{64,0},{80,16},{96,32},{112,48},{1... | collective-permute-start | bytes 245768 | tf_op jit(solution)/shard_map/ppermute | solution.py:548
  20.2 6.9 %collective-permute-start.5 = (bf16[2,160,128]{2,1,0:T(8,128)(2,1)S(1)}, bf16[2,160,128]{2,1,0:T(8,128)(2,1)S(1)}, u32[]{:S(2)}, u32[]{:S(2)}) collective-permute-start(bf16[2,160,128]{2,1,0:T(8,128)(2,1)S(1)} %get-tuple-element.91.refs_0_.near0), channel_id=1, source_target_pairs={{0,32},{16,48},{32,0},{48,16},{64,96},{80,112},{96,64},{112,80},{1... | collective-permute-start | bytes 245768 | tf_op jit(solution)/shard_map/ppermute | solution.py:548
  27.2 3.5 %collective-permute-start.8 = (bf16[4,2,160,128]{3,2,1,0:T(8,128)(2,1)S(1)}, bf16[4,2,160,128]{3,2,1,0:T(8,128)(2,1)S(1)}, u32[]{:S(2)}, u32[]{:S(2)}) collective-permute-start(bf16[4,2,160,128]{3,2,1,0:T(8,128)(2,1)S(1)} %stack_eight.1), channel_id=1, source_target_pairs={{0,16},{16,0},{32,48},{48,32},{64,80},{80,64},{96,112},{112,96},{1... | collective-permute-start | bytes 983048 | tf_op jit(solution)/shard_map/ppermute | solution.py:548
  34.2 5.1 %collective-permute-start.9 = (bf16[8,160,128]{2,1,0:T(8,128)(2,1)S(1)}, bf16[8,160,128]{2,1,0:T(8,128)(2,1)S(1)}, u32[]{:S(2)}, u32[]{:S(2)}) collective-permute-start(bf16[8,160,128]{2,1,0:T(8,128)(2,1)S(1)} %get-tuple-element.104), channel_id=1, source_target_pairs={{0,16},{16,0},{32,48},{48,32},{64,80},{80,64},{96,112},{112,96},{1... | collective-permute-start | bytes 983048 | tf_op jit(solution)/shard_map/ppermute | solution.py:548
  37.6 1.7 %collective-permute-start.10 = (bf16[8,144,128]{2,1,0:T(8,128)(2,1)S(1)}, bf16[8,144,128]{2,1,0:T(8,128)(2,1)S(1)}, u32[]{:S(2)}, u32[]{:S(2)}) collective-permute-start(bf16[8,144,128]{2,1,0:T(8,128)(2,1)S(1)} %get-tuple-element.105), channel_id=1, source_target_pairs={{0,16},{16,0},{32,48},{48,32},{64,80},{80,64},{96,112},{112,96},{1... | collective-permute-start | bytes 884744 | tf_op jit(solution)/shard_map/ppermute | solution.py:548
  95.4 6.6 %collective-permute-start.11 = (bf16[16,72,128]{2,1,0:T(8,128)(2,1)S(1)}, bf16[16,72,128]{2,1,0:T(8,128)(2,1)S(1)}, u32[]{:S(2)}, u32[]{:S(2)}) collective-permute-start(bf16[16,72,128]{2,1,0:T(8,128)(2,1)S(1)} %all_to_all.23.mine), channel_id=1, source_target_pairs={{0,16},{16,0},{32,48},{48,32},{64,80},{80,64},{96,112},{112,96},{1... | collective-permute-start | bytes 884744 | tf_op jit(solution)/shard_map/ppermute | solution.py:548
